TPU v7x, 32 devices: a whole 2x2x4 slice. The times are simulated.
32 devices in a mesh: groups: 2 (over x), row: 4 (over y, core), col: 4 (over z).
Axes of the slice: x: 2, y: 2, z: 4, core: 2. Of those that a mesh axis runs over, the one named last changes fastest.
Arguments:
- state_blocks: bfloat16 [128, 64, 1024], P(('groups', 'row')), parts along dimension 0, may hold values from -6 to 6
- left_env: bfloat16 [64, 64, 1536], P(('groups', 'row'), None, 'col'), parts along dimension 0, may hold values from -0.75 to 0.75
- right_env: bfloat16 [64, 64, 1536], P(('groups', 'row')), parts along dimension 0, may hold values from -0.15625 to 0.15625
- mpo_tensor: bfloat16 [24, 24, 256], replicated, may hold values from -0.3125 to 0.3125
- block_left: int32 [128], P(('groups', 'row')), parts along dimension 0, may hold values from 0 to 7
- block_owner: int32 [128, 1], P(('groups', 'row')), parts along dimension 0, may hold values from 0 to 3; in each aligned block of 16 rows (0 to 15, 16 to 31, ...) at most 8 rows name the same one
- block_sub: int32 [128], P(('groups', 'row')), parts along dimension 0, may hold values from 0 to 7
Outputs:
- applied_blocks: bfloat16 [128, 64, 1024], P(('groups', 'row'), None, 'col'), parts along dimension 0
There are 2 independent parts, one for each index of `groups`. A program takes and returns all parts, laid end to end along the dimension named above; an argument that names none is the same for every part. Nothing has to cross between parts.
Inputs may be any that keep to these rules, and one draw needn't show every extreme that they name: `block_owner`: among the 16 blocks of one row index, no owner is named by more than 8 blocks, a bound that some block reaches.
All inputs are finite; a program needn't handle non-finite values.
Results may differ from a plain program's by a relative error of at most 0.0057.
Values may be sent and summed in bfloat16 or wider, within the bound.
No kernel may reach another device: no remote copies, remote signals or barrier semaphores. Data moves between devices by JAX's collectives and lax.ppermute only.
A program may use at most 256 MiB of HBM per device.

v0:
```python
import jax
import jax.numpy as jnp
from jax import lax
from jax.sharding import PartitionSpec as P


def pick_sectors(selector, sector_table):
    onehot = (
        selector[:, None] == jnp.arange(sector_table.shape[0], dtype=jnp.int32)[None, :]
    ).astype(jnp.bfloat16)
    picked = jnp.einsum("pk,kxc->pxc", onehot, sector_table, preferred_element_type=jnp.float32)
    return picked.astype(jnp.bfloat16)


def mix_channels(blocks, left_full, mpo_columns):
    block_size = blocks.shape[1]
    state_share = mpo_columns.shape[0]
    mpo_width = mpo_columns.shape[2]

    def single(operands):
        block, left_rows = operands
        left_flat = left_rows.reshape(block_size * mpo_width, block_size)
        first = jnp.dot(left_flat, block, preferred_element_type=jnp.float32).astype(jnp.bfloat16)
        first = first.reshape(block_size, mpo_columns.shape[1], block_size)
        pieces = []
        for target in range(state_share):
            mixed = jnp.einsum(
                "xkb,kv->xbv", first, mpo_columns[target], preferred_element_type=jnp.float32
            )
            pieces.append(mixed.astype(jnp.bfloat16))
        return jnp.stack(pieces, axis=0)

    return lax.map(single, (blocks, left_full))


def apply_right(arrived, sub_index, right_env):
    slot_count = arrived.shape[0]
    state_share = arrived.shape[1]
    block_size = right_env.shape[1]
    mpo_width = right_env.shape[2] // block_size
    right_pick = pick_sectors(sub_index, right_env).reshape(
        slot_count, block_size * mpo_width, block_size
    )
    flat_in = arrived.reshape(slot_count, state_share, block_size, block_size * mpo_width)
    result = jnp.einsum("qtxk,qky->qtxy", flat_in, right_pick, preferred_element_type=jnp.float32)
    return result.astype(jnp.bfloat16)


def shards(state_blocks, left_env, right_env, mpo_tensor, block_left, block_owner, block_sub):
    row_count = lax.axis_size("row")
    col_count = lax.axis_size("col")
    block_count = state_blocks.shape[0]
    block_size = state_blocks.shape[1]
    local_states = state_blocks.shape[2] // block_size
    mpo_width = mpo_tensor.shape[0]
    state_share = local_states // col_count
    mpo_full = mpo_tensor.reshape(mpo_width, mpo_width, local_states, local_states)
    mpo_local = lax.dynamic_slice_in_dim(
        mpo_full, lax.axis_index("col") * state_share, state_share, 2
    )
    mpo_columns = jnp.transpose(mpo_local, (2, 0, 3, 1)).reshape(
        state_share, mpo_width * local_states, mpo_width
    )
    full_env = lax.all_gather(left_env, "col", axis=2, tiled=True)
    capacity = max(2, (2 * block_count + row_count - 1) // row_count)
    slot_count = row_count * capacity
    owners = block_owner[:, 0]
    matches = owners[:, None] == owners[None, :]
    before = jnp.arange(block_count)[None, :] < jnp.arange(block_count)[:, None]
    ranking = jnp.sum(jnp.logical_and(matches, before), axis=1)
    targets = owners * capacity + ranking
    placed_mask = jnp.arange(slot_count, dtype=jnp.int32)[:, None] == targets[None, :]
    has_block = jnp.any(placed_mask, axis=1)
    sub_slot = jnp.where(
        has_block, jnp.sum(jnp.where(placed_mask, block_sub[None, :], 0), axis=1), -1
    )
    placer = placed_mask.astype(jnp.bfloat16)
    channels = mix_channels(state_blocks, pick_sectors(block_left, full_env), mpo_columns)
    outgoing = jnp.einsum(
        "qp,ptxbv->qtxbv", placer, channels, preferred_element_type=jnp.float32
    ).astype(jnp.bfloat16)
    arrived, sub_in = (
        lax.all_to_all(outgoing, "row", split_axis=0, concat_axis=0, tiled=True),
        lax.all_to_all(sub_slot, "row", split_axis=0, concat_axis=0, tiled=True),
    )
    finished = apply_right(arrived, sub_in, right_env)
    returned = lax.all_to_all(finished, "row", split_axis=0, concat_axis=0, tiled=True)
    result = jnp.einsum("qp,qtxy->pxty", placer, returned, preferred_element_type=jnp.float32)
    return result.astype(jnp.bfloat16).reshape(block_count, block_size, state_share * block_size)


def solution(mesh):
    placed = (
        P(("groups", "row"), None, None),
        P(("groups", "row"), None, "col"),
        P(("groups", "row"), None, None),
        P(),
        P(("groups", "row")),
        P(("groups", "row"), None),
        P(("groups", "row")),
    )
    return jax.shard_map(
        shards,
        mesh=mesh,
        in_specs=placed,
        out_specs=P(("groups", "row"), None, "col"),
        check_vma=False,
    )
```

profile of v0, /device:TPU:0, one launch (start us, length us, event | category | flops | bytes accessed | tf_op | source)
XLA Modules:
  0.0 998.5 jit_solution(17439726431589568828)
XLA Ops:
  21.9 26.7 %all-gather.2.cloned.1.call-done = bf16[8,64,1536]{2,0,1:T(8,128)(2,1)} async-done(((bf16[8,64,384]{2,0,1:T(8,128)(2,1)}), bf16[8,64,1536]{2,0,1:T(8,128)(2,1)}) %all-gather.2.cloned.1.call-update) | async-done | bytes 1572880 | tf_op jit(solution)/shard_map/all_gather | solution.py:64
  54.5 363.7 %while.10 = (s32[]{:T(128)}, bf16[16,4,64,64,24]{3,4,2,1,0:T(8,128)(2,1)}, bf16[16,64,1536]{2,1,0:T(8,128)(2,1)}, bf16[16,64,1024]{2,1,0:T(8,128)(2,1)}, bf16[4,384,24]{1,2,0:T(8,128)(2,1)S(1)}, /*index=5*/s32[]{:T(128)}) while((s32[]{:T(128)}, bf16[16,4,64,64,24]{3,4,2,1,0:T(8,128)(2,1)}, bf16[16,64,1536]{2,1,0:T(8,128)(2,1)}, ...), condition=%wide.region_2.3_spmd, body=%wide.region_1.0_spmd.sunk | while | flops 508428288 | bytes 48374884 | solution.py:33
  59.2 9.2 reshape.86
  81.9 9.2 reshape.86
  104.6 9.2 reshape.86
  127.4 9.2 reshape.86
  150.1 9.2 reshape.86
  172.8 9.2 reshape.86
  195.6 9.2 reshape.86
  218.3 9.2 reshape.86
  241.0 9.2 reshape.86
  263.8 9.2 reshape.86
  286.5 9.2 reshape.86
  309.2 9.2 reshape.86
  377.5 9.2 reshape.86
  418.2 28.6 %convolution_convert_fusion.5 = bf16[32,4,64,64,24]{3,0,4,2,1:T(8,128)(2,1)} fusion(bf16[16,4,64,64,24]{3,4,2,1,0:T(8,128)(2,1)} %get-tuple-element.32, s32[16]{0:T(128)S(1)} %multiply_add_fusion), kind=kOutput, calls=%fused_computation.23 | convolution fusion | flops 415236608 | bytes 37748800 | tf_op jit(solution)/shard_map/qp,ptxbv->qtxbv/dot_general | solution.py:79
  446.8 33.8 %copy.81 = bf16[32,4,64,64,24]{3,4,2,1,0:T(8,128)(2,1)} copy(bf16[32,4,64,64,24]{3,0,4,2,1:T(8,128)(2,1)} %convolution_convert_fusion.5) | data formatting | bytes 50331648 | tf_op jit(solution)/shard_map/convert_element_type | solution.py:81
  480.6 36.7 %reshape.79 = bf16[4,2,1572864]{2,1,0:T(2,128)(2,1)} reshape(bf16[32,4,64,24,64]{4,3,2,1,0:T(8,128)(2,1)} %bitcast.110) | data formatting | bytes 50331648
  536.1 16.3 %reshape.59 = bf16[32,1536,64]{2,1,0:T(8,128)(2,1)} reshape(bf16[32,64,1536]{2,1,0:T(8,128)(2,1)} %copy.54) | data formatting | bytes 12582912 | tf_op jit(solution)/shard_map/reshape | solution.py:41
  552.4 246.6 %all-to-all-done = bf16[4,2,1572864]{2,1,0:T(2,128)(2,1)} async-done(((bf16[4,2,1572864]{2,1,0:T(2,128)(2,1)}), bf16[4,2,1572864]{2,1,0:T(2,128)(2,1)}, u32[]{:S(2)}, u32[]{:S(2)}) %all-to-all-start) | async-done | bytes 25165856 | tf_op jit(solution)/shard_map/all_to_all | solution.py:83
  798.9 68.6 %reshape.80 = bf16[32,4,64,24,64]{4,3,2,1,0:T(8,128)(2,1)} reshape(bf16[4,2,1572864]{2,1,0:T(2,128)(2,1)} %all-to-all-done) | data formatting | bytes 50331648
  867.5 68.8 %copy.51 = bf16[32,4,64,64,24]{2,4,3,1,0:T(8,128)(2,1)} copy(bf16[32,4,64,64,24]{3,4,2,1,0:T(8,128)(2,1)} %bitcast.111) | data formatting | bytes 50331648 | tf_op jit(solution)/shard_map/all_to_all | solution.py:83
  936.3 24.4 %fusion.21 = bf16[32,4,64,64]{3,2,1,0:T(8,128)(2,1)} fusion(bf16[32,4,64,1536]{2,3,1,0:T(8,128)(2,1)} %bitcast.112, bf16[32,1536,64]{2,1,0:T(8,128)(2,1)} %reshape.59), kind=kOutput, calls=%fused_computation.31 | convolution fusion | flops 1611137024 | bytes 32505856 | tf_op jit(solution)/shard_map/qtxk,qky->qtxy/dot_general | solution.py:45
  964.1 17.6 %all_to_all.16 = bf16[4,2,65536]{2,1,0:T(2,128)(2,1)} all-to-all(bf16[4,2,65536]{2,1,0:T(2,128)(2,1)S(1)} %reshape.81), channel_id=1, replica_groups=mesh['groups'=2,'row'=4,'col'=4] {'row'}, dimensions={0} | all-to-all | bytes 2097152 | tf_op jit(solution)/shard_map/all_to_all | solution.py:87
  (196 shorter events, 296.9 us)
Async XLA Ops:
  6.5 521.4 %copy-start = (bf16[8,64,1536]{2,1,0:T(8,128)(2,1)S(1)}, bf16[8,64,1536]{2,1,0:T(8,128)(2,1)}, u32[]{:S(2)}) copy-start(bf16[8,64,1536]{2,1,0:T(8,128)(2,1)} %param.11) | copy-start | bytes 4718596
  6.5 42.1 %copy-start.2 = (s32[16]{0:T(128)S(1)}, s32[16]{0:T(128)}, u32[]{:S(2)}) copy-start(s32[16]{0:T(128)} %param.13) | copy-start | bytes 196
  6.5 42.1 %all-gather.2.cloned.1.call-start = ((), (), s32[]{:S(2)}) async-start(), calls=%async_computation.3 | async-start | bytes 1966080 | tf_op jit(solution)/shard_map/all_gather | solution.py:64
  11.8 505.6 %all-to-all-start.1 = ((s32[4,8,1]{1,2,0:T(1,128)}), s32[4,8,1]{1,2,0:T(1,128)}, u32[]{:S(2)}, u32[]{:S(2)}) async-start(s32[4,8,1]{1,2,0:T(1,128)} %bitcast.20), calls=%async_computation.1 | async-start | bytes 4096 | tf_op jit(solution)/shard_map/all_to_all | solution.py:84
  68.4 4.6 copy-start.1
  91.1 4.6 copy-start.1
  113.8 4.6 copy-start.1
  136.6 4.6 copy-start.1
  159.3 4.6 copy-start.1
  182.0 4.6 copy-start.1
  204.8 4.6 copy-start.1
  227.5 4.6 copy-start.1
  250.2 4.6 copy-start.1
  273.0 4.6 copy-start.1
  295.7 4.6 copy-start.1
  318.4 4.6 copy-start.1
  341.2 4.6 copy-start.1
  363.9 4.6 copy-start.1
  386.7 4.6 copy-start.1
  409.4 4.6 copy-start.1
  517.3 281.6 %all-to-all-start = ((bf16[4,2,1572864]{2,1,0:T(2,128)(2,1)}), bf16[4,2,1572864]{2,1,0:T(2,128)(2,1)}, u32[]{:S(2)}, u32[]{:S(2)}) async-start(bf16[4,2,1572864]{2,1,0:T(2,128)(2,1)} %reshape.79), calls=%async_computation | async-start | bytes 50331648 | tf_op jit(solution)/shard_map/all_to_all | solution.py:83
Sparse Core Ops, SparseCore 0:
  8.9 39.6 all-gather.1
where the time goes:
time: 1010 us; the launch traced here: 999 us
  local copies, waits for them, and re-layouts  431 us (43%)
  waiting for transfers between devices  273 us (27%)
  matrix products  223 us (22%)
  other arithmetic  27.3 us (3%)
  blocking collectives  17.6 us (2%)
  between operations  13.9 us (1%)
  starting transfers between devices  12.9 us (1%)
    all_to_all x1, waiting for transfers between devices, shards(): lax.all_to_all(outgoing, 'row', split_axis=0, concat_axis=0, tiled=True)  247 us
    reshape x16, local copies, waits for them, and re-layouts, single(): first = first.reshape(block_size, mpo_columns.shape[1], block_size)  147 us
    unnamed x9, local copies, waits for them, and re-layouts  115 us
    dot_general x64, matrix products, single(): jnp.einsum('xkb,kv->xbv', first, mpo_columns[target], preferred_element_t...  106 us
    all_to_all x1, local copies, waits for them, and re-layouts, shards(): lax.all_to_all(outgoing, 'row', split_axis=0, concat_axis=0, tiled=True)  68.8 us
    dot_general x16, matrix products, single(): jnp.dot(left_flat, block, preferred_element_type=jnp.float32)  55.9 us
    convert_element_type x1, local copies, waits for them, and re-layouts, shards(): outgoing = jnp.einsum('qp,ptxbv->qtxbv', placer, channels, preferred_elem...  33.8 us
    dot_general x1, matrix products, shards(): jnp.einsum('qp,ptxbv->qtxbv', placer, channels, preferred_element_type=jn...  28.6 us
  transfers between devices with their start and end apart: 3, of which 2 were waited for; matrix products, arithmetic and copies ran while one was open for 49% of the time, Pallas kernels for 0%

commit v1 on v0

v1 whole, which is shorter than its diff:
```python
import functools

import jax
import jax.numpy as jnp
from jax import lax
from jax.experimental import pallas as pl
from jax.experimental.pallas import tpu as pltpu
from jax.sharding import PartitionSpec as P


def route_kernel(cols, rows, near, left_ref, owner_ref, sub_ref, env_ref, send_ref, order_ref, want_ref, slot_ref, sem):
    count = left_ref.shape[0]
    for owner in range(rows):
        for slot in range(near):
            want_ref[owner, slot] = 0
    owners = [owner_ref[p] for p in range(count)]
    copies = []
    mine = lax.axis_index("col")
    for p in range(count):
        rank = jnp.int32(0)
        first = jnp.int32(0)
        for other in range(count):
            less = (owners[other] < owners[p]).astype(jnp.int32)
            first = first + less
            if other < p:
                rank = rank + (owners[other] == owners[p]).astype(jnp.int32)
        place = first + rank
        col = lax.rem(place, cols)
        step = lax.div(place, cols)
        order_ref[place] = p
        start_col = lax.rem(first, cols)
        offset = lax.rem(col - start_col + cols, cols)
        slot = lax.div(rank - offset, cols)
        slot_ref[place] = owners[p] * near + slot

        @pl.when(col == mine)
        def _():
            want_ref[owners[p], slot] = sub_ref[p]

        copy = pltpu.make_async_copy(env_ref.at[left_ref[p]], send_ref.at[col, step], sem.at[p])
        copy.start()
        copies.append(copy)
    for copy in copies:
        copy.wait()


def route(block_left, owners, block_sub, left_env, rows, cols, near):
    count = block_left.shape[0]
    size, width = left_env.shape[1:]
    smem = pl.BlockSpec(memory_space=pltpu.SMEM)
    hbm = pl.BlockSpec(memory_space=pl.ANY)
    return pl.pallas_call(
        functools.partial(route_kernel, cols, rows, near),
        out_shape=(
            jax.ShapeDtypeStruct((cols, count // cols, size, width), left_env.dtype),
            jax.ShapeDtypeStruct((count,), jnp.int32),
            jax.ShapeDtypeStruct((rows, near), jnp.int32),
            jax.ShapeDtypeStruct((count,), jnp.int32),
        ),
        in_specs=[smem, smem, smem, hbm],
        out_specs=(hbm, smem, smem, smem),
        scratch_shapes=[pltpu.SemaphoreType.DMA((count,))],
        name="route",
    )(block_left, owners, block_sub, left_env)


def pick_kernel(want_ref, env_ref, send_ref, sem):
    rows, near = want_ref.shape
    copies = []
    for row in range(rows):
        for slot in range(near):
            copy = pltpu.make_async_copy(
                env_ref.at[want_ref[row, slot]], send_ref.at[row, slot], sem.at[row * near + slot]
            )
            copy.start()
            copies.append(copy)
    for copy in copies:
        copy.wait()


def pick(wanted, right_env):
    rows, near = wanted.shape
    return pl.pallas_call(
        pick_kernel,
        out_shape=jax.ShapeDtypeStruct((rows, near) + right_env.shape[1:], right_env.dtype),
        in_specs=[pl.BlockSpec(memory_space=pltpu.SMEM), pl.BlockSpec(memory_space=pl.ANY)],
        out_specs=pl.BlockSpec(memory_space=pl.ANY),
        scratch_shapes=[pltpu.SemaphoreType.DMA((rows * near,))],
        name="pick",
    )(wanted, right_env)


def halves(tile, low):
    swapped = pltpu.roll(tile, tile.shape[1] // 2, 1)
    zero = jnp.zeros_like(tile)
    return (
        jnp.where(low, tile, zero),
        jnp.where(low, zero, swapped),
        jnp.where(low, swapped, zero),
        jnp.where(low, zero, tile),
    )


def apply_kernel(
    states, chunk, order_ref, slot_ref, block_ref, left_ref, right_ref, mpo_ref, out_ref,
    left_rows, state_diag, right_diag, mixed, result,
):
    size = block_ref.shape[1]
    half = size // 2
    lanes = 2 * size
    width = mpo_ref.shape[0] // states
    cols = left_ref.shape[0]
    share = width // cols
    low = lax.broadcasted_iota(jnp.int32, (size, lanes), 1) < size

    for v in range(0, width, 2):
        tile = right_ref[0, 0, :, v * size : (v + 2) * size].astype(jnp.float32)
        parts = halves(tile, low)
        for i in range(4):
            at = v * lanes + i * size
            right_diag[at : at + size, :] = parts[i].astype(jnp.bfloat16)
    for s in range(0, states, 2):
        tile = block_ref[0, :, s * size : (s + 2) * size].astype(jnp.float32)
        parts = halves(tile, low)
        for i in range(4):
            row, col = (i % 2) * size, (s + i // 2) * lanes
            state_diag[row : row + size, col : col + lanes] = parts[i].astype(jnp.bfloat16)
    for c in range(cols):
        for k in range(share):
            w = c * share + k
            piece = left_ref[c, 0, :, k * size : (k + 1) * size].astype(jnp.float32)
            both = jnp.concatenate([piece[:half], piece[half:]], axis=1)
            left_rows[pl.ds(w, half, stride=width), :] = both

    for start in range(0, half, chunk):
        rows = left_rows[start * width : (start + chunk) * width, :].astype(jnp.bfloat16)
        first = jnp.dot(rows, state_diag[...], preferred_element_type=jnp.float32)
        columns = []
        for x in range(chunk):
            one = first[x * width : (x + 1) * width, :]
            columns.append(
                jnp.concatenate(
                    [one[:, s * lanes : (s + 1) * lanes] for s in range(states)], axis=0
                ).astype(jnp.bfloat16)
            )
        gathered = jnp.concatenate(columns, axis=1)
        channels = jnp.dot(mpo_ref[...], gathered, preferred_element_type=jnp.float32).astype(jnp.bfloat16)
        for x in range(chunk):
            for v in range(width):
                mixed[(start + x) * states : (start + x + 1) * states, v * lanes : (v + 1) * lanes] = channels[
                    v * states : (v + 1) * states, x * lanes : (x + 1) * lanes
                ]
    result[...] = jnp.dot(mixed[...], right_diag[...], preferred_element_type=jnp.float32)
    low = low[:half]
    per = states // cols
    for t in range(0, states, 2):
        one = result[pl.ds(t, half, stride=states), :]
        two = result[pl.ds(t + 1, half, stride=states), :]
        upper = jnp.where(low, one, pltpu.roll(two, size, 1))
        lower = jnp.where(low, pltpu.roll(one, size, 1), two)
        at = (t % per) * size
        out_ref[t // per, 0, :half, at : at + lanes] = upper.astype(jnp.bfloat16)
        out_ref[t // per, 0, half:, at : at + lanes] = lower.astype(jnp.bfloat16)


def apply_blocks(order, slots, state_blocks, left, right, mpo_rows, states):
    cols, steps, size, share = left.shape
    near = right.shape[1]
    width = mpo_rows.shape[0] // states
    half, lanes = size // 2, 2 * size
    chunk = 8
    grid_spec = pltpu.PrefetchScalarGridSpec(
        num_scalar_prefetch=2,
        grid=(steps,),
        in_specs=[
            pl.BlockSpec((1, size, states * size), lambda k, o, s: (o[k], 0, 0)),
            pl.BlockSpec((cols, 1, size, share), lambda k, o, s: (0, k, 0, 0)),
            pl.BlockSpec((1, 1, size, width * size), lambda k, o, s: (s[k] // near, s[k] % near, 0, 0)),
            pl.BlockSpec(mpo_rows.shape, lambda k, o, s: (0, 0)),
        ],
        out_specs=pl.BlockSpec((cols, 1, size, states // cols * size), lambda k, o, s: (0, k, 0, 0)),
        scratch_shapes=[
            pltpu.VMEM((half * width, lanes), jnp.float32),
            pltpu.VMEM((lanes, states * lanes), jnp.bfloat16),
            pltpu.VMEM((width * lanes, lanes), jnp.bfloat16),
            pltpu.VMEM((half * states, width * lanes), jnp.bfloat16),
            pltpu.VMEM((half * states, lanes), jnp.float32),
        ],
    )
    return pl.pallas_call(
        functools.partial(apply_kernel, states, chunk),
        out_shape=jax.ShapeDtypeStruct((cols, steps, size, states // cols * size), jnp.bfloat16),
        grid_spec=grid_spec,
        compiler_params=pltpu.CompilerParams(vmem_limit_bytes=40 << 20),
        name="apply",
    )(order, slots, state_blocks, left, right, mpo_rows)


def place_kernel(order_ref, came_ref, out_ref, sem):
    cols, steps = came_ref.shape[:2]
    copies = []
    for col in range(cols):
        for step in range(steps):
            place = step * cols + col
            copy = pltpu.make_async_copy(came_ref.at[col, step], out_ref.at[order_ref[place]], sem.at[place])
            copy.start()
            copies.append(copy)
    for copy in copies:
        copy.wait()


def place_blocks(order, came):
    count = order.shape[0]
    return pl.pallas_call(
        place_kernel,
        out_shape=jax.ShapeDtypeStruct((count,) + came.shape[2:], came.dtype),
        in_specs=[pl.BlockSpec(memory_space=pltpu.SMEM), pl.BlockSpec(memory_space=pl.ANY)],
        out_specs=pl.BlockSpec(memory_space=pl.ANY),
        scratch_shapes=[pltpu.SemaphoreType.DMA((count,))],
        name="place",
    )(order, came)


def shards(state_blocks, left_env, right_env, mpo_tensor, block_left, block_owner, block_sub):
    rows = lax.axis_size("row")
    cols = lax.axis_size("col")
    count, size = state_blocks.shape[:2]
    states = state_blocks.shape[2] // size
    width = mpo_tensor.shape[0]
    most = max(2, (2 * count + rows - 1) // rows)
    near = -(-most // cols)

    mpo_rows = jnp.transpose(mpo_tensor.reshape(width, width, states, states), (1, 2, 3, 0)).reshape(
        width * states, states * width
    )
    left_out, order, wanted, slots = route(block_left, block_owner[:, 0], block_sub, left_env, rows, cols, near)
    asked = lax.all_to_all(wanted, "row", split_axis=0, concat_axis=0, tiled=True)
    left = lax.all_to_all(left_out, "col", split_axis=0, concat_axis=0, tiled=True)
    right = lax.all_to_all(pick(asked, right_env), "row", split_axis=0, concat_axis=0, tiled=True)
    mine = lax.axis_index("col")
    my_order = lax.dynamic_slice_in_dim(order.reshape(-1, cols), mine, 1, 1)[:, 0]
    my_slots = lax.dynamic_slice_in_dim(slots.reshape(-1, cols), mine, 1, 1)[:, 0]
    done = apply_blocks(my_order, my_slots, state_blocks, left, right, mpo_rows, states)
    came = lax.all_to_all(done, "col", split_axis=0, concat_axis=0, tiled=True)
    return place_blocks(order, came)


def solution(mesh):
    placed = (
        P(("groups", "row"), None, None),
        P(("groups", "row"), None, "col"),
        P(("groups", "row"), None, None),
        P(),
        P(("groups", "row")),
        P(("groups", "row"), None),
        P(("groups", "row")),
    )
    return jax.shard_map(
        shards,
        mesh=mesh,
        in_specs=placed,
        out_specs=P(("groups", "row"), None, "col"),
        check_vma=False,
    )
```

time: 1010 us -> 169 us (0.17); the launches traced: 999 us -> 168 us
  local copies, waits for them, and re-layouts: 431 us -> 12.1 us
  waiting for transfers between devices: 273 us -> 9.49 us
  matrix products: 223 us -> 0 us
  Pallas kernels: 0 us -> 110 us
  other arithmetic: 27.3 us -> 0 us
  between operations: 13.9 us -> 0.09 us
  blocking collectives: 17.6 us -> 27.8 us
    all_to_all x2, waiting for transfers between devices: 247 us -> 9.49 us  [the longest x1 9.49 us: shards(): lax.all_to_all(pick(asked, right_env), 'row', split_axis=0, concat_axis=0...]
    dot_general x85 -> x0, matrix products: 223 us -> none  [the longest x64 106 us: single(): jnp.einsum('xkb,kv->xbv', first, mpo_columns[target], preferred_element_t...]
    reshape x36 -> x4, local copies, waits for them, and re-layouts: 173 us -> 5.62 us  [the longest x1 2.81 us: shards(): jnp.transpose(mpo_tensor.reshape(width, width, states, states), (1, 2, 3,...]
    unnamed x9 -> x8, local copies, waits for them, and re-layouts: 115 us -> 1.61 us
    pallas_call x0 -> x4, Pallas kernels: none -> 110 us  [the longest x1 49.5 us: pick(): pl.pallas_call(pick_kernel, out_shape=jax.ShapeDtypeStruct((rows, near) +...]
    all_to_all x2 -> x0, local copies, waits for them, and re-layouts: 69.3 us -> none  [the longest x1 68.8 us: shards(): lax.all_to_all(outgoing, 'row', split_axis=0, concat_axis=0, tiled=True)]
    convert_element_type x3 -> x0, local copies, waits for them, and re-layouts: 40.7 us -> none  [the longest x1 33.8 us: shards(): outgoing = jnp.einsum('qp,ptxbv->qtxbv', placer, channels, preferred_elem...]
    all_gather x1 -> x0, waiting for transfers between devices: 26.7 us -> none  [shards(): full_env = lax.all_gather(left_env, 'col', axis=2, tiled=True)]
  transfers between devices with their start and end apart: 3 -> 2, of which waited for: 2 -> 1; matrix products, arithmetic and copies ran while one was open for 49% -> 6% of each run, Pallas kernels for 0% -> 29%
where the time goes in v1:
time: 169 us; the launch traced here: 168 us
  Pallas kernels  110 us (65%)
  blocking collectives  27.8 us (16%)
  local copies, waits for them, and re-layouts  12.1 us (7%)
  waiting for transfers between devices  9.49 us (6%)
  starting transfers between devices  9.09 us (5%)
    pallas_call x1, Pallas kernels, pick(): pl.pallas_call(pick_kernel, out_shape=jax.ShapeDtypeStruct((rows, near) +...  49.5 us
    pallas_call x1, Pallas kernels, route(): pl.pallas_call(functools.partial(route_kernel, cols, rows, near), out_sha...  26.4 us
    all_to_all x1, blocking collectives, shards(): came = lax.all_to_all(done, 'col', split_axis=0, concat_axis=0, tiled=True)  19.3 us
    pallas_call x1, Pallas kernels, place_blocks(): pl.pallas_call(place_kernel, out_shape=jax.ShapeDtypeStruct((count,) + ca...  17.8 us
    pallas_call x1, Pallas kernels, apply_blocks(): pl.pallas_call(functools.partial(apply_kernel, states, chunk), out_shape=...  16.1 us
    all_to_all x1, waiting for transfers between devices, shards(): lax.all_to_all(pick(asked, right_env), 'row', split_axis=0, concat_axis=0...  9.49 us
    all_to_all x1, blocking collectives, shards(): lax.all_to_all(wanted, 'row', split_axis=0, concat_axis=0, tiled=True)  8.48 us
    all_to_all x1, starting transfers between devices, shards(): lax.all_to_all(left_out, 'col', split_axis=0, concat_axis=0, tiled=True)  5.38 us
  transfers between devices with their start and end apart: 2, of which 1 were waited for; matrix products, arithmetic and copies ran while one was open for 6% of the time, Pallas kernels for 29%

profile of v1, /device:TPU:0, one launch (start us, length us, event | category | flops | bytes accessed | tf_op | source)
XLA Modules:
  0.0 168.3 jit_solution(435990646089901204)
XLA Ops:
  0.0 26.4 %route.1 = (bf16[4,4,64,384]{3,2,1,0:T(8,128)(2,1)}, s32[16]{0:T(128)}, s32[4,2]{1,0:T(4,128)}, s32[16]{0:T(128)}) custom-call(s32[16]{0:T(128)} %left_ref.1, s32[16]{0:T(128)} %bitcast.11, s32[16]{0:T(128)} %sub_ref.1, bf16[8,64,384]{2,1,0:T(8,128)(2,1)} %env_ref.2), custom_call_target="tpu_custom_call" | custom-call | tf_op jit(solution)/shard_map/route/pallas_call | solution.py:52
  26.4 8.5 %all_to_all.26 = s32[4,1,2]{2,1,0:T(1,128)} all-to-all(s32[4,1,2]{2,1,0:T(1,128)} %bitcast.10), channel_id=1, replica_groups=mesh['groups'=2,'row'=4,'col'=4] {'row'}, dimensions={0} | all-to-all | bytes 64 | tf_op jit(solution)/shard_map/all_to_all | solution.py:237
  34.9 5.4 %all-to-all-start = ((bf16[4,4,64,384]{3,2,1,0:T(8,128)(2,1)}), bf16[4,4,64,384]{3,2,1,0:T(8,128)(2,1)S(1)}, u32[]{:S(2)}, u32[]{:S(2)}) async-start(bf16[4,4,64,384]{3,2,1,0:T(8,128)(2,1)} %get-tuple-element.11), calls=%async_computation | async-start | bytes 1572864 | tf_op jit(solution)/shard_map/all_to_all | solution.py:238
  40.2 49.5 %pick.1 = bf16[4,2,64,1536]{3,2,1,0:T(8,128)(2,1)} custom-call(s32[4,2]{1,0:T(4,128)} %bitcast.9, bf16[8,64,1536]{2,1,0:T(8,128)(2,1)} %env_ref.3), custom_call_target="tpu_custom_call" | custom-call | tf_op jit(solution)/shard_map/pick/pallas_call | solution.py:83
  89.8 0.0 copy-start.3
  89.8 0.0 copy-start.2
  89.8 0.0 copy-start.1
  89.8 0.0 all-to-all-done.left_ref
  89.8 3.7 %all-to-all-start.2 = ((bf16[4,2,64,1536]{3,2,1,0:T(8,128)(2,1)}), bf16[4,2,64,1536]{3,2,1,0:T(8,128)(2,1)S(1)}, u32[]{:S(2)}, u32[]{:S(2)}) async-start(bf16[4,2,64,1536]{3,2,1,0:T(8,128)(2,1)} %pick.1), calls=%async_computation.2 | async-start | bytes 3145728 | tf_op jit(solution)/shard_map/all_to_all | solution.py:239
  93.5 0.0 copy-done.3
  93.5 0.1 reshape.15
  93.6 0.0 copy-done.2
  93.6 0.1 reshape.14
  93.7 0.0 copy-done.1
  93.7 2.7 %reshape.16 = bf16[24,24,16,16]{3,2,1,0:T(8,128)(2,1)} reshape(bf16[24,24,256]{2,1,0:T(8,128)(2,1)S(1)} %copy-done.1) | data formatting | bytes 589824 | tf_op jit(solution)/shard_map/reshape | solution.py:233
  96.3 4.7 %copy.18 = bf16[24,16,16,24]{3,2,1,0:T(8,128)(2,1)} copy(bf16[24,16,16,24]{2,1,0,3:T(8,128)(2,1)} %bitcast.8) | data formatting | bytes 589824 | tf_op jit(solution)/shard_map/transpose | solution.py:233
  101.0 2.8 %reshape.17.mpo_ref = bf16[384,384]{1,0:T(8,128)(2,1)S(1)} reshape(bf16[24,16,16,24]{3,2,1,0:T(8,128)(2,1)} %copy.18) | data formatting | bytes 589824 | tf_op jit(solution)/shard_map/reshape | solution.py:233
  103.9 0.2 dynamic-slice_reduce_fusion
  104.1 9.5 %all-to-all-done.2.right_ref = bf16[4,2,64,1536]{3,2,1,0:T(8,128)(2,1)S(1)} async-done(((bf16[4,2,64,1536]{3,2,1,0:T(8,128)(2,1)}), bf16[4,2,64,1536]{3,2,1,0:T(8,128)(2,1)S(1)}, u32[]{:S(2)}, u32[]{:S(2)}) %all-to-all-start.2) | async-done | bytes 1572896 | tf_op jit(solution)/shard_map/all_to_all | solution.py:239
  113.6 0.0 copy-start
  113.6 1.6 copy-done
  115.2 16.1 %apply.1 = bf16[4,4,64,256]{3,2,1,0:T(8,128)(2,1)S(1)} custom-call(s32[4]{0:T(128)S(1)} %get-tuple-element.14.order_ref, s32[4]{0:T(128)S(1)} %get-tuple-element.13.slot_ref, bf16[16,64,1024]{2,1,0:T(8,128)(2,1)S(1)} %copy-done, bf16[4,4,64,384]{3,2,1,0:T(8,128)(2,1)S(1)} %all-to-all-done.left_ref, bf16[4,2,64,1536]{3,2,1,0:T(8,128)(2,1)S(1)} %all-to-all-done.2.right_ref, ...), custom_call_target="tpu_custom_call" | custom-call | tf_op jit(solution)/shard_map/apply/pallas_call | solution.py:190
  131.2 19.3 %all_to_all.27.came_ref = bf16[4,4,64,256]{3,2,1,0:T(8,128)(2,1)} all-to-all(bf16[4,4,64,256]{3,2,1,0:T(8,128)(2,1)S(1)} %apply.1), channel_id=1, replica_groups=mesh['groups'=2,'row'=4,'col'=4] {'col'}, dimensions={0} | all-to-all | bytes 1048576 | tf_op jit(solution)/shard_map/all_to_all | solution.py:244
  150.5 17.8 %place.1 = bf16[16,64,256]{2,1,0:T(8,128)(2,1)} custom-call(s32[16]{0:T(128)} %get-tuple-element.9.order_ref, bf16[4,4,64,256]{3,2,1,0:T(8,128)(2,1)} %all_to_all.27.came_ref), custom_call_target="tpu_custom_call" | custom-call | tf_op jit(solution)/shard_map/place/pallas_call | solution.py:214
Async XLA Ops:
  34.9 54.9 %all-to-all-start = ((bf16[4,4,64,384]{3,2,1,0:T(8,128)(2,1)}), bf16[4,4,64,384]{3,2,1,0:T(8,128)(2,1)S(1)}, u32[]{:S(2)}, u32[]{:S(2)}) async-start(bf16[4,4,64,384]{3,2,1,0:T(8,128)(2,1)} %get-tuple-element.11), calls=%async_computation | async-start | bytes 1572864 | tf_op jit(solution)/shard_map/all_to_all | solution.py:238
  89.8 3.8 %copy-start.3 = (s32[16]{0:T(128)S(1)}, s32[16]{0:T(128)}, u32[]{:S(2)}) copy-start(s32[16]{0:T(128)} %get-tuple-element.10) | copy-start | bytes 196
  89.8 3.8 %copy-start.2 = (s32[16]{0:T(128)S(1)}, s32[16]{0:T(128)}, u32[]{:S(2)}) copy-start(s32[16]{0:T(128)} %get-tuple-element.9.order_ref) | copy-start | bytes 196
  89.8 3.9 %copy-start.1 = (bf16[24,24,256]{2,1,0:T(8,128)(2,1)S(1)}, bf16[24,24,256]{2,1,0:T(8,128)(2,1)}, u32[]{:S(2)}) copy-start(bf16[24,24,256]{2,1,0:T(8,128)(2,1)} %param.10) | copy-start | bytes 884740
  89.8 23.8 %all-to-all-start.2 = ((bf16[4,2,64,1536]{3,2,1,0:T(8,128)(2,1)}), bf16[4,2,64,1536]{3,2,1,0:T(8,128)(2,1)S(1)}, u32[]{:S(2)}, u32[]{:S(2)}) async-start(bf16[4,2,64,1536]{3,2,1,0:T(8,128)(2,1)} %pick.1), calls=%async_computation.2 | async-start | bytes 3145728 | tf_op jit(solution)/shard_map/all_to_all | solution.py:239
  113.6 1.6 copy-start

commit v2 on v1

v2 whole, which is shorter than its diff:
```python
import functools

import jax
import jax.numpy as jnp
from jax import lax
from jax.experimental import pallas as pl
from jax.experimental.pallas import tpu as pltpu
from jax.sharding import PartitionSpec as P

PARTS = 2
CHUNK = 8
SMEM = pl.BlockSpec(memory_space=pltpu.SMEM)
VMEM = pl.BlockSpec(memory_space=pltpu.VMEM)
ANY = pl.BlockSpec(memory_space=pl.ANY)


def swap(array, axis, step):
    size = lax.axis_size(axis)
    return lax.ppermute(array, axis, [(i, i ^ step) for i in range(size)])


def run_copies(copies):
    for copy in copies:
        copy.start()
    for copy in copies:
        copy.wait()


def route_kernel(rows, cols, near, parts, left_ref, key_ref, env_ref, *refs):
    sends = refs[: cols * parts]
    order_ref, slot_ref, by_place, place_slot, sem = refs[cols * parts :]
    count = left_ref.shape[0]
    steps = count // cols
    per_part = steps // parts
    mine = lax.axis_index("col")
    owners = [lax.div(key_ref[p], 1 << 16) for p in range(count)]
    for p in range(count):
        rank = jnp.int32(0)
        first = jnp.int32(0)
        for other in range(count):
            first = first + (owners[other] < owners[p]).astype(jnp.int32)
            if other < p:
                rank = rank + (owners[other] == owners[p]).astype(jnp.int32)
        place = first + rank
        offset = lax.rem(lax.rem(place, cols) - lax.rem(first, cols) + cols, cols)
        by_place[place] = p
        place_slot[place] = lax.div(rank - offset, cols)
    for col in range(cols):
        at = jnp.int32(col * steps)
        for slot in range(near):
            for step in range(steps):
                place = step * cols + col

                @pl.when(place_slot[place] == slot)
                def _():
                    p = by_place[place]
                    order_ref[at] = p
                    slot_ref[at] = lax.div(key_ref[p], 1 << 16) * near + slot

                at = at + (place_slot[place] == slot).astype(jnp.int32)
    copies = []
    for part in range(parts):
        for other in range(cols):
            col = jnp.bitwise_xor(mine, other)
            for step in range(per_part):
                p = order_ref[col * steps + part * per_part + step]
                copies.append(
                    pltpu.make_async_copy(
                        env_ref.at[left_ref[p]],
                        sends[part * cols + other].at[step],
                        sem.at[(part * cols + other) * per_part + step],
                    )
                )
    run_copies(copies)


def route(block_left, keys, left_env, rows, cols, near, parts):
    count = block_left.shape[0]
    size, width = left_env.shape[1:]
    piece = jax.ShapeDtypeStruct((count // cols // parts, size, width), left_env.dtype)
    listed = jax.ShapeDtypeStruct((count,), jnp.int32)
    *sends, order, slots = pl.pallas_call(
        functools.partial(route_kernel, rows, cols, near, parts),
        out_shape=(piece,) * (cols * parts) + (listed, listed),
        in_specs=[SMEM, SMEM, ANY],
        out_specs=(VMEM,) * (cols * parts) + (SMEM, SMEM),
        scratch_shapes=[
            pltpu.SMEM((count,), jnp.int32),
            pltpu.SMEM((count,), jnp.int32),
            pltpu.SemaphoreType.DMA((count,)),
        ],
        name="route",
    )(block_left, keys, left_env)
    return [sends[part * cols : (part + 1) * cols] for part in range(parts)], order, slots


def pick_kernel(rows, cols, near, *refs):
    key_refs = refs[: rows - 1]
    env_ref = refs[rows - 1]
    sends = refs[rows : rows + (rows - 1) * near]
    want, sem = refs[rows + (rows - 1) * near :]
    count = key_refs[0].shape[0]
    me = lax.axis_index("row")
    mine = lax.axis_index("col")
    copies = []
    for other in range(rows - 1):
        for slot in range(near):
            want[slot] = 0
        keys = [key_refs[other][p] for p in range(count)]
        owners = [lax.div(key, 1 << 16) for key in keys]
        place = jnp.int32(0)
        for p in range(count):
            place = place + (owners[p] < me).astype(jnp.int32)
        offset = lax.rem(mine - lax.rem(place, cols) + cols, cols)
        rank = jnp.int32(0)
        for p in range(count):
            here = owners[p] == me
            past = rank - offset

            @pl.when(here & (past >= 0) & (lax.rem(past + cols, cols) == 0))
            def _():
                want[lax.div(past, cols)] = lax.rem(keys[p], 1 << 16)

            rank = rank + here.astype(jnp.int32)
        for slot in range(near):
            at = slot * (rows - 1) + other
            copies.append(pltpu.make_async_copy(env_ref.at[want[slot]], sends[at], sem.at[at]))
            copies[-1].start()
    for copy in copies:
        copy.wait()


def pick(keys, right_env, cols, near):
    rows = len(keys) + 1
    sends = (rows - 1) * near
    piece = jax.ShapeDtypeStruct(right_env.shape[1:], right_env.dtype)
    return pl.pallas_call(
        functools.partial(pick_kernel, rows, cols, near),
        out_shape=(piece,) * sends,
        in_specs=[SMEM] * (rows - 1) + [ANY],
        out_specs=(VMEM,) * sends,
        scratch_shapes=[pltpu.SMEM((near,), jnp.int32), pltpu.SemaphoreType.DMA((sends,))],
        name="pick",
    )(*keys, right_env)


def halves(tile, low):
    swapped = pltpu.roll(tile, tile.shape[1] // 2, 1)
    zero = jnp.zeros_like(tile)
    return (
        jnp.where(low, tile, zero),
        jnp.where(low, zero, swapped),
        jnp.where(low, swapped, zero),
        jnp.where(low, zero, tile),
    )


def apply_kernel(states, rows, cols, near, waves, part, order_ref, slot_ref, key_ref, state_ref, mpo_ref, env_ref, *refs):
    lefts = refs[:cols]
    rights = refs[cols : cols + waves * (rows - 1)]
    outs = refs[cols + waves * (rows - 1) : 2 * cols + waves * (rows - 1)]
    block, right_now, left_rows, state_diag, right_diag, mixed, result, sem = refs[2 * cols + waves * (rows - 1) :]
    per_part, size = block.shape[:2]
    half = size // 2
    lanes = 2 * size
    width = mpo_ref.shape[0] // states
    share = width // cols
    steps = order_ref.shape[0] // cols
    low = lax.broadcasted_iota(jnp.int32, (size, lanes), 1) < size
    me = lax.axis_index("row")
    mine = lax.axis_index("col")
    step = pl.program_id(0)

    @pl.when(step == 0)
    def _():
        for k in range(per_part):
            at = mine * steps + part * per_part + k
            p = order_ref[at]
            owner = lax.div(slot_ref[at], near)
            slot = lax.rem(slot_ref[at], near)
            apart = jnp.bitwise_xor(owner, me)
            pltpu.make_async_copy(state_ref.at[p], block.at[k], sem.at[0, k]).start()

            @pl.when(apart == 0)
            def _():
                sector = lax.rem(key_ref[p], 1 << 16)
                pltpu.make_async_copy(env_ref.at[sector], right_now.at[k], sem.at[1, k]).start()

            for other in range(1, rows):
                for wave in range(waves):

                    @pl.when((apart == other) & (slot == wave))
                    def _():
                        pltpu.make_async_copy(
                            rights[wave * (rows - 1) + other - 1], right_now.at[k], sem.at[1, k]
                        ).start()

    pltpu.make_async_copy(state_ref.at[0], block.at[step], sem.at[0, step]).wait()
    for s in range(0, states, 2):
        tile = block[step, :, s * size : (s + 2) * size].astype(jnp.float32)
        pieces = halves(tile, low)
        for i in range(4):
            row, col = (i % 2) * size, (s + i // 2) * lanes
            state_diag[row : row + size, col : col + lanes] = pieces[i].astype(jnp.bfloat16)
    for other in range(cols):
        col = jnp.bitwise_xor(mine, other)
        for k in range(share):
            piece = lefts[other][0, :, k * size : (k + 1) * size].astype(jnp.float32)
            both = jnp.concatenate([piece[:half], piece[half:]], axis=1)
            left_rows[pl.ds(col * share + k, half, stride=width), :] = both

    for start in range(0, half, CHUNK):
        taken = left_rows[start * width : (start + CHUNK) * width, :].astype(jnp.bfloat16)
        first = jnp.dot(taken, state_diag[...], preferred_element_type=jnp.float32)
        columns = []
        for x in range(CHUNK):
            one = first[x * width : (x + 1) * width, :]
            columns.append(
                jnp.concatenate(
                    [one[:, s * lanes : (s + 1) * lanes] for s in range(states)], axis=0
                ).astype(jnp.bfloat16)
            )
        gathered = jnp.concatenate(columns, axis=1)
        channels = jnp.dot(mpo_ref[...], gathered, preferred_element_type=jnp.float32).astype(jnp.bfloat16)
        for x in range(CHUNK):
            for v in range(width):
                mixed[(start + x) * states : (start + x + 1) * states, v * lanes : (v + 1) * lanes] = channels[
                    v * states : (v + 1) * states, x * lanes : (x + 1) * lanes
                ]
    pltpu.make_async_copy(env_ref.at[0], right_now.at[step], sem.at[1, step]).wait()
    for v in range(0, width, 2):
        tile = right_now[step, :, v * size : (v + 2) * size].astype(jnp.float32)
        pieces = halves(tile, low)
        for i in range(4):
            at = v * lanes + i * size
            right_diag[at : at + size, :] = pieces[i].astype(jnp.bfloat16)
    result[...] = jnp.dot(mixed[...], right_diag[...], preferred_element_type=jnp.float32)
    low = low[:half]
    per = states // cols
    for other in range(cols):
        col = jnp.bitwise_xor(mine, other)
        for t in range(0, per, 2):
            one = result[pl.ds(col * per + t, half, stride=states), :]
            two = result[pl.ds(col * per + t + 1, half, stride=states), :]
            upper = jnp.where(low, one, pltpu.roll(two, size, 1))
            lower = jnp.where(low, pltpu.roll(one, size, 1), two)
            outs[other][0, :half, t * size : (t + 2) * size] = upper.astype(jnp.bfloat16)
            outs[other][0, half:, t * size : (t + 2) * size] = lower.astype(jnp.bfloat16)


def apply_blocks(order, slots, keys, state_blocks, mpo_rows, right_env, lefts, waves_of, states, rows, near, part):
    cols = len(lefts)
    per_part, size, share = lefts[0].shape
    waves = len(waves_of)
    width = mpo_rows.shape[0] // states
    half, lanes = size // 2, 2 * size
    out = (per_part, size, states // cols * size)
    flops = 2 * per_part * (width * size * size * states * size + (width * states) ** 2 * size * size)
    return pl.pallas_call(
        functools.partial(apply_kernel, states, rows, cols, near, waves, part),
        out_shape=[jax.ShapeDtypeStruct(out, jnp.bfloat16)] * cols,
        grid=(per_part,),
        in_specs=[SMEM, SMEM, SMEM, ANY, VMEM, ANY]
        + [pl.BlockSpec((1, size, share), lambda k: (k, 0, 0))] * cols
        + [ANY] * (waves * (rows - 1)),
        out_specs=[pl.BlockSpec((1,) + out[1:], lambda k: (k, 0, 0))] * cols,
        scratch_shapes=[
            pltpu.VMEM((per_part, size, states * size), jnp.bfloat16),
            pltpu.VMEM((per_part, size, width * size), jnp.bfloat16),
            pltpu.VMEM((half * width, lanes), jnp.float32),
            pltpu.VMEM((lanes, states * lanes), jnp.bfloat16),
            pltpu.VMEM((width * lanes, lanes), jnp.bfloat16),
            pltpu.VMEM((half * states, width * lanes), jnp.bfloat16),
            pltpu.VMEM((half * states, lanes), jnp.float32),
            pltpu.SemaphoreType.DMA((2, per_part)),
        ],
        compiler_params=pltpu.CompilerParams(vmem_limit_bytes=40 << 20),
        cost_estimate=pl.CostEstimate(flops=flops, bytes_accessed=4 << 20, transcendentals=0),
        name="apply",
    )(order, slots, keys, state_blocks, mpo_rows, right_env, *lefts, *[piece for wave in waves_of for piece in wave])


def place_kernel(cols, parts, order_ref, *refs):
    came = refs[: cols * parts]
    out_ref, sem = refs[cols * parts :]
    per_part = came[0].shape[0]
    steps = per_part * parts
    mine = lax.axis_index("col")
    copies = []
    for part in range(parts):
        for other in range(cols):
            col = jnp.bitwise_xor(mine, other)
            for step in range(per_part):
                p = order_ref[col * steps + part * per_part + step]
                copies.append(
                    pltpu.make_async_copy(
                        came[part * cols + other].at[step], out_ref.at[p], sem.at[len(copies)]
                    )
                )
    run_copies(copies)


def place_blocks(order, came):
    parts, cols = len(came), len(came[0])
    count = order.shape[0]
    pieces = [piece for part in came for piece in part]
    return pl.pallas_call(
        functools.partial(place_kernel, cols, parts),
        out_shape=jax.ShapeDtypeStruct((count,) + pieces[0].shape[1:], pieces[0].dtype),
        in_specs=[SMEM] + [ANY] * len(pieces),
        out_specs=VMEM,
        scratch_shapes=[pltpu.SemaphoreType.DMA((count,))],
        name="place",
    )(order, *pieces)


def shards(state_blocks, left_env, right_env, mpo_tensor, block_left, block_owner, block_sub):
    rows = lax.axis_size("row")
    cols = lax.axis_size("col")
    count, size = state_blocks.shape[:2]
    states = state_blocks.shape[2] // size
    width = mpo_tensor.shape[0]
    most = max(2, (2 * count + rows - 1) // rows)
    near = -(-most // cols)
    parts = PARTS

    keys = block_owner[:, 0] * (1 << 16) + block_sub
    others = [swap(keys, "row", step) for step in range(1, rows)]
    mpo_rows = jnp.transpose(mpo_tensor.reshape(width, width, states, states), (1, 2, 3, 0)).reshape(
        width * states, states * width
    )
    sends, order, slots = route(block_left, keys, left_env, rows, cols, near, parts)
    lefts = [[sends[part][0]] + [swap(sends[part][d], "col", d) for d in range(1, cols)] for part in range(parts)]
    picked = pick(others, right_env, cols, near)
    waves = [
        [swap(picked[slot * (rows - 1) + d - 1], "row", d) for d in range(1, rows)] for slot in range(near)
    ]
    came = []
    for part in range(parts):
        usable = near if part > 0 or parts == 1 else 1
        outs = apply_blocks(
            order, slots, keys, state_blocks, mpo_rows, right_env, lefts[part], waves[:usable], states, rows, near, part
        )
        came.append([outs[0]] + [swap(outs[d], "col", d) for d in range(1, cols)])
    return place_blocks(order, came)


def solution(mesh):
    placed = (
        P(("groups", "row"), None, None),
        P(("groups", "row"), None, "col"),
        P(("groups", "row"), None, None),
        P(),
        P(("groups", "row")),
        P(("groups", "row"), None),
        P(("groups", "row")),
    )
    return jax.shard_map(
        shards,
        mesh=mesh,
        in_specs=placed,
        out_specs=P(("groups", "row"), None, "col"),
        check_vma=False,
    )
```

time: 169 us -> 76.7 us (0.45)
  Pallas kernels: 110 us -> 29.7 us
  blocking collectives: 27.8 us -> 0 us
  starting transfers between devices: 9.09 us -> 25.1 us
  waiting for transfers between devices: 9.49 us -> 5.65 us
  local copies, waits for them, and re-layouts: 12.1 us -> 14.8 us
    pallas_call x4 -> x5, Pallas kernels: 110 us -> 29.7 us  [the longest x2 19.9 us: apply_blocks(): pl.pallas_call(functools.partial(apply_kernel, states, rows, cols, near,...]
    all_to_all x2 -> x0, blocking collectives: 27.8 us -> none  [the longest x1 19.3 us: shards(): came = lax.all_to_all(done, 'col', split_axis=0, concat_axis=0, tiled=True)]
    ppermute x0 -> x21, starting transfers between devices: none -> 25.1 us  [swap(): return lax.ppermute(array, axis, [(i, i ^ step) for i in range(size)])]
    all_to_all x2 -> x0, waiting for transfers between devices: 9.49 us -> none  [the longest x1 9.49 us: shards(): lax.all_to_all(pick(asked, right_env), 'row', split_axis=0, concat_axis=0...]
    all_to_all x2 -> x0, starting transfers between devices: 9.09 us -> none  [the longest x1 5.38 us: shards(): lax.all_to_all(left_out, 'col', split_axis=0, concat_axis=0, tiled=True)]
    ppermute x0 -> x21, waiting for transfers between devices: none -> 5.65 us  [swap(): return lax.ppermute(array, axis, [(i, i ^ step) for i in range(size)])]
    unnamed x8 -> x46, local copies, waits for them, and re-layouts: 1.61 us -> 4.51 us
  transfers between devices with their start and end apart: 2 -> 21, of which waited for: 1 -> 3; matrix products, arithmetic and copies ran while one was open for 6% -> 13% of each run, Pallas kernels for 29% -> 35%
where the time goes in v2:
time: 76.7 us; the launch traced here: 76.3 us
  Pallas kernels  29.7 us (39%)
  starting transfers between devices  25.1 us (33%)
  local copies, waits for them, and re-layouts  14.8 us (19%)
  waiting for transfers between devices  5.65 us (7%)
    ppermute x21, starting transfers between devices, swap(): return lax.ppermute(array, axis, [(i, i ^ step) for i in range(size)])  25.1 us
    pallas_call x2, Pallas kernels, apply_blocks(): pl.pallas_call(functools.partial(apply_kernel, states, rows, cols, near,...  19.9 us
    ppermute x21, waiting for transfers between devices, swap(): return lax.ppermute(array, axis, [(i, i ^ step) for i in range(size)])  5.65 us
    transpose x1, local copies, waits for them, and re-layouts, shards(): jnp.transpose(mpo_tensor.reshape(width, width, states, states), (1, 2, 3,...  4.85 us
    unnamed x46, local copies, waits for them, and re-layouts  4.51 us
    pallas_call x1, Pallas kernels, route(): pl.pallas_call(functools.partial(route_kernel, rows, cols, near, parts),...  3.73 us
    pallas_call x1, Pallas kernels, pick(): pl.pallas_call(functools.partial(pick_kernel, rows, cols, near), out_shap...  3.41 us
    reshape x1, local copies, waits for them, and re-layouts, shards(): jnp.transpose(mpo_tensor.reshape(width, width, states, states), (1, 2, 3,...  2.81 us
  transfers between devices with their start and end apart: 21, of which 3 were waited for; matrix products, arithmetic and copies ran while one was open for 13% of the time, Pallas kernels for 35%

profile of v2, /device:TPU:0, one launch (start us, length us, event | category | flops | bytes accessed | tf_op | source)
XLA Modules:
  0.0 76.3 jit_solution(14759402268868275618)
XLA Ops:
  0.0 0.7 bitcast_add_fusion.key_ref
  1.2 2.6 %collective-permute-start.4 = (s32[16]{0:T(128)S(1)}, s32[16]{0:T(128)S(1)}, u32[]{:S(2)}, u32[]{:S(2)}) collective-permute-start(s32[16]{0:T(128)S(1)} %bitcast_add_fusion.key_ref), channel_id=1, source_target_pairs={{0,8},{4,12},{8,0},{12,4},{1,9},{5,13},{9,1},{13,5},{2,10},{6,14},... | collective-permute-start | bytes 200 | tf_op jit(solution)/shard_map/ppermute | solution.py:19
  3.8 3.7 %route.1 = (bf16[2,64,384]{2,1,0:T(8,128)(2,1)}, bf16[2,64,384]{2,1,0:T(8,128)(2,1)}, bf16[2,64,384]{2,1,0:T(8,128)(2,1)}, bf16[2,64,384]{2,1,0:T(8,128)(2,1)}, ...) custom-call(s32[16]{0:T(128)} %left_ref.1, ...), custom_call_target="tpu_custom_call" | custom-call | tf_op jit(solution)/shard_map/route/pallas_call | solution.py:82
  7.6 1.9 %collective-permute-start = (bf16[2,64,384]{2,1,0:T(8,128)(2,1)}, bf16[2,64,384]{2,1,0:T(8,128)(2,1)S(1)}, u32[]{:S(2)}, u32[]{:S(2)}) collective-permute-start(bf16[2,64,384]{2,1,0:T(8,128)(2,1)} %get-tuple-element.32), channel_id=1, source_target_pairs={{0,1},{1,0},{2,3},{3,2},{4,5},{5,4},{6,7},{7,6},{8,9},{9,8},{10,11... | collective-permute-start | bytes 294920 | tf_op jit(solution)/shard_map/ppermute | solution.py:19
  9.4 2.6 %collective-permute-start.1 = (bf16[2,64,384]{2,1,0:T(8,128)(2,1)}, bf16[2,64,384]{2,1,0:T(8,128)(2,1)S(1)}, u32[]{:S(2)}, u32[]{:S(2)}) collective-permute-start(bf16[2,64,384]{2,1,0:T(8,128)(2,1)} %get-tuple-element.33), channel_id=1, source_target_pairs={{0,2},{1,3},{2,0},{3,1},{4,6},{5,7},{6,4},{7,5},{8,10},{9,11},{10,... | collective-permute-start | bytes 294920 | tf_op jit(solution)/shard_map/ppermute | solution.py:19
  13.1 3.4 %pick.1 = (bf16[64,1536]{1,0:T(8,128)(2,1)}, bf16[64,1536]{1,0:T(8,128)(2,1)}, bf16[64,1536]{1,0:T(8,128)(2,1)}, bf16[64,1536]{1,0:T(8,128)(2,1)}, bf16[64,1536]{1,0:T(8,128)(2,1)}, /*index=5*/bf16[64,1536]{1,0:T(8,128)(2,1)}) custom-call(s32[16]{0:T(128)} %copy-done.17, s32[16]{0:T(128)} %copy-done.18, s32[16]{0:T(128)} %copy-done.19, ...), custom_call_target="tpu_custom_call" | custom-call | tf_op jit(solution)/shard_map/pick/pallas_call | solution.py:137
  16.6 1.8 %collective-permute-start.7 = (bf16[64,1536]{1,0:T(8,128)(2,1)}, bf16[64,1536]{1,0:T(8,128)(2,1)S(1)}, u32[]{:S(2)}, u32[]{:S(2)}) collective-permute-start(bf16[64,1536]{1,0:T(8,128)(2,1)} %get-tuple-element.36), channel_id=1, source_target_pairs={{0,8},{4,12},{8,0},{12,4},{1,9},{5,13},{9,1},{13,5},{2,10},{6,14},... | collective-permute-start | bytes 589832 | tf_op jit(solution)/shard_map/ppermute | solution.py:19
  19.0 0.7 collective-permute-start.12
  19.7 2.6 %reshape.8 = bf16[24,24,16,16]{3,2,1,0:T(8,128)(2,1)} reshape(bf16[24,24,256]{2,1,0:T(8,128)(2,1)S(1)} %copy-done.10) | data formatting | bytes 589824 | tf_op jit(solution)/shard_map/reshape | solution.py:329
  22.4 4.8 %copy.9 = bf16[24,16,16,24]{3,2,1,0:T(8,128)(2,1)} copy(bf16[24,16,16,24]{2,1,0,3:T(8,128)(2,1)} %bitcast.5) | data formatting | bytes 589824 | tf_op jit(solution)/shard_map/transpose | solution.py:329
  27.2 2.8 %reshape.9.mpo_ref = bf16[384,384]{1,0:T(8,128)(2,1)S(1)} reshape(bf16[24,16,16,24]{3,2,1,0:T(8,128)(2,1)} %copy.9) | data formatting | bytes 589824 | tf_op jit(solution)/shard_map/reshape | solution.py:329
  30.0 3.2 %collective-permute-start.13 = (bf16[2,64,384]{2,1,0:T(8,128)(2,1)}, bf16[2,64,384]{2,1,0:T(8,128)(2,1)S(1)}, u32[]{:S(2)}, u32[]{:S(2)}) collective-permute-start(bf16[2,64,384]{2,1,0:T(8,128)(2,1)} %get-tuple-element.44), channel_id=1, source_target_pairs={{0,2},{1,3},{2,0},{3,1},{4,6},{5,7},{6,4},{7,5},{8,10},{9,11},{10,... | collective-permute-start | bytes 294920 | tf_op jit(solution)/shard_map/ppermute | solution.py:19
  33.8 1.2 %collective-permute-start.16 = (bf16[64,1536]{1,0:T(8,128)(2,1)S(1)}, bf16[64,1536]{1,0:T(8,128)(2,1)S(1)}, u32[]{:S(2)}, u32[]{:S(2)}) collective-permute-start(bf16[64,1536]{1,0:T(8,128)(2,1)S(1)} %copy-done.21), channel_id=1, source_target_pairs={{0,8},{4,12},{8,0},{12,4},{1,9},{5,13},{9,1},{13,5},{2,10},{6,14},... | collective-permute-start | bytes 589832 | tf_op jit(solution)/shard_map/ppermute | solution.py:19
  35.0 0.6 collective-permute-start.17
  35.7 1.6 %copy-done.6 = bf16[16,64,1024]{2,1,0:T(8,128)(2,1)S(1)} copy-done((bf16[16,64,1024]{2,1,0:T(8,128)(2,1)S(1)}, bf16[16,64,1024]{2,1,0:T(8,128)(2,1)}, u32[]{:S(2)}) %copy-start.6) | copy-done | bytes 2097176
  37.3 9.9 %apply.2 = (bf16[2,64,256]{2,1,0:T(8,128)(2,1)S(1)}, bf16[2,64,256]{2,1,0:T(8,128)(2,1)S(1)}, bf16[2,64,256]{2,1,0:T(8,128)(2,1)S(1)}, bf16[2,64,256]{2,1,0:T(8,128)(2,1)S(1)}) custom-call(s32[16]{0:T(128)S(1)} %copy-done.3, s32[16]{0:T(128)S(1)} %copy-done.9, s32[16]{0:T(128)S(1)} %copy-done.5, bf16[16,64,1024]{2,1,0:T(8,128)(2,1)S(1)} %copy-done.6, ...), custom_call_target="tpu_custom_call" | custom-call | flops 2818572288 | bytes 4194304 | tf_op jit(solution)/shard_map/apply/pallas_call | solution.py:259
  47.2 0.6 copy-done.1
  48.0 3.7 %collective-permute-start.10 = (bf16[2,64,256]{2,1,0:T(8,128)(2,1)S(1)}, bf16[2,64,256]{2,1,0:T(8,128)(2,1)S(1)}, u32[]{:S(2)}, u32[]{:S(2)}) collective-permute-start(bf16[2,64,256]{2,1,0:T(8,128)(2,1)S(1)} %get-tuple-element.40), channel_id=1, source_target_pairs={{0,2},{1,3},{2,0},{3,1},{4,6},{5,7},{6,4},{7,5},{8,10},{9,11},{10,... | collective-permute-start | bytes 196616 | tf_op jit(solution)/shard_map/ppermute | solution.py:19
  52.2 10.0 %apply.3 = (bf16[2,64,256]{2,1,0:T(8,128)(2,1)S(1)}, bf16[2,64,256]{2,1,0:T(8,128)(2,1)S(1)}, bf16[2,64,256]{2,1,0:T(8,128)(2,1)S(1)}, bf16[2,64,256]{2,1,0:T(8,128)(2,1)S(1)}) custom-call(s32[16]{0:T(128)S(1)} %copy-done.3, s32[16]{0:T(128)S(1)} %copy-done.9, s32[16]{0:T(128)S(1)} %copy-done.5, bf16[16,64,1024]{2,1,0:T(8,128)(2,1)S(1)} %copy-done.6, ...), custom_call_target="tpu_custom_call" | custom-call | flops 2818572288 | bytes 4194304 | tf_op jit(solution)/shard_map/apply/pallas_call | solution.py:259
  62.3 0.6 copy-done.2
  63.1 3.8 %collective-permute-start.19 = (bf16[2,64,256]{2,1,0:T(8,128)(2,1)S(1)}, bf16[2,64,256]{2,1,0:T(8,128)(2,1)S(1)}, u32[]{:S(2)}, u32[]{:S(2)}) collective-permute-start(bf16[2,64,256]{2,1,0:T(8,128)(2,1)S(1)} %get-tuple-element.51), channel_id=1, source_target_pairs={{0,2},{1,3},{2,0},{3,1},{4,6},{5,7},{6,4},{7,5},{8,10},{9,11},{10,... | collective-permute-start | bytes 196616 | tf_op jit(solution)/shard_map/ppermute | solution.py:19
  67.7 3.5 %collective-permute-done.19.refs_6_ = bf16[2,64,256]{2,1,0:T(8,128)(2,1)S(1)} collective-permute-done((bf16[2,64,256]{2,1,0:T(8,128)(2,1)S(1)}, bf16[2,64,256]{2,1,0:T(8,128)(2,1)S(1)}, u32[]{:S(2)}, u32[]{:S(2)}) %collective-permute-start.19) | collective-permute-done | bytes 65568 | tf_op jit(solution)/shard_map/ppermute | solution.py:19
  71.2 1.8 %collective-permute-done.20.refs_7_ = bf16[2,64,256]{2,1,0:T(8,128)(2,1)S(1)} collective-permute-done((bf16[2,64,256]{2,1,0:T(8,128)(2,1)S(1)}, bf16[2,64,256]{2,1,0:T(8,128)(2,1)S(1)}, u32[]{:S(2)}, u32[]{:S(2)}) %collective-permute-start.20) | collective-permute-done | bytes 65568 | tf_op jit(solution)/shard_map/ppermute | solution.py:19
  73.5 2.6 %place.1 = bf16[16,64,256]{2,1,0:T(8,128)(2,1)} custom-call(s32[16]{0:T(128)} %get-tuple-element.29.order_ref, bf16[2,64,256]{2,1,0:T(8,128)(2,1)} %copy-done.1, bf16[2,64,256]{2,1,0:T(8,128)(2,1)} %copy-done.11, bf16[2,64,256]{2,1,0:T(8,128)(2,1)} %copy-done.12, bf16[2,64,256]{2,1,0:T(8,128)(2,1)} %copy-done.13, bf16[2,64,256]{2,1,0:T(8,128)(2,1)} %copy-done.2, ...), custom_call_target="tpu_custom_call" | custom-call | tf_op jit(solution)/shard_map/place/pallas_call | solution.py:307
  (73 shorter events, 5.1 us)
Async XLA Ops:
  0.0 19.7 %copy-start.10 = (bf16[24,24,256]{2,1,0:T(8,128)(2,1)S(1)}, bf16[24,24,256]{2,1,0:T(8,128)(2,1)}, u32[]{:S(2)}) copy-start(bf16[24,24,256]{2,1,0:T(8,128)(2,1)} %param.10) | copy-start | bytes 884740
  0.7 11.3 %collective-permute-start.3 = (s32[16]{0:T(128)S(1)}, s32[16]{0:T(128)S(1)}, u32[]{:S(2)}, u32[]{:S(2)}) collective-permute-start(s32[16]{0:T(128)S(1)} %bitcast_add_fusion.key_ref), channel_id=1, source_target_pairs={{0,4},{4,0},{8,12},{12,8},{1,5},{5,1},{9,13},{13,9},{2,6},{6,2},{1... | collective-permute-start | bytes 200 | tf_op jit(solution)/shard_map/ppermute | solution.py:19
  1.2 10.8 %collective-permute-start.4 = (s32[16]{0:T(128)S(1)}, s32[16]{0:T(128)S(1)}, u32[]{:S(2)}, u32[]{:S(2)}) collective-permute-start(s32[16]{0:T(128)S(1)} %bitcast_add_fusion.key_ref), channel_id=1, source_target_pairs={{0,8},{4,12},{8,0},{12,4},{1,9},{5,13},{9,1},{13,5},{2,10},{6,14},... | collective-permute-start | bytes 200 | tf_op jit(solution)/shard_map/ppermute | solution.py:19
  3.8 8.3 %collective-permute-start.5 = (s32[16]{0:T(128)S(1)}, s32[16]{0:T(128)S(1)}, u32[]{:S(2)}, u32[]{:S(2)}) collective-permute-start(s32[16]{0:T(128)S(1)} %bitcast_add_fusion.key_ref), channel_id=1, source_target_pairs={{0,12},{4,8},{8,4},{12,0},{1,13},{5,9},{9,5},{13,1},{2,14},{6,10},... | collective-permute-start | bytes 200 | tf_op jit(solution)/shard_map/ppermute | solution.py:19
  7.6 10.9 %collective-permute-start = (bf16[2,64,384]{2,1,0:T(8,128)(2,1)}, bf16[2,64,384]{2,1,0:T(8,128)(2,1)S(1)}, u32[]{:S(2)}, u32[]{:S(2)}) collective-permute-start(bf16[2,64,384]{2,1,0:T(8,128)(2,1)} %get-tuple-element.32), channel_id=1, source_target_pairs={{0,1},{1,0},{2,3},{3,2},{4,5},{5,4},{6,7},{7,6},{8,9},{9,8},{10,11... | collective-permute-start | bytes 294920 | tf_op jit(solution)/shard_map/ppermute | solution.py:19
  9.4 9.5 %collective-permute-start.1 = (bf16[2,64,384]{2,1,0:T(8,128)(2,1)}, bf16[2,64,384]{2,1,0:T(8,128)(2,1)S(1)}, u32[]{:S(2)}, u32[]{:S(2)}) collective-permute-start(bf16[2,64,384]{2,1,0:T(8,128)(2,1)} %get-tuple-element.33), channel_id=1, source_target_pairs={{0,2},{1,3},{2,0},{3,1},{4,6},{5,7},{6,4},{7,5},{8,10},{9,11},{10,... | collective-permute-start | bytes 294920 | tf_op jit(solution)/shard_map/ppermute | solution.py:19
  16.5 17.3 %collective-permute-start.6 = (bf16[64,1536]{1,0:T(8,128)(2,1)}, bf16[64,1536]{1,0:T(8,128)(2,1)S(1)}, u32[]{:S(2)}, u32[]{:S(2)}) collective-permute-start(bf16[64,1536]{1,0:T(8,128)(2,1)} %get-tuple-element.35), channel_id=1, source_target_pairs={{0,4},{4,0},{8,12},{12,8},{1,5},{5,1},{9,13},{13,9},{2,6},{6,2},{1... | collective-permute-start | bytes 589832 | tf_op jit(solution)/shard_map/ppermute | solution.py:19
  16.6 17.2 %collective-permute-start.7 = (bf16[64,1536]{1,0:T(8,128)(2,1)}, bf16[64,1536]{1,0:T(8,128)(2,1)S(1)}, u32[]{:S(2)}, u32[]{:S(2)}) collective-permute-start(bf16[64,1536]{1,0:T(8,128)(2,1)} %get-tuple-element.36), channel_id=1, source_target_pairs={{0,8},{4,12},{8,0},{12,4},{1,9},{5,13},{9,1},{13,5},{2,10},{6,14},... | collective-permute-start | bytes 589832 | tf_op jit(solution)/shard_map/ppermute | solution.py:19
  18.4 16.6 %collective-permute-start.8 = (bf16[64,1536]{1,0:T(8,128)(2,1)}, bf16[64,1536]{1,0:T(8,128)(2,1)S(1)}, u32[]{:S(2)}, u32[]{:S(2)}) collective-permute-start(bf16[64,1536]{1,0:T(8,128)(2,1)} %get-tuple-element.37), channel_id=1, source_target_pairs={{0,12},{4,8},{8,4},{12,0},{1,13},{5,9},{9,5},{13,1},{2,14},{6,10},... | collective-permute-start | bytes 589832 | tf_op jit(solution)/shard_map/ppermute | solution.py:19
  18.5 11.6 %collective-permute-start.2 = (bf16[2,64,384]{2,1,0:T(8,128)(2,1)}, bf16[2,64,384]{2,1,0:T(8,128)(2,1)S(1)}, u32[]{:S(2)}, u32[]{:S(2)}) collective-permute-start(bf16[2,64,384]{2,1,0:T(8,128)(2,1)} %get-tuple-element.34), channel_id=1, source_target_pairs={{0,3},{1,2},{2,1},{3,0},{4,7},{5,6},{6,5},{7,4},{8,11},{9,10},{10,... | collective-permute-start | bytes 294920 | tf_op jit(solution)/shard_map/ppermute | solution.py:19
  19.0 14.3 %collective-permute-start.12 = (bf16[2,64,384]{2,1,0:T(8,128)(2,1)}, bf16[2,64,384]{2,1,0:T(8,128)(2,1)S(1)}, u32[]{:S(2)}, u32[]{:S(2)}) collective-permute-start(bf16[2,64,384]{2,1,0:T(8,128)(2,1)} %get-tuple-element.43), channel_id=1, source_target_pairs={{0,1},{1,0},{2,3},{3,2},{4,5},{5,4},{6,7},{7,6},{8,9},{9,8},{10,11... | collective-permute-start | bytes 294920 | tf_op jit(solution)/shard_map/ppermute | solution.py:19
  22.3 13.4 %copy-start = (bf16[8,64,1536]{2,1,0:T(8,128)(2,1)S(1)}, bf16[8,64,1536]{2,1,0:T(8,128)(2,1)}, u32[]{:S(2)}) copy-start(bf16[8,64,1536]{2,1,0:T(8,128)(2,1)} %env_ref.5) | copy-start | bytes 4718596
  30.0 17.8 %collective-permute-start.13 = (bf16[2,64,384]{2,1,0:T(8,128)(2,1)}, bf16[2,64,384]{2,1,0:T(8,128)(2,1)S(1)}, u32[]{:S(2)}, u32[]{:S(2)}) collective-permute-start(bf16[2,64,384]{2,1,0:T(8,128)(2,1)} %get-tuple-element.44), channel_id=1, source_target_pairs={{0,2},{1,3},{2,0},{3,1},{4,6},{5,7},{6,4},{7,5},{8,10},{9,11},{10,... | collective-permute-start | bytes 294920 | tf_op jit(solution)/shard_map/ppermute | solution.py:19
  33.3 14.7 %collective-permute-start.14 = (bf16[2,64,384]{2,1,0:T(8,128)(2,1)}, bf16[2,64,384]{2,1,0:T(8,128)(2,1)S(1)}, u32[]{:S(2)}, u32[]{:S(2)}) collective-permute-start(bf16[2,64,384]{2,1,0:T(8,128)(2,1)} %get-tuple-element.45), channel_id=1, source_target_pairs={{0,3},{1,2},{2,1},{3,0},{4,7},{5,6},{6,5},{7,4},{8,11},{9,10},{10,... | collective-permute-start | bytes 294920 | tf_op jit(solution)/shard_map/ppermute | solution.py:19
  33.8 18.0 %collective-permute-start.15 = (bf16[64,1536]{1,0:T(8,128)(2,1)S(1)}, bf16[64,1536]{1,0:T(8,128)(2,1)S(1)}, u32[]{:S(2)}, u32[]{:S(2)}) collective-permute-start(bf16[64,1536]{1,0:T(8,128)(2,1)S(1)} %copy-done.22), channel_id=1, source_target_pairs={{0,4},{4,0},{8,12},{12,8},{1,5},{5,1},{9,13},{13,9},{2,6},{6,2},{1... | collective-permute-start | bytes 589832 | tf_op jit(solution)/shard_map/ppermute | solution.py:19
  33.8 18.4 %collective-permute-start.16 = (bf16[64,1536]{1,0:T(8,128)(2,1)S(1)}, bf16[64,1536]{1,0:T(8,128)(2,1)S(1)}, u32[]{:S(2)}, u32[]{:S(2)}) collective-permute-start(bf16[64,1536]{1,0:T(8,128)(2,1)S(1)} %copy-done.21), channel_id=1, source_target_pairs={{0,8},{4,12},{8,0},{12,4},{1,9},{5,13},{9,1},{13,5},{2,10},{6,14},... | collective-permute-start | bytes 589832 | tf_op jit(solution)/shard_map/ppermute | solution.py:19
  35.0 17.2 %collective-permute-start.17 = (bf16[64,1536]{1,0:T(8,128)(2,1)S(1)}, bf16[64,1536]{1,0:T(8,128)(2,1)S(1)}, u32[]{:S(2)}, u32[]{:S(2)}) collective-permute-start(bf16[64,1536]{1,0:T(8,128)(2,1)S(1)} %copy-done.20), channel_id=1, source_target_pairs={{0,12},{4,8},{8,4},{12,0},{1,13},{5,9},{9,5},{13,1},{2,14},{6,10},... | collective-permute-start | bytes 589832 | tf_op jit(solution)/shard_map/ppermute | solution.py:19
  37.3 14.9 %copy-start.7 = (bf16[2,64,384]{2,1,0:T(8,128)(2,1)S(1)}, bf16[2,64,384]{2,1,0:T(8,128)(2,1)}, u32[]{:S(2)}) copy-start(bf16[2,64,384]{2,1,0:T(8,128)(2,1)} %get-tuple-element.42.refs_0_) | copy-start | bytes 294916
  47.8 19.0 %collective-permute-start.9 = (bf16[2,64,256]{2,1,0:T(8,128)(2,1)S(1)}, bf16[2,64,256]{2,1,0:T(8,128)(2,1)S(1)}, u32[]{:S(2)}, u32[]{:S(2)}) collective-permute-start(bf16[2,64,256]{2,1,0:T(8,128)(2,1)S(1)} %get-tuple-element.39), channel_id=1, source_target_pairs={{0,1},{1,0},{2,3},{3,2},{4,5},{5,4},{6,7},{7,6},{8,9},{9,8},{10,11... | collective-permute-start | bytes 196616 | tf_op jit(solution)/shard_map/ppermute | solution.py:19
  48.0 19.3 %collective-permute-start.10 = (bf16[2,64,256]{2,1,0:T(8,128)(2,1)S(1)}, bf16[2,64,256]{2,1,0:T(8,128)(2,1)S(1)}, u32[]{:S(2)}, u32[]{:S(2)}) collective-permute-start(bf16[2,64,256]{2,1,0:T(8,128)(2,1)S(1)} %get-tuple-element.40), channel_id=1, source_target_pairs={{0,2},{1,3},{2,0},{3,1},{4,6},{5,7},{6,4},{7,5},{8,10},{9,11},{10,... | collective-permute-start | bytes 196616 | tf_op jit(solution)/shard_map/ppermute | solution.py:19
  51.7 15.5 %collective-permute-start.11 = (bf16[2,64,256]{2,1,0:T(8,128)(2,1)S(1)}, bf16[2,64,256]{2,1,0:T(8,128)(2,1)S(1)}, u32[]{:S(2)}, u32[]{:S(2)}) collective-permute-start(bf16[2,64,256]{2,1,0:T(8,128)(2,1)S(1)} %get-tuple-element.41), channel_id=1, source_target_pairs={{0,3},{1,2},{2,1},{3,0},{4,7},{5,6},{6,5},{7,4},{8,11},{9,10},{10,... | collective-permute-start | bytes 196616 | tf_op jit(solution)/shard_map/ppermute | solution.py:19
  62.9 4.8 %collective-permute-start.18 = (bf16[2,64,256]{2,1,0:T(8,128)(2,1)S(1)}, bf16[2,64,256]{2,1,0:T(8,128)(2,1)S(1)}, u32[]{:S(2)}, u32[]{:S(2)}) collective-permute-start(bf16[2,64,256]{2,1,0:T(8,128)(2,1)S(1)} %get-tuple-element.50), channel_id=1, source_target_pairs={{0,1},{1,0},{2,3},{3,2},{4,5},{5,4},{6,7},{7,6},{8,9},{9,8},{10,11... | collective-permute-start | bytes 196616 | tf_op jit(solution)/shard_map/ppermute | solution.py:19
  63.1 8.1 %collective-permute-start.19 = (bf16[2,64,256]{2,1,0:T(8,128)(2,1)S(1)}, bf16[2,64,256]{2,1,0:T(8,128)(2,1)S(1)}, u32[]{:S(2)}, u32[]{:S(2)}) collective-permute-start(bf16[2,64,256]{2,1,0:T(8,128)(2,1)S(1)} %get-tuple-element.51), channel_id=1, source_target_pairs={{0,2},{1,3},{2,0},{3,1},{4,6},{5,7},{6,4},{7,5},{8,10},{9,11},{10,... | collective-permute-start | bytes 196616 | tf_op jit(solution)/shard_map/ppermute | solution.py:19
  66.8 6.1 %collective-permute-start.20 = (bf16[2,64,256]{2,1,0:T(8,128)(2,1)S(1)}, bf16[2,64,256]{2,1,0:T(8,128)(2,1)S(1)}, u32[]{:S(2)}, u32[]{:S(2)}) collective-permute-start(bf16[2,64,256]{2,1,0:T(8,128)(2,1)S(1)} %get-tuple-element.52), channel_id=1, source_target_pairs={{0,3},{1,2},{2,1},{3,0},{4,7},{5,6},{6,5},{7,4},{8,11},{9,10},{10,... | collective-permute-start | bytes 196616 | tf_op jit(solution)/shard_map/ppermute | solution.py:19
  (20 other events, 121.6 us)

commit v3 on v2

v3 whole, which is shorter than its diff:
```python
import functools

import jax
import jax.numpy as jnp
from jax import lax
from jax.experimental import pallas as pl
from jax.experimental.pallas import tpu as pltpu
from jax.sharding import PartitionSpec as P

CHUNK = 8
SHIFT = 16
SMEM = pl.BlockSpec(memory_space=pltpu.SMEM)
VMEM = pl.BlockSpec(memory_space=pltpu.VMEM)
HBM = pl.BlockSpec(memory_space=pltpu.HBM)
ANY = pl.BlockSpec(memory_space=pl.ANY)


def swap(array, axis, step):
    size = lax.axis_size(axis)
    return lax.ppermute(array, axis, [(i, i ^ step) for i in range(size)])


def run_copies(copies):
    for copy in copies:
        copy.start()
    for copy in copies:
        copy.wait()


def owner_of(key):
    return lax.shift_right_logical(key, SHIFT)


def sub_of(key):
    return jnp.bitwise_and(key, (1 << SHIFT) - 1)


def route_kernel(cols, near, left_ref, key_ref, env_ref, *refs):
    sends = refs[:cols]
    order_ref, slot_ref, by_place, sem = refs[cols:]
    count = left_ref.shape[0]
    steps = count // cols
    mine = lax.axis_index("col")
    owners = [owner_of(key_ref[p]) for p in range(count)]
    for p in range(count):
        place = jnp.int32(0)
        for other in range(count):
            if other < p:
                place = place + (owners[other] <= owners[p]).astype(jnp.int32)
            elif other > p:
                place = place + (owners[other] < owners[p]).astype(jnp.int32)
        by_place[place] = p
    for col in range(cols):
        before = None
        for step in range(steps):
            p = by_place[step * cols + col]
            owner = owner_of(key_ref[p])
            if before is None:
                slot = jnp.int32(0)
            else:
                slot = jnp.where(owner == before[0], before[1] + 1, 0)
            before = owner, slot
            order_ref[col * steps + step] = p
            slot_ref[col * steps + step] = owner * near + slot
    copies = []
    for other in range(cols):
        col = jnp.bitwise_xor(mine, other)
        for step in range(steps):
            p = order_ref[col * steps + step]
            copies.append(
                pltpu.make_async_copy(env_ref.at[left_ref[p]], sends[other].at[step], sem.at[len(copies)])
            )
    run_copies(copies)


def route(block_left, keys, left_env, cols, near):
    count = block_left.shape[0]
    size, width = left_env.shape[1:]
    piece = jax.ShapeDtypeStruct((count // cols, size, width), left_env.dtype)
    listed = jax.ShapeDtypeStruct((count,), jnp.int32)
    *sends, order, slots = pl.pallas_call(
        functools.partial(route_kernel, cols, near),
        out_shape=(piece,) * cols + (listed, listed),
        in_specs=[SMEM, SMEM, ANY],
        out_specs=(VMEM,) * cols + (SMEM, SMEM),
        scratch_shapes=[pltpu.SMEM((count,), jnp.int32), pltpu.SemaphoreType.DMA((count,))],
        name="route",
    )(block_left, keys, left_env)
    return sends, order, slots


def pick_kernel(rows, cols, near, *refs):
    key_refs = refs[: rows - 1]
    env_ref = refs[rows - 1]
    sends = refs[rows : 2 * rows - 1]
    sem = refs[2 * rows - 1]
    count = key_refs[0].shape[0]
    me = lax.axis_index("row")
    mine = lax.axis_index("col")
    copies = []
    for other in range(rows - 1):
        keys = [key_refs[other][p] for p in range(count)]
        owners = [owner_of(key) for key in keys]
        first = jnp.int32(0)
        for p in range(count):
            first = first + (owners[p] < me).astype(jnp.int32)
        past = -lax.rem(mine - lax.rem(first, cols) + cols, cols)
        wanted = [jnp.int32(0)] * near
        for p in range(count):
            here = owners[p] == me
            for slot in range(near):
                wanted[slot] = jnp.where(here & (past == slot * cols), sub_of(keys[p]), wanted[slot])
            past = past + here.astype(jnp.int32)
        for slot in range(near):
            copies.append(
                pltpu.make_async_copy(env_ref.at[wanted[slot]], sends[other].at[slot], sem.at[len(copies)])
            )
            copies[-1].start()
    for copy in copies:
        copy.wait()


def pick(keys, right_env, cols, near):
    rows = len(keys) + 1
    piece = jax.ShapeDtypeStruct((near,) + right_env.shape[1:], right_env.dtype)
    return pl.pallas_call(
        functools.partial(pick_kernel, rows, cols, near),
        out_shape=[piece] * (rows - 1),
        in_specs=[SMEM] * (rows - 1) + [HBM],
        out_specs=(VMEM,) * (rows - 1),
        scratch_shapes=[pltpu.SemaphoreType.DMA(((rows - 1) * near,))],
        name="pick",
    )(*keys, right_env)


def halves(tile, low):
    swapped = pltpu.roll(tile, tile.shape[1] // 2, 1)
    zero = jnp.zeros_like(tile)
    return (
        jnp.where(low, tile, zero),
        jnp.where(low, zero, swapped),
        jnp.where(low, swapped, zero),
        jnp.where(low, zero, tile),
    )


def apply_kernel(states, rows, cols, near, order_ref, slot_ref, key_ref, state_ref, mpo_ref, env_ref, *refs):
    lefts = refs[:cols]
    rights = refs[cols : cols + rows - 1]
    outs = refs[cols + rows - 1 : 2 * cols + rows - 1]
    block, right_now, left_rows, state_diag, right_diag, mixed, result, sem = refs[2 * cols + rows - 1 :]
    steps, size = block.shape[:2]
    half = size // 2
    lanes = 2 * size
    width = mpo_ref.shape[0] // states
    share = width // cols
    low = lax.broadcasted_iota(jnp.int32, (size, lanes), 1) < size
    me = lax.axis_index("row")
    mine = lax.axis_index("col")
    step = pl.program_id(0)

    @pl.when(step == 0)
    def _():
        for k in range(steps):
            p = order_ref[mine * steps + k]
            pltpu.make_async_copy(state_ref.at[p], block.at[k], sem.at[0, k]).start()
        for k in range(steps):
            at = mine * steps + k
            owner = lax.div(slot_ref[at], near)
            slot = lax.rem(slot_ref[at], near)
            apart = jnp.bitwise_xor(owner, me)

            @pl.when(apart == 0)
            def _():
                sector = sub_of(key_ref[order_ref[at]])
                pltpu.make_async_copy(env_ref.at[sector], right_now.at[k], sem.at[1, k]).start()

            for other in range(1, rows):

                @pl.when(apart == other)
                def _():
                    pltpu.make_async_copy(rights[other - 1].at[slot], right_now.at[k], sem.at[1, k]).start()

    pltpu.make_async_copy(state_ref.at[0], block.at[step], sem.at[0, step]).wait()
    for s in range(0, states, 2):
        tile = block[step, :, s * size : (s + 2) * size].astype(jnp.float32)
        pieces = halves(tile, low)
        for i in range(4):
            row, col = (i % 2) * size, (s + i // 2) * lanes
            state_diag[row : row + size, col : col + lanes] = pieces[i].astype(jnp.bfloat16)
    for other in range(cols):
        col = jnp.bitwise_xor(mine, other)
        for k in range(share):
            piece = lefts[other][0, :, k * size : (k + 1) * size].astype(jnp.float32)
            both = jnp.concatenate([piece[:half], piece[half:]], axis=1)
            left_rows[pl.ds(col * share + k, half, stride=width), :] = both

    for start in range(0, half, CHUNK):
        taken = left_rows[start * width : (start + CHUNK) * width, :].astype(jnp.bfloat16)
        first = jnp.dot(taken, state_diag[...], preferred_element_type=jnp.float32)
        columns = []
        for x in range(CHUNK):
            one = first[x * width : (x + 1) * width, :]
            columns.append(
                jnp.concatenate(
                    [one[:, s * lanes : (s + 1) * lanes] for s in range(states)], axis=0
                ).astype(jnp.bfloat16)
            )
        gathered = jnp.concatenate(columns, axis=1)
        channels = jnp.dot(mpo_ref[...], gathered, preferred_element_type=jnp.float32).astype(jnp.bfloat16)
        for x in range(CHUNK):
            for v in range(width):
                mixed[(start + x) * states : (start + x + 1) * states, v * lanes : (v + 1) * lanes] = channels[
                    v * states : (v + 1) * states, x * lanes : (x + 1) * lanes
                ]
    pltpu.make_async_copy(env_ref.at[0], right_now.at[step], sem.at[1, step]).wait()
    for v in range(0, width, 2):
        tile = right_now[step, :, v * size : (v + 2) * size].astype(jnp.float32)
        pieces = halves(tile, low)
        for i in range(4):
            at = v * lanes + i * size
            right_diag[at : at + size, :] = pieces[i].astype(jnp.bfloat16)
    result[...] = jnp.dot(mixed[...], right_diag[...], preferred_element_type=jnp.float32)
    low = low[:half]
    per = states // cols
    for other in range(cols):
        col = jnp.bitwise_xor(mine, other)
        for t in range(0, per, 2):
            one = result[pl.ds(col * per + t, half, stride=states), :]
            two = result[pl.ds(col * per + t + 1, half, stride=states), :]
            upper = jnp.where(low, one, pltpu.roll(two, size, 1))
            lower = jnp.where(low, pltpu.roll(one, size, 1), two)
            outs[other][0, :half, t * size : (t + 2) * size] = upper.astype(jnp.bfloat16)
            outs[other][0, half:, t * size : (t + 2) * size] = lower.astype(jnp.bfloat16)


def apply_blocks(order, slots, keys, state_blocks, mpo_rows, right_env, lefts, rights, states, near):
    cols, rows = len(lefts), len(rights) + 1
    steps, size, share = lefts[0].shape
    width = mpo_rows.shape[0] // states
    half, lanes = size // 2, 2 * size
    out = (steps, size, states // cols * size)
    flops = 2 * steps * (width * size * size * states * size + (width * states) ** 2 * size * size)
    return pl.pallas_call(
        functools.partial(apply_kernel, states, rows, cols, near),
        out_shape=[jax.ShapeDtypeStruct(out, jnp.bfloat16)] * cols,
        grid=(steps,),
        in_specs=[SMEM, SMEM, SMEM, HBM, VMEM, HBM]
        + [pl.BlockSpec((1, size, share), lambda k: (k, 0, 0))] * cols
        + [ANY] * (rows - 1),
        out_specs=[pl.BlockSpec((1,) + out[1:], lambda k: (k, 0, 0))] * cols,
        scratch_shapes=[
            pltpu.VMEM((steps, size, states * size), jnp.bfloat16),
            pltpu.VMEM((steps, size, width * size), jnp.bfloat16),
            pltpu.VMEM((half * width, lanes), jnp.float32),
            pltpu.VMEM((lanes, states * lanes), jnp.bfloat16),
            pltpu.VMEM((width * lanes, lanes), jnp.bfloat16),
            pltpu.VMEM((half * states, width * lanes), jnp.bfloat16),
            pltpu.VMEM((half * states, lanes), jnp.float32),
            pltpu.SemaphoreType.DMA((2, steps)),
        ],
        compiler_params=pltpu.CompilerParams(vmem_limit_bytes=40 << 20),
        cost_estimate=pl.CostEstimate(flops=flops, bytes_accessed=4 << 20, transcendentals=0),
        name="apply",
    )(order, slots, keys, state_blocks, mpo_rows, right_env, *lefts, *rights)


def place_kernel(cols, order_ref, *refs):
    came = refs[:cols]
    out_ref, sem = refs[cols:]
    steps = came[0].shape[0]
    mine = lax.axis_index("col")
    copies = []
    for other in range(cols):
        col = jnp.bitwise_xor(mine, other)
        for step in range(steps):
            p = order_ref[col * steps + step]
            copies.append(pltpu.make_async_copy(came[other].at[step], out_ref.at[p], sem.at[len(copies)]))
    run_copies(copies)


def place_blocks(order, came):
    cols = len(came)
    count = order.shape[0]
    return pl.pallas_call(
        functools.partial(place_kernel, cols),
        out_shape=jax.ShapeDtypeStruct((count,) + came[0].shape[1:], came[0].dtype),
        in_specs=[SMEM] + [VMEM] * cols,
        out_specs=HBM,
        scratch_shapes=[pltpu.SemaphoreType.DMA((count,))],
        name="place",
    )(order, *came)


def shards(state_blocks, left_env, right_env, mpo_tensor, block_left, block_owner, block_sub):
    rows = lax.axis_size("row")
    cols = lax.axis_size("col")
    count, size = state_blocks.shape[:2]
    states = state_blocks.shape[2] // size
    width = mpo_tensor.shape[0]
    most = max(2, (2 * count + rows - 1) // rows)
    near = -(-most // cols)

    keys = jnp.bitwise_or(lax.shift_left(block_owner[:, 0], SHIFT), block_sub)
    others = [swap(keys, "row", step) for step in range(1, rows)]
    sends, order, slots = route(block_left, keys, left_env, cols, near)
    picked = pick(others, right_env, cols, near)
    near_send, first_pick = lax.optimization_barrier((sends[1], picked[0]))
    sends = [sends[0], near_send, *sends[2:]]
    picked = [first_pick, *picked[1:]]
    lefts = [sends[0]] + [swap(sends[d], "col", d) for d in range(1, cols)]
    rights = [swap(picked[d - 1], "row", d) for d in range(1, rows)]
    mpo_rows = jnp.transpose(mpo_tensor.reshape(width, width, states, states), (1, 2, 3, 0)).reshape(
        width * states, states * width
    )
    outs = apply_blocks(order, slots, keys, state_blocks, mpo_rows, right_env, lefts, rights, states, near)
    return place_blocks(order, [outs[0]] + [swap(outs[d], "col", d) for d in range(1, cols)])


def solution(mesh):
    placed = (
        P(("groups", "row"), None, None),
        P(("groups", "row"), None, "col"),
        P(("groups", "row"), None, None),
        P(),
        P(("groups", "row")),
        P(("groups", "row"), None),
        P(("groups", "row")),
    )
    return jax.shard_map(
        shards,
        mesh=mesh,
        in_specs=placed,
        out_specs=P(("groups", "row"), None, "col"),
        check_vma=False,
    )
```

time: 76.7 us -> 74.3 us (0.969)
  starting transfers between devices: 25.1 us -> 15.3 us
  waiting for transfers between devices: 5.65 us -> 14.3 us
  Pallas kernels: 29.7 us -> 28.5 us
    ppermute x21 -> x12, starting transfers between devices: 25.1 us -> 15.3 us  [swap(): return lax.ppermute(array, axis, [(i, i ^ step) for i in range(size)])]
    ppermute x21 -> x12, waiting for transfers between devices: 5.65 us -> 14.3 us  [swap(): return lax.ppermute(array, axis, [(i, i ^ step) for i in range(size)])]
    pallas_call x4 -> x3, Pallas kernels: 26.2 us -> 25 us  [the longest x1 19.6 us: apply_blocks(): pl.pallas_call(functools.partial(apply_kernel, states, rows, cols, near),...]
    unnamed x46 -> x30, local copies, waits for them, and re-layouts: 4.51 us -> 4.07 us
  transfers between devices with their start and end apart: 21 -> 12, of which waited for: 3 -> 4; matrix products, arithmetic and copies ran while one was open for 13% -> 14% of each run, Pallas kernels for 35% -> 9%
where the time goes in v3:
time: 74.3 us; the launch traced here: 73.3 us
  Pallas kernels  28.5 us (38%)
  starting transfers between devices  15.3 us (21%)
  local copies, waits for them, and re-layouts  14.3 us (19%)
  waiting for transfers between devices  14.3 us (19%)
    pallas_call x1, Pallas kernels, apply_blocks(): pl.pallas_call(functools.partial(apply_kernel, states, rows, cols, near),...  19.6 us
    ppermute x12, starting transfers between devices, swap(): return lax.ppermute(array, axis, [(i, i ^ step) for i in range(size)])  15.3 us
    ppermute x12, waiting for transfers between devices, swap(): return lax.ppermute(array, axis, [(i, i ^ step) for i in range(size)])  14.3 us
    transpose x1, local copies, waits for them, and re-layouts, shards(): jnp.transpose(mpo_tensor.reshape(width, width, states, states), (1, 2, 3,...  4.81 us
    unnamed x30, local copies, waits for them, and re-layouts  4.07 us
    pallas_call x1, Pallas kernels, pick(): pl.pallas_call(functools.partial(pick_kernel, rows, cols, near), out_shap...  3.5 us
    pallas_call x1, Pallas kernels, route(): pl.pallas_call(functools.partial(route_kernel, cols, near), out_shape=(pi...  3.38 us
    reshape x1, local copies, waits for them, and re-layouts, shards(): jnp.transpose(mpo_tensor.reshape(width, width, states, states), (1, 2, 3,...  2.81 us
  transfers between devices with their start and end apart: 12, of which 4 were waited for; matrix products, arithmetic and copies ran while one was open for 14% of the time, Pallas kernels for 9%

profile of v3, /device:TPU:0, one launch (start us, length us, event | category | flops | bytes accessed | tf_op | source)
XLA Modules:
  0.0 73.3 jit_solution(9231603920141006652)
XLA Ops:
  0.0 0.7 bitcast_or_fusion.key_ref
  1.2 2.6 %collective-permute-start.1 = (s32[16]{0:T(128)S(1)}, s32[16]{0:T(128)S(1)}, u32[]{:S(2)}, u32[]{:S(2)}) collective-permute-start(s32[16]{0:T(128)S(1)} %bitcast_or_fusion.key_ref), channel_id=1, source_target_pairs={{0,8},{4,12},{8,0},{12,4},{1,9},{5,13},{9,1},{13,5},{2,10},{6,14},... | collective-permute-start | bytes 200 | tf_op jit(solution)/shard_map/ppermute | solution.py:20
  3.8 3.4 %route.1 = (bf16[4,64,384]{2,1,0:T(8,128)(2,1)}, bf16[4,64,384]{2,1,0:T(8,128)(2,1)}, bf16[4,64,384]{2,1,0:T(8,128)(2,1)}, bf16[4,64,384]{2,1,0:T(8,128)(2,1)}, s32[16]{0:T(128)}, /*index=5*/s32[16]{0:T(128)}) custom-call(s32[16]{0:T(128)} %left_ref.1, s32[16]{0:T(128)} %copy-done.3, bf16[8,64,384]{2,1,0:T(8,128)(2,1)} %env_ref.2), custom_call_target="tpu_custom_call" | custom-call | tf_op jit(solution)/shard_map/route/pallas_call | solution.py:81
  7.2 2.8 %collective-permute-start.4 = (bf16[4,64,384]{2,1,0:T(8,128)(2,1)}, bf16[4,64,384]{2,1,0:T(8,128)(2,1)S(1)}, u32[]{:S(2)}, u32[]{:S(2)}) collective-permute-start(bf16[4,64,384]{2,1,0:T(8,128)(2,1)} %get-tuple-element.26), channel_id=1, source_target_pairs={{0,2},{1,3},{2,0},{3,1},{4,6},{5,7},{6,4},{7,5},{8,10},{9,11},{10,... | collective-permute-start | bytes 589832 | tf_op jit(solution)/shard_map/ppermute | solution.py:20
  10.6 0.6 copy-done.14
  11.2 3.5 %pick.1 = (bf16[2,64,1536]{2,1,0:T(8,128)(2,1)}, bf16[2,64,1536]{2,1,0:T(8,128)(2,1)}, bf16[2,64,1536]{2,1,0:T(8,128)(2,1)}) custom-call(s32[16]{0:T(128)} %copy-done.12, s32[16]{0:T(128)} %copy-done.13, s32[16]{0:T(128)} %copy-done.14, bf16[8,64,1536]{2,1,0:T(8,128)(2,1)} %env_ref.3), custom_call_target="tpu_custom_call" | custom-call | tf_op jit(solution)/shard_map/pick/pallas_call | solution.py:126
  14.8 1.8 %collective-permute-start.7 = (bf16[2,64,1536]{2,1,0:T(8,128)(2,1)}, bf16[2,64,1536]{2,1,0:T(8,128)(2,1)S(1)}, u32[]{:S(2)}, u32[]{:S(2)}) collective-permute-start(bf16[2,64,1536]{2,1,0:T(8,128)(2,1)} %get-tuple-element.29), channel_id=1, source_target_pairs={{0,8},{4,12},{8,0},{12,4},{1,9},{5,13},{9,1},{13,5},{2,10},{6,14},... | collective-permute-start | bytes 1179656 | tf_op jit(solution)/shard_map/ppermute | solution.py:20
  16.7 1.3 %collective-permute-start.5 = (bf16[4,64,384]{2,1,0:T(8,128)(2,1)}, bf16[4,64,384]{2,1,0:T(8,128)(2,1)}, u32[]{:S(2)}, u32[]{:S(2)}) collective-permute-start(bf16[4,64,384]{2,1,0:T(8,128)(2,1)} %get-tuple-element.27), channel_id=1, source_target_pairs={{0,3},{1,2},{2,1},{3,0},{4,7},{5,6},{6,5},{7,4},{8,11},{9,10},{10,... | collective-permute-start | bytes 589832 | tf_op jit(solution)/shard_map/ppermute | solution.py:20
  18.0 1.7 %collective-permute-done.4.refs_2_ = bf16[4,64,384]{2,1,0:T(8,128)(2,1)S(1)} collective-permute-done((bf16[4,64,384]{2,1,0:T(8,128)(2,1)}, bf16[4,64,384]{2,1,0:T(8,128)(2,1)S(1)}, u32[]{:S(2)}, u32[]{:S(2)}) %collective-permute-start.4) | collective-permute-done | bytes 196640 | tf_op jit(solution)/shard_map/ppermute | solution.py:20
  19.7 0.9 %collective-permute-start.3 = (bf16[4,64,384]{2,1,0:T(8,128)(2,1)}, bf16[4,64,384]{2,1,0:T(8,128)(2,1)}, u32[]{:S(2)}, u32[]{:S(2)}) collective-permute-start(bf16[4,64,384]{2,1,0:T(8,128)(2,1)} %get-tuple-element.25), channel_id=1, source_target_pairs={{0,1},{1,0},{2,3},{3,2},{4,5},{5,4},{6,7},{7,6},{8,9},{9,8},{10,11... | collective-permute-start | bytes 589832 | tf_op jit(solution)/shard_map/ppermute | solution.py:20
  20.6 2.6 %reshape.8 = bf16[24,24,16,16]{3,2,1,0:T(8,128)(2,1)} reshape(bf16[24,24,256]{2,1,0:T(8,128)(2,1)S(1)} %copy-done.8) | data formatting | bytes 589824 | tf_op jit(solution)/shard_map/reshape | solution.py:313
  23.3 4.8 %copy.9 = bf16[24,16,16,24]{3,2,1,0:T(8,128)(2,1)} copy(bf16[24,16,16,24]{2,1,0,3:T(8,128)(2,1)} %bitcast.5) | data formatting | bytes 589824 | tf_op jit(solution)/shard_map/transpose | solution.py:313
  28.1 2.8 %reshape.9.mpo_ref = bf16[384,384]{1,0:T(8,128)(2,1)S(1)} reshape(bf16[24,16,16,24]{3,2,1,0:T(8,128)(2,1)} %copy.9) | data formatting | bytes 589824 | tf_op jit(solution)/shard_map/reshape | solution.py:313
  30.9 3.6 %collective-permute-done.8.refs_6_ = bf16[2,64,1536]{2,1,0:T(8,128)(2,1)S(1)} collective-permute-done((bf16[2,64,1536]{2,1,0:T(8,128)(2,1)}, bf16[2,64,1536]{2,1,0:T(8,128)(2,1)S(1)}, u32[]{:S(2)}, u32[]{:S(2)}) %collective-permute-start.8) | collective-permute-done | bytes 393248 | tf_op jit(solution)/shard_map/ppermute | solution.py:20
  34.6 1.6 %copy-done.5 = bf16[16,64,1024]{2,1,0:T(8,128)(2,1)S(1)} copy-done((bf16[16,64,1024]{2,1,0:T(8,128)(2,1)S(1)}, bf16[16,64,1024]{2,1,0:T(8,128)(2,1)}, u32[]{:S(2)}) %copy-start.5) | copy-done | bytes 2097176
  36.1 19.6 %apply.1 = (bf16[4,64,256]{2,1,0:T(8,128)(2,1)S(1)}, bf16[4,64,256]{2,1,0:T(8,128)(2,1)S(1)}, bf16[4,64,256]{2,1,0:T(8,128)(2,1)S(1)}, bf16[4,64,256]{2,1,0:T(8,128)(2,1)S(1)}) custom-call(s32[16]{0:T(128)S(1)} %copy-done.2, s32[16]{0:T(128)S(1)} %copy-done.7, s32[16]{0:T(128)S(1)} %copy-done.4, bf16[16,64,1024]{2,1,0:T(8,128)(2,1)S(1)} %copy-done.5, ...), custom_call_target="tpu_custom_call" | custom-call | flops 5637144576 | bytes 4194304 | tf_op jit(solution)/shard_map/apply/pallas_call | solution.py:244
  55.8 0.6 copy-done.1
  56.4 1.3 %collective-permute-start.9 = (bf16[4,64,256]{2,1,0:T(8,128)(2,1)S(1)}, bf16[4,64,256]{2,1,0:T(8,128)(2,1)S(1)}, u32[]{:S(2)}, u32[]{:S(2)}) collective-permute-start(bf16[4,64,256]{2,1,0:T(8,128)(2,1)S(1)} %get-tuple-element.32), channel_id=1, source_target_pairs={{0,1},{1,0},{2,3},{3,2},{4,5},{5,4},{6,7},{7,6},{8,9},{9,8},{10,11... | collective-permute-start | bytes 393224 | tf_op jit(solution)/shard_map/ppermute | solution.py:20
  57.7 2.4 %collective-permute-start.10 = (bf16[4,64,256]{2,1,0:T(8,128)(2,1)S(1)}, bf16[4,64,256]{2,1,0:T(8,128)(2,1)S(1)}, u32[]{:S(2)}, u32[]{:S(2)}) collective-permute-start(bf16[4,64,256]{2,1,0:T(8,128)(2,1)S(1)} %get-tuple-element.33), channel_id=1, source_target_pairs={{0,2},{1,3},{2,0},{3,1},{4,6},{5,7},{6,4},{7,5},{8,10},{9,11},{10,... | collective-permute-start | bytes 393224 | tf_op jit(solution)/shard_map/ppermute | solution.py:20
  60.1 1.5 %collective-permute-start.11 = (bf16[4,64,256]{2,1,0:T(8,128)(2,1)S(1)}, bf16[4,64,256]{2,1,0:T(8,128)(2,1)S(1)}, u32[]{:S(2)}, u32[]{:S(2)}) collective-permute-start(bf16[4,64,256]{2,1,0:T(8,128)(2,1)S(1)} %get-tuple-element.34), channel_id=1, source_target_pairs={{0,3},{1,2},{2,1},{3,0},{4,7},{5,6},{6,5},{7,4},{8,11},{9,10},{10,... | collective-permute-start | bytes 393224 | tf_op jit(solution)/shard_map/ppermute | solution.py:20
  61.6 2.7 %collective-permute-done.9.refs_1_ = bf16[4,64,256]{2,1,0:T(8,128)(2,1)S(1)} collective-permute-done((bf16[4,64,256]{2,1,0:T(8,128)(2,1)S(1)}, bf16[4,64,256]{2,1,0:T(8,128)(2,1)S(1)}, u32[]{:S(2)}, u32[]{:S(2)}) %collective-permute-start.9) | collective-permute-done | bytes 131104 | tf_op jit(solution)/shard_map/ppermute | solution.py:20
  64.3 6.2 %collective-permute-done.10.refs_2_ = bf16[4,64,256]{2,1,0:T(8,128)(2,1)S(1)} collective-permute-done((bf16[4,64,256]{2,1,0:T(8,128)(2,1)S(1)}, bf16[4,64,256]{2,1,0:T(8,128)(2,1)S(1)}, u32[]{:S(2)}, u32[]{:S(2)}) %collective-permute-start.10) | collective-permute-done | bytes 131104 | tf_op jit(solution)/shard_map/ppermute | solution.py:20
  70.6 0.6 copy-done.10
  71.3 2.0 %place.1 = bf16[16,64,256]{2,1,0:T(8,128)(2,1)} custom-call(s32[16]{0:T(128)} %get-tuple-element.20.order_ref, bf16[4,64,256]{2,1,0:T(8,128)(2,1)} %copy-done.1, bf16[4,64,256]{2,1,0:T(8,128)(2,1)} %copy-done.9, bf16[4,64,256]{2,1,0:T(8,128)(2,1)} %copy-done.10, bf16[4,64,256]{2,1,0:T(8,128)(2,1)} %copy-done.11), custom_call_target="tpu_custom_call" | custom-call | tf_op jit(solution)/shard_map/place/pallas_call | solution.py:285
  (38 shorter events, 1.3 us)
Async XLA Ops:
  0.0 20.6 %copy-start.8 = (bf16[24,24,256]{2,1,0:T(8,128)(2,1)S(1)}, bf16[24,24,256]{2,1,0:T(8,128)(2,1)}, u32[]{:S(2)}) copy-start(bf16[24,24,256]{2,1,0:T(8,128)(2,1)} %param.10) | copy-start | bytes 884740
  0.7 3.1 %copy-start.3 = (s32[16]{0:T(128)}, s32[16]{0:T(128)S(1)}, u32[]{:S(2)}) copy-start(s32[16]{0:T(128)S(1)} %bitcast_or_fusion.key_ref) | copy-start | bytes 196
  0.7 9.4 %collective-permute-start = (s32[16]{0:T(128)S(1)}, s32[16]{0:T(128)S(1)}, u32[]{:S(2)}, u32[]{:S(2)}) collective-permute-start(s32[16]{0:T(128)S(1)} %bitcast_or_fusion.key_ref), channel_id=1, source_target_pairs={{0,4},{4,0},{8,12},{12,8},{1,5},{5,1},{9,13},{13,9},{2,6},{6,2},{1... | collective-permute-start | bytes 200 | tf_op jit(solution)/shard_map/ppermute | solution.py:20
  1.2 8.9 %collective-permute-start.1 = (s32[16]{0:T(128)S(1)}, s32[16]{0:T(128)S(1)}, u32[]{:S(2)}, u32[]{:S(2)}) collective-permute-start(s32[16]{0:T(128)S(1)} %bitcast_or_fusion.key_ref), channel_id=1, source_target_pairs={{0,8},{4,12},{8,0},{12,4},{1,9},{5,13},{9,1},{13,5},{2,10},{6,14},... | collective-permute-start | bytes 200 | tf_op jit(solution)/shard_map/ppermute | solution.py:20
  3.8 6.3 %collective-permute-start.2 = (s32[16]{0:T(128)S(1)}, s32[16]{0:T(128)S(1)}, u32[]{:S(2)}, u32[]{:S(2)}) collective-permute-start(s32[16]{0:T(128)S(1)} %bitcast_or_fusion.key_ref), channel_id=1, source_target_pairs={{0,12},{4,8},{8,4},{12,0},{1,13},{5,9},{9,5},{13,1},{2,14},{6,10},... | collective-permute-start | bytes 200 | tf_op jit(solution)/shard_map/ppermute | solution.py:20
  7.2 12.5 %collective-permute-start.4 = (bf16[4,64,384]{2,1,0:T(8,128)(2,1)}, bf16[4,64,384]{2,1,0:T(8,128)(2,1)S(1)}, u32[]{:S(2)}, u32[]{:S(2)}) collective-permute-start(bf16[4,64,384]{2,1,0:T(8,128)(2,1)} %get-tuple-element.26), channel_id=1, source_target_pairs={{0,2},{1,3},{2,0},{3,1},{4,6},{5,7},{6,4},{7,5},{8,10},{9,11},{10,... | collective-permute-start | bytes 589832 | tf_op jit(solution)/shard_map/ppermute | solution.py:20
  14.7 16.2 %collective-permute-start.6 = (bf16[2,64,1536]{2,1,0:T(8,128)(2,1)}, bf16[2,64,1536]{2,1,0:T(8,128)(2,1)S(1)}, u32[]{:S(2)}, u32[]{:S(2)}) collective-permute-start(bf16[2,64,1536]{2,1,0:T(8,128)(2,1)} %get-tuple-element.28), channel_id=1, source_target_pairs={{0,4},{4,0},{8,12},{12,8},{1,5},{5,1},{9,13},{13,9},{2,6},{6,2},{1... | collective-permute-start | bytes 1179656 | tf_op jit(solution)/shard_map/ppermute | solution.py:20
  14.8 16.1 %collective-permute-start.7 = (bf16[2,64,1536]{2,1,0:T(8,128)(2,1)}, bf16[2,64,1536]{2,1,0:T(8,128)(2,1)S(1)}, u32[]{:S(2)}, u32[]{:S(2)}) collective-permute-start(bf16[2,64,1536]{2,1,0:T(8,128)(2,1)} %get-tuple-element.29), channel_id=1, source_target_pairs={{0,8},{4,12},{8,0},{12,4},{1,9},{5,13},{9,1},{13,5},{2,10},{6,14},... | collective-permute-start | bytes 1179656 | tf_op jit(solution)/shard_map/ppermute | solution.py:20
  16.6 17.9 %collective-permute-start.8 = (bf16[2,64,1536]{2,1,0:T(8,128)(2,1)}, bf16[2,64,1536]{2,1,0:T(8,128)(2,1)S(1)}, u32[]{:S(2)}, u32[]{:S(2)}) collective-permute-start(bf16[2,64,1536]{2,1,0:T(8,128)(2,1)} %get-tuple-element.30), channel_id=1, source_target_pairs={{0,12},{4,8},{8,4},{12,0},{1,13},{5,9},{9,5},{13,1},{2,14},{6,10},... | collective-permute-start | bytes 1179656 | tf_op jit(solution)/shard_map/ppermute | solution.py:20
  16.7 14.2 %collective-permute-start.5 = (bf16[4,64,384]{2,1,0:T(8,128)(2,1)}, bf16[4,64,384]{2,1,0:T(8,128)(2,1)}, u32[]{:S(2)}, u32[]{:S(2)}) collective-permute-start(bf16[4,64,384]{2,1,0:T(8,128)(2,1)} %get-tuple-element.27), channel_id=1, source_target_pairs={{0,3},{1,2},{2,1},{3,0},{4,7},{5,6},{6,5},{7,4},{8,11},{9,10},{10,... | collective-permute-start | bytes 589832 | tf_op jit(solution)/shard_map/ppermute | solution.py:20
  19.7 11.2 %collective-permute-start.3 = (bf16[4,64,384]{2,1,0:T(8,128)(2,1)}, bf16[4,64,384]{2,1,0:T(8,128)(2,1)}, u32[]{:S(2)}, u32[]{:S(2)}) collective-permute-start(bf16[4,64,384]{2,1,0:T(8,128)(2,1)} %get-tuple-element.25), channel_id=1, source_target_pairs={{0,1},{1,0},{2,3},{3,2},{4,5},{5,4},{6,7},{7,6},{8,9},{9,8},{10,11... | collective-permute-start | bytes 589832 | tf_op jit(solution)/shard_map/ppermute | solution.py:20
  23.2 11.3 %copy-start = (bf16[8,64,1536]{2,1,0:T(8,128)(2,1)S(1)}, bf16[8,64,1536]{2,1,0:T(8,128)(2,1)}, u32[]{:S(2)}) copy-start(bf16[8,64,1536]{2,1,0:T(8,128)(2,1)} %env_ref.3) | copy-start | bytes 4718596
  23.2 11.3 %copy-start.2 = (s32[16]{0:T(128)S(1)}, s32[16]{0:T(128)}, u32[]{:S(2)}) copy-start(s32[16]{0:T(128)} %get-tuple-element.20.order_ref) | copy-start | bytes 196
  23.2 11.3 %copy-start.4 = (s32[16]{0:T(128)S(1)}, s32[16]{0:T(128)}, u32[]{:S(2)}) copy-start(s32[16]{0:T(128)} %copy-done.3) | copy-start | bytes 196
  23.2 11.3 %copy-start.6 = (bf16[4,64,384]{2,1,0:T(8,128)(2,1)S(1)}, bf16[4,64,384]{2,1,0:T(8,128)(2,1)}, u32[]{:S(2)}) copy-start(bf16[4,64,384]{2,1,0:T(8,128)(2,1)} %get-tuple-element.22.refs_0_) | copy-start | bytes 589828
  23.2 11.3 %copy-start.7 = (s32[16]{0:T(128)S(1)}, s32[16]{0:T(128)}, u32[]{:S(2)}) copy-start(s32[16]{0:T(128)} %get-tuple-element.21.slot_ref) | copy-start | bytes 196
  34.6 1.6 %copy-start.5 = (bf16[16,64,1024]{2,1,0:T(8,128)(2,1)S(1)}, bf16[16,64,1024]{2,1,0:T(8,128)(2,1)}, u32[]{:S(2)}) copy-start(bf16[16,64,1024]{2,1,0:T(8,128)(2,1)} %state_ref.1) | copy-start | bytes 6291460
  55.7 0.7 copy-start.1
  56.4 7.9 %collective-permute-start.9 = (bf16[4,64,256]{2,1,0:T(8,128)(2,1)S(1)}, bf16[4,64,256]{2,1,0:T(8,128)(2,1)S(1)}, u32[]{:S(2)}, u32[]{:S(2)}) collective-permute-start(bf16[4,64,256]{2,1,0:T(8,128)(2,1)S(1)} %get-tuple-element.32), channel_id=1, source_target_pairs={{0,1},{1,0},{2,3},{3,2},{4,5},{5,4},{6,7},{7,6},{8,9},{9,8},{10,11... | collective-permute-start | bytes 393224 | tf_op jit(solution)/shard_map/ppermute | solution.py:20
  57.7 12.8 %collective-permute-start.10 = (bf16[4,64,256]{2,1,0:T(8,128)(2,1)S(1)}, bf16[4,64,256]{2,1,0:T(8,128)(2,1)S(1)}, u32[]{:S(2)}, u32[]{:S(2)}) collective-permute-start(bf16[4,64,256]{2,1,0:T(8,128)(2,1)S(1)} %get-tuple-element.33), channel_id=1, source_target_pairs={{0,2},{1,3},{2,0},{3,1},{4,6},{5,7},{6,4},{7,5},{8,10},{9,11},{10,... | collective-permute-start | bytes 393224 | tf_op jit(solution)/shard_map/ppermute | solution.py:20
  60.1 10.4 %collective-permute-start.11 = (bf16[4,64,256]{2,1,0:T(8,128)(2,1)S(1)}, bf16[4,64,256]{2,1,0:T(8,128)(2,1)S(1)}, u32[]{:S(2)}, u32[]{:S(2)}) collective-permute-start(bf16[4,64,256]{2,1,0:T(8,128)(2,1)S(1)} %get-tuple-element.34), channel_id=1, source_target_pairs={{0,3},{1,2},{2,1},{3,0},{4,7},{5,6},{6,5},{7,4},{8,11},{9,10},{10,... | collective-permute-start | bytes 393224 | tf_op jit(solution)/shard_map/ppermute | solution.py:20
  64.3 6.2 %copy-start.9 = (bf16[4,64,256]{2,1,0:T(8,128)(2,1)}, bf16[4,64,256]{2,1,0:T(8,128)(2,1)S(1)}, u32[]{:S(2)}) copy-start(bf16[4,64,256]{2,1,0:T(8,128)(2,1)S(1)} %collective-permute-done.9.refs_1_) | copy-start | bytes 393220
  70.5 0.6 copy-start.10
  70.6 0.7 copy-start.11
  (3 other events, 1.7 us)

commit v4 on v3

v4 whole, which is shorter than its diff:
```python
import functools

import jax
import jax.numpy as jnp
from jax import lax
from jax.experimental import pallas as pl
from jax.experimental.pallas import tpu as pltpu
from jax.sharding import PartitionSpec as P

CHUNK = 8
SHIFT = 16
SMEM = pl.BlockSpec(memory_space=pltpu.SMEM)
VMEM = pl.BlockSpec(memory_space=pltpu.VMEM)
HBM = pl.BlockSpec(memory_space=pltpu.HBM)
ANY = pl.BlockSpec(memory_space=pl.ANY)


def swap(array, axis, step):
    size = lax.axis_size(axis)
    return lax.ppermute(array, axis, [(i, i ^ step) for i in range(size)])


def run_copies(copies):
    for copy in copies:
        copy.start()
    for copy in copies:
        copy.wait()


def owner_of(key):
    return lax.shift_right_logical(key, SHIFT)


def sub_of(key):
    return jnp.bitwise_and(key, (1 << SHIFT) - 1)


def route_kernel(cols, near, left_ref, key_ref, env_ref, *refs):
    sends = refs[:cols]
    order_ref, slot_ref, by_place = refs[cols:]
    count = left_ref.shape[0]
    steps = count // cols
    mine = lax.axis_index("col")
    owners = [owner_of(key_ref[p]) for p in range(count)]
    for p in range(count):
        place = jnp.int32(0)
        for other in range(count):
            if other < p:
                place = place + (owners[other] <= owners[p]).astype(jnp.int32)
            elif other > p:
                place = place + (owners[other] < owners[p]).astype(jnp.int32)
        by_place[place] = p
    for col in range(cols):
        before = None
        for step in range(steps):
            p = by_place[step * cols + col]
            owner = owner_of(key_ref[p])
            if before is None:
                slot = jnp.int32(0)
            else:
                slot = jnp.where(owner == before[0], before[1] + 1, 0)
            before = owner, slot
            order_ref[col * steps + step] = p
            slot_ref[col * steps + step] = owner * near + slot
    for other in range(cols):
        col = jnp.bitwise_xor(mine, other)
        for step in range(steps):
            p = order_ref[col * steps + step]
            sends[other][step] = env_ref[left_ref[p]]


def route(block_left, keys, left_env, cols, near):
    count = block_left.shape[0]
    size, width = left_env.shape[1:]
    piece = jax.ShapeDtypeStruct((count // cols, size, width), left_env.dtype)
    listed = jax.ShapeDtypeStruct((count,), jnp.int32)
    *sends, order, slots = pl.pallas_call(
        functools.partial(route_kernel, cols, near),
        out_shape=(piece,) * cols + (listed, listed),
        in_specs=[SMEM, SMEM, VMEM],
        out_specs=(VMEM,) * cols + (SMEM, SMEM),
        scratch_shapes=[pltpu.SMEM((count,), jnp.int32)],
        name="route",
    )(block_left, keys, left_env)
    return sends, order, slots


def pick_kernel(rows, cols, near, *refs):
    key_refs = refs[: rows - 1]
    env_ref = refs[rows - 1]
    sends = refs[rows:]
    count = key_refs[0].shape[0]
    me = lax.axis_index("row")
    mine = lax.axis_index("col")
    for other in range(rows - 1):
        keys = [key_refs[other][p] for p in range(count)]
        owners = [owner_of(key) for key in keys]
        first = jnp.int32(0)
        for p in range(count):
            first = first + (owners[p] < me).astype(jnp.int32)
        past = -lax.rem(mine - lax.rem(first, cols) + cols, cols)
        wanted = [jnp.int32(0)] * near
        for p in range(count):
            here = owners[p] == me
            for slot in range(near):
                wanted[slot] = jnp.where(here & (past == slot * cols), sub_of(keys[p]), wanted[slot])
            past = past + here.astype(jnp.int32)
        for slot in range(near):
            sends[other][slot] = env_ref[wanted[slot]]


def pick(keys, right_env, cols, near):
    rows = len(keys) + 1
    piece = jax.ShapeDtypeStruct((near,) + right_env.shape[1:], right_env.dtype)
    return pl.pallas_call(
        functools.partial(pick_kernel, rows, cols, near),
        out_shape=[piece] * (rows - 1),
        in_specs=[SMEM] * (rows - 1) + [VMEM],
        out_specs=(VMEM,) * (rows - 1),
        name="pick",
    )(*keys, right_env)


def halves(tile, low):
    swapped = pltpu.roll(tile, tile.shape[1] // 2, 1)
    zero = jnp.zeros_like(tile)
    return (
        jnp.where(low, tile, zero),
        jnp.where(low, zero, swapped),
        jnp.where(low, swapped, zero),
        jnp.where(low, zero, tile),
    )


def spread_state(block, state_diag, low):
    size = block.shape[0]
    for s in range(0, block.shape[1] // size, 2):
        pieces = halves(block[:, s * size : (s + 2) * size].astype(jnp.float32), low)
        for i in range(4):
            row, col = (i % 2) * size, (s + i // 2) * 2 * size
            state_diag[row : row + size, col : col + 2 * size] = pieces[i].astype(jnp.bfloat16)


def spread_right(right, right_diag, low):
    size = right.shape[0]
    for v in range(0, right.shape[1] // size, 2):
        pieces = halves(right[:, v * size : (v + 2) * size].astype(jnp.float32), low)
        for i in range(4):
            at = (2 * v + i) * size
            right_diag[at : at + size, :] = pieces[i].astype(jnp.bfloat16)


def spread_left(lefts, step, left_rows):
    cols = len(lefts)
    size = lefts[0].shape[1]
    half, share = size // 2, lefts[0].shape[2] // size
    mine = lax.axis_index("col")
    for other in range(cols):
        col = jnp.bitwise_xor(mine, other)
        for k in range(share):
            piece = lefts[other][step, :, k * size : (k + 1) * size].astype(jnp.float32)
            both = jnp.concatenate([piece[:half], piece[half:]], axis=1)
            left_rows[pl.ds(col * share + k, half, stride=cols * share), :] = both


def mix_block(states, left_rows, state_diag, mpo_ref, mixed):
    width = mpo_ref.shape[0] // states
    lanes = left_rows.shape[1]
    half = left_rows.shape[0] // width
    for start in range(0, half, CHUNK):
        taken = left_rows[start * width : (start + CHUNK) * width, :].astype(jnp.bfloat16)
        first = jnp.dot(taken, state_diag[...], preferred_element_type=jnp.float32)
        columns = []
        for x in range(CHUNK):
            one = first[x * width : (x + 1) * width, :]
            columns.append(
                jnp.concatenate(
                    [one[:, s * lanes : (s + 1) * lanes] for s in range(states)], axis=0
                ).astype(jnp.bfloat16)
            )
        gathered = jnp.concatenate(columns, axis=1)
        channels = jnp.dot(mpo_ref[...], gathered, preferred_element_type=jnp.float32).astype(jnp.bfloat16)
        for x in range(CHUNK):
            for v in range(width):
                mixed[(start + x) * states : (start + x + 1) * states, v * lanes : (v + 1) * lanes] = channels[
                    v * states : (v + 1) * states, x * lanes : (x + 1) * lanes
                ]


def finish_block(states, mixed, right_diag, result, outs, step, low):
    cols = len(outs)
    size = low.shape[0]
    half, per = size // 2, states // cols
    mine = lax.axis_index("col")
    result[...] = jnp.dot(mixed[...], right_diag[...], preferred_element_type=jnp.float32)
    low = low[:half]
    for other in range(cols):
        col = jnp.bitwise_xor(mine, other)
        for t in range(0, per, 2):
            one = result[pl.ds(col * per + t, half, stride=states), :]
            two = result[pl.ds(col * per + t + 1, half, stride=states), :]
            upper = jnp.where(low, one, pltpu.roll(two, size, 1))
            lower = jnp.where(low, pltpu.roll(one, size, 1), two)
            outs[other][step, :half, t * size : (t + 2) * size] = upper.astype(jnp.bfloat16)
            outs[other][step, half:, t * size : (t + 2) * size] = lower.astype(jnp.bfloat16)


def fetch_right(rows, near, first, order_ref, slot_ref, key_ref, env_ref, rights, right_now):
    steps = order_ref.shape[0] // lax.axis_size("col")
    me = lax.axis_index("row")
    for k in range(right_now.shape[0]):
        at = lax.axis_index("col") * steps + first + k
        slot = lax.rem(slot_ref[at], near)
        apart = jnp.bitwise_xor(lax.div(slot_ref[at], near), me)

        @pl.when(apart == 0)
        def _():
            right_now[k] = env_ref[sub_of(key_ref[order_ref[at]])]

        for other in range(1, rows):

            @pl.when(apart == other)
            def _():
                right_now[k] = rights[other - 1][slot]


def half_mask(size):
    return lax.broadcasted_iota(jnp.int32, (size, 2 * size), 1) < size


def mix_kernel(states, cols, count, order_ref, state_ref, mpo_ref, *refs):
    lefts, mixed, (state_diag, left_rows) = refs[:cols], refs[cols : cols + count], refs[cols + count :]
    low = half_mask(state_ref.shape[1])
    at = lax.axis_index("col") * (order_ref.shape[0] // cols)
    for k in range(count):
        spread_state(state_ref.at[order_ref[at + k]], state_diag.at[k], low)
        spread_left(lefts, k, left_rows.at[k])
    for k in range(count):
        mix_block(states, left_rows.at[k], state_diag.at[k], mpo_ref, mixed[k])


def put_own(first, order_ref, own, out_ref, sem):
    at = lax.axis_index("col") * (order_ref.shape[0] // lax.axis_size("col")) + first
    return [
        pltpu.make_async_copy(own.at[k], out_ref.at[order_ref[at + k]], sem.at[k]) for k in range(own.shape[0])
    ]


def right_kernel(states, rows, cols, near, order_ref, slot_ref, key_ref, env_ref, *refs):
    rights, refs = refs[: rows - 1], refs[rows - 1 :]
    own, right_now, right_diag, result, sem = refs[-5:]
    count = own.shape[0]
    mixed, out_ref, outs = refs[:count], refs[count], refs[count + 1 : count + cols]
    low = half_mask(env_ref.shape[1])
    fetch_right(rows, near, 0, order_ref, slot_ref, key_ref, env_ref, rights, right_now)
    for k in range(count):
        spread_right(right_now.at[k], right_diag.at[k], low)
    for k in range(count):
        finish_block(states, mixed[k], right_diag.at[k], result.at[k], (own,) + outs, k, low)
    run_copies(put_own(0, order_ref, own, out_ref, sem))


def apply_kernel(
    states, rows, cols, near, first, order_ref, slot_ref, key_ref, env_ref, state_ref, mpo_ref, out_in, *refs
):
    rights, lefts, refs = refs[: rows - 1], refs[rows - 1 : rows - 1 + cols], refs[rows - 1 + cols :]
    out_ref, outs = refs[0], refs[1:cols]
    own, right_now, state_diag, left_rows, right_diag, mixed, result, sem = refs[cols:]
    count = own.shape[0]
    low = half_mask(env_ref.shape[1])
    at = lax.axis_index("col") * (order_ref.shape[0] // cols) + first
    fetch_right(rows, near, first, order_ref, slot_ref, key_ref, env_ref, rights, right_now)
    for k in range(count):
        spread_state(state_ref.at[order_ref[at + k]], state_diag.at[k], low)
        spread_left(lefts, first + k, left_rows.at[k])
        spread_right(right_now.at[k], right_diag.at[k], low)
    for k in range(count):
        mix_block(states, left_rows.at[k], state_diag.at[k], mpo_ref, mixed.at[k])
        finish_block(states, mixed.at[k], right_diag.at[k], result.at[k], (own,) + outs, k, low)
    run_copies(put_own(first, order_ref, own, out_ref, sem))


def apply_blocks(order, slots, keys, state_blocks, mpo_rows, right_env, lefts, rights, states, near):
    cols, rows = len(lefts), len(rights) + 1
    steps, size, share = lefts[0].shape
    count = max(1, steps // 2)
    width = mpo_rows.shape[0] // states
    half, lanes = size // 2, 2 * size
    whole = jax.ShapeDtypeStruct((order.shape[0], size, states // cols * size), jnp.bfloat16)
    params = pltpu.CompilerParams(vmem_limit_bytes=32 << 20)

    def cost(blocks, mix, right):
        flops = mix * (width * size * size * states * size + (width * states) ** 2 * size * size)
        flops = 2 * blocks * (flops + right * states * size * size * width * size)
        return pl.CostEstimate(flops=flops, bytes_accessed=4 << 20, transcendentals=0)

    def sent(blocks):
        return [jax.ShapeDtypeStruct((blocks,) + whole.shape[1:], jnp.bfloat16)] * (cols - 1)

    def scratch(blocks, *names):
        kinds = dict(
            own=pltpu.VMEM((blocks,) + whole.shape[1:], jnp.bfloat16),
            right_now=pltpu.VMEM((blocks, size, width * size), jnp.bfloat16),
            state_diag=pltpu.VMEM((blocks, lanes, states * lanes), jnp.bfloat16),
            left_rows=pltpu.VMEM((blocks, half * width, lanes), jnp.float32),
            right_diag=pltpu.VMEM((blocks, width * lanes, lanes), jnp.bfloat16),
            mixed=pltpu.VMEM((blocks, half * states, width * lanes), jnp.bfloat16),
            result=pltpu.VMEM((blocks, half * states, lanes), jnp.float32),
            sem=pltpu.SemaphoreType.DMA((blocks,)),
        )
        return [kinds[name] for name in names]

    mixed = pl.pallas_call(
        functools.partial(mix_kernel, states, cols, count),
        out_shape=[jax.ShapeDtypeStruct((half * states, width * lanes), jnp.bfloat16)] * count,
        in_specs=[SMEM] + [VMEM] * (2 + cols),
        out_specs=[VMEM] * count,
        scratch_shapes=scratch(count, "state_diag", "left_rows"),
        compiler_params=params,
        cost_estimate=cost(count, 1, 0),
        name="mix",
    )(order, state_blocks, mpo_rows, *lefts)
    out, *early = pl.pallas_call(
        functools.partial(right_kernel, states, rows, cols, near),
        out_shape=[whole] + sent(count),
        in_specs=[SMEM] * 3 + [VMEM] * (rows + count),
        out_specs=[HBM] + [VMEM] * (cols - 1),
        scratch_shapes=scratch(count, "own", "right_now", "right_diag", "result", "sem"),
        compiler_params=params,
        cost_estimate=cost(count, 0, 1),
        name="right",
    )(order, slots, keys, right_env, *rights, *mixed)
    if count == steps:
        return out, [early]
    out, *late = pl.pallas_call(
        functools.partial(apply_kernel, states, rows, cols, near, count),
        out_shape=[whole] + sent(steps - count),
        in_specs=[SMEM] * 3 + [VMEM] * 3 + [HBM] + [VMEM] * (rows - 1 + cols),
        out_specs=[HBM] + [VMEM] * (cols - 1),
        scratch_shapes=scratch(
            steps - count,
            "own", "right_now", "state_diag", "left_rows", "right_diag", "mixed", "result", "sem",
        ),
        input_output_aliases={6: 0},
        compiler_params=params,
        cost_estimate=cost(steps - count, 1, 1),
        name="apply",
    )(order, slots, keys, right_env, state_blocks, mpo_rows, out, *rights, *lefts)
    return out, [early, late]


def place_kernel(cols, first, order_ref, out_in, *refs):
    came, (out_ref, sem) = refs[: cols - 1], refs[cols - 1 :]
    steps = order_ref.shape[0] // cols
    mine = lax.axis_index("col")
    copies = []
    for other in range(1, cols):
        col = jnp.bitwise_xor(mine, other)
        for k in range(came[0].shape[0]):
            p = order_ref[col * steps + first + k]
            copies.append(pltpu.make_async_copy(came[other - 1].at[k], out_ref.at[p], sem.at[len(copies)]))
    run_copies(copies)


def place_blocks(order, out, came, first):
    cols = len(came) + 1
    return pl.pallas_call(
        functools.partial(place_kernel, cols, first),
        out_shape=jax.ShapeDtypeStruct(out.shape, out.dtype),
        in_specs=[SMEM, HBM] + [VMEM] * (cols - 1),
        out_specs=HBM,
        scratch_shapes=[pltpu.SemaphoreType.DMA(((cols - 1) * came[0].shape[0],))],
        input_output_aliases={1: 0},
        name="place",
    )(order, out, *came)


def shards(state_blocks, left_env, right_env, mpo_tensor, block_left, block_owner, block_sub):
    rows = lax.axis_size("row")
    cols = lax.axis_size("col")
    count, size = state_blocks.shape[:2]
    states = state_blocks.shape[2] // size
    width = mpo_tensor.shape[0]
    most = max(2, (2 * count + rows - 1) // rows)
    near = -(-most // cols)

    keys = jnp.bitwise_or(lax.shift_left(block_owner[:, 0], SHIFT), block_sub)
    others = [swap(keys, "row", step) for step in range(1, rows)]
    sends, order, slots = route(block_left, keys, left_env, cols, near)
    order, *others = lax.optimization_barrier((order, *others))
    picked = pick(others, right_env, cols, near)
    rights = [swap(picked[d - 1], "row", d) for d in range(1, rows)]
    near_send, rights[0] = lax.optimization_barrier((sends[1], rights[0]))
    sends = [sends[0], near_send, *sends[2:]]
    lefts = [sends[0]] + [swap(sends[d], "col", d) for d in range(1, cols)]
    mpo_rows = jnp.transpose(mpo_tensor.reshape(width, width, states, states), (1, 2, 3, 0)).reshape(
        width * states, states * width
    )
    out, parts = apply_blocks(order, slots, keys, state_blocks, mpo_rows, right_env, lefts, rights, states, near)
    first, came = 0, []
    for sent in parts:
        joined = lax.optimization_barrier((*sent, *came))
        arrived = [swap(joined[d - 1], "col", d) for d in range(1, cols)]
        if came:
            out = place_blocks(order, out, joined[cols - 1 :], first)
            first += came[0].shape[0]
        came = arrived
    return place_blocks(order, out, came, first)


def solution(mesh):
    placed = (
        P(("groups", "row"), None, None),
        P(("groups", "row"), None, "col"),
        P(("groups", "row"), None, None),
        P(),
        P(("groups", "row")),
        P(("groups", "row"), None),
        P(("groups", "row")),
    )
    return jax.shard_map(
        shards,
        mesh=mesh,
        in_specs=placed,
        out_specs=P(("groups", "row"), None, "col"),
        check_vma=False,
    )
```

time: 74.3 us -> 69.1 us (0.930)
  waiting for transfers between devices: 14.3 us -> 5.07 us
  starting transfers between devices: 15.3 us -> 20.1 us
    ppermute x12 -> x15, waiting for transfers between devices: 14.3 us -> 5.07 us  [swap(): return lax.ppermute(array, axis, [(i, i ^ step) for i in range(size)])]
    ppermute x12 -> x15, starting transfers between devices: 15.3 us -> 20.1 us  [swap(): return lax.ppermute(array, axis, [(i, i ^ step) for i in range(size)])]
    pallas_call x2 -> x5, Pallas kernels: 21.6 us -> 23.4 us  [the longest x1 10.4 us: apply_blocks(): pl.pallas_call(functools.partial(apply_kernel, states, rows, cols, near,...]
    unnamed x30 -> x34, local copies, waits for them, and re-layouts: 4.07 us -> 2.84 us
    pallas_call x1, Pallas kernels: 3.38 us -> 2.3 us  [route(): pl.pallas_call(functools.partial(route_kernel, cols, near), out_shape=(pi...]
    reshape x1, local copies, waits for them, and re-layouts: 2.64 us -> 3.66 us  [shards(): mpo_tensor.reshape(width, width, states, states)]
    pallas_call x1, Pallas kernels: 3.5 us -> 2.73 us  [pick(): pl.pallas_call(functools.partial(pick_kernel, rows, cols, near), out_shap...]
  transfers between devices with their start and end apart: 12 -> 15, of which waited for: 4 -> 5; matrix products, arithmetic and copies ran while one was open for 14% -> 16% of each run, Pallas kernels for 9% -> 30%
where the time goes in v4:
time: 69.1 us; the launch traced here: 68.6 us
  Pallas kernels  28.4 us (41%)
  starting transfers between devices  20.1 us (29%)
  local copies, waits for them, and re-layouts  14 us (20%)
  waiting for transfers between devices  5.07 us (7%)
    ppermute x15, starting transfers between devices, swap(): return lax.ppermute(array, axis, [(i, i ^ step) for i in range(size)])  20.1 us
    pallas_call x1, Pallas kernels, apply_blocks(): pl.pallas_call(functools.partial(apply_kernel, states, rows, cols, near,...  10.4 us
    pallas_call x1, Pallas kernels, apply_blocks(): pl.pallas_call(functools.partial(mix_kernel, states, cols, count), out_sh...  6.25 us
    ppermute x15, waiting for transfers between devices, swap(): return lax.ppermute(array, axis, [(i, i ^ step) for i in range(size)])  5.07 us
    transpose x1, local copies, waits for them, and re-layouts, shards(): jnp.transpose(mpo_tensor.reshape(width, width, states, states), (1, 2, 3,...  4.73 us
    reshape x1, local copies, waits for them, and re-layouts, shards(): mpo_tensor.reshape(width, width, states, states)  3.66 us
    pallas_call x1, Pallas kernels, apply_blocks(): pl.pallas_call(functools.partial(right_kernel, states, rows, cols, near),...  3.42 us
    pallas_call x2, Pallas kernels, place_blocks(): pl.pallas_call(functools.partial(place_kernel, cols, first), out_shape=ja...  3.29 us
  transfers between devices with their start and end apart: 15, of which 5 were waited for; matrix products, arithmetic and copies ran while one was open for 16% of the time, Pallas kernels for 30%

profile of v4, /device:TPU:0, one launch (start us, length us, event | category | flops | bytes accessed | tf_op | source)
XLA Modules:
  0.0 68.6 jit_solution(15607208751072946529)
XLA Ops:
  0.0 0.7 bitcast_or_fusion.key_ref
  0.7 2.4 %collective-permute-start.2 = (s32[16]{0:T(128)S(1)}, s32[16]{0:T(128)S(1)}, u32[]{:S(2)}, u32[]{:S(2)}) collective-permute-start(s32[16]{0:T(128)S(1)} %bitcast_or_fusion.key_ref), channel_id=1, source_target_pairs={{0,12},{4,8},{8,4},{12,0},{1,13},{5,9},{9,5},{13,1},{2,14},{6,10},... | collective-permute-start | bytes 200 | tf_op jit(solution)/shard_map/ppermute | solution.py:20
  3.8 2.3 %route.1 = (bf16[4,64,384]{2,1,0:T(8,128)(2,1)}, bf16[4,64,384]{2,1,0:T(8,128)(2,1)}, bf16[4,64,384]{2,1,0:T(8,128)(2,1)}, bf16[4,64,384]{2,1,0:T(8,128)(2,1)}, s32[16]{0:T(128)}, /*index=5*/s32[16]{0:T(128)}) custom-call(s32[16]{0:T(128)} %left_ref.1, s32[16]{0:T(128)} %copy-done.2, bf16[8,64,384]{2,1,0:T(8,128)(2,1)} %env_ref.3), custom_call_target="tpu_custom_call" | custom-call | tf_op jit(solution)/shard_map/route/pallas_call | solution.py:77
  7.2 2.7 %pick.1 = (bf16[2,64,1536]{2,1,0:T(8,128)(2,1)}, bf16[2,64,1536]{2,1,0:T(8,128)(2,1)}, bf16[2,64,1536]{2,1,0:T(8,128)(2,1)}) custom-call(s32[16]{0:T(128)} %copy-done.16, s32[16]{0:T(128)} %copy-done.15, s32[16]{0:T(128)} %copy-done.14, bf16[8,64,1536]{2,1,0:T(8,128)(2,1)} %env_ref.5), custom_call_target="tpu_custom_call" | custom-call | tf_op jit(solution)/shard_map/pick/pallas_call | solution.py:115
  9.9 2.6 %collective-permute-start.7 = (bf16[4,64,384]{2,1,0:T(8,128)(2,1)}, bf16[4,64,384]{2,1,0:T(8,128)(2,1)S(1)}, u32[]{:S(2)}, u32[]{:S(2)}) collective-permute-start(bf16[4,64,384]{2,1,0:T(8,128)(2,1)} %get-tuple-element.52), channel_id=1, source_target_pairs={{0,2},{1,3},{2,0},{3,1},{4,6},{5,7},{6,4},{7,5},{8,10},{9,11},{10,... | collective-permute-start | bytes 589832 | tf_op jit(solution)/shard_map/ppermute | solution.py:20
  12.5 1.3 %collective-permute-start.8 = (bf16[4,64,384]{2,1,0:T(8,128)(2,1)}, bf16[4,64,384]{2,1,0:T(8,128)(2,1)S(1)}, u32[]{:S(2)}, u32[]{:S(2)}) collective-permute-start(bf16[4,64,384]{2,1,0:T(8,128)(2,1)} %get-tuple-element.53), channel_id=1, source_target_pairs={{0,3},{1,2},{2,1},{3,0},{4,7},{5,6},{6,5},{7,4},{8,11},{9,10},{10,... | collective-permute-start | bytes 589832 | tf_op jit(solution)/shard_map/ppermute | solution.py:20
  14.1 1.3 %collective-permute-start.4 = (bf16[2,64,1536]{2,1,0:T(8,128)(2,1)}, bf16[2,64,1536]{2,1,0:T(8,128)(2,1)S(1)}, u32[]{:S(2)}, u32[]{:S(2)}) collective-permute-start(bf16[2,64,1536]{2,1,0:T(8,128)(2,1)} %get-tuple-element.48), channel_id=1, source_target_pairs={{0,8},{4,12},{8,0},{12,4},{1,9},{5,13},{9,1},{13,5},{2,10},{6,14},... | collective-permute-start | bytes 1179656 | tf_op jit(solution)/shard_map/ppermute | solution.py:20
  15.5 3.7 %reshape.8 = bf16[24,24,16,16]{3,2,1,0:T(8,128)(2,1)} reshape(bf16[24,24,256]{2,1,0:T(8,128)(2,1)} %param.10) | data formatting | bytes 589824 | tf_op jit(solution)/shard_map/reshape | solution.py:396
  19.1 4.7 %copy.12 = bf16[24,16,16,24]{3,2,1,0:T(8,128)(2,1)} copy(bf16[24,16,16,24]{2,1,0,3:T(8,128)(2,1)} %bitcast.5) | data formatting | bytes 589824 | tf_op jit(solution)/shard_map/transpose | solution.py:396
  23.9 2.8 %reshape.9.mpo_ref = bf16[384,384]{1,0:T(8,128)(2,1)S(1)} reshape(bf16[24,16,16,24]{3,2,1,0:T(8,128)(2,1)} %copy.12) | data formatting | bytes 589824 | tf_op jit(solution)/shard_map/reshape | solution.py:396
  27.2 0.9 %collective-permute-done.6.refs_1_.refs_4_ = bf16[4,64,384]{2,1,0:T(8,128)(2,1)S(1)} collective-permute-done((bf16[4,64,384]{2,1,0:T(8,128)(2,1)}, bf16[4,64,384]{2,1,0:T(8,128)(2,1)S(1)}, u32[]{:S(2)}, u32[]{:S(2)}) %collective-permute-start.6) | collective-permute-done | bytes 196640 | tf_op jit(solution)/shard_map/ppermute | solution.py:20
  28.2 1.6 %copy-done.5 = bf16[16,64,1024]{2,1,0:T(8,128)(2,1)S(1)} copy-done((bf16[16,64,1024]{2,1,0:T(8,128)(2,1)S(1)}, bf16[16,64,1024]{2,1,0:T(8,128)(2,1)}, u32[]{:S(2)}) %copy-start.5) | copy-done | bytes 2097176
  29.8 6.3 %mix.1 = (bf16[512,3072]{1,0:T(8,128)(2,1)S(1)}, bf16[512,3072]{1,0:T(8,128)(2,1)S(1)}) custom-call(s32[16]{0:T(128)S(1)} %copy-done.1, bf16[16,64,1024]{2,1,0:T(8,128)(2,1)S(1)} %copy-done.5, bf16[384,384]{1,0:T(8,128)(2,1)S(1)} %reshape.9.mpo_ref, bf16[4,64,384]{2,1,0:T(8,128)(2,1)S(1)} %copy-done.7, ...), custom_call_target="tpu_custom_call" | custom-call | flops 2818572288 | bytes 4194304 | tf_op jit(solution)/shard_map/mix/pallas_call | solution.py:313
  36.1 3.4 %right.1 = (bf16[16,64,256]{2,1,0:T(8,128)(2,1)}, bf16[2,64,256]{2,1,0:T(8,128)(2,1)S(1)}, bf16[2,64,256]{2,1,0:T(8,128)(2,1)S(1)}, bf16[2,64,256]{2,1,0:T(8,128)(2,1)S(1)}) custom-call(s32[16]{0:T(128)S(1)} %copy-done.1, s32[16]{0:T(128)S(1)} %copy-done.4, s32[16]{0:T(128)S(1)} %copy-done.3, bf16[8,64,1536]{2,1,0:T(8,128)(2,1)S(1)} %copy-done, ...), custom_call_target="tpu_custom_call" | custom-call | flops 402653184 | bytes 4194304 | tf_op jit(solution)/shard_map/right/pallas_call | solution.py:323
  39.5 3.7 %collective-permute-start.9 = (bf16[2,64,256]{2,1,0:T(8,128)(2,1)S(1)}, bf16[2,64,256]{2,1,0:T(8,128)(2,1)S(1)}, u32[]{:S(2)}, u32[]{:S(2)}) collective-permute-start(bf16[2,64,256]{2,1,0:T(8,128)(2,1)S(1)} %get-tuple-element.64), channel_id=1, source_target_pairs={{0,1},{1,0},{2,3},{3,2},{4,5},{5,4},{6,7},{7,6},{8,9},{9,8},{10,11... | collective-permute-start | bytes 196616 | tf_op jit(solution)/shard_map/ppermute | solution.py:20
  43.3 1.9 %collective-permute-start.10 = (bf16[2,64,256]{2,1,0:T(8,128)(2,1)S(1)}, bf16[2,64,256]{2,1,0:T(8,128)(2,1)S(1)}, u32[]{:S(2)}, u32[]{:S(2)}) collective-permute-start(bf16[2,64,256]{2,1,0:T(8,128)(2,1)S(1)} %get-tuple-element.65), channel_id=1, source_target_pairs={{0,2},{1,3},{2,0},{3,1},{4,6},{5,7},{6,4},{7,5},{8,10},{9,11},{10,... | collective-permute-start | bytes 196616 | tf_op jit(solution)/shard_map/ppermute | solution.py:20
  45.1 1.4 %collective-permute-start.11 = (bf16[2,64,256]{2,1,0:T(8,128)(2,1)S(1)}, bf16[2,64,256]{2,1,0:T(8,128)(2,1)S(1)}, u32[]{:S(2)}, u32[]{:S(2)}) collective-permute-start(bf16[2,64,256]{2,1,0:T(8,128)(2,1)S(1)} %get-tuple-element.66), channel_id=1, source_target_pairs={{0,3},{1,2},{2,1},{3,0},{4,7},{5,6},{6,5},{7,4},{8,11},{9,10},{10,... | collective-permute-start | bytes 196616 | tf_op jit(solution)/shard_map/ppermute | solution.py:20
  46.5 10.4 %apply.1 = (bf16[16,64,256]{2,1,0:T(8,128)(2,1)}, bf16[2,64,256]{2,1,0:T(8,128)(2,1)S(1)}, bf16[2,64,256]{2,1,0:T(8,128)(2,1)S(1)}, bf16[2,64,256]{2,1,0:T(8,128)(2,1)S(1)}) custom-call(s32[16]{0:T(128)S(1)} %copy-done.1, s32[16]{0:T(128)S(1)} %copy-done.4, s32[16]{0:T(128)S(1)} %copy-done.3, ...), custom_call_target="tpu_custom_call", output_to_operand_aliasing={{0}: (6, {})} | custom-call | flops 3221225472 | bytes 4194304 | tf_op jit(solution)/shard_map/apply/pallas_call | solution.py:335
  57.7 2.4 %collective-permute-start.13 = (bf16[2,64,256]{2,1,0:T(8,128)(2,1)S(1)}, bf16[2,64,256]{2,1,0:T(8,128)(2,1)S(1)}, u32[]{:S(2)}, u32[]{:S(2)}) collective-permute-start(bf16[2,64,256]{2,1,0:T(8,128)(2,1)S(1)} %get-tuple-element.71), channel_id=1, source_target_pairs={{0,2},{1,3},{2,0},{3,1},{4,6},{5,7},{6,4},{7,5},{8,10},{9,11},{10,... | collective-permute-start | bytes 196616 | tf_op jit(solution)/shard_map/ppermute | solution.py:20
  60.1 1.4 %collective-permute-start.14 = (bf16[2,64,256]{2,1,0:T(8,128)(2,1)S(1)}, bf16[2,64,256]{2,1,0:T(8,128)(2,1)S(1)}, u32[]{:S(2)}, u32[]{:S(2)}) collective-permute-start(bf16[2,64,256]{2,1,0:T(8,128)(2,1)S(1)} %get-tuple-element.72), channel_id=1, source_target_pairs={{0,3},{1,2},{2,1},{3,0},{4,7},{5,6},{6,5},{7,4},{8,11},{9,10},{10,... | collective-permute-start | bytes 196616 | tf_op jit(solution)/shard_map/ppermute | solution.py:20
  61.5 1.6 %place.2.out_in = bf16[16,64,256]{2,1,0:T(8,128)(2,1)} custom-call(s32[16]{0:T(128)} %get-tuple-element.40.order_ref, bf16[16,64,256]{2,1,0:T(8,128)(2,1)} %get-tuple-element.57.out_in, bf16[2,64,256]{2,1,0:T(8,128)(2,1)} %copy-done.8, bf16[2,64,256]{2,1,0:T(8,128)(2,1)} %copy-done.9, bf16[2,64,256]{2,1,0:T(8,128)(2,1)} %copy-done.10), custom_call_target="tpu_custom_call", output_to_operand_aliasing={{}: (1, {})} | custom-call | tf_op jit(solution)/shard_map/place/pallas_call | solution.py:367
  63.2 1.6 %collective-permute-done.13.refs_1_ = bf16[2,64,256]{2,1,0:T(8,128)(2,1)S(1)} collective-permute-done((bf16[2,64,256]{2,1,0:T(8,128)(2,1)S(1)}, bf16[2,64,256]{2,1,0:T(8,128)(2,1)S(1)}, u32[]{:S(2)}, u32[]{:S(2)}) %collective-permute-start.13) | collective-permute-done | bytes 65568 | tf_op jit(solution)/shard_map/ppermute | solution.py:20
  64.8 1.4 %collective-permute-done.14.refs_2_ = bf16[2,64,256]{2,1,0:T(8,128)(2,1)S(1)} collective-permute-done((bf16[2,64,256]{2,1,0:T(8,128)(2,1)S(1)}, bf16[2,64,256]{2,1,0:T(8,128)(2,1)S(1)}, u32[]{:S(2)}, u32[]{:S(2)}) %collective-permute-start.14) | collective-permute-done | bytes 65568 | tf_op jit(solution)/shard_map/ppermute | solution.py:20
  66.8 1.6 %place.3 = bf16[16,64,256]{2,1,0:T(8,128)(2,1)} custom-call(s32[16]{0:T(128)} %get-tuple-element.40.order_ref, bf16[16,64,256]{2,1,0:T(8,128)(2,1)} %place.2.out_in, bf16[2,64,256]{2,1,0:T(8,128)(2,1)} %copy-done.11, bf16[2,64,256]{2,1,0:T(8,128)(2,1)} %copy-done.12, bf16[2,64,256]{2,1,0:T(8,128)(2,1)} %copy-done.13), custom_call_target="tpu_custom_call", output_to_operand_aliasing={{}: (1, {})} | custom-call | tf_op jit(solution)/shard_map/place/pallas_call | solution.py:367
  (51 shorter events, 3.9 us)
Async XLA Ops:
  0.7 5.4 %collective-permute-start.2 = (s32[16]{0:T(128)S(1)}, s32[16]{0:T(128)S(1)}, u32[]{:S(2)}, u32[]{:S(2)}) collective-permute-start(s32[16]{0:T(128)S(1)} %bitcast_or_fusion.key_ref), channel_id=1, source_target_pairs={{0,12},{4,8},{8,4},{12,0},{1,13},{5,9},{9,5},{13,1},{2,14},{6,10},... | collective-permute-start | bytes 200 | tf_op jit(solution)/shard_map/ppermute | solution.py:20
  3.1 3.5 %collective-permute-start.1 = (s32[16]{0:T(128)S(1)}, s32[16]{0:T(128)S(1)}, u32[]{:S(2)}, u32[]{:S(2)}) collective-permute-start(s32[16]{0:T(128)S(1)} %bitcast_or_fusion.key_ref), channel_id=1, source_target_pairs={{0,8},{4,12},{8,0},{12,4},{1,9},{5,13},{9,1},{13,5},{2,10},{6,14},... | collective-permute-start | bytes 200 | tf_op jit(solution)/shard_map/ppermute | solution.py:20
  3.7 2.9 %collective-permute-start = (s32[16]{0:T(128)S(1)}, s32[16]{0:T(128)S(1)}, u32[]{:S(2)}, u32[]{:S(2)}) collective-permute-start(s32[16]{0:T(128)S(1)} %bitcast_or_fusion.key_ref), channel_id=1, source_target_pairs={{0,4},{4,0},{8,12},{12,8},{1,5},{5,1},{9,13},{13,9},{2,6},{6,2},{1... | collective-permute-start | bytes 200 | tf_op jit(solution)/shard_map/ppermute | solution.py:20
  9.9 3.9 %collective-permute-start.3 = (bf16[2,64,1536]{2,1,0:T(8,128)(2,1)}, bf16[2,64,1536]{2,1,0:T(8,128)(2,1)S(1)}, u32[]{:S(2)}, u32[]{:S(2)}) collective-permute-start(bf16[2,64,1536]{2,1,0:T(8,128)(2,1)} %get-tuple-element.46), channel_id=1, source_target_pairs={{0,4},{4,0},{8,12},{12,8},{1,5},{5,1},{9,13},{13,9},{2,6},{6,2},{1... | collective-permute-start | bytes 1179656 | tf_op jit(solution)/shard_map/ppermute | solution.py:20
  9.9 17.3 %collective-permute-start.7 = (bf16[4,64,384]{2,1,0:T(8,128)(2,1)}, bf16[4,64,384]{2,1,0:T(8,128)(2,1)S(1)}, u32[]{:S(2)}, u32[]{:S(2)}) collective-permute-start(bf16[4,64,384]{2,1,0:T(8,128)(2,1)} %get-tuple-element.52), channel_id=1, source_target_pairs={{0,2},{1,3},{2,0},{3,1},{4,6},{5,7},{6,4},{7,5},{8,10},{9,11},{10,... | collective-permute-start | bytes 589832 | tf_op jit(solution)/shard_map/ppermute | solution.py:20
  12.5 14.7 %collective-permute-start.8 = (bf16[4,64,384]{2,1,0:T(8,128)(2,1)}, bf16[4,64,384]{2,1,0:T(8,128)(2,1)S(1)}, u32[]{:S(2)}, u32[]{:S(2)}) collective-permute-start(bf16[4,64,384]{2,1,0:T(8,128)(2,1)} %get-tuple-element.53), channel_id=1, source_target_pairs={{0,3},{1,2},{2,1},{3,0},{4,7},{5,6},{6,5},{7,4},{8,11},{9,10},{10,... | collective-permute-start | bytes 589832 | tf_op jit(solution)/shard_map/ppermute | solution.py:20
  13.9 14.3 %collective-permute-start.6 = (bf16[4,64,384]{2,1,0:T(8,128)(2,1)}, bf16[4,64,384]{2,1,0:T(8,128)(2,1)S(1)}, u32[]{:S(2)}, u32[]{:S(2)}) collective-permute-start(bf16[4,64,384]{2,1,0:T(8,128)(2,1)} %get-tuple-element.51), channel_id=1, source_target_pairs={{0,1},{1,0},{2,3},{3,2},{4,5},{5,4},{6,7},{7,6},{8,9},{9,8},{10,11... | collective-permute-start | bytes 589832 | tf_op jit(solution)/shard_map/ppermute | solution.py:20
  14.1 21.9 %collective-permute-start.4 = (bf16[2,64,1536]{2,1,0:T(8,128)(2,1)}, bf16[2,64,1536]{2,1,0:T(8,128)(2,1)S(1)}, u32[]{:S(2)}, u32[]{:S(2)}) collective-permute-start(bf16[2,64,1536]{2,1,0:T(8,128)(2,1)} %get-tuple-element.48), channel_id=1, source_target_pairs={{0,8},{4,12},{8,0},{12,4},{1,9},{5,13},{9,1},{13,5},{2,10},{6,14},... | collective-permute-start | bytes 1179656 | tf_op jit(solution)/shard_map/ppermute | solution.py:20
  15.5 20.6 %collective-permute-start.5 = (bf16[2,64,1536]{2,1,0:T(8,128)(2,1)}, bf16[2,64,1536]{2,1,0:T(8,128)(2,1)S(1)}, u32[]{:S(2)}, u32[]{:S(2)}) collective-permute-start(bf16[2,64,1536]{2,1,0:T(8,128)(2,1)} %get-tuple-element.49), channel_id=1, source_target_pairs={{0,12},{4,8},{8,4},{12,0},{1,13},{5,9},{9,5},{13,1},{2,14},{6,10},... | collective-permute-start | bytes 1179656 | tf_op jit(solution)/shard_map/ppermute | solution.py:20
  19.1 9.0 %copy-start.1 = (s32[16]{0:T(128)S(1)}, s32[16]{0:T(128)}, u32[]{:S(2)}) copy-start(s32[16]{0:T(128)} %get-tuple-element.40.order_ref) | copy-start | bytes 196
  19.1 9.0 %copy-start.7 = (bf16[4,64,384]{2,1,0:T(8,128)(2,1)S(1)}, bf16[4,64,384]{2,1,0:T(8,128)(2,1)}, u32[]{:S(2)}) copy-start(bf16[4,64,384]{2,1,0:T(8,128)(2,1)} %get-tuple-element.50.refs_0_.refs_3_) | copy-start | bytes 589828
  29.8 6.3 %copy-start = (bf16[8,64,1536]{2,1,0:T(8,128)(2,1)S(1)}, bf16[8,64,1536]{2,1,0:T(8,128)(2,1)}, u32[]{:S(2)}) copy-start(bf16[8,64,1536]{2,1,0:T(8,128)(2,1)} %env_ref.5) | copy-start | bytes 4718596
  29.8 6.3 %copy-start.3 = (s32[16]{0:T(128)S(1)}, s32[16]{0:T(128)}, u32[]{:S(2)}) copy-start(s32[16]{0:T(128)} %copy-done.2) | copy-start | bytes 196
  29.8 6.3 %copy-start.4 = (s32[16]{0:T(128)S(1)}, s32[16]{0:T(128)}, u32[]{:S(2)}) copy-start(s32[16]{0:T(128)} %get-tuple-element.41.slot_ref) | copy-start | bytes 196
  36.1 10.5 %copy-start.6 = (bf16[16,64,1024]{2,1,0:T(8,128)(2,1)S(1)}, bf16[16,64,1024]{2,1,0:T(8,128)(2,1)}, u32[]{:S(2)}) copy-start(bf16[16,64,1024]{2,1,0:T(8,128)(2,1)} %state_ref.3) | copy-start | bytes 6291460
  39.5 17.5 %collective-permute-start.9 = (bf16[2,64,256]{2,1,0:T(8,128)(2,1)S(1)}, bf16[2,64,256]{2,1,0:T(8,128)(2,1)S(1)}, u32[]{:S(2)}, u32[]{:S(2)}) collective-permute-start(bf16[2,64,256]{2,1,0:T(8,128)(2,1)S(1)} %get-tuple-element.64), channel_id=1, source_target_pairs={{0,1},{1,0},{2,3},{3,2},{4,5},{5,4},{6,7},{7,6},{8,9},{9,8},{10,11... | collective-permute-start | bytes 196616 | tf_op jit(solution)/shard_map/ppermute | solution.py:20
  43.3 13.7 %collective-permute-start.10 = (bf16[2,64,256]{2,1,0:T(8,128)(2,1)S(1)}, bf16[2,64,256]{2,1,0:T(8,128)(2,1)S(1)}, u32[]{:S(2)}, u32[]{:S(2)}) collective-permute-start(bf16[2,64,256]{2,1,0:T(8,128)(2,1)S(1)} %get-tuple-element.65), channel_id=1, source_target_pairs={{0,2},{1,3},{2,0},{3,1},{4,6},{5,7},{6,4},{7,5},{8,10},{9,11},{10,... | collective-permute-start | bytes 196616 | tf_op jit(solution)/shard_map/ppermute | solution.py:20
  45.1 11.9 %collective-permute-start.11 = (bf16[2,64,256]{2,1,0:T(8,128)(2,1)S(1)}, bf16[2,64,256]{2,1,0:T(8,128)(2,1)S(1)}, u32[]{:S(2)}, u32[]{:S(2)}) collective-permute-start(bf16[2,64,256]{2,1,0:T(8,128)(2,1)S(1)} %get-tuple-element.66), channel_id=1, source_target_pairs={{0,3},{1,2},{2,1},{3,0},{4,7},{5,6},{6,5},{7,4},{8,11},{9,10},{10,... | collective-permute-start | bytes 196616 | tf_op jit(solution)/shard_map/ppermute | solution.py:20
  57.0 4.5 %copy-start.8 = (bf16[2,64,256]{2,1,0:T(8,128)(2,1)}, bf16[2,64,256]{2,1,0:T(8,128)(2,1)S(1)}, u32[]{:S(2)}) copy-start(bf16[2,64,256]{2,1,0:T(8,128)(2,1)S(1)} %collective-permute-done.9.refs_0_) | copy-start | bytes 196612
  57.0 4.5 %copy-start.9 = (bf16[2,64,256]{2,1,0:T(8,128)(2,1)}, bf16[2,64,256]{2,1,0:T(8,128)(2,1)S(1)}, u32[]{:S(2)}) copy-start(bf16[2,64,256]{2,1,0:T(8,128)(2,1)S(1)} %collective-permute-done.10.refs_1_) | copy-start | bytes 196612
  57.0 4.5 %copy-start.10 = (bf16[2,64,256]{2,1,0:T(8,128)(2,1)}, bf16[2,64,256]{2,1,0:T(8,128)(2,1)S(1)}, u32[]{:S(2)}) copy-start(bf16[2,64,256]{2,1,0:T(8,128)(2,1)S(1)} %collective-permute-done.11.refs_2_) | copy-start | bytes 196612
  57.0 6.1 %collective-permute-start.12 = (bf16[2,64,256]{2,1,0:T(8,128)(2,1)S(1)}, bf16[2,64,256]{2,1,0:T(8,128)(2,1)S(1)}, u32[]{:S(2)}, u32[]{:S(2)}) collective-permute-start(bf16[2,64,256]{2,1,0:T(8,128)(2,1)S(1)} %get-tuple-element.70), channel_id=1, source_target_pairs={{0,1},{1,0},{2,3},{3,2},{4,5},{5,4},{6,7},{7,6},{8,9},{9,8},{10,11... | collective-permute-start | bytes 196616 | tf_op jit(solution)/shard_map/ppermute | solution.py:20
  57.7 7.1 %collective-permute-start.13 = (bf16[2,64,256]{2,1,0:T(8,128)(2,1)S(1)}, bf16[2,64,256]{2,1,0:T(8,128)(2,1)S(1)}, u32[]{:S(2)}, u32[]{:S(2)}) collective-permute-start(bf16[2,64,256]{2,1,0:T(8,128)(2,1)S(1)} %get-tuple-element.71), channel_id=1, source_target_pairs={{0,2},{1,3},{2,0},{3,1},{4,6},{5,7},{6,4},{7,5},{8,10},{9,11},{10,... | collective-permute-start | bytes 196616 | tf_op jit(solution)/shard_map/ppermute | solution.py:20
  60.1 6.1 %collective-permute-start.14 = (bf16[2,64,256]{2,1,0:T(8,128)(2,1)S(1)}, bf16[2,64,256]{2,1,0:T(8,128)(2,1)S(1)}, u32[]{:S(2)}, u32[]{:S(2)}) collective-permute-start(bf16[2,64,256]{2,1,0:T(8,128)(2,1)S(1)} %get-tuple-element.72), channel_id=1, source_target_pairs={{0,3},{1,2},{2,1},{3,0},{4,7},{5,6},{6,5},{7,4},{8,11},{9,10},{10,... | collective-permute-start | bytes 196616 | tf_op jit(solution)/shard_map/ppermute | solution.py:20
  (8 other events, 11.5 us)

commit v5 on v4

v5 whole, which is shorter than its diff:
```python
import functools

import jax
import jax.numpy as jnp
from jax import lax
from jax.experimental import pallas as pl
from jax.experimental.pallas import tpu as pltpu
from jax.sharding import PartitionSpec as P

CHUNK = 8
SHIFT = 16
SMEM = pl.BlockSpec(memory_space=pltpu.SMEM)
VMEM = pl.BlockSpec(memory_space=pltpu.VMEM)
HBM = pl.BlockSpec(memory_space=pltpu.HBM)
ANY = pl.BlockSpec(memory_space=pl.ANY)


def swap(array, axis, step):
    size = lax.axis_size(axis)
    return lax.ppermute(array, axis, [(i, i ^ step) for i in range(size)])


def run_copies(copies):
    for copy in copies:
        copy.start()
    for copy in copies:
        copy.wait()


def owner_of(key):
    return lax.shift_right_logical(key, SHIFT)


def sub_of(key):
    return jnp.bitwise_and(key, (1 << SHIFT) - 1)


def route_kernel(cols, near, left_ref, key_ref, env_ref, *refs):
    sends = refs[:cols]
    order_ref, slot_ref, by_place = refs[cols:]
    count = left_ref.shape[0]
    steps = count // cols
    mine = lax.axis_index("col")
    owners = [owner_of(key_ref[p]) for p in range(count)]
    for p in range(count):
        place = jnp.int32(0)
        for other in range(count):
            if other < p:
                place = place + (owners[other] <= owners[p]).astype(jnp.int32)
            elif other > p:
                place = place + (owners[other] < owners[p]).astype(jnp.int32)
        by_place[place] = p
    for col in range(cols):
        before = None
        for step in range(steps):
            p = by_place[step * cols + col]
            owner = owner_of(key_ref[p])
            if before is None:
                slot = jnp.int32(0)
            else:
                slot = jnp.where(owner == before[0], before[1] + 1, 0)
            before = owner, slot
            order_ref[col * steps + step] = p
            slot_ref[col * steps + step] = owner * near + slot
    for other in range(cols):
        col = jnp.bitwise_xor(mine, other)
        for step in range(steps):
            p = order_ref[col * steps + step]
            sends[other][step] = env_ref[left_ref[p]]


def route(block_left, keys, left_env, cols, near):
    count = block_left.shape[0]
    size, width = left_env.shape[1:]
    piece = jax.ShapeDtypeStruct((count // cols, size, width), left_env.dtype)
    listed = jax.ShapeDtypeStruct((count,), jnp.int32)
    *sends, order, slots = pl.pallas_call(
        functools.partial(route_kernel, cols, near),
        out_shape=(piece,) * cols + (listed, listed),
        in_specs=[SMEM, SMEM, VMEM],
        out_specs=(VMEM,) * cols + (SMEM, SMEM),
        scratch_shapes=[pltpu.SMEM((count,), jnp.int32)],
        compiler_params=pltpu.CompilerParams(vmem_limit_bytes=6 << 20),
        name="route",
    )(block_left, keys, left_env)
    return sends, order, slots


def pick_kernel(rows, cols, near, *refs):
    key_refs = refs[: rows - 1]
    env_ref = refs[rows - 1]
    sends = refs[rows:]
    count = key_refs[0].shape[0]
    me = lax.axis_index("row")
    mine = lax.axis_index("col")
    for other in range(rows - 1):
        keys = [key_refs[other][p] for p in range(count)]
        owners = [owner_of(key) for key in keys]
        first = jnp.int32(0)
        for p in range(count):
            first = first + (owners[p] < me).astype(jnp.int32)
        past = -lax.rem(mine - lax.rem(first, cols) + cols, cols)
        wanted = [jnp.int32(0)] * near
        for p in range(count):
            here = owners[p] == me
            for slot in range(near):
                wanted[slot] = jnp.where(here & (past == slot * cols), sub_of(keys[p]), wanted[slot])
            past = past + here.astype(jnp.int32)
        for slot in range(near):
            sends[other][slot] = env_ref[wanted[slot]]


def pick(keys, right_env, cols, near):
    rows = len(keys) + 1
    piece = jax.ShapeDtypeStruct((near,) + right_env.shape[1:], right_env.dtype)
    return pl.pallas_call(
        functools.partial(pick_kernel, rows, cols, near),
        out_shape=[piece] * (rows - 1),
        in_specs=[SMEM] * (rows - 1) + [VMEM],
        out_specs=(VMEM,) * (rows - 1),
        compiler_params=pltpu.CompilerParams(vmem_limit_bytes=8 << 20),
        name="pick",
    )(*keys, right_env)


def halves(tile, low):
    swapped = pltpu.roll(tile, tile.shape[1] // 2, 1)
    zero = jnp.zeros_like(tile)
    return (
        jnp.where(low, tile, zero),
        jnp.where(low, zero, swapped),
        jnp.where(low, swapped, zero),
        jnp.where(low, zero, tile),
    )


def spread_state(block, state_diag, low):
    size = block.shape[0]
    for s in range(0, block.shape[1] // size, 2):
        pieces = halves(block[:, s * size : (s + 2) * size].astype(jnp.float32), low)
        for i in range(4):
            row, col = (i % 2) * size, (s + i // 2) * 2 * size
            state_diag[row : row + size, col : col + 2 * size] = pieces[i].astype(jnp.bfloat16)


def spread_right(right, right_diag, low):
    size = right.shape[0]
    for v in range(0, right.shape[1] // size, 2):
        pieces = halves(right[:, v * size : (v + 2) * size].astype(jnp.float32), low)
        for i in range(4):
            at = (2 * v + i) * size
            right_diag[at : at + size, :] = pieces[i].astype(jnp.bfloat16)


def spread_left(lefts, step, left_rows, at):
    cols = len(lefts)
    size = lefts[0].shape[1]
    half, share = size // 2, lefts[0].shape[2] // size
    mine = lax.axis_index("col")
    for other in range(cols):
        col = jnp.bitwise_xor(mine, other)
        for k in range(share):
            piece = lefts[other][step, :, k * size : (k + 1) * size].astype(jnp.float32)
            both = jnp.concatenate([piece[:half], piece[half:]], axis=1)
            left_rows[pl.ds(at + col * share + k, half, stride=cols * share), :] = both


def mix_blocks(states, first, count, lefts, diag_ref, mpo_ref, left_rows, one_ref, two_ref, mixed):
    width = mpo_ref.shape[0] // states
    lanes = left_rows.shape[1]
    half = lanes // 4
    chunks = half // CHUNK
    total = count * chunks

    def spread(k, carry):
        spread_left(lefts, first + k, left_rows, k * (half * width))
        return carry

    lax.fori_loop(0, count, spread, 0)

    def first_sum(i, into):
        rows = CHUNK * width
        taken = left_rows[pl.ds(pl.multiple_of(i * rows, rows), rows), :].astype(jnp.bfloat16)
        summed = jnp.dot(taken, diag_ref[first + lax.div(i, chunks)], preferred_element_type=jnp.float32)
        for x in range(CHUNK):
            one = summed[x * width : (x + 1) * width, :]
            for s in range(0, states, 2):
                both = jnp.concatenate(
                    [one[:, s * lanes : (s + 1) * lanes], one[:, (s + 1) * lanes : (s + 2) * lanes]], axis=0
                )
                into[s * width : (s + 2) * width, x * lanes : (x + 1) * lanes] = both.astype(jnp.bfloat16)

    def second_sum(i, taken):
        channels = jnp.dot(mpo_ref[...], taken[...], preferred_element_type=jnp.float32).astype(jnp.bfloat16)
        for x in range(CHUNK):
            row = pl.ds(pl.multiple_of((i * CHUNK + x) * states, states), states)
            for v in range(width):
                mixed[row, v * lanes : (v + 1) * lanes] = channels[
                    v * states : (v + 1) * states, x * lanes : (x + 1) * lanes
                ]

    first_sum(0, one_ref)

    def body(j, carry):
        first_sum(2 * j + 1, two_ref)
        second_sum(2 * j, one_ref)
        first_sum(jnp.minimum(2 * j + 2, total - 1), one_ref)
        second_sum(2 * j + 1, two_ref)
        return carry

    lax.fori_loop(0, total // 2, body, 0)


def finish_block(states, mixed, right_diag, result, outs, step, low):
    cols = len(outs)
    size = low.shape[0]
    half, per = size // 2, states // cols
    rows = half * states
    mine = lax.axis_index("col")
    taken = mixed[pl.ds(pl.multiple_of(step * rows, rows), rows), :]
    result[...] = jnp.dot(taken, right_diag[...], preferred_element_type=jnp.float32)
    low = low[:half]
    for other in range(cols):
        col = jnp.bitwise_xor(mine, other)
        for t in range(0, per, 2):
            one = result[pl.ds(col * per + t, half, stride=states), :]
            two = result[pl.ds(col * per + t + 1, half, stride=states), :]
            upper = jnp.where(low, one, pltpu.roll(two, size, 1))
            lower = jnp.where(low, pltpu.roll(one, size, 1), two)
            outs[other][step, :half, t * size : (t + 2) * size] = upper.astype(jnp.bfloat16)
            outs[other][step, half:, t * size : (t + 2) * size] = lower.astype(jnp.bfloat16)


def finish_blocks(
    states, rows, near, first, count, order_ref, slot_ref, key_ref, env_ref, rights, mixed, right_diag, result, outs
):
    cols = len(outs)
    me = lax.axis_index("row")
    low = half_mask(env_ref.shape[1])

    def body(k, carry):
        at = lax.axis_index("col") * (order_ref.shape[0] // cols) + first + k
        slot = lax.rem(slot_ref[at], near)
        apart = jnp.bitwise_xor(lax.div(slot_ref[at], near), me)

        @pl.when(apart == 0)
        def _():
            spread_right(env_ref.at[sub_of(key_ref[order_ref[at]])], right_diag, low)

        for other in range(1, rows):

            @pl.when(apart == other)
            def _():
                spread_right(rights[other - 1].at[slot], right_diag, low)

        finish_block(states, mixed, right_diag, result, outs, k, low)
        return carry

    lax.fori_loop(0, count, body, 0)


def half_mask(size):
    return lax.broadcasted_iota(jnp.int32, (size, 2 * size), 1) < size


def gather_kernel(states, order_ref, state_ref, after_ref, diag_ref, block, sem):
    steps, size = block.shape[:2]
    low = half_mask(size)
    at = lax.axis_index("col") * steps
    copies = [
        pltpu.make_async_copy(state_ref.at[order_ref[at + k]], block.at[k], sem.at[k]) for k in range(steps)
    ]
    run_copies(copies)

    def body(k, carry):
        spread_state(block.at[k], diag_ref.at[k], low)
        return carry

    lax.fori_loop(0, steps, body, 0)


def gather(order, state_blocks, after, cols, states):
    count, size = state_blocks.shape[:2]
    steps = count // cols
    return pl.pallas_call(
        functools.partial(gather_kernel, states),
        out_shape=jax.ShapeDtypeStruct((steps, 2 * size, 2 * states * size), jnp.bfloat16),
        in_specs=[SMEM, ANY, ANY],
        out_specs=VMEM,
        scratch_shapes=[
            pltpu.VMEM((steps, size, states * size), jnp.bfloat16),
            pltpu.SemaphoreType.DMA((steps,)),
        ],
        compiler_params=pltpu.CompilerParams(vmem_limit_bytes=8 << 20),
        name="gather",
    )(order, state_blocks, after)


def mix_kernel(states, cols, count, diag_ref, mpo_ref, *refs):
    lefts, (mixed, left_rows, one_ref, two_ref) = refs[:cols], refs[cols:]
    mix_blocks(states, 0, count, lefts, diag_ref, mpo_ref, left_rows, one_ref, two_ref, mixed)


def right_kernel(states, rows, cols, near, count, order_ref, slot_ref, key_ref, env_ref, *refs):
    rights, (mixed, *outs) = refs[: rows - 1], refs[rows - 1 : rows + cols]
    right_diag, result = refs[rows + cols :]
    finish_blocks(
        states, rows, near, 0, count, order_ref, slot_ref, key_ref, env_ref, rights, mixed, right_diag, result, outs
    )


def apply_kernel(
    states, rows, cols, near, first, count, order_ref, slot_ref, key_ref, env_ref, diag_ref, mpo_ref, *refs
):
    rights, lefts, refs = refs[: rows - 1], refs[rows - 1 : rows - 1 + cols], refs[rows - 1 + cols :]
    outs, (left_rows, one_ref, two_ref, mixed, right_diag, result) = refs[:cols], refs[cols:]
    mix_blocks(states, first, count, lefts, diag_ref, mpo_ref, left_rows, one_ref, two_ref, mixed)
    finish_blocks(
        states, rows, near, first, count, order_ref, slot_ref, key_ref, env_ref, rights, mixed, right_diag, result, outs
    )


def apply_blocks(order, slots, keys, state_diag, mpo_rows, right_env, lefts, rights, near):
    cols = len(lefts)
    rows = len(rights) + 1
    steps, size, share = lefts[0].shape
    count = max(1, steps // 2)
    width = share // size * cols
    states = mpo_rows.shape[0] // width
    half, lanes = size // 2, 2 * size
    params = pltpu.CompilerParams(vmem_limit_bytes=24 << 20)

    def cost(blocks, mix, right):
        flops = mix * (width * size * size * states * size + (width * states) ** 2 * size * size)
        flops = 2 * blocks * (flops + right * states * size * size * width * size)
        return pl.CostEstimate(flops=flops, bytes_accessed=4 << 20, transcendentals=0)

    def outs(blocks):
        return [jax.ShapeDtypeStruct((blocks, size, states // cols * size), jnp.bfloat16)] * cols

    def mix_scratch(blocks):
        return [
            pltpu.VMEM((blocks * half * width, lanes), jnp.float32),
            pltpu.VMEM((states * width, CHUNK * lanes), jnp.bfloat16),
            pltpu.VMEM((states * width, CHUNK * lanes), jnp.bfloat16),
        ]

    def mixed_shape(blocks):
        return (blocks * half * states, width * lanes)

    right_scratch = [pltpu.VMEM((width * lanes, lanes), jnp.bfloat16), pltpu.VMEM((half * states, lanes), jnp.float32)]
    mixed = pl.pallas_call(
        functools.partial(mix_kernel, states, cols, count),
        out_shape=jax.ShapeDtypeStruct(mixed_shape(count), jnp.bfloat16),
        in_specs=[VMEM] * (2 + cols),
        out_specs=VMEM,
        scratch_shapes=mix_scratch(count),
        compiler_params=params,
        cost_estimate=cost(count, 1, 0),
        name="mix",
    )(state_diag, mpo_rows, *lefts)
    early = pl.pallas_call(
        functools.partial(right_kernel, states, rows, cols, near, count),
        out_shape=outs(count),
        in_specs=[SMEM] * 3 + [VMEM] * (rows + 1),
        out_specs=[VMEM] * cols,
        scratch_shapes=right_scratch,
        compiler_params=params,
        cost_estimate=cost(count, 0, 1),
        name="right",
    )(order, slots, keys, right_env, *rights, mixed)
    if count == steps:
        return [early]
    late = pl.pallas_call(
        functools.partial(apply_kernel, states, rows, cols, near, count, steps - count),
        out_shape=outs(steps - count),
        in_specs=[SMEM] * 3 + [VMEM] * (3 + rows - 1 + cols),
        out_specs=[VMEM] * cols,
        scratch_shapes=mix_scratch(steps - count)
        + [pltpu.VMEM(mixed_shape(steps - count), jnp.bfloat16)]
        + right_scratch,
        compiler_params=params,
        cost_estimate=cost(steps - count, 1, 1),
        name="apply",
    )(order, slots, keys, right_env, state_diag, mpo_rows, *rights, *lefts)
    return [early, late]


def place_kernel(cols, pieces, begun, order_ref, *refs):
    came = refs[begun : begun + len(pieces)]
    out_ref, sem = refs[begun + len(pieces) :]
    steps = order_ref.shape[0] // cols
    mine = lax.axis_index("col")
    copies = []
    for piece, (other, first) in zip(came, pieces):
        col = jnp.bitwise_xor(mine, other)
        for k in range(piece.shape[0]):
            p = order_ref[col * steps + first + k]
            copies.append(pltpu.make_async_copy(piece.at[k], out_ref.at[p], sem.at[len(copies)]))
    run_copies(copies)


def place_blocks(order, out, came, pieces, cols):
    begun = [] if out is None else [out]
    return pl.pallas_call(
        functools.partial(place_kernel, cols, pieces, len(begun)),
        out_shape=jax.ShapeDtypeStruct((order.shape[0],) + came[0].shape[1:], came[0].dtype),
        in_specs=[SMEM] + [HBM] * len(begun) + [VMEM] * len(came),
        out_specs=HBM,
        scratch_shapes=[pltpu.SemaphoreType.DMA((sum(piece.shape[0] for piece in came),))],
        input_output_aliases={1: 0} if begun else {},
        compiler_params=pltpu.CompilerParams(vmem_limit_bytes=4 << 20),
        name="place",
    )(order, *begun, *came)


def shards(state_blocks, left_env, right_env, mpo_tensor, block_left, block_owner, block_sub):
    rows = lax.axis_size("row")
    cols = lax.axis_size("col")
    count, size = state_blocks.shape[:2]
    states = state_blocks.shape[2] // size
    width = mpo_tensor.shape[0]
    most = max(2, (2 * count + rows - 1) // rows)
    near = -(-most // cols)

    keys = jnp.bitwise_or(lax.shift_left(block_owner[:, 0], SHIFT), block_sub)
    others = [swap(keys, "row", step) for step in range(1, rows)]
    block_left, *others = lax.optimization_barrier((block_left, *others))
    sends, order, slots = route(block_left, keys, left_env, cols, near)
    lefts = [sends[0]] + [swap(sends[d], "col", d) for d in range(1, cols)]
    picked = pick(others, right_env, cols, near)
    rights = [None] + [swap(picked[d - 1], "row", d) for d in range(2, rows)]
    after, mpo_tensor = lax.optimization_barrier((picked[0], mpo_tensor))
    mpo_rows = jnp.transpose(mpo_tensor.reshape(width, width, states, states), (1, 2, 3, 0)).reshape(
        width * states, states * width
    )
    state_diag = gather(order, state_blocks, after, cols, states)
    near_send, state_diag, mpo_rows, *lefts[1:] = lax.optimization_barrier((after, state_diag, mpo_rows, *lefts[1:]))
    rights[0] = swap(near_send, "row", 1)
    parts = apply_blocks(order, slots, keys, state_diag, mpo_rows, right_env, lefts, rights, near)
    if len(parts) == 1:
        came = [swap(parts[0][d], "col", d) for d in range(1, cols)]
        return place_blocks(order, None, [parts[0][0], *came], [(d, 0) for d in range(cols)], cols)
    early, late = parts
    half = early[0].shape[0]
    came = [swap(early[d], "col", d) for d in range(1, cols)]
    late = list(late)
    joined = lax.optimization_barrier((*late[1:], *came))
    late[1:], came = joined[: cols - 1], joined[cols - 1 :]
    last = [swap(late[d], "col", d) for d in range(1, cols)]
    pieces = [(0, 0)] + [(d, 0) for d in range(1, cols)] + [(0, half)]
    out = place_blocks(order, None, [early[0], *came, late[0]], pieces, cols)
    return place_blocks(order, out, last, [(d, half) for d in range(1, cols)], cols)


def solution(mesh):
    placed = (
        P(("groups", "row"), None, None),
        P(("groups", "row"), None, "col"),
        P(("groups", "row"), None, None),
        P(),
        P(("groups", "row")),
        P(("groups", "row"), None),
        P(("groups", "row")),
    )
    return jax.shard_map(
        shards,
        mesh=mesh,
        in_specs=placed,
        out_specs=P(("groups", "row"), None, "col"),
        check_vma=False,
    )
```

time: 69.1 us -> 70.5 us (1.020)
  waiting for transfers between devices: 5.07 us -> 7.37 us
  starting transfers between devices: 20.1 us -> 18.6 us
  Pallas kernels: 28.4 us -> 29.3 us
    ppermute x15, waiting for transfers between devices: 5.07 us -> 7.37 us  [swap(): return lax.ppermute(array, axis, [(i, i ^ step) for i in range(size)])]
    pallas_call x1, Pallas kernels: 6.25 us -> 7.97 us  [apply_blocks(): pl.pallas_call(functools.partial(mix_kernel, states, cols, count), out_sh...]
    ppermute x15, starting transfers between devices: 20.1 us -> 18.6 us  [swap(): return lax.ppermute(array, axis, [(i, i ^ step) for i in range(size)])]
    reshape x1, local copies, waits for them, and re-layouts: 3.66 us -> 2.63 us  [shards(): mpo_tensor.reshape(width, width, states, states)]
    pallas_call x1, Pallas kernels: 2.73 us -> 1.73 us  [pick(): pl.pallas_call(functools.partial(pick_kernel, rows, cols, near), out_shap...]
    pallas_call x3 -> x4, Pallas kernels: 6.7 us -> 7.49 us  [the longest x1 3.12 us: apply_blocks(): pl.pallas_call(functools.partial(right_kernel, states, rows, cols, near,...]
    unnamed x34 -> x14, local copies, waits for them, and re-layouts: 2.84 us -> 3.07 us
  transfers between devices with their start and end apart: 15 -> 15, of which waited for: 5 -> 4; matrix products, arithmetic and copies ran while one was open for 16% -> 16% of each run, Pallas kernels for 30% -> 33%
where the time goes in v5:
time: 70.5 us; the launch traced here: 70.2 us
  Pallas kernels  29.3 us (42%)
  starting transfers between devices  18.6 us (26%)
  local copies, waits for them, and re-layouts  14 us (20%)
  waiting for transfers between devices  7.37 us (10%)
    ppermute x15, starting transfers between devices, swap(): return lax.ppermute(array, axis, [(i, i ^ step) for i in range(size)])  18.6 us
    pallas_call x1, Pallas kernels, apply_blocks(): pl.pallas_call(functools.partial(apply_kernel, states, rows, cols, near,...  10.4 us
    pallas_call x1, Pallas kernels, apply_blocks(): pl.pallas_call(functools.partial(mix_kernel, states, cols, count), out_sh...  7.97 us
    ppermute x15, waiting for transfers between devices, swap(): return lax.ppermute(array, axis, [(i, i ^ step) for i in range(size)])  7.37 us
    transpose x1, local copies, waits for them, and re-layouts, shards(): jnp.transpose(mpo_tensor.reshape(width, width, states, states), (1, 2, 3,...  4.83 us
    reshape x1, local copies, waits for them, and re-layouts, shards(): jnp.transpose(mpo_tensor.reshape(width, width, states, states), (1, 2, 3,...  3.47 us
    pallas_call x1, Pallas kernels, apply_blocks(): pl.pallas_call(functools.partial(right_kernel, states, rows, cols, near,...  3.12 us
    unnamed x14, local copies, waits for them, and re-layouts  3.07 us
  transfers between devices with their start and end apart: 15, of which 4 were waited for; matrix products, arithmetic and copies ran while one was open for 16% of the time, Pallas kernels for 33%

profile of v5, /device:TPU:0, one launch (start us, length us, event | category | flops | bytes accessed | tf_op | source)
XLA Modules:
  0.0 70.2 jit_solution(13331972094507448776)
XLA Ops:
  0.0 0.7 bitcast_or_fusion.key_ref
  0.7 2.4 %collective-permute-start.2 = (s32[16]{0:T(128)S(1)}, s32[16]{0:T(128)S(1)}, u32[]{:S(2)}, u32[]{:S(2)}) collective-permute-start(s32[16]{0:T(128)S(1)} %bitcast_or_fusion.key_ref), channel_id=1, source_target_pairs={{0,12},{4,8},{8,4},{12,0},{1,13},{5,9},{9,5},{13,1},{2,14},{6,10},... | collective-permute-start | bytes 200 | tf_op jit(solution)/shard_map/ppermute | solution.py:20
  4.4 2.2 %collective-permute-done.1.refs_1_ = s32[16]{0:T(128)S(1)} collective-permute-done((s32[16]{0:T(128)S(1)}, s32[16]{0:T(128)S(1)}, u32[]{:S(2)}, u32[]{:S(2)}) %collective-permute-start.1) | collective-permute-done | bytes 96 | tf_op jit(solution)/shard_map/ppermute | solution.py:20
  6.6 1.0 %copy-done.3 = bf16[8,64,384]{2,1,0:T(8,128)(2,1)S(1)} copy-done((bf16[8,64,384]{2,1,0:T(8,128)(2,1)S(1)}, bf16[8,64,384]{2,1,0:T(8,128)(2,1)}, u32[]{:S(2)}) %copy-start.3) | copy-done | bytes 393240
  8.3 1.7 %route.1 = (bf16[4,64,384]{2,1,0:T(8,128)(2,1)S(1)}, bf16[4,64,384]{2,1,0:T(8,128)(2,1)}, bf16[4,64,384]{2,1,0:T(8,128)(2,1)}, bf16[4,64,384]{2,1,0:T(8,128)(2,1)}, s32[16]{0:T(128)S(1)}, /*index=5*/s32[16]{0:T(128)S(1)}) custom-call(s32[16]{0:T(128)S(1)} %copy-done.5, s32[16]{0:T(128)S(1)} %bitcast_or_fusion.key_ref, bf16[8,64,384]{2,1,0:T(8,128)(2,1)S(1)} %copy-done.3), custom_call_target="tpu_custom_call" | custom-call | tf_op jit(solution)/shard_map/route/pallas_call | solution.py:77
  10.0 1.6 %collective-permute-start.3 = (bf16[4,64,384]{2,1,0:T(8,128)(2,1)}, bf16[4,64,384]{2,1,0:T(8,128)(2,1)}, u32[]{:S(2)}, u32[]{:S(2)}) collective-permute-start(bf16[4,64,384]{2,1,0:T(8,128)(2,1)} %get-tuple-element.49), channel_id=1, source_target_pairs={{0,1},{1,0},{2,3},{3,2},{4,5},{5,4},{6,7},{7,6},{8,9},{9,8},{10,11... | collective-permute-start | bytes 589832 | tf_op jit(solution)/shard_map/ppermute | solution.py:20
  11.7 2.6 %collective-permute-start.4 = (bf16[4,64,384]{2,1,0:T(8,128)(2,1)}, bf16[4,64,384]{2,1,0:T(8,128)(2,1)}, u32[]{:S(2)}, u32[]{:S(2)}) collective-permute-start(bf16[4,64,384]{2,1,0:T(8,128)(2,1)} %get-tuple-element.50), channel_id=1, source_target_pairs={{0,2},{1,3},{2,0},{3,1},{4,6},{5,7},{6,4},{7,5},{8,10},{9,11},{10,... | collective-permute-start | bytes 589832 | tf_op jit(solution)/shard_map/ppermute | solution.py:20
  14.5 1.4 %copy-done = bf16[8,64,1536]{2,1,0:T(8,128)(2,1)S(1)} copy-done((bf16[8,64,1536]{2,1,0:T(8,128)(2,1)S(1)}, bf16[8,64,1536]{2,1,0:T(8,128)(2,1)}, u32[]{:S(2)}) %copy-start) | copy-done | bytes 1572888
  15.9 1.7 %pick.1 = (bf16[2,64,1536]{2,1,0:T(8,128)(2,1)S(1)}, bf16[2,64,1536]{2,1,0:T(8,128)(2,1)}, bf16[2,64,1536]{2,1,0:T(8,128)(2,1)}) custom-call(s32[16]{0:T(128)S(1)} %collective-permute-done.refs_0_, s32[16]{0:T(128)S(1)} %collective-permute-done.1.refs_1_, s32[16]{0:T(128)S(1)} %collective-permute-done.2.refs_2_, bf16[8,64,1536]{2,1,0:T(8,128)(2,1)S(1)} %copy-done), custom_call_target="tpu_custom_call" | custom-call | tf_op jit(solution)/shard_map/pick/pallas_call | solution.py:116
  18.2 2.6 %reshape.8 = bf16[24,24,16,16]{3,2,1,0:T(8,128)(2,1)} reshape(bf16[24,24,256]{2,1,0:T(8,128)(2,1)S(1)} %copy-done.6) | data formatting | bytes 589824 | tf_op jit(solution)/shard_map/reshape | solution.py:434
  20.9 4.8 %copy.10 = bf16[24,16,16,24]{3,2,1,0:T(8,128)(2,1)} copy(bf16[24,16,16,24]{2,1,0,3:T(8,128)(2,1)} %bitcast.5) | data formatting | bytes 589824 | tf_op jit(solution)/shard_map/transpose | solution.py:434
  25.7 3.5 %reshape.9.mpo_ref = bf16[384,384]{1,0:T(8,128)(2,1)} reshape(bf16[24,16,16,24]{3,2,1,0:T(8,128)(2,1)} %copy.10) | data formatting | bytes 589824 | tf_op jit(solution)/shard_map/reshape | solution.py:434
  29.2 1.8 %gather.1.diag_ref = bf16[4,128,2048]{2,1,0:T(8,128)(2,1)S(1)} custom-call(s32[16]{0:T(128)S(1)} %get-tuple-element.41.order_ref, bf16[16,64,1024]{2,1,0:T(8,128)(2,1)S(1)} %copy-done.2, bf16[2,64,1536]{2,1,0:T(8,128)(2,1)S(1)} %get-tuple-element.52.after_ref), custom_call_target="tpu_custom_call" | custom-call | tf_op jit(solution)/shard_map/gather/pallas_call | solution.py:285
  30.9 1.6 %collective-permute-start.6 = (bf16[2,64,1536]{2,1,0:T(8,128)(2,1)S(1)}, bf16[2,64,1536]{2,1,0:T(8,128)(2,1)S(1)}, u32[]{:S(2)}, u32[]{:S(2)}) collective-permute-start(bf16[2,64,1536]{2,1,0:T(8,128)(2,1)S(1)} %get-tuple-element.52.after_ref), channel_id=1, source_target_pairs={{0,4},{4,0},{8,12},{12,8},{1,5},{5,1},{9,13},{13,9},{2,6},{6,2},{1... | collective-permute-start | bytes 1179656 | tf_op jit(solution)/shard_map/ppermute | solution.py:20
  32.6 8.0 %mix.1.refs_3_ = bf16[1024,3072]{1,0:T(8,128)(2,1)S(1)} custom-call(bf16[4,128,2048]{2,1,0:T(8,128)(2,1)S(1)} %gather.1.diag_ref, bf16[384,384]{1,0:T(8,128)(2,1)S(1)} %copy-done.4, bf16[4,64,384]{2,1,0:T(8,128)(2,1)S(1)} %get-tuple-element.57.refs_0_.refs_3_, bf16[4,64,384]{2,1,0:T(8,128)(2,1)} %collective-permute-done.3.refs_1_.refs_4_, ...), custom_call_target="tpu_custom_call" | custom-call | flops 2818572288 | bytes 4194304 | tf_op jit(solution)/shard_map/mix/pallas_call | solution.py:352
  40.6 3.1 %right.1 = (bf16[2,64,256]{2,1,0:T(8,128)(2,1)S(1)}, bf16[2,64,256]{2,1,0:T(8,128)(2,1)S(1)}, bf16[2,64,256]{2,1,0:T(8,128)(2,1)S(1)}, bf16[2,64,256]{2,1,0:T(8,128)(2,1)S(1)}) custom-call(s32[16]{0:T(128)S(1)} %get-tuple-element.41.order_ref, s32[16]{0:T(128)S(1)} %get-tuple-element.42.slot_ref, s32[16]{0:T(128)S(1)} %bitcast_or_fusion.key_ref, ...), custom_call_target="tpu_custom_call" | custom-call | flops 402653184 | bytes 4194304 | tf_op jit(solution)/shard_map/right/pallas_call | solution.py:362
  43.7 0.8 %collective-permute-start.9 = (bf16[2,64,256]{2,1,0:T(8,128)(2,1)S(1)}, bf16[2,64,256]{2,1,0:T(8,128)(2,1)S(1)}, u32[]{:S(2)}, u32[]{:S(2)}) collective-permute-start(bf16[2,64,256]{2,1,0:T(8,128)(2,1)S(1)} %get-tuple-element.65), channel_id=1, source_target_pairs={{0,1},{1,0},{2,3},{3,2},{4,5},{5,4},{6,7},{7,6},{8,9},{9,8},{10,11... | collective-permute-start | bytes 196616 | tf_op jit(solution)/shard_map/ppermute | solution.py:20
  44.5 3.5 %collective-permute-start.10 = (bf16[2,64,256]{2,1,0:T(8,128)(2,1)S(1)}, bf16[2,64,256]{2,1,0:T(8,128)(2,1)S(1)}, u32[]{:S(2)}, u32[]{:S(2)}) collective-permute-start(bf16[2,64,256]{2,1,0:T(8,128)(2,1)S(1)} %get-tuple-element.66), channel_id=1, source_target_pairs={{0,2},{1,3},{2,0},{3,1},{4,6},{5,7},{6,4},{7,5},{8,10},{9,11},{10,... | collective-permute-start | bytes 196616 | tf_op jit(solution)/shard_map/ppermute | solution.py:20
  48.2 10.4 %apply.1 = (bf16[2,64,256]{2,1,0:T(8,128)(2,1)S(1)}, bf16[2,64,256]{2,1,0:T(8,128)(2,1)S(1)}, bf16[2,64,256]{2,1,0:T(8,128)(2,1)S(1)}, bf16[2,64,256]{2,1,0:T(8,128)(2,1)S(1)}) custom-call(s32[16]{0:T(128)S(1)} %get-tuple-element.41.order_ref, s32[16]{0:T(128)S(1)} %get-tuple-element.42.slot_ref, s32[16]{0:T(128)S(1)} %bitcast_or_fusion.key_ref, ...), custom_call_target="tpu_custom_call" | custom-call | flops 3221225472 | bytes 4194304 | tf_op jit(solution)/shard_map/apply/pallas_call | solution.py:374
  59.0 3.8 %collective-permute-start.13 = (bf16[2,64,256]{2,1,0:T(8,128)(2,1)S(1)}, bf16[2,64,256]{2,1,0:T(8,128)(2,1)S(1)}, u32[]{:S(2)}, u32[]{:S(2)}) collective-permute-start(bf16[2,64,256]{2,1,0:T(8,128)(2,1)S(1)} %get-tuple-element.73), channel_id=1, source_target_pairs={{0,2},{1,3},{2,0},{3,1},{4,6},{5,7},{6,4},{7,5},{8,10},{9,11},{10,... | collective-permute-start | bytes 196616 | tf_op jit(solution)/shard_map/ppermute | solution.py:20
  63.1 1.3 %place.2.refs_0_ = bf16[16,64,256]{2,1,0:T(8,128)(2,1)} custom-call(s32[16]{0:T(128)S(1)} %get-tuple-element.41.order_ref, bf16[2,64,256]{2,1,0:T(8,128)(2,1)S(1)} %get-tuple-element.61.refs_0_, bf16[2,64,256]{2,1,0:T(8,128)(2,1)S(1)} %collective-permute-done.9.refs_1_, bf16[2,64,256]{2,1,0:T(8,128)(2,1)S(1)} %collective-permute-done.10.refs_2_, ...), custom_call_target="tpu_custom_call" | custom-call | tf_op jit(solution)/shard_map/place/pallas_call | solution.py:405
  64.4 2.4 %collective-permute-done.13.refs_2_ = bf16[2,64,256]{2,1,0:T(8,128)(2,1)S(1)} collective-permute-done((bf16[2,64,256]{2,1,0:T(8,128)(2,1)S(1)}, bf16[2,64,256]{2,1,0:T(8,128)(2,1)S(1)}, u32[]{:S(2)}, u32[]{:S(2)}) %collective-permute-start.13) | collective-permute-done | bytes 65568 | tf_op jit(solution)/shard_map/ppermute | solution.py:20
  66.8 2.1 %collective-permute-done.14.refs_3_ = bf16[2,64,256]{2,1,0:T(8,128)(2,1)S(1)} collective-permute-done((bf16[2,64,256]{2,1,0:T(8,128)(2,1)S(1)}, bf16[2,64,256]{2,1,0:T(8,128)(2,1)S(1)}, u32[]{:S(2)}, u32[]{:S(2)}) %collective-permute-start.14) | collective-permute-done | bytes 65568 | tf_op jit(solution)/shard_map/ppermute | solution.py:20
  68.9 1.3 %place.3 = bf16[16,64,256]{2,1,0:T(8,128)(2,1)} custom-call(s32[16]{0:T(128)S(1)} %get-tuple-element.41.order_ref, bf16[16,64,256]{2,1,0:T(8,128)(2,1)} %place.2.refs_0_, bf16[2,64,256]{2,1,0:T(8,128)(2,1)S(1)} %collective-permute-done.12.refs_1_, bf16[2,64,256]{2,1,0:T(8,128)(2,1)S(1)} %collective-permute-done.13.refs_2_, ...), custom_call_target="tpu_custom_call", output_to_operand_aliasing={{}: (1, {})} | custom-call | tf_op jit(solution)/shard_map/place/pallas_call | solution.py:405
  (32 shorter events, 3.7 us)
Async XLA Ops:
  0.7 3.7 %collective-permute-start.2 = (s32[16]{0:T(128)S(1)}, s32[16]{0:T(128)S(1)}, u32[]{:S(2)}, u32[]{:S(2)}) collective-permute-start(s32[16]{0:T(128)S(1)} %bitcast_or_fusion.key_ref), channel_id=1, source_target_pairs={{0,12},{4,8},{8,4},{12,0},{1,13},{5,9},{9,5},{13,1},{2,14},{6,10},... | collective-permute-start | bytes 200 | tf_op jit(solution)/shard_map/ppermute | solution.py:20
  3.1 3.5 %collective-permute-start.1 = (s32[16]{0:T(128)S(1)}, s32[16]{0:T(128)S(1)}, u32[]{:S(2)}, u32[]{:S(2)}) collective-permute-start(s32[16]{0:T(128)S(1)} %bitcast_or_fusion.key_ref), channel_id=1, source_target_pairs={{0,8},{4,12},{8,0},{12,4},{1,9},{5,13},{9,1},{13,5},{2,10},{6,14},... | collective-permute-start | bytes 200 | tf_op jit(solution)/shard_map/ppermute | solution.py:20
  3.7 2.9 %collective-permute-start = (s32[16]{0:T(128)S(1)}, s32[16]{0:T(128)S(1)}, u32[]{:S(2)}, u32[]{:S(2)}) collective-permute-start(s32[16]{0:T(128)S(1)} %bitcast_or_fusion.key_ref), channel_id=1, source_target_pairs={{0,4},{4,0},{8,12},{12,8},{1,5},{5,1},{9,13},{13,9},{2,6},{6,2},{1... | collective-permute-start | bytes 200 | tf_op jit(solution)/shard_map/ppermute | solution.py:20
  6.6 1.0 %copy-start.3 = (bf16[8,64,384]{2,1,0:T(8,128)(2,1)S(1)}, bf16[8,64,384]{2,1,0:T(8,128)(2,1)}, u32[]{:S(2)}) copy-start(bf16[8,64,384]{2,1,0:T(8,128)(2,1)} %env_ref.3) | copy-start | bytes 1179652
  7.6 0.7 copy-start.5
  8.3 9.9 %copy-start.6 = (bf16[24,24,256]{2,1,0:T(8,128)(2,1)S(1)}, bf16[24,24,256]{2,1,0:T(8,128)(2,1)}, u32[]{:S(2)}) copy-start(bf16[24,24,256]{2,1,0:T(8,128)(2,1)} %param.10) | copy-start | bytes 884740
  10.0 20.9 %collective-permute-start.3 = (bf16[4,64,384]{2,1,0:T(8,128)(2,1)}, bf16[4,64,384]{2,1,0:T(8,128)(2,1)}, u32[]{:S(2)}, u32[]{:S(2)}) collective-permute-start(bf16[4,64,384]{2,1,0:T(8,128)(2,1)} %get-tuple-element.49), channel_id=1, source_target_pairs={{0,1},{1,0},{2,3},{3,2},{4,5},{5,4},{6,7},{7,6},{8,9},{9,8},{10,11... | collective-permute-start | bytes 589832 | tf_op jit(solution)/shard_map/ppermute | solution.py:20
  11.7 19.3 %collective-permute-start.4 = (bf16[4,64,384]{2,1,0:T(8,128)(2,1)}, bf16[4,64,384]{2,1,0:T(8,128)(2,1)}, u32[]{:S(2)}, u32[]{:S(2)}) collective-permute-start(bf16[4,64,384]{2,1,0:T(8,128)(2,1)} %get-tuple-element.50), channel_id=1, source_target_pairs={{0,2},{1,3},{2,0},{3,1},{4,6},{5,7},{6,4},{7,5},{8,10},{9,11},{10,... | collective-permute-start | bytes 589832 | tf_op jit(solution)/shard_map/ppermute | solution.py:20
  14.3 16.7 %collective-permute-start.5 = (bf16[4,64,384]{2,1,0:T(8,128)(2,1)}, bf16[4,64,384]{2,1,0:T(8,128)(2,1)}, u32[]{:S(2)}, u32[]{:S(2)}) collective-permute-start(bf16[4,64,384]{2,1,0:T(8,128)(2,1)} %get-tuple-element.51), channel_id=1, source_target_pairs={{0,3},{1,2},{2,1},{3,0},{4,7},{5,6},{6,5},{7,4},{8,11},{9,10},{10,... | collective-permute-start | bytes 589832 | tf_op jit(solution)/shard_map/ppermute | solution.py:20
  14.5 1.4 %copy-start = (bf16[8,64,1536]{2,1,0:T(8,128)(2,1)S(1)}, bf16[8,64,1536]{2,1,0:T(8,128)(2,1)}, u32[]{:S(2)}) copy-start(bf16[8,64,1536]{2,1,0:T(8,128)(2,1)} %env_ref.5) | copy-start | bytes 4718596
  17.6 22.9 %collective-permute-start.7 = (bf16[2,64,1536]{2,1,0:T(8,128)(2,1)}, bf16[2,64,1536]{2,1,0:T(8,128)(2,1)S(1)}, u32[]{:S(2)}, u32[]{:S(2)}) collective-permute-start(bf16[2,64,1536]{2,1,0:T(8,128)(2,1)} %get-tuple-element.53), channel_id=1, source_target_pairs={{0,8},{4,12},{8,0},{12,4},{1,9},{5,13},{9,1},{13,5},{2,10},{6,14},... | collective-permute-start | bytes 1179656 | tf_op jit(solution)/shard_map/ppermute | solution.py:20
  18.2 22.3 %collective-permute-start.8 = (bf16[2,64,1536]{2,1,0:T(8,128)(2,1)}, bf16[2,64,1536]{2,1,0:T(8,128)(2,1)S(1)}, u32[]{:S(2)}, u32[]{:S(2)}) collective-permute-start(bf16[2,64,1536]{2,1,0:T(8,128)(2,1)} %get-tuple-element.54), channel_id=1, source_target_pairs={{0,12},{4,8},{8,4},{12,0},{1,13},{5,9},{9,5},{13,1},{2,14},{6,10},... | collective-permute-start | bytes 1179656 | tf_op jit(solution)/shard_map/ppermute | solution.py:20
  20.9 8.3 %copy-start.2 = (bf16[16,64,1024]{2,1,0:T(8,128)(2,1)S(1)}, bf16[16,64,1024]{2,1,0:T(8,128)(2,1)}, u32[]{:S(2)}) copy-start(bf16[16,64,1024]{2,1,0:T(8,128)(2,1)} %state_ref.1) | copy-start | bytes 6291460
  29.2 3.4 %copy-start.4 = (bf16[384,384]{1,0:T(8,128)(2,1)S(1)}, bf16[384,384]{1,0:T(8,128)(2,1)}, u32[]{:S(2)}) copy-start(bf16[384,384]{1,0:T(8,128)(2,1)} %reshape.9.mpo_ref) | copy-start | bytes 884740
  30.9 9.6 %collective-permute-start.6 = (bf16[2,64,1536]{2,1,0:T(8,128)(2,1)S(1)}, bf16[2,64,1536]{2,1,0:T(8,128)(2,1)S(1)}, u32[]{:S(2)}, u32[]{:S(2)}) collective-permute-start(bf16[2,64,1536]{2,1,0:T(8,128)(2,1)S(1)} %get-tuple-element.52.after_ref), channel_id=1, source_target_pairs={{0,4},{4,0},{8,12},{12,8},{1,5},{5,1},{9,13},{13,9},{2,6},{6,2},{1... | collective-permute-start | bytes 1179656 | tf_op jit(solution)/shard_map/ppermute | solution.py:20
  32.6 8.0 %copy-start.1 = (bf16[8,64,1536]{2,1,0:T(8,128)(2,1)S(1)}, bf16[8,64,1536]{2,1,0:T(8,128)(2,1)}, u32[]{:S(2)}) copy-start(bf16[8,64,1536]{2,1,0:T(8,128)(2,1)} %env_ref.5) | copy-start | bytes 4718596
  43.7 14.9 %collective-permute-start.9 = (bf16[2,64,256]{2,1,0:T(8,128)(2,1)S(1)}, bf16[2,64,256]{2,1,0:T(8,128)(2,1)S(1)}, u32[]{:S(2)}, u32[]{:S(2)}) collective-permute-start(bf16[2,64,256]{2,1,0:T(8,128)(2,1)S(1)} %get-tuple-element.65), channel_id=1, source_target_pairs={{0,1},{1,0},{2,3},{3,2},{4,5},{5,4},{6,7},{7,6},{8,9},{9,8},{10,11... | collective-permute-start | bytes 196616 | tf_op jit(solution)/shard_map/ppermute | solution.py:20
  44.5 14.1 %collective-permute-start.10 = (bf16[2,64,256]{2,1,0:T(8,128)(2,1)S(1)}, bf16[2,64,256]{2,1,0:T(8,128)(2,1)S(1)}, u32[]{:S(2)}, u32[]{:S(2)}) collective-permute-start(bf16[2,64,256]{2,1,0:T(8,128)(2,1)S(1)} %get-tuple-element.66), channel_id=1, source_target_pairs={{0,2},{1,3},{2,0},{3,1},{4,6},{5,7},{6,4},{7,5},{8,10},{9,11},{10,... | collective-permute-start | bytes 196616 | tf_op jit(solution)/shard_map/ppermute | solution.py:20
  47.9 10.7 %collective-permute-start.11 = (bf16[2,64,256]{2,1,0:T(8,128)(2,1)S(1)}, bf16[2,64,256]{2,1,0:T(8,128)(2,1)S(1)}, u32[]{:S(2)}, u32[]{:S(2)}) collective-permute-start(bf16[2,64,256]{2,1,0:T(8,128)(2,1)S(1)} %get-tuple-element.67), channel_id=1, source_target_pairs={{0,3},{1,2},{2,1},{3,0},{4,7},{5,6},{6,5},{7,4},{8,11},{9,10},{10,... | collective-permute-start | bytes 196616 | tf_op jit(solution)/shard_map/ppermute | solution.py:20
  58.6 5.8 %collective-permute-start.12 = (bf16[2,64,256]{2,1,0:T(8,128)(2,1)S(1)}, bf16[2,64,256]{2,1,0:T(8,128)(2,1)S(1)}, u32[]{:S(2)}, u32[]{:S(2)}) collective-permute-start(bf16[2,64,256]{2,1,0:T(8,128)(2,1)S(1)} %get-tuple-element.72), channel_id=1, source_target_pairs={{0,1},{1,0},{2,3},{3,2},{4,5},{5,4},{6,7},{7,6},{8,9},{9,8},{10,11... | collective-permute-start | bytes 196616 | tf_op jit(solution)/shard_map/ppermute | solution.py:20
  59.0 7.8 %collective-permute-start.13 = (bf16[2,64,256]{2,1,0:T(8,128)(2,1)S(1)}, bf16[2,64,256]{2,1,0:T(8,128)(2,1)S(1)}, u32[]{:S(2)}, u32[]{:S(2)}) collective-permute-start(bf16[2,64,256]{2,1,0:T(8,128)(2,1)S(1)} %get-tuple-element.73), channel_id=1, source_target_pairs={{0,2},{1,3},{2,0},{3,1},{4,6},{5,7},{6,4},{7,5},{8,10},{9,11},{10,... | collective-permute-start | bytes 196616 | tf_op jit(solution)/shard_map/ppermute | solution.py:20
  62.8 6.1 %collective-permute-start.14 = (bf16[2,64,256]{2,1,0:T(8,128)(2,1)S(1)}, bf16[2,64,256]{2,1,0:T(8,128)(2,1)S(1)}, u32[]{:S(2)}, u32[]{:S(2)}) collective-permute-start(bf16[2,64,256]{2,1,0:T(8,128)(2,1)S(1)} %get-tuple-element.74), channel_id=1, source_target_pairs={{0,3},{1,2},{2,1},{3,0},{4,7},{5,6},{6,5},{7,4},{8,11},{9,10},{10,... | collective-permute-start | bytes 196616 | tf_op jit(solution)/shard_map/ppermute | solution.py:20

commit v6 on v5

v6 whole, which is shorter than its diff:
```python
import functools

import jax
import jax.numpy as jnp
from jax import lax
from jax.experimental import pallas as pl
from jax.experimental.pallas import tpu as pltpu
from jax.sharding import PartitionSpec as P

CHUNK = 8
SHIFT = 16
SMEM = pl.BlockSpec(memory_space=pltpu.SMEM)
VMEM = pl.BlockSpec(memory_space=pltpu.VMEM)
HBM = pl.BlockSpec(memory_space=pltpu.HBM)
ANY = pl.BlockSpec(memory_space=pl.ANY)


def swap(array, axis, step):
    size = lax.axis_size(axis)
    return lax.ppermute(array, axis, [(i, i ^ step) for i in range(size)])


def run_copies(copies):
    for copy in copies:
        copy.start()
    for copy in copies:
        copy.wait()


def owner_of(key):
    return lax.shift_right_logical(key, SHIFT)


def sub_of(key):
    return jnp.bitwise_and(key, (1 << SHIFT) - 1)


def route_kernel(cols, near, parts, left_ref, key_ref, env_ref, *refs):
    sends = refs[: 2 + (cols - 2) * parts]
    order_ref, slot_ref, by_place, sem = refs[len(sends) :]
    count = left_ref.shape[0]
    steps = count // cols
    per_part = steps // parts
    mine = lax.axis_index("col")
    owners = [owner_of(key_ref[p]) for p in range(count)]
    for p in range(count):
        place = jnp.int32(0)
        for other in range(count):
            if other < p:
                place = place + (owners[other] <= owners[p]).astype(jnp.int32)
            elif other > p:
                place = place + (owners[other] < owners[p]).astype(jnp.int32)
        by_place[place] = p
    for col in range(cols):
        before = None
        for step in range(steps):
            p = by_place[step * cols + col]
            owner = owner_of(key_ref[p])
            if before is None:
                slot = jnp.int32(0)
            else:
                slot = jnp.where(owner == before[0], before[1] + 1, 0)
            before = owner, slot
            order_ref[col * steps + step] = p
            slot_ref[col * steps + step] = owner * near + slot
    copies = []
    for other in range(cols):
        col = jnp.bitwise_xor(mine, other)
        for step in range(steps):
            sector = left_ref[order_ref[col * steps + step]]
            if other < 2:
                target = sends[other].at[step]
            else:
                target = sends[2 + step // per_part * (cols - 2) + other - 2].at[step % per_part]
            copies.append(pltpu.make_async_copy(env_ref.at[sector], target, sem.at[len(copies)]))
            copies[-1].start()
    for copy in copies:
        copy.wait()


def route(block_left, keys, left_env, cols, near, parts):
    count = block_left.shape[0]
    size, width = left_env.shape[1:]
    steps = count // cols
    whole = jax.ShapeDtypeStruct((steps, size, width), left_env.dtype)
    piece = jax.ShapeDtypeStruct((steps // parts, size, width), left_env.dtype)
    listed = jax.ShapeDtypeStruct((count,), jnp.int32)
    far = (cols - 2) * parts
    *sends, order, slots = pl.pallas_call(
        functools.partial(route_kernel, cols, near, parts),
        out_shape=[whole] * 2 + [piece] * far + [listed] * 2,
        in_specs=[SMEM, SMEM, ANY],
        out_specs=[VMEM] * (2 + far) + [SMEM] * 2,
        scratch_shapes=[pltpu.SMEM((count,), jnp.int32), pltpu.SemaphoreType.DMA((count,))],
        name="route",
    )(block_left, keys, left_env)
    return sends, order, slots


def pick_kernel(rows, cols, near, *refs):
    key_refs, (env_ref, send_ref, sem) = refs[:rows], refs[rows:]
    count = key_refs[0].shape[0]
    me = lax.axis_index("row")
    mine = lax.axis_index("col")
    copies = []
    for other in range(rows):
        keys = [key_refs[other][p] for p in range(count)]
        owners = [owner_of(key) for key in keys]
        first = jnp.int32(0)
        for p in range(count):
            first = first + (owners[p] < me).astype(jnp.int32)
        past = -lax.rem(mine - lax.rem(first, cols) + cols, cols)
        wanted = [jnp.int32(0)] * near
        for p in range(count):
            here = owners[p] == me
            for slot in range(near):
                wanted[slot] = jnp.where(here & (past == slot * cols), sub_of(keys[p]), wanted[slot])
            past = past + here.astype(jnp.int32)
        for slot in range(near):
            target = send_ref.at[jnp.bitwise_xor(me, other), slot]
            copies.append(pltpu.make_async_copy(env_ref.at[wanted[slot]], target, sem.at[len(copies)]))
            copies[-1].start()
    for copy in copies:
        copy.wait()


def pick(keys, right_env, cols, near):
    rows = len(keys)
    return pl.pallas_call(
        functools.partial(pick_kernel, rows, cols, near),
        out_shape=jax.ShapeDtypeStruct((rows, near) + right_env.shape[1:], right_env.dtype),
        in_specs=[SMEM] * rows + [ANY],
        out_specs=VMEM,
        scratch_shapes=[pltpu.SemaphoreType.DMA((rows * near,))],
        name="pick",
    )(*keys, right_env)


def halves(tile, low):
    swapped = pltpu.roll(tile, tile.shape[1] // 2, 1)
    zero = jnp.zeros_like(tile)
    return (
        jnp.where(low, tile, zero),
        jnp.where(low, zero, swapped),
        jnp.where(low, swapped, zero),
        jnp.where(low, zero, tile),
    )


def spread_state(block, state_diag, low):
    size = block.shape[0]
    for s in range(0, block.shape[1] // size, 2):
        pieces = halves(block[:, s * size : (s + 2) * size].astype(jnp.float32), low)
        for i in range(4):
            row, col = (i % 2) * size, (s + i // 2) * 2 * size
            state_diag[row : row + size, col : col + 2 * size] = pieces[i].astype(jnp.bfloat16)


def spread_right(right, right_diag, low):
    size = right.shape[0]
    for v in range(0, right.shape[1] // size, 2):
        pieces = halves(right[:, v * size : (v + 2) * size].astype(jnp.float32), low)
        for i in range(4):
            at = (2 * v + i) * size
            right_diag[at : at + size, :] = pieces[i].astype(jnp.bfloat16)


def spread_left(lefts, left_rows):
    cols = len(lefts)
    size = lefts[0].shape[0]
    half, share = size // 2, lefts[0].shape[1] // size
    mine = lax.axis_index("col")
    for other in range(cols):
        col = jnp.bitwise_xor(mine, other)
        for k in range(share):
            piece = lefts[other][:, k * size : (k + 1) * size].astype(jnp.float32)
            both = jnp.concatenate([piece[:half], piece[half:]], axis=1)
            left_rows[pl.ds(col * share + k, half, stride=cols * share), :] = both


def mix_block(states, left_rows, state_diag, mpo_ref, mixed):
    width = mpo_ref.shape[0] // states
    lanes = left_rows.shape[1]
    half = left_rows.shape[0] // width
    for start in range(0, half, CHUNK):
        taken = left_rows[start * width : (start + CHUNK) * width, :].astype(jnp.bfloat16)
        first = jnp.dot(taken, state_diag[...], preferred_element_type=jnp.float32)
        columns = []
        for x in range(CHUNK):
            one = first[x * width : (x + 1) * width, :]
            columns.append(
                jnp.concatenate(
                    [one[:, s * lanes : (s + 1) * lanes] for s in range(states)], axis=0
                ).astype(jnp.bfloat16)
            )
        gathered = jnp.concatenate(columns, axis=1)
        channels = jnp.dot(mpo_ref[...], gathered, preferred_element_type=jnp.float32).astype(jnp.bfloat16)
        for x in range(CHUNK):
            for v in range(width):
                mixed[(start + x) * states : (start + x + 1) * states, v * lanes : (v + 1) * lanes] = channels[
                    v * states : (v + 1) * states, x * lanes : (x + 1) * lanes
                ]


def finish_block(states, mixed, right_diag, result, outs, low):
    cols = len(outs)
    size = low.shape[0]
    half, per = size // 2, states // cols
    mine = lax.axis_index("col")
    result[...] = jnp.dot(mixed[...], right_diag[...], preferred_element_type=jnp.float32)
    low = low[:half]
    for other in range(cols):
        col = jnp.bitwise_xor(mine, other)
        for t in range(0, per, 2):
            one = result[pl.ds(col * per + t, half, stride=states), :]
            two = result[pl.ds(col * per + t + 1, half, stride=states), :]
            upper = jnp.where(low, one, pltpu.roll(two, size, 1))
            lower = jnp.where(low, pltpu.roll(one, size, 1), two)
            outs[other][:half, t * size : (t + 2) * size] = upper.astype(jnp.bfloat16)
            outs[other][half:, t * size : (t + 2) * size] = lower.astype(jnp.bfloat16)


def half_mask(size):
    return lax.broadcasted_iota(jnp.int32, (size, 2 * size), 1) < size


def prepare_kernel(states, order_ref, state_ref, mpo_ref, after_ref, diag_ref, rows_ref, block, flat, sem):
    steps, size = block.shape[:2]
    width = mpo_ref.shape[0]
    low = half_mask(size)
    at = lax.axis_index("col") * steps
    copies = [
        pltpu.make_async_copy(state_ref.at[order_ref[at + k]], block.at[k], sem.at[k]) for k in range(steps)
    ]
    for copy in copies:
        copy.start()
    both = (states * states, states * states)
    row, col = lax.broadcasted_iota(jnp.int32, both, 0), lax.broadcasted_iota(jnp.int32, both, 1)
    turned = lax.rem(row, states) * states + lax.div(row, states)
    turn = jnp.where(turned == col, 1.0, 0.0).astype(jnp.bfloat16)
    split = flat.shape[0]
    for w in range(width):
        turned = jnp.dot(mpo_ref[w], turn, preferred_element_type=jnp.float32)
        for i in range(split):
            flat[i, w * width : (w + 1) * width, :] = turned[:, i * 128 : (i + 1) * 128]

    def one_channel(v, carry):
        taken = [jnp.transpose(flat[i, pl.ds(v, width, stride=width), :]) for i in range(split)]
        taken = jnp.concatenate(taken, axis=0)
        line = jnp.concatenate([taken[s * states : (s + 1) * states, :] for s in range(states)], axis=1)
        rows_ref[pl.ds(pl.multiple_of(v * states, states), states), :] = line.astype(jnp.bfloat16)
        return carry

    lax.fori_loop(0, width, one_channel, 0)
    for copy in copies:
        copy.wait()

    def one_block(k, carry):
        spread_state(block.at[k], diag_ref.at[k], low)
        return carry

    lax.fori_loop(0, steps, one_block, 0)


def prepare(order, state_blocks, mpo_tensor, after, cols, states):
    count, size = state_blocks.shape[:2]
    steps, width = count // cols, mpo_tensor.shape[0]
    return pl.pallas_call(
        functools.partial(prepare_kernel, states),
        out_shape=[
            jax.ShapeDtypeStruct((steps, 2 * size, 2 * states * size), jnp.bfloat16),
            jax.ShapeDtypeStruct((width * states, states * width), jnp.bfloat16),
        ],
        in_specs=[SMEM, ANY, VMEM, ANY],
        out_specs=[VMEM, VMEM],
        scratch_shapes=[
            pltpu.VMEM((steps, size, states * size), jnp.bfloat16),
            pltpu.VMEM((states * states // 128, width * width, 128), jnp.float32),
            pltpu.SemaphoreType.DMA((steps,)),
        ],
        compiler_params=pltpu.CompilerParams(vmem_limit_bytes=10 << 20),
        name="prepare",
    )(order, state_blocks, mpo_tensor, after)


def mix_kernel(states, cols, count, diag_ref, mpo_ref, *refs):
    lefts, mixed, left_rows = refs[:cols], refs[cols : cols + count], refs[-1]
    for k in range(count):
        spread_left([left.at[k] for left in lefts], left_rows.at[k])
    for k in range(count):
        mix_block(states, left_rows.at[k], diag_ref.at[k], mpo_ref, mixed[k])


def right_kernel(states, cols, near, count, order_ref, slot_ref, right_ref, *refs):
    mixed, outs, (right_diag, result) = refs[:count], refs[count : count + cols], refs[count + cols :]
    low = half_mask(right_ref.shape[2])
    at = lax.axis_index("col") * (order_ref.shape[0] // cols)
    for k in range(count):
        slot = slot_ref[at + k]
        spread_right(right_ref.at[lax.div(slot, near), lax.rem(slot, near)], right_diag.at[k], low)
    for k in range(count):
        finish_block(states, mixed[k], right_diag.at[k], result.at[k], [out.at[k] for out in outs], low)


def apply_kernel(
    states, cols, near, first, count, order_ref, slot_ref, right_ref, diag_ref, mpo_ref, early_ref, *refs
):
    lefts, outs, (left_rows, mixed, right_diag, result) = refs[:cols], refs[cols : 2 * cols], refs[2 * cols :]
    low = half_mask(right_ref.shape[2])
    at = lax.axis_index("col") * (order_ref.shape[0] // cols) + first
    outs[1][:first] = early_ref[...]
    for k in range(count):
        spread_left([left.at[k if d > 1 else first + k] for d, left in enumerate(lefts)], left_rows.at[k])
        slot = slot_ref[at + k]
        spread_right(right_ref.at[lax.div(slot, near), lax.rem(slot, near)], right_diag.at[k], low)
    for k in range(count):
        mix_block(states, left_rows.at[k], diag_ref.at[first + k], mpo_ref, mixed.at[k])
        into = [out.at[first + k if d == 1 else k] for d, out in enumerate(outs)]
        finish_block(states, mixed.at[k], right_diag.at[k], result.at[k], into, low)


def cost_of(blocks, states, width, size, mix, right):
    flops = mix * (width * size * size * states * size + (width * states) ** 2 * size * size)
    flops = 2 * blocks * (flops + right * states * size * size * width * size)
    return pl.CostEstimate(flops=flops, bytes_accessed=4 << 20, transcendentals=0)


def first_blocks(order, slots, state_diag, mpo_rows, right, lefts, near):
    cols = len(lefts)
    count, (size, share) = lefts[-1].shape[0], lefts[0].shape[1:]
    width = share // size * cols
    states = mpo_rows.shape[0] // width
    half, lanes = size // 2, 2 * size
    params = pltpu.CompilerParams(vmem_limit_bytes=24 << 20)
    mixed = pl.pallas_call(
        functools.partial(mix_kernel, states, cols, count),
        out_shape=[jax.ShapeDtypeStruct((half * states, width * lanes), jnp.bfloat16)] * count,
        in_specs=[VMEM] * (2 + cols),
        out_specs=[VMEM] * count,
        scratch_shapes=[pltpu.VMEM((count, half * width, lanes), jnp.float32)],
        compiler_params=params,
        cost_estimate=cost_of(count, states, width, size, 1, 0),
        name="mix",
    )(state_diag, mpo_rows, *lefts)
    return pl.pallas_call(
        functools.partial(right_kernel, states, cols, near, count),
        out_shape=[jax.ShapeDtypeStruct((count, size, states // cols * size), jnp.bfloat16)] * cols,
        in_specs=[SMEM] * 2 + [VMEM] * (1 + count),
        out_specs=[VMEM] * cols,
        scratch_shapes=[
            pltpu.VMEM((count, width * lanes, lanes), jnp.bfloat16),
            pltpu.VMEM((count, half * states, lanes), jnp.float32),
        ],
        compiler_params=params,
        cost_estimate=cost_of(count, states, width, size, 0, 1),
        name="right",
    )(order, slots, right, *mixed)


def last_blocks(order, slots, state_diag, mpo_rows, right, lefts, early, near):
    cols = len(lefts)
    first, count, (size, share) = early.shape[0], lefts[-1].shape[0], lefts[0].shape[1:]
    width = share // size * cols
    states = mpo_rows.shape[0] // width
    half, lanes = size // 2, 2 * size

    def out(blocks):
        return jax.ShapeDtypeStruct((blocks, size, states // cols * size), jnp.bfloat16)

    return pl.pallas_call(
        functools.partial(apply_kernel, states, cols, near, first, count),
        out_shape=[out(first + count if d == 1 else count) for d in range(cols)],
        in_specs=[SMEM] * 2 + [VMEM] * (4 + cols),
        out_specs=[VMEM] * cols,
        scratch_shapes=[
            pltpu.VMEM((count, half * width, lanes), jnp.float32),
            pltpu.VMEM((count, half * states, width * lanes), jnp.bfloat16),
            pltpu.VMEM((count, width * lanes, lanes), jnp.bfloat16),
            pltpu.VMEM((count, half * states, lanes), jnp.float32),
        ],
        compiler_params=pltpu.CompilerParams(vmem_limit_bytes=24 << 20),
        cost_estimate=cost_of(count, states, width, size, 1, 1),
        name="apply",
    )(order, slots, right, state_diag, mpo_rows, early, *lefts)


def place_kernel(cols, pieces, begun, order_ref, *refs):
    came = refs[begun : begun + len(pieces)]
    out_ref, sem = refs[begun + len(pieces) :]
    steps = order_ref.shape[0] // cols
    mine = lax.axis_index("col")
    copies = []
    for piece, (other, first) in zip(came, pieces):
        col = jnp.bitwise_xor(mine, other)
        for k in range(piece.shape[0]):
            p = order_ref[col * steps + first + k]
            copies.append(pltpu.make_async_copy(piece.at[k], out_ref.at[p], sem.at[len(copies)]))
    run_copies(copies)


def place_blocks(order, out, came, pieces, cols):
    begun = [] if out is None else [out]
    return pl.pallas_call(
        functools.partial(place_kernel, cols, pieces, len(begun)),
        out_shape=jax.ShapeDtypeStruct((order.shape[0],) + came[0].shape[1:], came[0].dtype),
        in_specs=[SMEM] + [HBM] * len(begun) + [VMEM] * len(came),
        out_specs=HBM,
        scratch_shapes=[pltpu.SemaphoreType.DMA((sum(piece.shape[0] for piece in came),))],
        input_output_aliases={1: 0} if begun else {},
        compiler_params=pltpu.CompilerParams(vmem_limit_bytes=4 << 20),
        name="place",
    )(order, *begun, *came)


def shards(state_blocks, left_env, right_env, mpo_tensor, block_left, block_owner, block_sub):
    rows = lax.axis_size("row")
    cols = lax.axis_size("col")
    count, size = state_blocks.shape[:2]
    states = state_blocks.shape[2] // size
    width = mpo_tensor.shape[0]
    most = max(2, (2 * count + rows - 1) // rows)
    near = -(-most // cols)

    parts = 2

    keys = jnp.bitwise_or(lax.shift_left(block_owner[:, 0], SHIFT), block_sub)
    others = [keys] + [swap(keys, "row", step) for step in range(1, rows)]
    picked = pick(others, right_env, cols, near)
    right = lax.all_to_all(picked, "row", split_axis=0, concat_axis=0, tiled=True)
    block_left, picked = lax.optimization_barrier((block_left, picked))
    sends, order, slots = route(block_left, keys, left_env, cols, near, parts)
    whole = [sends[0], swap(sends[1], "col", 1)]
    lefts = []
    for part in range(parts):
        far = sends[2 + part * (cols - 2) : 2 + (part + 1) * (cols - 2)]
        lefts.append(whole + [swap(far[d - 2], "col", d) for d in range(2, cols)])
    state_diag, mpo_rows = prepare(order, state_blocks, mpo_tensor, sends[0], cols, states)
    early = first_blocks(order, slots, state_diag, mpo_rows, right, lefts[0], near)
    came = [swap(early[d], "col", d) for d in range(2, cols)]
    late = last_blocks(order, slots, state_diag, mpo_rows, right, lefts[1], early[1], near)
    joined = lax.optimization_barrier((*late[1:], *came))
    sent, came = joined[: cols - 1], joined[cols - 1 :]
    last = [swap(sent[d - 1], "col", d) for d in range(1, cols)]
    half = early[0].shape[0]
    pieces = [(0, 0)] + [(d, 0) for d in range(2, cols)] + [(0, half)]
    out = place_blocks(order, None, [early[0], *came, late[0]], pieces, cols)
    pieces = [(1, 0)] + [(d, half) for d in range(2, cols)]
    return place_blocks(order, out, last, pieces, cols)


def solution(mesh):
    placed = (
        P(("groups", "row"), None, None),
        P(("groups", "row"), None, "col"),
        P(("groups", "row"), None, None),
        P(),
        P(("groups", "row")),
        P(("groups", "row"), None),
        P(("groups", "row")),
    )
    return jax.shard_map(
        shards,
        mesh=mesh,
        in_specs=placed,
        out_specs=P(("groups", "row"), None, "col"),
        check_vma=False,
    )
```

time: 70.5 us -> 77.7 us (1.10)
  Pallas kernels: 29.3 us -> 34.2 us
  starting transfers between devices: 18.6 us -> 23.1 us
  local copies, waits for them, and re-layouts: 14 us -> 12.8 us
  waiting for transfers between devices: 7.37 us -> 6.23 us
    unnamed x14 -> x34, local copies, waits for them, and re-layouts: 3.07 us -> 12.8 us
    reshape x2 -> x0, local copies, waits for them, and re-layouts: 6.09 us -> none  [the longest x1 3.47 us: shards(): jnp.transpose(mpo_tensor.reshape(width, width, states, states), (1, 2, 3,...]
    transpose x1 -> x0, local copies, waits for them, and re-layouts: 4.83 us -> none  [shards(): jnp.transpose(mpo_tensor.reshape(width, width, states, states), (1, 2, 3,...]
    all_to_all x0 -> x1, starting transfers between devices: none -> 3.71 us  [shards(): lax.all_to_all(picked, 'row', split_axis=0, concat_axis=0, tiled=True)]
    pallas_call x5, Pallas kernels: 25 us -> 28 us  [the longest x1 9.51 us: last_blocks(): pl.pallas_call(functools.partial(apply_kernel, states, cols, near, first,...]
    pallas_call x1, Pallas kernels: 1.73 us -> 3.52 us  [pick(): pl.pallas_call(functools.partial(pick_kernel, rows, cols, near), out_shap...]
    ppermute x15 -> x13, waiting for transfers between devices: 7.37 us -> 6.22 us  [swap(): return lax.ppermute(array, axis, [(i, i ^ step) for i in range(size)])]
    ppermute x15 -> x13, starting transfers between devices: 18.6 us -> 19.4 us  [swap(): return lax.ppermute(array, axis, [(i, i ^ step) for i in range(size)])]
  transfers between devices with their start and end apart: 15 -> 14, of which waited for: 4 -> 3; matrix products, arithmetic and copies ran while one was open for 16% -> 0% of each run, Pallas kernels for 33% -> 38%
where the time goes in v6:
time: 77.7 us; the launch traced here: 77.3 us
  Pallas kernels  34.2 us (44%)
  starting transfers between devices  23.1 us (30%)
  local copies, waits for them, and re-layouts  12.8 us (16%)
  waiting for transfers between devices  6.23 us (8%)
    ppermute x13, starting transfers between devices, swap(): return lax.ppermute(array, axis, [(i, i ^ step) for i in range(size)])  19.4 us
    unnamed x34, local copies, waits for them, and re-layouts  12.8 us
    pallas_call x1, Pallas kernels, last_blocks(): pl.pallas_call(functools.partial(apply_kernel, states, cols, near, first,...  9.51 us
    pallas_call x1, Pallas kernels, prepare(): pl.pallas_call(functools.partial(prepare_kernel, states), out_shape=[jax....  6.97 us
    ppermute x13, waiting for transfers between devices, swap(): return lax.ppermute(array, axis, [(i, i ^ step) for i in range(size)])  6.22 us
    pallas_call x1, Pallas kernels, first_blocks(): pl.pallas_call(functools.partial(mix_kernel, states, cols, count), out_sh...  5.63 us
    all_to_all x1, starting transfers between devices, shards(): lax.all_to_all(picked, 'row', split_axis=0, concat_axis=0, tiled=True)  3.71 us
    pallas_call x1, Pallas kernels, pick(): pl.pallas_call(functools.partial(pick_kernel, rows, cols, near), out_shap...  3.52 us
  transfers between devices with their start and end apart: 14, of which 3 were waited for; matrix products, arithmetic and copies ran while one was open for 0% of the time, Pallas kernels for 38%

profile of v6, /device:TPU:0, one launch (start us, length us, event | category | flops | bytes accessed | tf_op | source)
XLA Modules:
  0.0 77.3 jit_solution(4823279811211416413)
XLA Ops:
  0.7 2.4 %collective-permute-start.2 = (s32[16]{0:T(128)S(1)}, s32[16]{0:T(128)S(1)}, u32[]{:S(2)}, u32[]{:S(2)}) collective-permute-start(s32[16]{0:T(128)S(1)} %bitcast_or_fusion.refs_0_.key_ref), channel_id=1, source_target_pairs={{0,12},{4,8},{8,4},{12,0},{1,13},{5,9},{9,5},{13,1},{2,14},{6,10},... | collective-permute-start | bytes 200 | tf_op jit(solution)/shard_map/ppermute | solution.py:20
  4.4 2.2 %collective-permute-done.1.refs_2_ = s32[16]{0:T(128)S(1)} collective-permute-done((s32[16]{0:T(128)S(1)}, s32[16]{0:T(128)S(1)}, u32[]{:S(2)}, u32[]{:S(2)}) %collective-permute-start.1) | collective-permute-done | bytes 96 | tf_op jit(solution)/shard_map/ppermute | solution.py:20
  7.7 3.5 %pick.1 = bf16[4,2,64,1536]{3,2,1,0:T(8,128)(2,1)} custom-call(s32[16]{0:T(128)} %copy-done.13, s32[16]{0:T(128)} %copy-done.16, s32[16]{0:T(128)} %copy-done.15, s32[16]{0:T(128)} %copy-done.14, bf16[8,64,1536]{2,1,0:T(8,128)(2,1)} %refs_4_.1), custom_call_target="tpu_custom_call" | custom-call | tf_op jit(solution)/shard_map/pick/pallas_call | solution.py:129
  11.3 3.7 %all-to-all-start = ((bf16[4,2,64,1536]{3,2,1,0:T(8,128)(2,1)}), bf16[4,2,64,1536]{3,2,1,0:T(8,128)(2,1)S(1)}, u32[]{:S(2)}, u32[]{:S(2)}) async-start(bf16[4,2,64,1536]{3,2,1,0:T(8,128)(2,1)} %pick.1), calls=%async_computation | async-start | bytes 3145728 | tf_op jit(solution)/shard_map/all_to_all | solution.py:429
  15.0 3.2 %route.1 = (bf16[4,64,384]{2,1,0:T(8,128)(2,1)}, bf16[4,64,384]{2,1,0:T(8,128)(2,1)}, bf16[2,64,384]{2,1,0:T(8,128)(2,1)}, bf16[2,64,384]{2,1,0:T(8,128)(2,1)}, ...) custom-call(s32[16]{0:T(128)} %left_ref, s32[16]{0:T(128)} %copy-done.13, ...), custom_call_target="tpu_custom_call" | custom-call | tf_op jit(solution)/shard_map/route/pallas_call | solution.py:89
  18.2 1.7 %collective-permute-start.3 = (bf16[4,64,384]{2,1,0:T(8,128)(2,1)}, bf16[4,64,384]{2,1,0:T(8,128)(2,1)S(1)}, u32[]{:S(2)}, u32[]{:S(2)}) collective-permute-start(bf16[4,64,384]{2,1,0:T(8,128)(2,1)} %get-tuple-element.37), channel_id=1, source_target_pairs={{0,1},{1,0},{2,3},{3,2},{4,5},{5,4},{6,7},{7,6},{8,9},{9,8},{10,11... | collective-permute-start | bytes 589832 | tf_op jit(solution)/shard_map/ppermute | solution.py:20
  19.9 2.6 %collective-permute-start.4 = (bf16[2,64,384]{2,1,0:T(8,128)(2,1)}, bf16[2,64,384]{2,1,0:T(8,128)(2,1)S(1)}, u32[]{:S(2)}, u32[]{:S(2)}) collective-permute-start(bf16[2,64,384]{2,1,0:T(8,128)(2,1)} %get-tuple-element.38), channel_id=1, source_target_pairs={{0,2},{1,3},{2,0},{3,1},{4,6},{5,7},{6,4},{7,5},{8,10},{9,11},{10,... | collective-permute-start | bytes 294920 | tf_op jit(solution)/shard_map/ppermute | solution.py:20
  22.7 1.7 %collective-permute-start.6 = (bf16[2,64,384]{2,1,0:T(8,128)(2,1)}, bf16[2,64,384]{2,1,0:T(8,128)(2,1)S(1)}, u32[]{:S(2)}, u32[]{:S(2)}) collective-permute-start(bf16[2,64,384]{2,1,0:T(8,128)(2,1)} %get-tuple-element.44), channel_id=1, source_target_pairs={{0,2},{1,3},{2,0},{3,1},{4,6},{5,7},{6,4},{7,5},{8,10},{9,11},{10,... | collective-permute-start | bytes 294920 | tf_op jit(solution)/shard_map/ppermute | solution.py:20
  24.4 2.0 %collective-permute-start.7 = (bf16[2,64,384]{2,1,0:T(8,128)(2,1)}, bf16[2,64,384]{2,1,0:T(8,128)(2,1)S(1)}, u32[]{:S(2)}, u32[]{:S(2)}) collective-permute-start(bf16[2,64,384]{2,1,0:T(8,128)(2,1)} %get-tuple-element.45), channel_id=1, source_target_pairs={{0,3},{1,2},{2,1},{3,0},{4,7},{5,6},{6,5},{7,4},{8,11},{9,10},{10,... | collective-permute-start | bytes 294920 | tf_op jit(solution)/shard_map/ppermute | solution.py:20
  26.4 1.6 %copy-done.4 = bf16[16,64,1024]{2,1,0:T(8,128)(2,1)S(1)} copy-done((bf16[16,64,1024]{2,1,0:T(8,128)(2,1)S(1)}, bf16[16,64,1024]{2,1,0:T(8,128)(2,1)}, u32[]{:S(2)}) %copy-start.4) | copy-done | bytes 2097176
  29.5 7.0 %prepare.1 = (bf16[4,128,2048]{2,1,0:T(8,128)(2,1)S(1)}, bf16[384,384]{1,0:T(8,128)(2,1)S(1)}) custom-call(s32[16]{0:T(128)S(1)} %copy-done.8, bf16[16,64,1024]{2,1,0:T(8,128)(2,1)S(1)} %copy-done.4, bf16[24,24,256]{2,1,0:T(8,128)(2,1)S(1)} %copy-done.5, bf16[4,64,384]{2,1,0:T(8,128)(2,1)S(1)} %copy-done.6), custom_call_target="tpu_custom_call" | custom-call | tf_op jit(solution)/shard_map/prepare/pallas_call | solution.py:268
  36.6 5.6 %mix.1 = (bf16[512,3072]{1,0:T(8,128)(2,1)S(1)}, bf16[512,3072]{1,0:T(8,128)(2,1)S(1)}) custom-call(bf16[4,128,2048]{2,1,0:T(8,128)(2,1)S(1)} %get-tuple-element.35.diag_ref, bf16[384,384]{1,0:T(8,128)(2,1)S(1)} %get-tuple-element.36.mpo_ref, bf16[4,64,384]{2,1,0:T(8,128)(2,1)S(1)} %copy-done.7, bf16[4,64,384]{2,1,0:T(8,128)(2,1)S(1)} %collective-permute-done.3.refs_1_, ...), custom_call_target="tpu_custom_call" | custom-call | flops 2818572288 | bytes 4194304 | tf_op jit(solution)/shard_map/mix/pallas_call | solution.py:335
  42.2 1.6 %copy-done = bf16[512,3072]{1,0:T(8,128)(2,1)} copy-done((bf16[512,3072]{1,0:T(8,128)(2,1)}, bf16[512,3072]{1,0:T(8,128)(2,1)S(1)}, u32[]{:S(2)}) %copy-start) | copy-done | bytes 3145752
  43.9 1.7 %copy-done.2 = bf16[512,3072]{1,0:T(8,128)(2,1)} copy-done((bf16[512,3072]{1,0:T(8,128)(2,1)}, bf16[512,3072]{1,0:T(8,128)(2,1)S(1)}, u32[]{:S(2)}) %copy-start.2) | copy-done | bytes 3145752
  45.6 1.4 %copy-done.11 = bf16[4,128,2048]{2,1,0:T(8,128)(2,1)} copy-done((bf16[4,128,2048]{2,1,0:T(8,128)(2,1)}, bf16[4,128,2048]{2,1,0:T(8,128)(2,1)S(1)}, u32[]{:S(2)}) %copy-start.11) | copy-done | bytes 2097176
  47.0 1.9 %copy-done.1 = bf16[512,3072]{1,0:T(8,128)(2,1)S(1)} copy-done((bf16[512,3072]{1,0:T(8,128)(2,1)S(1)}, bf16[512,3072]{1,0:T(8,128)(2,1)}, u32[]{:S(2)}) %copy-start.1) | copy-done | bytes 3145752
  48.9 1.9 %copy-done.3 = bf16[512,3072]{1,0:T(8,128)(2,1)S(1)} copy-done((bf16[512,3072]{1,0:T(8,128)(2,1)S(1)}, bf16[512,3072]{1,0:T(8,128)(2,1)}, u32[]{:S(2)}) %copy-start.3) | copy-done | bytes 3145752
  50.8 2.7 %right.1 = (bf16[2,64,256]{2,1,0:T(8,128)(2,1)S(1)}, bf16[2,64,256]{2,1,0:T(8,128)(2,1)S(1)}, bf16[2,64,256]{2,1,0:T(8,128)(2,1)S(1)}, bf16[2,64,256]{2,1,0:T(8,128)(2,1)S(1)}) custom-call(s32[16]{0:T(128)S(1)} %copy-done.9, s32[16]{0:T(128)S(1)} %copy-done.10, bf16[4,2,64,1536]{3,2,1,0:T(8,128)(2,1)S(1)} %all-to-all-done.right_ref, ...), custom_call_target="tpu_custom_call" | custom-call | flops 402653184 | bytes 4194304 | tf_op jit(solution)/shard_map/right/pallas_call | solution.py:345
  53.4 2.3 %collective-permute-start.8 = (bf16[2,64,256]{2,1,0:T(8,128)(2,1)S(1)}, bf16[2,64,256]{2,1,0:T(8,128)(2,1)S(1)}, u32[]{:S(2)}, u32[]{:S(2)}) collective-permute-start(bf16[2,64,256]{2,1,0:T(8,128)(2,1)S(1)} %get-tuple-element.49), channel_id=1, source_target_pairs={{0,2},{1,3},{2,0},{3,1},{4,6},{5,7},{6,4},{7,5},{8,10},{9,11},{10,... | collective-permute-start | bytes 196616 | tf_op jit(solution)/shard_map/ppermute | solution.py:20
  55.7 1.4 %collective-permute-start.9 = (bf16[2,64,256]{2,1,0:T(8,128)(2,1)S(1)}, bf16[2,64,256]{2,1,0:T(8,128)(2,1)S(1)}, u32[]{:S(2)}, u32[]{:S(2)}) collective-permute-start(bf16[2,64,256]{2,1,0:T(8,128)(2,1)S(1)} %get-tuple-element.50), channel_id=1, source_target_pairs={{0,3},{1,2},{2,1},{3,0},{4,7},{5,6},{6,5},{7,4},{8,11},{9,10},{10,... | collective-permute-start | bytes 196616 | tf_op jit(solution)/shard_map/ppermute | solution.py:20
  57.1 9.5 %apply.1 = (bf16[2,64,256]{2,1,0:T(8,128)(2,1)S(1)}, bf16[4,64,256]{2,1,0:T(8,128)(2,1)S(1)}, bf16[2,64,256]{2,1,0:T(8,128)(2,1)S(1)}, bf16[2,64,256]{2,1,0:T(8,128)(2,1)S(1)}) custom-call(s32[16]{0:T(128)S(1)} %copy-done.9, s32[16]{0:T(128)S(1)} %copy-done.10, bf16[4,2,64,1536]{3,2,1,0:T(8,128)(2,1)S(1)} %all-to-all-done.right_ref, ...), custom_call_target="tpu_custom_call" | custom-call | flops 3221225472 | bytes 4194304 | tf_op jit(solution)/shard_map/apply/pallas_call | solution.py:370
  66.8 3.0 %collective-permute-start.11 = (bf16[2,64,256]{2,1,0:T(8,128)(2,1)S(1)}, bf16[2,64,256]{2,1,0:T(8,128)(2,1)S(1)}, u32[]{:S(2)}, u32[]{:S(2)}) collective-permute-start(bf16[2,64,256]{2,1,0:T(8,128)(2,1)S(1)} %get-tuple-element.55), channel_id=1, source_target_pairs={{0,2},{1,3},{2,0},{3,1},{4,6},{5,7},{6,4},{7,5},{8,10},{9,11},{10,... | collective-permute-start | bytes 196616 | tf_op jit(solution)/shard_map/ppermute | solution.py:20
  69.7 1.4 %collective-permute-start.12 = (bf16[2,64,256]{2,1,0:T(8,128)(2,1)S(1)}, bf16[2,64,256]{2,1,0:T(8,128)(2,1)S(1)}, u32[]{:S(2)}, u32[]{:S(2)}) collective-permute-start(bf16[2,64,256]{2,1,0:T(8,128)(2,1)S(1)} %get-tuple-element.56), channel_id=1, source_target_pairs={{0,3},{1,2},{2,1},{3,0},{4,7},{5,6},{6,5},{7,4},{8,11},{9,10},{10,... | collective-permute-start | bytes 196616 | tf_op jit(solution)/shard_map/ppermute | solution.py:20
  72.5 3.3 %collective-permute-done.12.refs_3_ = bf16[2,64,256]{2,1,0:T(8,128)(2,1)S(1)} collective-permute-done((bf16[2,64,256]{2,1,0:T(8,128)(2,1)S(1)}, bf16[2,64,256]{2,1,0:T(8,128)(2,1)S(1)}, u32[]{:S(2)}, u32[]{:S(2)}) %collective-permute-start.12) | collective-permute-done | bytes 65568 | tf_op jit(solution)/shard_map/ppermute | solution.py:20
  (47 shorter events, 7.5 us)
Async XLA Ops:
  0.7 6.0 %copy-start.13 = (s32[16]{0:T(128)}, s32[16]{0:T(128)S(1)}, u32[]{:S(2)}) copy-start(s32[16]{0:T(128)S(1)} %bitcast_or_fusion.refs_0_.key_ref) | copy-start | bytes 196
  0.7 3.7 %collective-permute-start.2 = (s32[16]{0:T(128)S(1)}, s32[16]{0:T(128)S(1)}, u32[]{:S(2)}, u32[]{:S(2)}) collective-permute-start(s32[16]{0:T(128)S(1)} %bitcast_or_fusion.refs_0_.key_ref), channel_id=1, source_target_pairs={{0,12},{4,8},{8,4},{12,0},{1,13},{5,9},{9,5},{13,1},{2,14},{6,10},... | collective-permute-start | bytes 200 | tf_op jit(solution)/shard_map/ppermute | solution.py:20
  3.1 3.5 %collective-permute-start.1 = (s32[16]{0:T(128)S(1)}, s32[16]{0:T(128)S(1)}, u32[]{:S(2)}, u32[]{:S(2)}) collective-permute-start(s32[16]{0:T(128)S(1)} %bitcast_or_fusion.refs_0_.key_ref), channel_id=1, source_target_pairs={{0,8},{4,12},{8,0},{12,4},{1,9},{5,13},{9,1},{13,5},{2,10},{6,14},... | collective-permute-start | bytes 200 | tf_op jit(solution)/shard_map/ppermute | solution.py:20
  3.7 2.9 %collective-permute-start = (s32[16]{0:T(128)S(1)}, s32[16]{0:T(128)S(1)}, u32[]{:S(2)}, u32[]{:S(2)}) collective-permute-start(s32[16]{0:T(128)S(1)} %bitcast_or_fusion.refs_0_.key_ref), channel_id=1, source_target_pairs={{0,4},{4,0},{8,12},{12,8},{1,5},{5,1},{9,13},{13,9},{2,6},{6,2},{1... | collective-permute-start | bytes 200 | tf_op jit(solution)/shard_map/ppermute | solution.py:20
  4.4 2.3 %copy-start.14 = (s32[16]{0:T(128)}, s32[16]{0:T(128)S(1)}, u32[]{:S(2)}) copy-start(s32[16]{0:T(128)S(1)} %collective-permute-done.2.refs_3_) | copy-start | bytes 196
  11.2 15.1 %copy-start.5 = (bf16[24,24,256]{2,1,0:T(8,128)(2,1)S(1)}, bf16[24,24,256]{2,1,0:T(8,128)(2,1)}, u32[]{:S(2)}) copy-start(bf16[24,24,256]{2,1,0:T(8,128)(2,1)} %mpo_ref.1) | copy-start | bytes 884740
  11.3 35.7 %all-to-all-start = ((bf16[4,2,64,1536]{3,2,1,0:T(8,128)(2,1)}), bf16[4,2,64,1536]{3,2,1,0:T(8,128)(2,1)S(1)}, u32[]{:S(2)}, u32[]{:S(2)}) async-start(bf16[4,2,64,1536]{3,2,1,0:T(8,128)(2,1)} %pick.1), calls=%async_computation | async-start | bytes 3145728 | tf_op jit(solution)/shard_map/all_to_all | solution.py:429
  18.2 18.3 %collective-permute-start.3 = (bf16[4,64,384]{2,1,0:T(8,128)(2,1)}, bf16[4,64,384]{2,1,0:T(8,128)(2,1)S(1)}, u32[]{:S(2)}, u32[]{:S(2)}) collective-permute-start(bf16[4,64,384]{2,1,0:T(8,128)(2,1)} %get-tuple-element.37), channel_id=1, source_target_pairs={{0,1},{1,0},{2,3},{3,2},{4,5},{5,4},{6,7},{7,6},{8,9},{9,8},{10,11... | collective-permute-start | bytes 589832 | tf_op jit(solution)/shard_map/ppermute | solution.py:20
  19.9 16.6 %collective-permute-start.4 = (bf16[2,64,384]{2,1,0:T(8,128)(2,1)}, bf16[2,64,384]{2,1,0:T(8,128)(2,1)S(1)}, u32[]{:S(2)}, u32[]{:S(2)}) collective-permute-start(bf16[2,64,384]{2,1,0:T(8,128)(2,1)} %get-tuple-element.38), channel_id=1, source_target_pairs={{0,2},{1,3},{2,0},{3,1},{4,6},{5,7},{6,4},{7,5},{8,10},{9,11},{10,... | collective-permute-start | bytes 294920 | tf_op jit(solution)/shard_map/ppermute | solution.py:20
  22.5 14.0 %collective-permute-start.5 = (bf16[2,64,384]{2,1,0:T(8,128)(2,1)}, bf16[2,64,384]{2,1,0:T(8,128)(2,1)S(1)}, u32[]{:S(2)}, u32[]{:S(2)}) collective-permute-start(bf16[2,64,384]{2,1,0:T(8,128)(2,1)} %get-tuple-element.39), channel_id=1, source_target_pairs={{0,3},{1,2},{2,1},{3,0},{4,7},{5,6},{6,5},{7,4},{8,11},{9,10},{10,... | collective-permute-start | bytes 294920 | tf_op jit(solution)/shard_map/ppermute | solution.py:20
  22.7 34.5 %collective-permute-start.6 = (bf16[2,64,384]{2,1,0:T(8,128)(2,1)}, bf16[2,64,384]{2,1,0:T(8,128)(2,1)S(1)}, u32[]{:S(2)}, u32[]{:S(2)}) collective-permute-start(bf16[2,64,384]{2,1,0:T(8,128)(2,1)} %get-tuple-element.44), channel_id=1, source_target_pairs={{0,2},{1,3},{2,0},{3,1},{4,6},{5,7},{6,4},{7,5},{8,10},{9,11},{10,... | collective-permute-start | bytes 294920 | tf_op jit(solution)/shard_map/ppermute | solution.py:20
  24.4 32.8 %collective-permute-start.7 = (bf16[2,64,384]{2,1,0:T(8,128)(2,1)}, bf16[2,64,384]{2,1,0:T(8,128)(2,1)S(1)}, u32[]{:S(2)}, u32[]{:S(2)}) collective-permute-start(bf16[2,64,384]{2,1,0:T(8,128)(2,1)} %get-tuple-element.45), channel_id=1, source_target_pairs={{0,3},{1,2},{2,1},{3,0},{4,7},{5,6},{6,5},{7,4},{8,11},{9,10},{10,... | collective-permute-start | bytes 294920 | tf_op jit(solution)/shard_map/ppermute | solution.py:20
  29.5 7.0 %copy-start.7 = (bf16[4,64,384]{2,1,0:T(8,128)(2,1)S(1)}, bf16[4,64,384]{2,1,0:T(8,128)(2,1)}, u32[]{:S(2)}) copy-start(bf16[4,64,384]{2,1,0:T(8,128)(2,1)} %get-tuple-element.34.after_ref.refs_0_) | copy-start | bytes 589828
  36.6 10.4 %copy-start.9 = (s32[16]{0:T(128)S(1)}, s32[16]{0:T(128)}, u32[]{:S(2)}) copy-start(s32[16]{0:T(128)} %get-tuple-element.32.order_ref) | copy-start | bytes 196
  36.6 10.4 %copy-start.10 = (s32[16]{0:T(128)S(1)}, s32[16]{0:T(128)}, u32[]{:S(2)}) copy-start(s32[16]{0:T(128)} %get-tuple-element.33.slot_ref) | copy-start | bytes 196
  43.9 1.7 %copy-start.2 = (bf16[512,3072]{1,0:T(8,128)(2,1)}, bf16[512,3072]{1,0:T(8,128)(2,1)S(1)}, u32[]{:S(2)}) copy-start(bf16[512,3072]{1,0:T(8,128)(2,1)S(1)} %get-tuple-element.41.refs_1_) | copy-start | bytes 9437188
  47.0 1.9 %copy-start.1 = (bf16[512,3072]{1,0:T(8,128)(2,1)S(1)}, bf16[512,3072]{1,0:T(8,128)(2,1)}, u32[]{:S(2)}) copy-start(bf16[512,3072]{1,0:T(8,128)(2,1)} %copy-done) | copy-start | bytes 9437188
  48.9 1.9 %copy-start.3 = (bf16[512,3072]{1,0:T(8,128)(2,1)S(1)}, bf16[512,3072]{1,0:T(8,128)(2,1)}, u32[]{:S(2)}) copy-start(bf16[512,3072]{1,0:T(8,128)(2,1)} %copy-done.2) | copy-start | bytes 9437188
  50.8 6.4 %copy-start.12 = (bf16[4,128,2048]{2,1,0:T(8,128)(2,1)S(1)}, bf16[4,128,2048]{2,1,0:T(8,128)(2,1)}, u32[]{:S(2)}) copy-start(bf16[4,128,2048]{2,1,0:T(8,128)(2,1)} %copy-done.11) | copy-start | bytes 6291460
  53.4 13.2 %collective-permute-start.8 = (bf16[2,64,256]{2,1,0:T(8,128)(2,1)S(1)}, bf16[2,64,256]{2,1,0:T(8,128)(2,1)S(1)}, u32[]{:S(2)}, u32[]{:S(2)}) collective-permute-start(bf16[2,64,256]{2,1,0:T(8,128)(2,1)S(1)} %get-tuple-element.49), channel_id=1, source_target_pairs={{0,2},{1,3},{2,0},{3,1},{4,6},{5,7},{6,4},{7,5},{8,10},{9,11},{10,... | collective-permute-start | bytes 196616 | tf_op jit(solution)/shard_map/ppermute | solution.py:20
  55.7 10.9 %collective-permute-start.9 = (bf16[2,64,256]{2,1,0:T(8,128)(2,1)S(1)}, bf16[2,64,256]{2,1,0:T(8,128)(2,1)S(1)}, u32[]{:S(2)}, u32[]{:S(2)}) collective-permute-start(bf16[2,64,256]{2,1,0:T(8,128)(2,1)S(1)} %get-tuple-element.50), channel_id=1, source_target_pairs={{0,3},{1,2},{2,1},{3,0},{4,7},{5,6},{6,5},{7,4},{8,11},{9,10},{10,... | collective-permute-start | bytes 196616 | tf_op jit(solution)/shard_map/ppermute | solution.py:20
  66.7 9.1 %collective-permute-start.10 = (bf16[4,64,256]{2,1,0:T(8,128)(2,1)S(1)}, bf16[4,64,256]{2,1,0:T(8,128)(2,1)S(1)}, u32[]{:S(2)}, u32[]{:S(2)}) collective-permute-start(bf16[4,64,256]{2,1,0:T(8,128)(2,1)S(1)} %get-tuple-element.54), channel_id=1, source_target_pairs={{0,1},{1,0},{2,3},{3,2},{4,5},{5,4},{6,7},{7,6},{8,9},{9,8},{10,11... | collective-permute-start | bytes 393224 | tf_op jit(solution)/shard_map/ppermute | solution.py:20
  66.8 5.7 %collective-permute-start.11 = (bf16[2,64,256]{2,1,0:T(8,128)(2,1)S(1)}, bf16[2,64,256]{2,1,0:T(8,128)(2,1)S(1)}, u32[]{:S(2)}, u32[]{:S(2)}) collective-permute-start(bf16[2,64,256]{2,1,0:T(8,128)(2,1)S(1)} %get-tuple-element.55), channel_id=1, source_target_pairs={{0,2},{1,3},{2,0},{3,1},{4,6},{5,7},{6,4},{7,5},{8,10},{9,11},{10,... | collective-permute-start | bytes 196616 | tf_op jit(solution)/shard_map/ppermute | solution.py:20
  69.7 6.1 %collective-permute-start.12 = (bf16[2,64,256]{2,1,0:T(8,128)(2,1)S(1)}, bf16[2,64,256]{2,1,0:T(8,128)(2,1)S(1)}, u32[]{:S(2)}, u32[]{:S(2)}) collective-permute-start(bf16[2,64,256]{2,1,0:T(8,128)(2,1)S(1)} %get-tuple-element.56), channel_id=1, source_target_pairs={{0,3},{1,2},{2,1},{3,0},{4,7},{5,6},{6,5},{7,4},{8,11},{9,10},{10,... | collective-permute-start | bytes 196616 | tf_op jit(solution)/shard_map/ppermute | solution.py:20
  (7 other events, 7.3 us)

commit v7 on v6

--- a/solution.py
+++ b/solution.py
@@ -35,12 +35,11 @@
     return jnp.bitwise_and(key, (1 << SHIFT) - 1)
 
 
-def route_kernel(cols, near, parts, left_ref, key_ref, env_ref, *refs):
-    sends = refs[: 2 + (cols - 2) * parts]
-    order_ref, slot_ref, by_place, sem = refs[len(sends) :]
+def route_kernel(cols, near, left_ref, key_ref, env_ref, *refs):
+    sends = refs[:cols]
+    order_ref, slot_ref, by_place = refs[cols:]
     count = left_ref.shape[0]
     steps = count // cols
-    per_part = steps // parts
     mine = lax.axis_index("col")
     owners = [owner_of(key_ref[p]) for p in range(count)]
     for p in range(count):
@@ -63,47 +62,37 @@
             before = owner, slot
             order_ref[col * steps + step] = p
             slot_ref[col * steps + step] = owner * near + slot
-    copies = []
     for other in range(cols):
         col = jnp.bitwise_xor(mine, other)
         for step in range(steps):
-            sector = left_ref[order_ref[col * steps + step]]
-            if other < 2:
-                target = sends[other].at[step]
-            else:
-                target = sends[2 + step // per_part * (cols - 2) + other - 2].at[step % per_part]
-            copies.append(pltpu.make_async_copy(env_ref.at[sector], target, sem.at[len(copies)]))
-            copies[-1].start()
-    for copy in copies:
-        copy.wait()
-
-
-def route(block_left, keys, left_env, cols, near, parts):
+            p = order_ref[col * steps + step]
+            sends[other][step] = env_ref[left_ref[p]]
+
+
+def route(block_left, keys, left_env, cols, near):
     count = block_left.shape[0]
     size, width = left_env.shape[1:]
-    steps = count // cols
-    whole = jax.ShapeDtypeStruct((steps, size, width), left_env.dtype)
-    piece = jax.ShapeDtypeStruct((steps // parts, size, width), left_env.dtype)
+    piece = jax.ShapeDtypeStruct((count // cols, size, width), left_env.dtype)
     listed = jax.ShapeDtypeStruct((count,), jnp.int32)
-    far = (cols - 2) * parts
     *sends, order, slots = pl.pallas_call(
-        functools.partial(route_kernel, cols, near, parts),
-        out_shape=[whole] * 2 + [piece] * far + [listed] * 2,
-        in_specs=[SMEM, SMEM, ANY],
-        out_specs=[VMEM] * (2 + far) + [SMEM] * 2,
-        scratch_shapes=[pltpu.SMEM((count,), jnp.int32), pltpu.SemaphoreType.DMA((count,))],
+        functools.partial(route_kernel, cols, near),
+        out_shape=(piece,) * cols + (listed, listed),
+        in_specs=[SMEM, SMEM, VMEM],
+        out_specs=(VMEM,) * cols + (SMEM, SMEM),
+        scratch_shapes=[pltpu.SMEM((count,), jnp.int32)],
         name="route",
     )(block_left, keys, left_env)
     return sends, order, slots
 
 
 def pick_kernel(rows, cols, near, *refs):
-    key_refs, (env_ref, send_ref, sem) = refs[:rows], refs[rows:]
+    key_refs = refs[: rows - 1]
+    env_ref = refs[rows - 1]
+    sends = refs[rows:]
     count = key_refs[0].shape[0]
     me = lax.axis_index("row")
     mine = lax.axis_index("col")
-    copies = []
-    for other in range(rows):
+    for other in range(rows - 1):
         keys = [key_refs[other][p] for p in range(count)]
         owners = [owner_of(key) for key in keys]
         first = jnp.int32(0)
@@ -117,21 +106,17 @@
                 wanted[slot] = jnp.where(here & (past == slot * cols), sub_of(keys[p]), wanted[slot])
             past = past + here.astype(jnp.int32)
         for slot in range(near):
-            target = send_ref.at[jnp.bitwise_xor(me, other), slot]
-            copies.append(pltpu.make_async_copy(env_ref.at[wanted[slot]], target, sem.at[len(copies)]))
-            copies[-1].start()
-    for copy in copies:
-        copy.wait()
+            sends[other][slot] = env_ref[wanted[slot]]
 
 
 def pick(keys, right_env, cols, near):
-    rows = len(keys)
+    rows = len(keys) + 1
+    piece = jax.ShapeDtypeStruct((near,) + right_env.shape[1:], right_env.dtype)
     return pl.pallas_call(
         functools.partial(pick_kernel, rows, cols, near),
-        out_shape=jax.ShapeDtypeStruct((rows, near) + right_env.shape[1:], right_env.dtype),
-        in_specs=[SMEM] * rows + [ANY],
-        out_specs=VMEM,
-        scratch_shapes=[pltpu.SemaphoreType.DMA((rows * near,))],
+        out_shape=[piece] * (rows - 1),
+        in_specs=[SMEM] * (rows - 1) + [VMEM],
+        out_specs=(VMEM,) * (rows - 1),
         name="pick",
     )(*keys, right_env)
 
@@ -224,7 +209,7 @@
     return lax.broadcasted_iota(jnp.int32, (size, 2 * size), 1) < size
 
 
-def prepare_kernel(states, order_ref, state_ref, mpo_ref, after_ref, diag_ref, rows_ref, block, flat, sem):
+def prepare_kernel(states, order_ref, state_ref, mpo_ref, diag_ref, rows_ref, block, flat, sem):
     steps, size = block.shape[:2]
     width = mpo_ref.shape[0]
     low = half_mask(size)
@@ -240,18 +225,23 @@
     turn = jnp.where(turned == col, 1.0, 0.0).astype(jnp.bfloat16)
     split = flat.shape[0]
     for w in range(width):
-        turned = jnp.dot(mpo_ref[w], turn, preferred_element_type=jnp.float32)
+        taken = mpo_ref[w].astype(jnp.float32)
         for i in range(split):
-            flat[i, w * width : (w + 1) * width, :] = turned[:, i * 128 : (i + 1) * 128]
-
-    def one_channel(v, carry):
-        taken = [jnp.transpose(flat[i, pl.ds(v, width, stride=width), :]) for i in range(split)]
-        taken = jnp.concatenate(taken, axis=0)
-        line = jnp.concatenate([taken[s * states : (s + 1) * states, :] for s in range(states)], axis=1)
-        rows_ref[pl.ds(pl.multiple_of(v * states, states), states), :] = line.astype(jnp.bfloat16)
+            flat[i, w * width : (w + 1) * width, :] = taken[:, i * 128 : (i + 1) * 128]
+    taken = jnp.concatenate([flat[i] for i in range(split)], axis=1).astype(jnp.bfloat16)
+    taken = jnp.dot(taken, turn, preferred_element_type=jnp.float32)
+    for i in range(split):
+        flat[i] = taken[:, i * 128 : (i + 1) * 128]
+
+    def some_channels(j, carry):
+        for v in range(4):
+            taken = [jnp.transpose(flat[i, pl.ds(4 * j + v, width, stride=width), :]) for i in range(split)]
+            taken = jnp.concatenate(taken, axis=0)
+            line = jnp.concatenate([taken[s * states : (s + 1) * states, :] for s in range(states)], axis=1)
+            rows_ref[pl.ds(pl.multiple_of((4 * j + v) * states, states), states), :] = line.astype(jnp.bfloat16)
         return carry
 
-    lax.fori_loop(0, width, one_channel, 0)
+    lax.fori_loop(0, width // 4, some_channels, 0)
     for copy in copies:
         copy.wait()
 
@@ -262,7 +252,7 @@
     lax.fori_loop(0, steps, one_block, 0)
 
 
-def prepare(order, state_blocks, mpo_tensor, after, cols, states):
+def prepare(order, state_blocks, mpo_tensor, cols, states):
     count, size = state_blocks.shape[:2]
     steps, width = count // cols, mpo_tensor.shape[0]
     return pl.pallas_call(
@@ -271,7 +261,7 @@
             jax.ShapeDtypeStruct((steps, 2 * size, 2 * states * size), jnp.bfloat16),
             jax.ShapeDtypeStruct((width * states, states * width), jnp.bfloat16),
         ],
-        in_specs=[SMEM, ANY, VMEM, ANY],
+        in_specs=[SMEM, ANY, VMEM],
         out_specs=[VMEM, VMEM],
         scratch_shapes=[
             pltpu.VMEM((steps, size, states * size), jnp.bfloat16),
@@ -280,7 +270,7 @@
         ],
         compiler_params=pltpu.CompilerParams(vmem_limit_bytes=10 << 20),
         name="prepare",
-    )(order, state_blocks, mpo_tensor, after)
+    )(order, state_blocks, mpo_tensor)
 
 
 def mix_kernel(states, cols, count, diag_ref, mpo_ref, *refs):
@@ -291,28 +281,47 @@
         mix_block(states, left_rows.at[k], diag_ref.at[k], mpo_ref, mixed[k])
 
 
-def right_kernel(states, cols, near, count, order_ref, slot_ref, right_ref, *refs):
-    mixed, outs, (right_diag, result) = refs[:count], refs[count : count + cols], refs[count + cols :]
-    low = half_mask(right_ref.shape[2])
+def fetch_right(near, key_ref, order_ref, slot_ref, at, env_ref, rights, right_now):
+    slot = lax.rem(slot_ref[at], near)
+    apart = jnp.bitwise_xor(lax.div(slot_ref[at], near), lax.axis_index("row"))
+
+    @pl.when(apart == 0)
+    def _():
+        right_now[...] = env_ref[sub_of(key_ref[order_ref[at]])]
+
+    for other, right in enumerate(rights, 1):
+
+        @pl.when(apart == other)
+        def _():
+            right_now[...] = right[slot]
+
+
+def right_kernel(states, rows, cols, near, count, order_ref, slot_ref, key_ref, env_ref, *refs):
+    rights, refs = refs[: rows - 1], refs[rows - 1 :]
+    mixed, outs, (right_now, right_diag, result) = refs[:count], refs[count : count + cols], refs[count + cols :]
+    low = half_mask(env_ref.shape[1])
     at = lax.axis_index("col") * (order_ref.shape[0] // cols)
     for k in range(count):
-        slot = slot_ref[at + k]
-        spread_right(right_ref.at[lax.div(slot, near), lax.rem(slot, near)], right_diag.at[k], low)
+        fetch_right(near, key_ref, order_ref, slot_ref, at + k, env_ref, rights, right_now.at[k])
+    for k in range(count):
+        spread_right(right_now.at[k], right_diag.at[k], low)
     for k in range(count):
         finish_block(states, mixed[k], right_diag.at[k], result.at[k], [out.at[k] for out in outs], low)
 
 
 def apply_kernel(
-    states, cols, near, first, count, order_ref, slot_ref, right_ref, diag_ref, mpo_ref, early_ref, *refs
+    states, rows, cols, near, first, count, order_ref, slot_ref, key_ref, env_ref, diag_ref, mpo_ref, early_ref, *refs
 ):
-    lefts, outs, (left_rows, mixed, right_diag, result) = refs[:cols], refs[cols : 2 * cols], refs[2 * cols :]
-    low = half_mask(right_ref.shape[2])
+    rights, lefts, refs = refs[: rows - 1], refs[rows - 1 : rows - 1 + cols], refs[rows - 1 + cols :]
+    outs, (left_rows, mixed, right_now, right_diag, result) = refs[:cols], refs[cols:]
+    low = half_mask(env_ref.shape[1])
     at = lax.axis_index("col") * (order_ref.shape[0] // cols) + first
+    for k in range(count):
+        fetch_right(near, key_ref, order_ref, slot_ref, at + k, env_ref, rights, right_now.at[k])
     outs[1][:first] = early_ref[...]
     for k in range(count):
-        spread_left([left.at[k if d > 1 else first + k] for d, left in enumerate(lefts)], left_rows.at[k])
-        slot = slot_ref[at + k]
-        spread_right(right_ref.at[lax.div(slot, near), lax.rem(slot, near)], right_diag.at[k], low)
+        spread_left([left.at[first + k] for left in lefts], left_rows.at[k])
+        spread_right(right_now.at[k], right_diag.at[k], low)
     for k in range(count):
         mix_block(states, left_rows.at[k], diag_ref.at[first + k], mpo_ref, mixed.at[k])
         into = [out.at[first + k if d == 1 else k] for d, out in enumerate(outs)]
@@ -325,9 +334,9 @@
     return pl.CostEstimate(flops=flops, bytes_accessed=4 << 20, transcendentals=0)
 
 
-def first_blocks(order, slots, state_diag, mpo_rows, right, lefts, near):
-    cols = len(lefts)
-    count, (size, share) = lefts[-1].shape[0], lefts[0].shape[1:]
+def first_blocks(count, order, slots, keys, state_diag, mpo_rows, right_env, rights, lefts, near):
+    cols, rows = len(lefts), len(rights) + 1
+    size, share = lefts[0].shape[1:]
     width = share // size * cols
     states = mpo_rows.shape[0] // width
     half, lanes = size // 2, 2 * size
@@ -343,23 +352,25 @@
         name="mix",
     )(state_diag, mpo_rows, *lefts)
     return pl.pallas_call(
-        functools.partial(right_kernel, states, cols, near, count),
+        functools.partial(right_kernel, states, rows, cols, near, count),
         out_shape=[jax.ShapeDtypeStruct((count, size, states // cols * size), jnp.bfloat16)] * cols,
-        in_specs=[SMEM] * 2 + [VMEM] * (1 + count),
+        in_specs=[SMEM] * 3 + [VMEM] * (rows + count),
         out_specs=[VMEM] * cols,
         scratch_shapes=[
+            pltpu.VMEM((count, size, width * size), jnp.bfloat16),
             pltpu.VMEM((count, width * lanes, lanes), jnp.bfloat16),
             pltpu.VMEM((count, half * states, lanes), jnp.float32),
         ],
         compiler_params=params,
         cost_estimate=cost_of(count, states, width, size, 0, 1),
         name="right",
-    )(order, slots, right, *mixed)
-
-
-def last_blocks(order, slots, state_diag, mpo_rows, right, lefts, early, near):
-    cols = len(lefts)
-    first, count, (size, share) = early.shape[0], lefts[-1].shape[0], lefts[0].shape[1:]
+    )(order, slots, keys, right_env, *rights, *mixed)
+
+
+def last_blocks(order, slots, keys, state_diag, mpo_rows, right_env, rights, lefts, early, near):
+    cols, rows = len(lefts), len(rights) + 1
+    first, (steps, size, share) = early.shape[0], lefts[0].shape
+    count = steps - first
     width = share // size * cols
     states = mpo_rows.shape[0] // width
     half, lanes = size // 2, 2 * size
@@ -368,20 +379,21 @@
         return jax.ShapeDtypeStruct((blocks, size, states // cols * size), jnp.bfloat16)
 
     return pl.pallas_call(
-        functools.partial(apply_kernel, states, cols, near, first, count),
-        out_shape=[out(first + count if d == 1 else count) for d in range(cols)],
-        in_specs=[SMEM] * 2 + [VMEM] * (4 + cols),
+        functools.partial(apply_kernel, states, rows, cols, near, first, count),
+        out_shape=[out(steps if d == 1 else count) for d in range(cols)],
+        in_specs=[SMEM] * 3 + [VMEM] * (4 + rows - 1 + cols),
         out_specs=[VMEM] * cols,
         scratch_shapes=[
             pltpu.VMEM((count, half * width, lanes), jnp.float32),
             pltpu.VMEM((count, half * states, width * lanes), jnp.bfloat16),
+            pltpu.VMEM((count, size, width * size), jnp.bfloat16),
             pltpu.VMEM((count, width * lanes, lanes), jnp.bfloat16),
             pltpu.VMEM((count, half * states, lanes), jnp.float32),
         ],
         compiler_params=pltpu.CompilerParams(vmem_limit_bytes=24 << 20),
         cost_estimate=cost_of(count, states, width, size, 1, 1),
         name="apply",
-    )(order, slots, right, state_diag, mpo_rows, early, *lefts)
+    )(order, slots, keys, right_env, state_diag, mpo_rows, early, *rights, *lefts)
 
 
 def place_kernel(cols, pieces, begun, order_ref, *refs):
@@ -421,27 +433,24 @@
     most = max(2, (2 * count + rows - 1) // rows)
     near = -(-most // cols)
 
-    parts = 2
+    half = count // cols // 2
 
     keys = jnp.bitwise_or(lax.shift_left(block_owner[:, 0], SHIFT), block_sub)
-    others = [keys] + [swap(keys, "row", step) for step in range(1, rows)]
+    others = [swap(keys, "row", step) for step in range(1, rows)]
+    block_left, *others = lax.optimization_barrier((block_left, *others))
+    sends, order, slots = route(block_left, keys, left_env, cols, near)
+    lefts = [sends[0]] + [swap(sends[d], "col", d) for d in range(1, cols)]
     picked = pick(others, right_env, cols, near)
-    right = lax.all_to_all(picked, "row", split_axis=0, concat_axis=0, tiled=True)
-    block_left, picked = lax.optimization_barrier((block_left, picked))
-    sends, order, slots = route(block_left, keys, left_env, cols, near, parts)
-    whole = [sends[0], swap(sends[1], "col", 1)]
-    lefts = []
-    for part in range(parts):
-        far = sends[2 + part * (cols - 2) : 2 + (part + 1) * (cols - 2)]
-        lefts.append(whole + [swap(far[d - 2], "col", d) for d in range(2, cols)])
-    state_diag, mpo_rows = prepare(order, state_blocks, mpo_tensor, sends[0], cols, states)
-    early = first_blocks(order, slots, state_diag, mpo_rows, right, lefts[0], near)
+    mpo_tensor, *far = lax.optimization_barrier((mpo_tensor, *picked))
+    state_diag, mpo_rows = prepare(order, state_blocks, mpo_tensor, cols, states)
+    core_send, state_diag = lax.optimization_barrier((far[0], state_diag))
+    rights = [swap(core_send, "row", 1)] + [swap(far[d - 1], "row", d) for d in range(2, rows)]
+    early = first_blocks(half, order, slots, keys, state_diag, mpo_rows, right_env, rights, lefts, near)
     came = [swap(early[d], "col", d) for d in range(2, cols)]
-    late = last_blocks(order, slots, state_diag, mpo_rows, right, lefts[1], early[1], near)
+    late = last_blocks(order, slots, keys, state_diag, mpo_rows, right_env, rights, lefts, early[1], near)
     joined = lax.optimization_barrier((*late[1:], *came))
     sent, came = joined[: cols - 1], joined[cols - 1 :]
     last = [swap(sent[d - 1], "col", d) for d in range(1, cols)]
-    half = early[0].shape[0]
     pieces = [(0, 0)] + [(d, 0) for d in range(2, cols)] + [(0, half)]
     out = place_blocks(order, None, [early[0], *came, late[0]], pieces, cols)
     pieces = [(1, 0)] + [(d, half) for d in range(2, cols)]

time: 77.7 us -> 62.8 us (0.81)
  local copies, waits for them, and re-layouts: 12.8 us -> 2.21 us
  Pallas kernels: 34.2 us -> 29.4 us
  waiting for transfers between devices: 6.23 us -> 10.3 us
  starting transfers between devices: 23.1 us -> 19.6 us
    unnamed x34 -> x26, local copies, waits for them, and re-layouts: 12.8 us -> 2.21 us
    ppermute x13 -> x14, waiting for transfers between devices: 6.22 us -> 10.3 us  [swap(): return lax.ppermute(array, axis, [(i, i ^ step) for i in range(size)])]
    all_to_all x1 -> x0, starting transfers between devices: 3.71 us -> none  [shards(): lax.all_to_all(picked, 'row', split_axis=0, concat_axis=0, tiled=True)]
    pallas_call x1, Pallas kernels: 6.97 us -> 3.41 us  [prepare(): pl.pallas_call(functools.partial(prepare_kernel, states), out_shape=[jax....]
    pallas_call x1, Pallas kernels: 3.52 us -> 2.74 us  [pick(): pl.pallas_call(functools.partial(pick_kernel, rows, cols, near), out_shap...]
    ppermute x13 -> x14, starting transfers between devices: 19.4 us -> 19.6 us  [swap(): return lax.ppermute(array, axis, [(i, i ^ step) for i in range(size)])]
  transfers between devices with their start and end apart: 14 -> 14, of which waited for: 3 -> 5; matrix products, arithmetic and copies ran while one was open for 0% -> 0% of each run, Pallas kernels for 38% -> 37%
where the time goes in v7:
time: 62.8 us; the launch traced here: 62.6 us
  Pallas kernels  29.4 us (47%)
  starting transfers between devices  19.6 us (31%)
  waiting for transfers between devices  10.3 us (16%)
  local copies, waits for them, and re-layouts  2.21 us (4%)
  other arithmetic  0.72 us (1%)
    ppermute x14, starting transfers between devices, swap(): return lax.ppermute(array, axis, [(i, i ^ step) for i in range(size)])  19.6 us
    ppermute x14, waiting for transfers between devices, swap(): return lax.ppermute(array, axis, [(i, i ^ step) for i in range(size)])  10.3 us
    pallas_call x1, Pallas kernels, last_blocks(): pl.pallas_call(functools.partial(apply_kernel, states, rows, cols, near,...  9.76 us
    pallas_call x1, Pallas kernels, first_blocks(): pl.pallas_call(functools.partial(mix_kernel, states, cols, count), out_sh...  5.66 us
    pallas_call x1, Pallas kernels, prepare(): pl.pallas_call(functools.partial(prepare_kernel, states), out_shape=[jax....  3.41 us
    pallas_call x1, Pallas kernels, first_blocks(): pl.pallas_call(functools.partial(right_kernel, states, rows, cols, near,...  2.81 us
    pallas_call x1, Pallas kernels, pick(): pl.pallas_call(functools.partial(pick_kernel, rows, cols, near), out_shap...  2.74 us
    pallas_call x2, Pallas kernels, place_blocks(): pl.pallas_call(functools.partial(place_kernel, cols, pieces, len(begun)),...  2.62 us
  transfers between devices with their start and end apart: 14, of which 5 were waited for; matrix products, arithmetic and copies ran while one was open for 0% of the time, Pallas kernels for 37%

profile of v7, /device:TPU:0, one launch (start us, length us, event | category | flops | bytes accessed | tf_op | source)
XLA Modules:
  0.0 62.6 jit_solution(513021444088443248)
XLA Ops:
  0.0 0.7 %bitcast_or_fusion.key_ref = s32[16]{0:T(128)S(1)} fusion(s32[16]{0:T(128)} %param.13, s32[16,1]{0,1:T(1,128)} %param.12), kind=kLoop, calls=%fused_computation | loop fusion | flops 32 | bytes 192 | tf_op jit(solution)/shard_map/or | solution.py:438
  0.7 2.4 %collective-permute-start.2 = (s32[16]{0:T(128)S(1)}, s32[16]{0:T(128)S(1)}, u32[]{:S(2)}, u32[]{:S(2)}) collective-permute-start(s32[16]{0:T(128)S(1)} %bitcast_or_fusion.key_ref), channel_id=1, source_target_pairs={{0,12},{4,8},{8,4},{12,0},{1,13},{5,9},{9,5},{13,1},{2,14},{6,10},... | collective-permute-start | bytes 200 | tf_op jit(solution)/shard_map/ppermute | solution.py:20
  3.1 0.6 collective-permute-start.1
  4.4 2.2 %collective-permute-done.1.refs_1_ = s32[16]{0:T(128)S(1)} collective-permute-done((s32[16]{0:T(128)S(1)}, s32[16]{0:T(128)S(1)}, u32[]{:S(2)}, u32[]{:S(2)}) %collective-permute-start.1) | collective-permute-done | bytes 96 | tf_op jit(solution)/shard_map/ppermute | solution.py:20
  6.7 2.4 %route.1 = (bf16[4,64,384]{2,1,0:T(8,128)(2,1)}, bf16[4,64,384]{2,1,0:T(8,128)(2,1)}, bf16[4,64,384]{2,1,0:T(8,128)(2,1)}, bf16[4,64,384]{2,1,0:T(8,128)(2,1)}, s32[16]{0:T(128)}, /*index=5*/s32[16]{0:T(128)}) custom-call(s32[16]{0:T(128)} %left_ref, s32[16]{0:T(128)} %copy-done.5, bf16[8,64,384]{2,1,0:T(8,128)(2,1)} %env_ref.3), custom_call_target="tpu_custom_call" | custom-call | tf_op jit(solution)/shard_map/route/pallas_call | solution.py:77
  9.1 1.6 %collective-permute-start.6 = (bf16[4,64,384]{2,1,0:T(8,128)(2,1)}, bf16[4,64,384]{2,1,0:T(8,128)(2,1)S(1)}, u32[]{:S(2)}, u32[]{:S(2)}) collective-permute-start(bf16[4,64,384]{2,1,0:T(8,128)(2,1)} %get-tuple-element.59), channel_id=1, source_target_pairs={{0,1},{1,0},{2,3},{3,2},{4,5},{5,4},{6,7},{7,6},{8,9},{9,8},{10,11... | collective-permute-start | bytes 589832 | tf_op jit(solution)/shard_map/ppermute | solution.py:20
  10.7 2.6 %collective-permute-start.7 = (bf16[4,64,384]{2,1,0:T(8,128)(2,1)}, bf16[4,64,384]{2,1,0:T(8,128)(2,1)S(1)}, u32[]{:S(2)}, u32[]{:S(2)}) collective-permute-start(bf16[4,64,384]{2,1,0:T(8,128)(2,1)} %get-tuple-element.60), channel_id=1, source_target_pairs={{0,2},{1,3},{2,0},{3,1},{4,6},{5,7},{6,4},{7,5},{8,10},{9,11},{10,... | collective-permute-start | bytes 589832 | tf_op jit(solution)/shard_map/ppermute | solution.py:20
  13.5 2.7 %pick.1 = (bf16[2,64,1536]{2,1,0:T(8,128)(2,1)}, bf16[2,64,1536]{2,1,0:T(8,128)(2,1)}, bf16[2,64,1536]{2,1,0:T(8,128)(2,1)}) custom-call(s32[16]{0:T(128)} %copy-done.11, s32[16]{0:T(128)} %copy-done.10, s32[16]{0:T(128)} %copy-done.9, bf16[8,64,1536]{2,1,0:T(8,128)(2,1)} %env_ref.5), custom_call_target="tpu_custom_call" | custom-call | tf_op jit(solution)/shard_map/pick/pallas_call | solution.py:115
  16.3 0.6 collective-permute-start.4
  16.9 1.6 %copy-done.1 = bf16[16,64,1024]{2,1,0:T(8,128)(2,1)S(1)} copy-done((bf16[16,64,1024]{2,1,0:T(8,128)(2,1)S(1)}, bf16[16,64,1024]{2,1,0:T(8,128)(2,1)}, u32[]{:S(2)}) %copy-start.1) | copy-done | bytes 2097176
  19.1 3.4 %prepare.1 = (bf16[4,128,2048]{2,1,0:T(8,128)(2,1)S(1)}, bf16[384,384]{1,0:T(8,128)(2,1)S(1)}) custom-call(s32[16]{0:T(128)S(1)} %copy-done.3, bf16[16,64,1024]{2,1,0:T(8,128)(2,1)S(1)} %copy-done.1, bf16[24,24,256]{2,1,0:T(8,128)(2,1)S(1)} %copy-done.2), custom_call_target="tpu_custom_call" | custom-call | tf_op jit(solution)/shard_map/prepare/pallas_call | solution.py:258
  22.5 1.6 %collective-permute-start.3 = (bf16[2,64,1536]{2,1,0:T(8,128)(2,1)S(1)}, bf16[2,64,1536]{2,1,0:T(8,128)(2,1)S(1)}, u32[]{:S(2)}, u32[]{:S(2)}) collective-permute-start(bf16[2,64,1536]{2,1,0:T(8,128)(2,1)S(1)} %copy-done.12), channel_id=1, source_target_pairs={{0,4},{4,0},{8,12},{12,8},{1,5},{5,1},{9,13},{13,9},{2,6},{6,2},{1... | collective-permute-start | bytes 1179656 | tf_op jit(solution)/shard_map/ppermute | solution.py:20
  24.1 4.0 %collective-permute-done.7.refs_2_.refs_5_ = bf16[4,64,384]{2,1,0:T(8,128)(2,1)S(1)} collective-permute-done((bf16[4,64,384]{2,1,0:T(8,128)(2,1)}, bf16[4,64,384]{2,1,0:T(8,128)(2,1)S(1)}, u32[]{:S(2)}, u32[]{:S(2)}) %collective-permute-start.7) | collective-permute-done | bytes 196640 | tf_op jit(solution)/shard_map/ppermute | solution.py:20
  28.1 5.7 %mix.1 = (bf16[512,3072]{1,0:T(8,128)(2,1)S(1)}, bf16[512,3072]{1,0:T(8,128)(2,1)S(1)}) custom-call(bf16[4,128,2048]{2,1,0:T(8,128)(2,1)S(1)} %get-tuple-element.56.diag_ref, bf16[384,384]{1,0:T(8,128)(2,1)S(1)} %get-tuple-element.57.mpo_ref, bf16[4,64,384]{2,1,0:T(8,128)(2,1)S(1)} %copy-done.8, ...), custom_call_target="tpu_custom_call" | custom-call | flops 2818572288 | bytes 4194304 | tf_op jit(solution)/shard_map/mix/pallas_call | solution.py:344
  33.9 2.8 %right.1 = (bf16[2,64,256]{2,1,0:T(8,128)(2,1)S(1)}, bf16[2,64,256]{2,1,0:T(8,128)(2,1)S(1)}, bf16[2,64,256]{2,1,0:T(8,128)(2,1)S(1)}, bf16[2,64,256]{2,1,0:T(8,128)(2,1)S(1)}) custom-call(s32[16]{0:T(128)S(1)} %copy-done.4, s32[16]{0:T(128)S(1)} %copy-done.7, s32[16]{0:T(128)S(1)} %copy-done.6, bf16[8,64,1536]{2,1,0:T(8,128)(2,1)S(1)} %copy-done, ...), custom_call_target="tpu_custom_call" | custom-call | flops 402653184 | bytes 4194304 | tf_op jit(solution)/shard_map/right/pallas_call | solution.py:354
  36.7 4.1 %collective-permute-start.9 = (bf16[2,64,256]{2,1,0:T(8,128)(2,1)S(1)}, bf16[2,64,256]{2,1,0:T(8,128)(2,1)S(1)}, u32[]{:S(2)}, u32[]{:S(2)}) collective-permute-start(bf16[2,64,256]{2,1,0:T(8,128)(2,1)S(1)} %get-tuple-element.69), channel_id=1, source_target_pairs={{0,2},{1,3},{2,0},{3,1},{4,6},{5,7},{6,4},{7,5},{8,10},{9,11},{10,... | collective-permute-start | bytes 196616 | tf_op jit(solution)/shard_map/ppermute | solution.py:20
  40.8 1.3 %collective-permute-start.10 = (bf16[2,64,256]{2,1,0:T(8,128)(2,1)S(1)}, bf16[2,64,256]{2,1,0:T(8,128)(2,1)S(1)}, u32[]{:S(2)}, u32[]{:S(2)}) collective-permute-start(bf16[2,64,256]{2,1,0:T(8,128)(2,1)S(1)} %get-tuple-element.70), channel_id=1, source_target_pairs={{0,3},{1,2},{2,1},{3,0},{4,7},{5,6},{6,5},{7,4},{8,11},{9,10},{10,... | collective-permute-start | bytes 196616 | tf_op jit(solution)/shard_map/ppermute | solution.py:20
  42.1 9.8 %apply.1 = (bf16[2,64,256]{2,1,0:T(8,128)(2,1)S(1)}, bf16[4,64,256]{2,1,0:T(8,128)(2,1)S(1)}, bf16[2,64,256]{2,1,0:T(8,128)(2,1)S(1)}, bf16[2,64,256]{2,1,0:T(8,128)(2,1)S(1)}) custom-call(s32[16]{0:T(128)S(1)} %copy-done.4, s32[16]{0:T(128)S(1)} %copy-done.7, s32[16]{0:T(128)S(1)} %copy-done.6, bf16[8,64,1536]{2,1,0:T(8,128)(2,1)S(1)} %copy-done, ...), custom_call_target="tpu_custom_call" | custom-call | flops 3221225472 | bytes 4194304 | tf_op jit(solution)/shard_map/apply/pallas_call | solution.py:381
  52.0 3.0 %collective-permute-start.12 = (bf16[2,64,256]{2,1,0:T(8,128)(2,1)S(1)}, bf16[2,64,256]{2,1,0:T(8,128)(2,1)S(1)}, u32[]{:S(2)}, u32[]{:S(2)}) collective-permute-start(bf16[2,64,256]{2,1,0:T(8,128)(2,1)S(1)} %get-tuple-element.75), channel_id=1, source_target_pairs={{0,2},{1,3},{2,0},{3,1},{4,6},{5,7},{6,4},{7,5},{8,10},{9,11},{10,... | collective-permute-start | bytes 196616 | tf_op jit(solution)/shard_map/ppermute | solution.py:20
  55.0 1.3 %collective-permute-start.13 = (bf16[2,64,256]{2,1,0:T(8,128)(2,1)S(1)}, bf16[2,64,256]{2,1,0:T(8,128)(2,1)S(1)}, u32[]{:S(2)}, u32[]{:S(2)}) collective-permute-start(bf16[2,64,256]{2,1,0:T(8,128)(2,1)S(1)} %get-tuple-element.76), channel_id=1, source_target_pairs={{0,3},{1,2},{2,1},{3,0},{4,7},{5,6},{6,5},{7,4},{8,11},{9,10},{10,... | collective-permute-start | bytes 196616 | tf_op jit(solution)/shard_map/ppermute | solution.py:20
  56.4 1.3 %place.2.refs_0_ = bf16[16,64,256]{2,1,0:T(8,128)(2,1)} custom-call(s32[16]{0:T(128)S(1)} %copy-done.4, bf16[2,64,256]{2,1,0:T(8,128)(2,1)S(1)} %get-tuple-element.64.refs_0_, bf16[2,64,256]{2,1,0:T(8,128)(2,1)S(1)} %collective-permute-done.9.refs_1_, bf16[2,64,256]{2,1,0:T(8,128)(2,1)S(1)} %collective-permute-done.10.refs_2_, ...), custom_call_target="tpu_custom_call" | custom-call | tf_op jit(solution)/shard_map/place/pallas_call | solution.py:415
  57.7 0.8 %collective-permute-done.12.refs_2_ = bf16[2,64,256]{2,1,0:T(8,128)(2,1)S(1)} collective-permute-done((bf16[2,64,256]{2,1,0:T(8,128)(2,1)S(1)}, bf16[2,64,256]{2,1,0:T(8,128)(2,1)S(1)}, u32[]{:S(2)}, u32[]{:S(2)}) %collective-permute-start.12) | collective-permute-done | bytes 65568 | tf_op jit(solution)/shard_map/ppermute | solution.py:20
  58.5 2.6 %collective-permute-done.13.refs_3_ = bf16[2,64,256]{2,1,0:T(8,128)(2,1)S(1)} collective-permute-done((bf16[2,64,256]{2,1,0:T(8,128)(2,1)S(1)}, bf16[2,64,256]{2,1,0:T(8,128)(2,1)S(1)}, u32[]{:S(2)}, u32[]{:S(2)}) %collective-permute-start.13) | collective-permute-done | bytes 65568 | tf_op jit(solution)/shard_map/ppermute | solution.py:20
  61.1 1.3 %place.3 = bf16[16,64,256]{2,1,0:T(8,128)(2,1)} custom-call(s32[16]{0:T(128)S(1)} %copy-done.4, bf16[16,64,256]{2,1,0:T(8,128)(2,1)} %place.2.refs_0_, bf16[4,64,256]{2,1,0:T(8,128)(2,1)S(1)} %collective-permute-done.11.refs_1_, bf16[2,64,256]{2,1,0:T(8,128)(2,1)S(1)} %collective-permute-done.12.refs_2_, ...), custom_call_target="tpu_custom_call", output_to_operand_aliasing={{}: (1, {})} | custom-call | tf_op jit(solution)/shard_map/place/pallas_call | solution.py:415
  (39 shorter events, 1.6 us)
Async XLA Ops:
  0.0 16.9 %copy-start.2 = (bf16[24,24,256]{2,1,0:T(8,128)(2,1)S(1)}, bf16[24,24,256]{2,1,0:T(8,128)(2,1)}, u32[]{:S(2)}) copy-start(bf16[24,24,256]{2,1,0:T(8,128)(2,1)} %mpo_ref) | copy-start | bytes 884740
  0.7 6.0 %copy-start.5 = (s32[16]{0:T(128)}, s32[16]{0:T(128)S(1)}, u32[]{:S(2)}) copy-start(s32[16]{0:T(128)S(1)} %bitcast_or_fusion.key_ref) | copy-start | bytes 196
  0.7 3.7 %collective-permute-start.2 = (s32[16]{0:T(128)S(1)}, s32[16]{0:T(128)S(1)}, u32[]{:S(2)}, u32[]{:S(2)}) collective-permute-start(s32[16]{0:T(128)S(1)} %bitcast_or_fusion.key_ref), channel_id=1, source_target_pairs={{0,12},{4,8},{8,4},{12,0},{1,13},{5,9},{9,5},{13,1},{2,14},{6,10},... | collective-permute-start | bytes 200 | tf_op jit(solution)/shard_map/ppermute | solution.py:20
  3.1 3.5 %collective-permute-start.1 = (s32[16]{0:T(128)S(1)}, s32[16]{0:T(128)S(1)}, u32[]{:S(2)}, u32[]{:S(2)}) collective-permute-start(s32[16]{0:T(128)S(1)} %bitcast_or_fusion.key_ref), channel_id=1, source_target_pairs={{0,8},{4,12},{8,0},{12,4},{1,9},{5,13},{9,1},{13,5},{2,10},{6,14},... | collective-permute-start | bytes 200 | tf_op jit(solution)/shard_map/ppermute | solution.py:20
  3.8 2.9 %collective-permute-start = (s32[16]{0:T(128)S(1)}, s32[16]{0:T(128)S(1)}, u32[]{:S(2)}, u32[]{:S(2)}) collective-permute-start(s32[16]{0:T(128)S(1)} %bitcast_or_fusion.key_ref), channel_id=1, source_target_pairs={{0,4},{4,0},{8,12},{12,8},{1,5},{5,1},{9,13},{13,9},{2,6},{6,2},{1... | collective-permute-start | bytes 200 | tf_op jit(solution)/shard_map/ppermute | solution.py:20
  4.4 9.1 %copy-start.9 = (s32[16]{0:T(128)}, s32[16]{0:T(128)S(1)}, u32[]{:S(2)}) copy-start(s32[16]{0:T(128)S(1)} %collective-permute-done.2.refs_2_) | copy-start | bytes 196
  6.7 6.8 %copy-start.10 = (s32[16]{0:T(128)}, s32[16]{0:T(128)S(1)}, u32[]{:S(2)}) copy-start(s32[16]{0:T(128)S(1)} %collective-permute-done.1.refs_1_) | copy-start | bytes 196
  6.7 6.8 %copy-start.11 = (s32[16]{0:T(128)}, s32[16]{0:T(128)S(1)}, u32[]{:S(2)}) copy-start(s32[16]{0:T(128)S(1)} %collective-permute-done.refs_0_) | copy-start | bytes 196
  9.1 19.0 %copy-start.8 = (bf16[4,64,384]{2,1,0:T(8,128)(2,1)S(1)}, bf16[4,64,384]{2,1,0:T(8,128)(2,1)}, u32[]{:S(2)}) copy-start(bf16[4,64,384]{2,1,0:T(8,128)(2,1)} %get-tuple-element.58.refs_0_.refs_3_) | copy-start | bytes 589828
  9.1 13.4 %collective-permute-start.6 = (bf16[4,64,384]{2,1,0:T(8,128)(2,1)}, bf16[4,64,384]{2,1,0:T(8,128)(2,1)S(1)}, u32[]{:S(2)}, u32[]{:S(2)}) collective-permute-start(bf16[4,64,384]{2,1,0:T(8,128)(2,1)} %get-tuple-element.59), channel_id=1, source_target_pairs={{0,1},{1,0},{2,3},{3,2},{4,5},{5,4},{6,7},{7,6},{8,9},{9,8},{10,11... | collective-permute-start | bytes 589832 | tf_op jit(solution)/shard_map/ppermute | solution.py:20
  10.7 17.4 %collective-permute-start.7 = (bf16[4,64,384]{2,1,0:T(8,128)(2,1)}, bf16[4,64,384]{2,1,0:T(8,128)(2,1)S(1)}, u32[]{:S(2)}, u32[]{:S(2)}) collective-permute-start(bf16[4,64,384]{2,1,0:T(8,128)(2,1)} %get-tuple-element.60), channel_id=1, source_target_pairs={{0,2},{1,3},{2,0},{3,1},{4,6},{5,7},{6,4},{7,5},{8,10},{9,11},{10,... | collective-permute-start | bytes 589832 | tf_op jit(solution)/shard_map/ppermute | solution.py:20
  13.3 14.8 %collective-permute-start.8 = (bf16[4,64,384]{2,1,0:T(8,128)(2,1)}, bf16[4,64,384]{2,1,0:T(8,128)(2,1)S(1)}, u32[]{:S(2)}, u32[]{:S(2)}) collective-permute-start(bf16[4,64,384]{2,1,0:T(8,128)(2,1)} %get-tuple-element.61), channel_id=1, source_target_pairs={{0,3},{1,2},{2,1},{3,0},{4,7},{5,6},{6,5},{7,4},{8,11},{9,10},{10,... | collective-permute-start | bytes 589832 | tf_op jit(solution)/shard_map/ppermute | solution.py:20
  16.3 17.5 %collective-permute-start.4 = (bf16[2,64,1536]{2,1,0:T(8,128)(2,1)}, bf16[2,64,1536]{2,1,0:T(8,128)(2,1)S(1)}, u32[]{:S(2)}, u32[]{:S(2)}) collective-permute-start(bf16[2,64,1536]{2,1,0:T(8,128)(2,1)} %get-tuple-element.54), channel_id=1, source_target_pairs={{0,8},{4,12},{8,0},{12,4},{1,9},{5,13},{9,1},{13,5},{2,10},{6,14},... | collective-permute-start | bytes 1179656 | tf_op jit(solution)/shard_map/ppermute | solution.py:20
  16.9 16.9 %collective-permute-start.5 = (bf16[2,64,1536]{2,1,0:T(8,128)(2,1)}, bf16[2,64,1536]{2,1,0:T(8,128)(2,1)S(1)}, u32[]{:S(2)}, u32[]{:S(2)}) collective-permute-start(bf16[2,64,1536]{2,1,0:T(8,128)(2,1)} %get-tuple-element.55), channel_id=1, source_target_pairs={{0,12},{4,8},{8,4},{12,0},{1,13},{5,9},{9,5},{13,1},{2,14},{6,10},... | collective-permute-start | bytes 1179656 | tf_op jit(solution)/shard_map/ppermute | solution.py:20
  22.5 11.3 %collective-permute-start.3 = (bf16[2,64,1536]{2,1,0:T(8,128)(2,1)S(1)}, bf16[2,64,1536]{2,1,0:T(8,128)(2,1)S(1)}, u32[]{:S(2)}, u32[]{:S(2)}) collective-permute-start(bf16[2,64,1536]{2,1,0:T(8,128)(2,1)S(1)} %copy-done.12), channel_id=1, source_target_pairs={{0,4},{4,0},{8,12},{12,8},{1,5},{5,1},{9,13},{13,9},{2,6},{6,2},{1... | collective-permute-start | bytes 1179656 | tf_op jit(solution)/shard_map/ppermute | solution.py:20
  28.1 5.7 %copy-start = (bf16[8,64,1536]{2,1,0:T(8,128)(2,1)S(1)}, bf16[8,64,1536]{2,1,0:T(8,128)(2,1)}, u32[]{:S(2)}) copy-start(bf16[8,64,1536]{2,1,0:T(8,128)(2,1)} %env_ref.5) | copy-start | bytes 4718596
  28.1 5.7 %copy-start.4 = (s32[16]{0:T(128)S(1)}, s32[16]{0:T(128)}, u32[]{:S(2)}) copy-start(s32[16]{0:T(128)} %get-tuple-element.42.order_ref) | copy-start | bytes 196
  28.1 5.7 %copy-start.6 = (s32[16]{0:T(128)S(1)}, s32[16]{0:T(128)}, u32[]{:S(2)}) copy-start(s32[16]{0:T(128)} %copy-done.5) | copy-start | bytes 196
  28.1 5.7 %copy-start.7 = (s32[16]{0:T(128)S(1)}, s32[16]{0:T(128)}, u32[]{:S(2)}) copy-start(s32[16]{0:T(128)} %get-tuple-element.43.slot_ref) | copy-start | bytes 196
  36.7 15.2 %collective-permute-start.9 = (bf16[2,64,256]{2,1,0:T(8,128)(2,1)S(1)}, bf16[2,64,256]{2,1,0:T(8,128)(2,1)S(1)}, u32[]{:S(2)}, u32[]{:S(2)}) collective-permute-start(bf16[2,64,256]{2,1,0:T(8,128)(2,1)S(1)} %get-tuple-element.69), channel_id=1, source_target_pairs={{0,2},{1,3},{2,0},{3,1},{4,6},{5,7},{6,4},{7,5},{8,10},{9,11},{10,... | collective-permute-start | bytes 196616 | tf_op jit(solution)/shard_map/ppermute | solution.py:20
  40.8 11.1 %collective-permute-start.10 = (bf16[2,64,256]{2,1,0:T(8,128)(2,1)S(1)}, bf16[2,64,256]{2,1,0:T(8,128)(2,1)S(1)}, u32[]{:S(2)}, u32[]{:S(2)}) collective-permute-start(bf16[2,64,256]{2,1,0:T(8,128)(2,1)S(1)} %get-tuple-element.70), channel_id=1, source_target_pairs={{0,3},{1,2},{2,1},{3,0},{4,7},{5,6},{6,5},{7,4},{8,11},{9,10},{10,... | collective-permute-start | bytes 196616 | tf_op jit(solution)/shard_map/ppermute | solution.py:20
  51.9 9.2 %collective-permute-start.11 = (bf16[4,64,256]{2,1,0:T(8,128)(2,1)S(1)}, bf16[4,64,256]{2,1,0:T(8,128)(2,1)S(1)}, u32[]{:S(2)}, u32[]{:S(2)}) collective-permute-start(bf16[4,64,256]{2,1,0:T(8,128)(2,1)S(1)} %get-tuple-element.74), channel_id=1, source_target_pairs={{0,1},{1,0},{2,3},{3,2},{4,5},{5,4},{6,7},{7,6},{8,9},{9,8},{10,11... | collective-permute-start | bytes 393224 | tf_op jit(solution)/shard_map/ppermute | solution.py:20
  52.0 6.5 %collective-permute-start.12 = (bf16[2,64,256]{2,1,0:T(8,128)(2,1)S(1)}, bf16[2,64,256]{2,1,0:T(8,128)(2,1)S(1)}, u32[]{:S(2)}, u32[]{:S(2)}) collective-permute-start(bf16[2,64,256]{2,1,0:T(8,128)(2,1)S(1)} %get-tuple-element.75), channel_id=1, source_target_pairs={{0,2},{1,3},{2,0},{3,1},{4,6},{5,7},{6,4},{7,5},{8,10},{9,11},{10,... | collective-permute-start | bytes 196616 | tf_op jit(solution)/shard_map/ppermute | solution.py:20
  55.0 6.1 %collective-permute-start.13 = (bf16[2,64,256]{2,1,0:T(8,128)(2,1)S(1)}, bf16[2,64,256]{2,1,0:T(8,128)(2,1)S(1)}, u32[]{:S(2)}, u32[]{:S(2)}) collective-permute-start(bf16[2,64,256]{2,1,0:T(8,128)(2,1)S(1)} %get-tuple-element.76), channel_id=1, source_target_pairs={{0,3},{1,2},{2,1},{3,0},{4,7},{5,6},{6,5},{7,4},{8,11},{9,10},{10,... | collective-permute-start | bytes 196616 | tf_op jit(solution)/shard_map/ppermute | solution.py:20
  (3 other events, 5.6 us)

commit v8 on v7

--- a/solution.py
+++ b/solution.py
@@ -7,7 +7,7 @@
 from jax.experimental.pallas import tpu as pltpu
 from jax.sharding import PartitionSpec as P
 
-CHUNK = 8
+CHUNK = 16
 SHIFT = 16
 SMEM = pl.BlockSpec(memory_space=pltpu.SMEM)
 VMEM = pl.BlockSpec(memory_space=pltpu.VMEM)
@@ -269,6 +269,7 @@
             pltpu.SemaphoreType.DMA((steps,)),
         ],
         compiler_params=pltpu.CompilerParams(vmem_limit_bytes=10 << 20),
+        cost_estimate=pl.CostEstimate(flops=0, bytes_accessed=0, transcendentals=0),
         name="prepare",
     )(order, state_blocks, mpo_tensor)
 
@@ -317,13 +318,15 @@
     low = half_mask(env_ref.shape[1])
     at = lax.axis_index("col") * (order_ref.shape[0] // cols) + first
     for k in range(count):
+        spread_left([left.at[first + k] for left in lefts], left_rows.at[k])
+    for k in range(count):
+        mix_block(states, left_rows.at[k], diag_ref.at[first + k], mpo_ref, mixed.at[k])
+    outs[1][:first] = early_ref[...]
+    for k in range(count):
         fetch_right(near, key_ref, order_ref, slot_ref, at + k, env_ref, rights, right_now.at[k])
-    outs[1][:first] = early_ref[...]
-    for k in range(count):
-        spread_left([left.at[first + k] for left in lefts], left_rows.at[k])
+    for k in range(count):
         spread_right(right_now.at[k], right_diag.at[k], low)
     for k in range(count):
-        mix_block(states, left_rows.at[k], diag_ref.at[first + k], mpo_ref, mixed.at[k])
         into = [out.at[first + k if d == 1 else k] for d, out in enumerate(outs)]
         finish_block(states, mixed.at[k], right_diag.at[k], result.at[k], into, low)
 
@@ -437,13 +440,12 @@
 
     keys = jnp.bitwise_or(lax.shift_left(block_owner[:, 0], SHIFT), block_sub)
     others = [swap(keys, "row", step) for step in range(1, rows)]
-    block_left, *others = lax.optimization_barrier((block_left, *others))
     sends, order, slots = route(block_left, keys, left_env, cols, near)
-    lefts = [sends[0]] + [swap(sends[d], "col", d) for d in range(1, cols)]
     picked = pick(others, right_env, cols, near)
-    mpo_tensor, *far = lax.optimization_barrier((mpo_tensor, *picked))
+    near_send, mpo_tensor, *far = lax.optimization_barrier((sends[1], mpo_tensor, *picked))
+    lefts = [sends[0], swap(near_send, "col", 1)] + [swap(sends[d], "col", d) for d in range(2, cols)]
     state_diag, mpo_rows = prepare(order, state_blocks, mpo_tensor, cols, states)
-    core_send, state_diag = lax.optimization_barrier((far[0], state_diag))
+    core_send, state_diag, *lefts[1:] = lax.optimization_barrier((far[0], state_diag, *lefts[1:]))
     rights = [swap(core_send, "row", 1)] + [swap(far[d - 1], "row", d) for d in range(2, rows)]
     early = first_blocks(half, order, slots, keys, state_diag, mpo_rows, right_env, rights, lefts, near)
     came = [swap(early[d], "col", d) for d in range(2, cols)]

time: 62.8 us -> 59 us (0.939)
  starting transfers between devices: 19.6 us -> 17.5 us
  Pallas kernels: 29.4 us -> 27.7 us
  local copies, waits for them, and re-layouts: 2.21 us -> 3.26 us
  waiting for transfers between devices: 10.3 us -> 9.36 us
    ppermute x14, starting transfers between devices: 19.6 us -> 17.5 us  [swap(): return lax.ppermute(array, axis, [(i, i ^ step) for i in range(size)])]
    pallas_call x1, Pallas kernels: 9.76 us -> 8.19 us  [last_blocks(): pl.pallas_call(functools.partial(apply_kernel, states, rows, cols, near,...]
    unnamed x26, local copies, waits for them, and re-layouts: 2.21 us -> 3.26 us
    ppermute x14, waiting for transfers between devices: 10.3 us -> 9.36 us  [swap(): return lax.ppermute(array, axis, [(i, i ^ step) for i in range(size)])]
  transfers between devices with their start and end apart: 14 -> 14, of which waited for: 5 -> 5; matrix products, arithmetic and copies ran while one was open for 0% -> 0% of each run, Pallas kernels for 37% -> 40%
where the time goes in v8:
time: 59 us; the launch traced here: 58.8 us
  Pallas kernels  27.7 us (47%)
  starting transfers between devices  17.5 us (30%)
  waiting for transfers between devices  9.36 us (16%)
  local copies, waits for them, and re-layouts  3.26 us (6%)
  other arithmetic  0.72 us (1%)
    ppermute x14, starting transfers between devices, swap(): return lax.ppermute(array, axis, [(i, i ^ step) for i in range(size)])  17.5 us
    ppermute x14, waiting for transfers between devices, swap(): return lax.ppermute(array, axis, [(i, i ^ step) for i in range(size)])  9.36 us
    pallas_call x1, Pallas kernels, last_blocks(): pl.pallas_call(functools.partial(apply_kernel, states, rows, cols, near,...  8.19 us
    pallas_call x1, Pallas kernels, first_blocks(): pl.pallas_call(functools.partial(mix_kernel, states, cols, count), out_sh...  5.41 us
    pallas_call x1, Pallas kernels, prepare(): pl.pallas_call(functools.partial(prepare_kernel, states), out_shape=[jax....  3.4 us
    unnamed x26, local copies, waits for them, and re-layouts  3.26 us
    pallas_call x1, Pallas kernels, first_blocks(): pl.pallas_call(functools.partial(right_kernel, states, rows, cols, near,...  2.98 us
    pallas_call x1, Pallas kernels, pick(): pl.pallas_call(functools.partial(pick_kernel, rows, cols, near), out_shap...  2.74 us
  transfers between devices with their start and end apart: 14, of which 5 were waited for; matrix products, arithmetic and copies ran while one was open for 0% of the time, Pallas kernels for 40%

profile of v8, /device:TPU:0, one launch (start us, length us, event | category | flops | bytes accessed | tf_op | source)
XLA Modules:
  0.0 58.8 jit_solution(13402845979324482402)
XLA Ops:
  0.0 0.7 %bitcast_or_fusion.key_ref = s32[16]{0:T(128)S(1)} fusion(s32[16]{0:T(128)} %param.13, s32[16,1]{0,1:T(1,128)} %param.12), kind=kLoop, calls=%fused_computation | loop fusion | flops 32 | bytes 192 | tf_op jit(solution)/shard_map/or | solution.py:441
  0.7 2.4 %collective-permute-start.2 = (s32[16]{0:T(128)S(1)}, s32[16]{0:T(128)S(1)}, u32[]{:S(2)}, u32[]{:S(2)}) collective-permute-start(s32[16]{0:T(128)S(1)} %bitcast_or_fusion.key_ref), channel_id=1, source_target_pairs={{0,12},{4,8},{8,4},{12,0},{1,13},{5,9},{9,5},{13,1},{2,14},{6,10},... | collective-permute-start | bytes 200 | tf_op jit(solution)/shard_map/ppermute | solution.py:20
  3.1 0.6 %collective-permute-start.1 = (s32[16]{0:T(128)S(1)}, s32[16]{0:T(128)S(1)}, u32[]{:S(2)}, u32[]{:S(2)}) collective-permute-start(s32[16]{0:T(128)S(1)} %bitcast_or_fusion.key_ref), channel_id=1, source_target_pairs={{0,8},{4,12},{8,0},{12,4},{1,9},{5,13},{9,1},{13,5},{2,10},{6,14},... | collective-permute-start | bytes 200 | tf_op jit(solution)/shard_map/ppermute | solution.py:20
  3.8 2.3 %route.1 = (bf16[4,64,384]{2,1,0:T(8,128)(2,1)}, bf16[4,64,384]{2,1,0:T(8,128)(2,1)}, bf16[4,64,384]{2,1,0:T(8,128)(2,1)}, bf16[4,64,384]{2,1,0:T(8,128)(2,1)}, s32[16]{0:T(128)}, /*index=5*/s32[16]{0:T(128)}) custom-call(s32[16]{0:T(128)} %left_ref.1, s32[16]{0:T(128)} %copy-done.5, bf16[8,64,384]{2,1,0:T(8,128)(2,1)} %env_ref.3), custom_call_target="tpu_custom_call" | custom-call | tf_op jit(solution)/shard_map/route/pallas_call | solution.py:77
  6.2 2.9 %collective-permute-start.4 = (bf16[4,64,384]{2,1,0:T(8,128)(2,1)}, bf16[4,64,384]{2,1,0:T(8,128)(2,1)S(1)}, u32[]{:S(2)}, u32[]{:S(2)}) collective-permute-start(bf16[4,64,384]{2,1,0:T(8,128)(2,1)} %get-tuple-element.51), channel_id=1, source_target_pairs={{0,2},{1,3},{2,0},{3,1},{4,6},{5,7},{6,4},{7,5},{8,10},{9,11},{10,... | collective-permute-start | bytes 589832 | tf_op jit(solution)/shard_map/ppermute | solution.py:20
  9.1 1.3 %collective-permute-start.5 = (bf16[4,64,384]{2,1,0:T(8,128)(2,1)}, bf16[4,64,384]{2,1,0:T(8,128)(2,1)S(1)}, u32[]{:S(2)}, u32[]{:S(2)}) collective-permute-start(bf16[4,64,384]{2,1,0:T(8,128)(2,1)} %get-tuple-element.52), channel_id=1, source_target_pairs={{0,3},{1,2},{2,1},{3,0},{4,7},{5,6},{6,5},{7,4},{8,11},{9,10},{10,... | collective-permute-start | bytes 589832 | tf_op jit(solution)/shard_map/ppermute | solution.py:20
  10.9 0.6 copy-done.11
  11.5 2.7 %pick.1 = (bf16[2,64,1536]{2,1,0:T(8,128)(2,1)}, bf16[2,64,1536]{2,1,0:T(8,128)(2,1)}, bf16[2,64,1536]{2,1,0:T(8,128)(2,1)}) custom-call(s32[16]{0:T(128)} %copy-done.11, s32[16]{0:T(128)} %copy-done.10, s32[16]{0:T(128)} %copy-done.9, bf16[8,64,1536]{2,1,0:T(8,128)(2,1)} %env_ref.5), custom_call_target="tpu_custom_call" | custom-call | tf_op jit(solution)/shard_map/pick/pallas_call | solution.py:115
  14.5 1.5 %collective-permute-start.7 = (bf16[2,64,1536]{2,1,0:T(8,128)(2,1)}, bf16[2,64,1536]{2,1,0:T(8,128)(2,1)S(1)}, u32[]{:S(2)}, u32[]{:S(2)}) collective-permute-start(bf16[2,64,1536]{2,1,0:T(8,128)(2,1)} %get-tuple-element.54), channel_id=1, source_target_pairs={{0,8},{4,12},{8,0},{12,4},{1,9},{5,13},{9,1},{13,5},{2,10},{6,14},... | collective-permute-start | bytes 1179656 | tf_op jit(solution)/shard_map/ppermute | solution.py:20
  16.0 1.6 %copy-done.1 = bf16[16,64,1024]{2,1,0:T(8,128)(2,1)S(1)} copy-done((bf16[16,64,1024]{2,1,0:T(8,128)(2,1)S(1)}, bf16[16,64,1024]{2,1,0:T(8,128)(2,1)}, u32[]{:S(2)}) %copy-start.1) | copy-done | bytes 2097176
  17.6 0.6 copy-done.3
  18.2 3.4 %prepare.1 = (bf16[4,128,2048]{2,1,0:T(8,128)(2,1)S(1)}, bf16[384,384]{1,0:T(8,128)(2,1)S(1)}) custom-call(s32[16]{0:T(128)S(1)} %copy-done.3, bf16[16,64,1024]{2,1,0:T(8,128)(2,1)S(1)} %copy-done.1, bf16[24,24,256]{2,1,0:T(8,128)(2,1)S(1)} %copy-done.2), custom_call_target="tpu_custom_call" | custom-call | tf_op jit(solution)/shard_map/prepare/pallas_call | solution.py:258
  21.6 1.9 %collective-permute-done.4.refs_2_.refs_5_ = bf16[4,64,384]{2,1,0:T(8,128)(2,1)S(1)} collective-permute-done((bf16[4,64,384]{2,1,0:T(8,128)(2,1)}, bf16[4,64,384]{2,1,0:T(8,128)(2,1)S(1)}, u32[]{:S(2)}, u32[]{:S(2)}) %collective-permute-start.4) | collective-permute-done | bytes 196640 | tf_op jit(solution)/shard_map/ppermute | solution.py:20
  23.5 3.7 %collective-permute-done.3.refs_1_.refs_4_ = bf16[4,64,384]{2,1,0:T(8,128)(2,1)S(1)} collective-permute-done((bf16[4,64,384]{2,1,0:T(8,128)(2,1)}, bf16[4,64,384]{2,1,0:T(8,128)(2,1)S(1)}, u32[]{:S(2)}, u32[]{:S(2)}) %collective-permute-start.3) | collective-permute-done | bytes 196640 | tf_op jit(solution)/shard_map/ppermute | solution.py:20
  27.3 5.4 %mix.1 = (bf16[512,3072]{1,0:T(8,128)(2,1)S(1)}, bf16[512,3072]{1,0:T(8,128)(2,1)S(1)}) custom-call(bf16[4,128,2048]{2,1,0:T(8,128)(2,1)S(1)} %get-tuple-element.56.diag_ref, bf16[384,384]{1,0:T(8,128)(2,1)S(1)} %get-tuple-element.57.mpo_ref, bf16[4,64,384]{2,1,0:T(8,128)(2,1)S(1)} %copy-done.8, ...), custom_call_target="tpu_custom_call" | custom-call | flops 2818572288 | bytes 4194304 | tf_op jit(solution)/shard_map/mix/pallas_call | solution.py:347
  32.9 3.0 %right.1 = (bf16[2,64,256]{2,1,0:T(8,128)(2,1)S(1)}, bf16[2,64,256]{2,1,0:T(8,128)(2,1)S(1)}, bf16[2,64,256]{2,1,0:T(8,128)(2,1)S(1)}, bf16[2,64,256]{2,1,0:T(8,128)(2,1)S(1)}) custom-call(s32[16]{0:T(128)S(1)} %copy-done.4, s32[16]{0:T(128)S(1)} %copy-done.7, s32[16]{0:T(128)S(1)} %copy-done.6, bf16[8,64,1536]{2,1,0:T(8,128)(2,1)S(1)} %copy-done, ...), custom_call_target="tpu_custom_call" | custom-call | flops 402653184 | bytes 4194304 | tf_op jit(solution)/shard_map/right/pallas_call | solution.py:357
  35.8 2.6 %collective-permute-start.9 = (bf16[2,64,256]{2,1,0:T(8,128)(2,1)S(1)}, bf16[2,64,256]{2,1,0:T(8,128)(2,1)S(1)}, u32[]{:S(2)}, u32[]{:S(2)}) collective-permute-start(bf16[2,64,256]{2,1,0:T(8,128)(2,1)S(1)} %get-tuple-element.69), channel_id=1, source_target_pairs={{0,2},{1,3},{2,0},{3,1},{4,6},{5,7},{6,4},{7,5},{8,10},{9,11},{10,... | collective-permute-start | bytes 196616 | tf_op jit(solution)/shard_map/ppermute | solution.py:20
  38.5 1.3 %collective-permute-start.10 = (bf16[2,64,256]{2,1,0:T(8,128)(2,1)S(1)}, bf16[2,64,256]{2,1,0:T(8,128)(2,1)S(1)}, u32[]{:S(2)}, u32[]{:S(2)}) collective-permute-start(bf16[2,64,256]{2,1,0:T(8,128)(2,1)S(1)} %get-tuple-element.70), channel_id=1, source_target_pairs={{0,3},{1,2},{2,1},{3,0},{4,7},{5,6},{6,5},{7,4},{8,11},{9,10},{10,... | collective-permute-start | bytes 196616 | tf_op jit(solution)/shard_map/ppermute | solution.py:20
  39.8 8.2 %apply.1 = (bf16[2,64,256]{2,1,0:T(8,128)(2,1)S(1)}, bf16[4,64,256]{2,1,0:T(8,128)(2,1)S(1)}, bf16[2,64,256]{2,1,0:T(8,128)(2,1)S(1)}, bf16[2,64,256]{2,1,0:T(8,128)(2,1)S(1)}) custom-call(s32[16]{0:T(128)S(1)} %copy-done.4, s32[16]{0:T(128)S(1)} %copy-done.7, s32[16]{0:T(128)S(1)} %copy-done.6, bf16[8,64,1536]{2,1,0:T(8,128)(2,1)S(1)} %copy-done, ...), custom_call_target="tpu_custom_call" | custom-call | flops 3221225472 | bytes 4194304 | tf_op jit(solution)/shard_map/apply/pallas_call | solution.py:384
  48.2 3.0 %collective-permute-start.12 = (bf16[2,64,256]{2,1,0:T(8,128)(2,1)S(1)}, bf16[2,64,256]{2,1,0:T(8,128)(2,1)S(1)}, u32[]{:S(2)}, u32[]{:S(2)}) collective-permute-start(bf16[2,64,256]{2,1,0:T(8,128)(2,1)S(1)} %get-tuple-element.75), channel_id=1, source_target_pairs={{0,2},{1,3},{2,0},{3,1},{4,6},{5,7},{6,4},{7,5},{8,10},{9,11},{10,... | collective-permute-start | bytes 196616 | tf_op jit(solution)/shard_map/ppermute | solution.py:20
  51.2 1.3 %collective-permute-start.13 = (bf16[2,64,256]{2,1,0:T(8,128)(2,1)S(1)}, bf16[2,64,256]{2,1,0:T(8,128)(2,1)S(1)}, u32[]{:S(2)}, u32[]{:S(2)}) collective-permute-start(bf16[2,64,256]{2,1,0:T(8,128)(2,1)S(1)} %get-tuple-element.76), channel_id=1, source_target_pairs={{0,3},{1,2},{2,1},{3,0},{4,7},{5,6},{6,5},{7,4},{8,11},{9,10},{10,... | collective-permute-start | bytes 196616 | tf_op jit(solution)/shard_map/ppermute | solution.py:20
  52.5 1.3 %place.2.refs_0_ = bf16[16,64,256]{2,1,0:T(8,128)(2,1)} custom-call(s32[16]{0:T(128)S(1)} %copy-done.4, bf16[2,64,256]{2,1,0:T(8,128)(2,1)S(1)} %get-tuple-element.64.refs_0_, bf16[2,64,256]{2,1,0:T(8,128)(2,1)S(1)} %collective-permute-done.9.refs_1_, bf16[2,64,256]{2,1,0:T(8,128)(2,1)S(1)} %collective-permute-done.10.refs_2_, ...), custom_call_target="tpu_custom_call" | custom-call | tf_op jit(solution)/shard_map/place/pallas_call | solution.py:418
  54.0 3.4 %collective-permute-done.13.refs_3_ = bf16[2,64,256]{2,1,0:T(8,128)(2,1)S(1)} collective-permute-done((bf16[2,64,256]{2,1,0:T(8,128)(2,1)S(1)}, bf16[2,64,256]{2,1,0:T(8,128)(2,1)S(1)}, u32[]{:S(2)}, u32[]{:S(2)}) %collective-permute-start.13) | collective-permute-done | bytes 65568 | tf_op jit(solution)/shard_map/ppermute | solution.py:20
  57.4 1.3 %place.3 = bf16[16,64,256]{2,1,0:T(8,128)(2,1)} custom-call(s32[16]{0:T(128)S(1)} %copy-done.4, bf16[16,64,256]{2,1,0:T(8,128)(2,1)} %place.2.refs_0_, bf16[4,64,256]{2,1,0:T(8,128)(2,1)S(1)} %collective-permute-done.11.refs_1_, bf16[2,64,256]{2,1,0:T(8,128)(2,1)S(1)} %collective-permute-done.12.refs_2_, ...), custom_call_target="tpu_custom_call", output_to_operand_aliasing={{}: (1, {})} | custom-call | tf_op jit(solution)/shard_map/place/pallas_call | solution.py:418
  (39 shorter events, 1.3 us)
Async XLA Ops:
  0.0 16.0 %copy-start.2 = (bf16[24,24,256]{2,1,0:T(8,128)(2,1)S(1)}, bf16[24,24,256]{2,1,0:T(8,128)(2,1)}, u32[]{:S(2)}) copy-start(bf16[24,24,256]{2,1,0:T(8,128)(2,1)} %mpo_ref) | copy-start | bytes 884740
  0.7 3.1 %copy-start.5 = (s32[16]{0:T(128)}, s32[16]{0:T(128)S(1)}, u32[]{:S(2)}) copy-start(s32[16]{0:T(128)S(1)} %bitcast_or_fusion.key_ref) | copy-start | bytes 196
  0.7 9.7 %collective-permute-start.2 = (s32[16]{0:T(128)S(1)}, s32[16]{0:T(128)S(1)}, u32[]{:S(2)}, u32[]{:S(2)}) collective-permute-start(s32[16]{0:T(128)S(1)} %bitcast_or_fusion.key_ref), channel_id=1, source_target_pairs={{0,12},{4,8},{8,4},{12,0},{1,13},{5,9},{9,5},{13,1},{2,14},{6,10},... | collective-permute-start | bytes 200 | tf_op jit(solution)/shard_map/ppermute | solution.py:20
  3.1 7.3 %collective-permute-start.1 = (s32[16]{0:T(128)S(1)}, s32[16]{0:T(128)S(1)}, u32[]{:S(2)}, u32[]{:S(2)}) collective-permute-start(s32[16]{0:T(128)S(1)} %bitcast_or_fusion.key_ref), channel_id=1, source_target_pairs={{0,8},{4,12},{8,0},{12,4},{1,9},{5,13},{9,1},{13,5},{2,10},{6,14},... | collective-permute-start | bytes 200 | tf_op jit(solution)/shard_map/ppermute | solution.py:20
  3.8 6.7 %collective-permute-start = (s32[16]{0:T(128)S(1)}, s32[16]{0:T(128)S(1)}, u32[]{:S(2)}, u32[]{:S(2)}) collective-permute-start(s32[16]{0:T(128)S(1)} %bitcast_or_fusion.key_ref), channel_id=1, source_target_pairs={{0,4},{4,0},{8,12},{12,8},{1,5},{5,1},{9,13},{13,9},{2,6},{6,2},{1... | collective-permute-start | bytes 200 | tf_op jit(solution)/shard_map/ppermute | solution.py:20
  6.2 21.1 %copy-start.8 = (bf16[4,64,384]{2,1,0:T(8,128)(2,1)S(1)}, bf16[4,64,384]{2,1,0:T(8,128)(2,1)}, u32[]{:S(2)}) copy-start(bf16[4,64,384]{2,1,0:T(8,128)(2,1)} %get-tuple-element.58.refs_0_.refs_3_) | copy-start | bytes 589828
  6.2 17.3 %collective-permute-start.4 = (bf16[4,64,384]{2,1,0:T(8,128)(2,1)}, bf16[4,64,384]{2,1,0:T(8,128)(2,1)S(1)}, u32[]{:S(2)}, u32[]{:S(2)}) collective-permute-start(bf16[4,64,384]{2,1,0:T(8,128)(2,1)} %get-tuple-element.51), channel_id=1, source_target_pairs={{0,2},{1,3},{2,0},{3,1},{4,6},{5,7},{6,4},{7,5},{8,10},{9,11},{10,... | collective-permute-start | bytes 589832 | tf_op jit(solution)/shard_map/ppermute | solution.py:20
  9.1 14.5 %collective-permute-start.5 = (bf16[4,64,384]{2,1,0:T(8,128)(2,1)}, bf16[4,64,384]{2,1,0:T(8,128)(2,1)S(1)}, u32[]{:S(2)}, u32[]{:S(2)}) collective-permute-start(bf16[4,64,384]{2,1,0:T(8,128)(2,1)} %get-tuple-element.52), channel_id=1, source_target_pairs={{0,3},{1,2},{2,1},{3,0},{4,7},{5,6},{6,5},{7,4},{8,11},{9,10},{10,... | collective-permute-start | bytes 589832 | tf_op jit(solution)/shard_map/ppermute | solution.py:20
  14.2 13.0 %collective-permute-start.3 = (bf16[4,64,384]{2,1,0:T(8,128)(2,1)}, bf16[4,64,384]{2,1,0:T(8,128)(2,1)S(1)}, u32[]{:S(2)}, u32[]{:S(2)}) collective-permute-start(bf16[4,64,384]{2,1,0:T(8,128)(2,1)} %get-tuple-element.50), channel_id=1, source_target_pairs={{0,1},{1,0},{2,3},{3,2},{4,5},{5,4},{6,7},{7,6},{8,9},{9,8},{10,11... | collective-permute-start | bytes 589832 | tf_op jit(solution)/shard_map/ppermute | solution.py:20
  14.5 18.2 %collective-permute-start.7 = (bf16[2,64,1536]{2,1,0:T(8,128)(2,1)}, bf16[2,64,1536]{2,1,0:T(8,128)(2,1)S(1)}, u32[]{:S(2)}, u32[]{:S(2)}) collective-permute-start(bf16[2,64,1536]{2,1,0:T(8,128)(2,1)} %get-tuple-element.54), channel_id=1, source_target_pairs={{0,8},{4,12},{8,0},{12,4},{1,9},{5,13},{9,1},{13,5},{2,10},{6,14},... | collective-permute-start | bytes 1179656 | tf_op jit(solution)/shard_map/ppermute | solution.py:20
  16.0 16.8 %collective-permute-start.8 = (bf16[2,64,1536]{2,1,0:T(8,128)(2,1)}, bf16[2,64,1536]{2,1,0:T(8,128)(2,1)S(1)}, u32[]{:S(2)}, u32[]{:S(2)}) collective-permute-start(bf16[2,64,1536]{2,1,0:T(8,128)(2,1)} %get-tuple-element.55), channel_id=1, source_target_pairs={{0,12},{4,8},{8,4},{12,0},{1,13},{5,9},{9,5},{13,1},{2,14},{6,10},... | collective-permute-start | bytes 1179656 | tf_op jit(solution)/shard_map/ppermute | solution.py:20
  16.0 1.6 %copy-start.1 = (bf16[16,64,1024]{2,1,0:T(8,128)(2,1)S(1)}, bf16[16,64,1024]{2,1,0:T(8,128)(2,1)}, u32[]{:S(2)}) copy-start(bf16[16,64,1024]{2,1,0:T(8,128)(2,1)} %state_ref.1) | copy-start | bytes 6291460
  17.6 0.6 copy-start.3
  18.2 9.1 %copy-start.12 = (bf16[2,64,1536]{2,1,0:T(8,128)(2,1)S(1)}, bf16[2,64,1536]{2,1,0:T(8,128)(2,1)}, u32[]{:S(2)}) copy-start(bf16[2,64,1536]{2,1,0:T(8,128)(2,1)} %get-tuple-element.53) | copy-start | bytes 1179652
  27.3 5.6 %collective-permute-start.6 = (bf16[2,64,1536]{2,1,0:T(8,128)(2,1)S(1)}, bf16[2,64,1536]{2,1,0:T(8,128)(2,1)S(1)}, u32[]{:S(2)}, u32[]{:S(2)}) collective-permute-start(bf16[2,64,1536]{2,1,0:T(8,128)(2,1)S(1)} %copy-done.12), channel_id=1, source_target_pairs={{0,4},{4,0},{8,12},{12,8},{1,5},{5,1},{9,13},{13,9},{2,6},{6,2},{1... | collective-permute-start | bytes 1179656 | tf_op jit(solution)/shard_map/ppermute | solution.py:20
  27.3 5.6 %copy-start = (bf16[8,64,1536]{2,1,0:T(8,128)(2,1)S(1)}, bf16[8,64,1536]{2,1,0:T(8,128)(2,1)}, u32[]{:S(2)}) copy-start(bf16[8,64,1536]{2,1,0:T(8,128)(2,1)} %env_ref.5) | copy-start | bytes 4718596
  27.3 5.6 %copy-start.4 = (s32[16]{0:T(128)S(1)}, s32[16]{0:T(128)}, u32[]{:S(2)}) copy-start(s32[16]{0:T(128)} %get-tuple-element.41.order_ref) | copy-start | bytes 196
  27.3 5.6 %copy-start.6 = (s32[16]{0:T(128)S(1)}, s32[16]{0:T(128)}, u32[]{:S(2)}) copy-start(s32[16]{0:T(128)} %copy-done.5) | copy-start | bytes 196
  27.3 5.6 %copy-start.7 = (s32[16]{0:T(128)S(1)}, s32[16]{0:T(128)}, u32[]{:S(2)}) copy-start(s32[16]{0:T(128)} %get-tuple-element.42.slot_ref) | copy-start | bytes 196
  35.8 12.2 %collective-permute-start.9 = (bf16[2,64,256]{2,1,0:T(8,128)(2,1)S(1)}, bf16[2,64,256]{2,1,0:T(8,128)(2,1)S(1)}, u32[]{:S(2)}, u32[]{:S(2)}) collective-permute-start(bf16[2,64,256]{2,1,0:T(8,128)(2,1)S(1)} %get-tuple-element.69), channel_id=1, source_target_pairs={{0,2},{1,3},{2,0},{3,1},{4,6},{5,7},{6,4},{7,5},{8,10},{9,11},{10,... | collective-permute-start | bytes 196616 | tf_op jit(solution)/shard_map/ppermute | solution.py:20
  38.5 9.5 %collective-permute-start.10 = (bf16[2,64,256]{2,1,0:T(8,128)(2,1)S(1)}, bf16[2,64,256]{2,1,0:T(8,128)(2,1)S(1)}, u32[]{:S(2)}, u32[]{:S(2)}) collective-permute-start(bf16[2,64,256]{2,1,0:T(8,128)(2,1)S(1)} %get-tuple-element.70), channel_id=1, source_target_pairs={{0,3},{1,2},{2,1},{3,0},{4,7},{5,6},{6,5},{7,4},{8,11},{9,10},{10,... | collective-permute-start | bytes 196616 | tf_op jit(solution)/shard_map/ppermute | solution.py:20
  48.0 9.3 %collective-permute-start.11 = (bf16[4,64,256]{2,1,0:T(8,128)(2,1)S(1)}, bf16[4,64,256]{2,1,0:T(8,128)(2,1)S(1)}, u32[]{:S(2)}, u32[]{:S(2)}) collective-permute-start(bf16[4,64,256]{2,1,0:T(8,128)(2,1)S(1)} %get-tuple-element.74), channel_id=1, source_target_pairs={{0,1},{1,0},{2,3},{3,2},{4,5},{5,4},{6,7},{7,6},{8,9},{9,8},{10,11... | collective-permute-start | bytes 393224 | tf_op jit(solution)/shard_map/ppermute | solution.py:20
  48.2 5.8 %collective-permute-start.12 = (bf16[2,64,256]{2,1,0:T(8,128)(2,1)S(1)}, bf16[2,64,256]{2,1,0:T(8,128)(2,1)S(1)}, u32[]{:S(2)}, u32[]{:S(2)}) collective-permute-start(bf16[2,64,256]{2,1,0:T(8,128)(2,1)S(1)} %get-tuple-element.75), channel_id=1, source_target_pairs={{0,2},{1,3},{2,0},{3,1},{4,6},{5,7},{6,4},{7,5},{8,10},{9,11},{10,... | collective-permute-start | bytes 196616 | tf_op jit(solution)/shard_map/ppermute | solution.py:20
  51.2 6.2 %collective-permute-start.13 = (bf16[2,64,256]{2,1,0:T(8,128)(2,1)S(1)}, bf16[2,64,256]{2,1,0:T(8,128)(2,1)S(1)}, u32[]{:S(2)}, u32[]{:S(2)}) collective-permute-start(bf16[2,64,256]{2,1,0:T(8,128)(2,1)S(1)} %get-tuple-element.76), channel_id=1, source_target_pairs={{0,3},{1,2},{2,1},{3,0},{4,7},{5,6},{6,5},{7,4},{8,11},{9,10},{10,... | collective-permute-start | bytes 196616 | tf_op jit(solution)/shard_map/ppermute | solution.py:20
  (3 other events, 1.6 us)

commit v9 on v8

--- a/solution.py
+++ b/solution.py
@@ -343,7 +343,7 @@
     width = share // size * cols
     states = mpo_rows.shape[0] // width
     half, lanes = size // 2, 2 * size
-    params = pltpu.CompilerParams(vmem_limit_bytes=24 << 20)
+    params = pltpu.CompilerParams(vmem_limit_bytes=32 << 20)
     mixed = pl.pallas_call(
         functools.partial(mix_kernel, states, cols, count),
         out_shape=[jax.ShapeDtypeStruct((half * states, width * lanes), jnp.bfloat16)] * count,
@@ -393,7 +393,7 @@
             pltpu.VMEM((count, width * lanes, lanes), jnp.bfloat16),
             pltpu.VMEM((count, half * states, lanes), jnp.float32),
         ],
-        compiler_params=pltpu.CompilerParams(vmem_limit_bytes=24 << 20),
+        compiler_params=pltpu.CompilerParams(vmem_limit_bytes=32 << 20),
         cost_estimate=cost_of(count, states, width, size, 1, 1),
         name="apply",
     )(order, slots, keys, right_env, state_diag, mpo_rows, early, *rights, *lefts)
@@ -436,14 +436,16 @@
     most = max(2, (2 * count + rows - 1) // rows)
     near = -(-most // cols)
 
-    half = count // cols // 2
+    half = count // cols - max(1, count // cols // 4)
 
     keys = jnp.bitwise_or(lax.shift_left(block_owner[:, 0], SHIFT), block_sub)
     others = [swap(keys, "row", step) for step in range(1, rows)]
     sends, order, slots = route(block_left, keys, left_env, cols, near)
     picked = pick(others, right_env, cols, near)
-    near_send, mpo_tensor, *far = lax.optimization_barrier((sends[1], mpo_tensor, *picked))
-    lefts = [sends[0], swap(near_send, "col", 1)] + [swap(sends[d], "col", d) for d in range(2, cols)]
+    rest = list(range(3, cols))
+    mpo_tensor, *held = lax.optimization_barrier((mpo_tensor, *picked, *[sends[d] for d in rest]))
+    far, sent = held[: rows - 1], dict(zip(rest, held[rows - 1 :]))
+    lefts = [sends[0]] + [swap(sent.get(d, sends[d]), "col", d) for d in range(1, cols)]
     state_diag, mpo_rows = prepare(order, state_blocks, mpo_tensor, cols, states)
     core_send, state_diag, *lefts[1:] = lax.optimization_barrier((far[0], state_diag, *lefts[1:]))
     rights = [swap(core_send, "row", 1)] + [swap(far[d - 1], "row", d) for d in range(2, rows)]

time: 59 us -> 60.2 us (1.020)
  starting transfers between devices: 17.5 us -> 20.9 us
  waiting for transfers between devices: 9.36 us -> 6.42 us
  local copies, waits for them, and re-layouts: 3.26 us -> 4.21 us
    pallas_call x1, Pallas kernels: 8.19 us -> 4.51 us  [last_blocks(): pl.pallas_call(functools.partial(apply_kernel, states, rows, cols, near,...]
    ppermute x14, starting transfers between devices: 17.5 us -> 20.9 us  [swap(): return lax.ppermute(array, axis, [(i, i ^ step) for i in range(size)])]
    ppermute x14, waiting for transfers between devices: 9.36 us -> 6.42 us  [swap(): return lax.ppermute(array, axis, [(i, i ^ step) for i in range(size)])]
    pallas_call x1, Pallas kernels: 5.41 us -> 7.86 us  [first_blocks(): pl.pallas_call(functools.partial(mix_kernel, states, cols, count), out_sh...]
    unnamed x26 -> x24, local copies, waits for them, and re-layouts: 3.26 us -> 4.21 us
    pallas_call x1, Pallas kernels: 2.98 us -> 3.92 us  [first_blocks(): pl.pallas_call(functools.partial(right_kernel, states, rows, cols, near,...]
  transfers between devices with their start and end apart: 14 -> 14, of which waited for: 5 -> 5; matrix products, arithmetic and copies ran while one was open for 0% -> 0% of each run, Pallas kernels for 40% -> 37%
where the time goes in v9:
time: 60.2 us; the launch traced here: 59.9 us
  Pallas kernels  27.4 us (46%)
  starting transfers between devices  20.9 us (35%)
  waiting for transfers between devices  6.42 us (11%)
  local copies, waits for them, and re-layouts  4.21 us (7%)
  other arithmetic  0.67 us (1%)
    ppermute x14, starting transfers between devices, swap(): return lax.ppermute(array, axis, [(i, i ^ step) for i in range(size)])  20.9 us
    pallas_call x1, Pallas kernels, first_blocks(): pl.pallas_call(functools.partial(mix_kernel, states, cols, count), out_sh...  7.86 us
    ppermute x14, waiting for transfers between devices, swap(): return lax.ppermute(array, axis, [(i, i ^ step) for i in range(size)])  6.42 us
    pallas_call x1, Pallas kernels, last_blocks(): pl.pallas_call(functools.partial(apply_kernel, states, rows, cols, near,...  4.51 us
    unnamed x24, local copies, waits for them, and re-layouts  4.21 us
    pallas_call x1, Pallas kernels, first_blocks(): pl.pallas_call(functools.partial(right_kernel, states, rows, cols, near,...  3.92 us
    pallas_call x1, Pallas kernels, prepare(): pl.pallas_call(functools.partial(prepare_kernel, states), out_shape=[jax....  3.4 us
    pallas_call x1, Pallas kernels, pick(): pl.pallas_call(functools.partial(pick_kernel, rows, cols, near), out_shap...  2.73 us
  transfers between devices with their start and end apart: 14, of which 5 were waited for; matrix products, arithmetic and copies ran while one was open for 0% of the time, Pallas kernels for 37%

profile of v9, /device:TPU:0, one launch (start us, length us, event | category | flops | bytes accessed | tf_op | source)
XLA Modules:
  0.0 59.9 jit_solution(15942452839384460772)
XLA Ops:
  0.0 0.7 %bitcast_or_fusion.key_ref = s32[16]{0:T(128)S(1)} fusion(s32[16]{0:T(128)} %param.13, s32[16,1]{0,1:T(1,128)} %param.12), kind=kLoop, calls=%fused_computation | loop fusion | flops 32 | bytes 192 | tf_op jit(solution)/shard_map/or | solution.py:441
  0.7 2.4 %collective-permute-start.2 = (s32[16]{0:T(128)S(1)}, s32[16]{0:T(128)S(1)}, u32[]{:S(2)}, u32[]{:S(2)}) collective-permute-start(s32[16]{0:T(128)S(1)} %bitcast_or_fusion.key_ref), channel_id=1, source_target_pairs={{0,12},{4,8},{8,4},{12,0},{1,13},{5,9},{9,5},{13,1},{2,14},{6,10},... | collective-permute-start | bytes 200 | tf_op jit(solution)/shard_map/ppermute | solution.py:20
  3.1 0.6 %collective-permute-start.1 = (s32[16]{0:T(128)S(1)}, s32[16]{0:T(128)S(1)}, u32[]{:S(2)}, u32[]{:S(2)}) collective-permute-start(s32[16]{0:T(128)S(1)} %bitcast_or_fusion.key_ref), channel_id=1, source_target_pairs={{0,8},{4,12},{8,0},{12,4},{1,9},{5,13},{9,1},{13,5},{2,10},{6,14},... | collective-permute-start | bytes 200 | tf_op jit(solution)/shard_map/ppermute | solution.py:20
  3.8 2.3 %route.1 = (bf16[4,64,384]{2,1,0:T(8,128)(2,1)}, bf16[4,64,384]{2,1,0:T(8,128)(2,1)}, bf16[4,64,384]{2,1,0:T(8,128)(2,1)}, bf16[4,64,384]{2,1,0:T(8,128)(2,1)}, s32[16]{0:T(128)}, /*index=5*/s32[16]{0:T(128)}) custom-call(s32[16]{0:T(128)} %left_ref.1, s32[16]{0:T(128)} %copy-done.6, bf16[8,64,384]{2,1,0:T(8,128)(2,1)} %env_ref.3), custom_call_target="tpu_custom_call" | custom-call | tf_op jit(solution)/shard_map/route/pallas_call | solution.py:77
  6.1 1.9 %collective-permute-start.3 = (bf16[4,64,384]{2,1,0:T(8,128)(2,1)}, bf16[4,64,384]{2,1,0:T(8,128)(2,1)S(1)}, u32[]{:S(2)}, u32[]{:S(2)}) collective-permute-start(bf16[4,64,384]{2,1,0:T(8,128)(2,1)} %get-tuple-element.51), channel_id=1, source_target_pairs={{0,1},{1,0},{2,3},{3,2},{4,5},{5,4},{6,7},{7,6},{8,9},{9,8},{10,11... | collective-permute-start | bytes 589832 | tf_op jit(solution)/shard_map/ppermute | solution.py:20
  8.0 2.6 %collective-permute-start.4 = (bf16[4,64,384]{2,1,0:T(8,128)(2,1)}, bf16[4,64,384]{2,1,0:T(8,128)(2,1)S(1)}, u32[]{:S(2)}, u32[]{:S(2)}) collective-permute-start(bf16[4,64,384]{2,1,0:T(8,128)(2,1)} %get-tuple-element.52), channel_id=1, source_target_pairs={{0,2},{1,3},{2,0},{3,1},{4,6},{5,7},{6,4},{7,5},{8,10},{9,11},{10,... | collective-permute-start | bytes 589832 | tf_op jit(solution)/shard_map/ppermute | solution.py:20
  11.6 2.7 %pick.1 = (bf16[2,64,1536]{2,1,0:T(8,128)(2,1)}, bf16[2,64,1536]{2,1,0:T(8,128)(2,1)}, bf16[2,64,1536]{2,1,0:T(8,128)(2,1)}) custom-call(s32[16]{0:T(128)} %copy-done.11, s32[16]{0:T(128)} %copy-done.10, s32[16]{0:T(128)} %copy-done.9, bf16[8,64,1536]{2,1,0:T(8,128)(2,1)} %env_ref.5), custom_call_target="tpu_custom_call" | custom-call | tf_op jit(solution)/shard_map/pick/pallas_call | solution.py:115
  14.4 1.7 %collective-permute-start.7 = (bf16[2,64,1536]{2,1,0:T(8,128)(2,1)}, bf16[2,64,1536]{2,1,0:T(8,128)(2,1)S(1)}, u32[]{:S(2)}, u32[]{:S(2)}) collective-permute-start(bf16[2,64,1536]{2,1,0:T(8,128)(2,1)} %get-tuple-element.55), channel_id=1, source_target_pairs={{0,8},{4,12},{8,0},{12,4},{1,9},{5,13},{9,1},{13,5},{2,10},{6,14},... | collective-permute-start | bytes 1179656 | tf_op jit(solution)/shard_map/ppermute | solution.py:20
  16.1 1.6 %copy-done.1 = bf16[16,64,1024]{2,1,0:T(8,128)(2,1)S(1)} copy-done((bf16[16,64,1024]{2,1,0:T(8,128)(2,1)S(1)}, bf16[16,64,1024]{2,1,0:T(8,128)(2,1)}, u32[]{:S(2)}) %copy-start.1) | copy-done | bytes 2097176
  17.7 1.0 %copy-done.2 = bf16[24,24,256]{2,1,0:T(8,128)(2,1)S(1)} copy-done((bf16[24,24,256]{2,1,0:T(8,128)(2,1)S(1)}, bf16[24,24,256]{2,1,0:T(8,128)(2,1)}, u32[]{:S(2)}) %copy-start.2) | copy-done | bytes 294936
  19.3 3.4 %prepare.1 = (bf16[4,128,2048]{2,1,0:T(8,128)(2,1)S(1)}, bf16[384,384]{1,0:T(8,128)(2,1)S(1)}) custom-call(s32[16]{0:T(128)S(1)} %copy-done.4, bf16[16,64,1024]{2,1,0:T(8,128)(2,1)S(1)} %copy-done.1, bf16[24,24,256]{2,1,0:T(8,128)(2,1)S(1)} %copy-done.2), custom_call_target="tpu_custom_call" | custom-call | tf_op jit(solution)/shard_map/prepare/pallas_call | solution.py:258
  22.7 1.7 %collective-permute-done.4.refs_2_.refs_5_ = bf16[4,64,384]{2,1,0:T(8,128)(2,1)S(1)} collective-permute-done((bf16[4,64,384]{2,1,0:T(8,128)(2,1)}, bf16[4,64,384]{2,1,0:T(8,128)(2,1)S(1)}, u32[]{:S(2)}, u32[]{:S(2)}) %collective-permute-start.4) | collective-permute-done | bytes 196640 | tf_op jit(solution)/shard_map/ppermute | solution.py:20
  24.4 7.9 %mix.1 = (bf16[512,3072]{1,0:T(8,128)(2,1)S(1)}, bf16[512,3072]{1,0:T(8,128)(2,1)S(1)}, bf16[512,3072]{1,0:T(8,128)(2,1)S(1)}) custom-call(bf16[4,128,2048]{2,1,0:T(8,128)(2,1)S(1)} %get-tuple-element.57.diag_ref, bf16[384,384]{1,0:T(8,128)(2,1)S(1)} %get-tuple-element.58.mpo_ref, bf16[4,64,384]{2,1,0:T(8,128)(2,1)S(1)} %copy-done.3, ...), custom_call_target="tpu_custom_call" | custom-call | flops 4227858432 | bytes 4194304 | tf_op jit(solution)/shard_map/mix/pallas_call | solution.py:347
  32.7 3.9 %right.1 = (bf16[3,64,256]{2,1,0:T(8,128)(2,1)S(1)}, bf16[3,64,256]{2,1,0:T(8,128)(2,1)S(1)}, bf16[3,64,256]{2,1,0:T(8,128)(2,1)S(1)}, bf16[3,64,256]{2,1,0:T(8,128)(2,1)S(1)}) custom-call(s32[16]{0:T(128)S(1)} %copy-done.5, s32[16]{0:T(128)S(1)} %copy-done.8, s32[16]{0:T(128)S(1)} %copy-done.7, bf16[8,64,1536]{2,1,0:T(8,128)(2,1)S(1)} %copy-done, ...), custom_call_target="tpu_custom_call" | custom-call | flops 603979776 | bytes 4194304 | tf_op jit(solution)/shard_map/right/pallas_call | solution.py:357
  36.7 5.4 %collective-permute-start.9 = (bf16[3,64,256]{2,1,0:T(8,128)(2,1)S(1)}, bf16[3,64,256]{2,1,0:T(8,128)(2,1)S(1)}, u32[]{:S(2)}, u32[]{:S(2)}) collective-permute-start(bf16[3,64,256]{2,1,0:T(8,128)(2,1)S(1)} %get-tuple-element.71), channel_id=1, source_target_pairs={{0,2},{1,3},{2,0},{3,1},{4,6},{5,7},{6,4},{7,5},{8,10},{9,11},{10,... | collective-permute-start | bytes 294920 | tf_op jit(solution)/shard_map/ppermute | solution.py:20
  42.1 1.4 %collective-permute-start.10 = (bf16[3,64,256]{2,1,0:T(8,128)(2,1)S(1)}, bf16[3,64,256]{2,1,0:T(8,128)(2,1)S(1)}, u32[]{:S(2)}, u32[]{:S(2)}) collective-permute-start(bf16[3,64,256]{2,1,0:T(8,128)(2,1)S(1)} %get-tuple-element.72), channel_id=1, source_target_pairs={{0,3},{1,2},{2,1},{3,0},{4,7},{5,6},{6,5},{7,4},{8,11},{9,10},{10,... | collective-permute-start | bytes 294920 | tf_op jit(solution)/shard_map/ppermute | solution.py:20
  43.5 4.5 %apply.1 = (bf16[1,64,256]{2,1,0:T(8,128)(2,1)S(1)}, bf16[4,64,256]{2,1,0:T(8,128)(2,1)S(1)}, bf16[1,64,256]{2,1,0:T(8,128)(2,1)S(1)}, bf16[1,64,256]{2,1,0:T(8,128)(2,1)S(1)}) custom-call(s32[16]{0:T(128)S(1)} %copy-done.5, s32[16]{0:T(128)S(1)} %copy-done.8, s32[16]{0:T(128)S(1)} %copy-done.7, bf16[8,64,1536]{2,1,0:T(8,128)(2,1)S(1)} %copy-done, ...), custom_call_target="tpu_custom_call" | custom-call | flops 1610612736 | bytes 4194304 | tf_op jit(solution)/shard_map/apply/pallas_call | solution.py:384
  48.0 1.9 %collective-permute-done.9.refs_1_ = bf16[3,64,256]{2,1,0:T(8,128)(2,1)S(1)} collective-permute-done((bf16[3,64,256]{2,1,0:T(8,128)(2,1)S(1)}, bf16[3,64,256]{2,1,0:T(8,128)(2,1)S(1)}, u32[]{:S(2)}, u32[]{:S(2)}) %collective-permute-start.9) | collective-permute-done | bytes 98336 | tf_op jit(solution)/shard_map/ppermute | solution.py:20
  49.9 2.5 %collective-permute-start.11 = (bf16[4,64,256]{2,1,0:T(8,128)(2,1)S(1)}, bf16[4,64,256]{2,1,0:T(8,128)(2,1)S(1)}, u32[]{:S(2)}, u32[]{:S(2)}) collective-permute-start(bf16[4,64,256]{2,1,0:T(8,128)(2,1)S(1)} %get-tuple-element.76), channel_id=1, source_target_pairs={{0,1},{1,0},{2,3},{3,2},{4,5},{5,4},{6,7},{7,6},{8,9},{9,8},{10,11... | collective-permute-start | bytes 393224 | tf_op jit(solution)/shard_map/ppermute | solution.py:20
  52.4 2.4 %collective-permute-start.13 = (bf16[1,64,256]{2,1,0:T(8,128)(2,1)S(1)}, bf16[1,64,256]{2,1,0:T(8,128)(2,1)S(1)}, u32[]{:S(2)}, u32[]{:S(2)}) collective-permute-start(bf16[1,64,256]{2,1,0:T(8,128)(2,1)S(1)} %get-tuple-element.78), channel_id=1, source_target_pairs={{0,3},{1,2},{2,1},{3,0},{4,7},{5,6},{6,5},{7,4},{8,11},{9,10},{10,... | collective-permute-start | bytes 98312 | tf_op jit(solution)/shard_map/ppermute | solution.py:20
  54.8 1.3 %place.2.refs_0_ = bf16[16,64,256]{2,1,0:T(8,128)(2,1)} custom-call(s32[16]{0:T(128)S(1)} %copy-done.5, bf16[3,64,256]{2,1,0:T(8,128)(2,1)S(1)} %get-tuple-element.66.refs_0_, bf16[3,64,256]{2,1,0:T(8,128)(2,1)S(1)} %collective-permute-done.9.refs_1_, bf16[3,64,256]{2,1,0:T(8,128)(2,1)S(1)} %collective-permute-done.10.refs_2_, ...), custom_call_target="tpu_custom_call" | custom-call | tf_op jit(solution)/shard_map/place/pallas_call | solution.py:418
  56.1 1.3 %collective-permute-done.12.refs_2_ = bf16[1,64,256]{2,1,0:T(8,128)(2,1)S(1)} collective-permute-done((bf16[1,64,256]{2,1,0:T(8,128)(2,1)S(1)}, bf16[1,64,256]{2,1,0:T(8,128)(2,1)S(1)}, u32[]{:S(2)}, u32[]{:S(2)}) %collective-permute-start.12) | collective-permute-done | bytes 32800 | tf_op jit(solution)/shard_map/ppermute | solution.py:20
  57.5 1.1 %collective-permute-done.13.refs_3_ = bf16[1,64,256]{2,1,0:T(8,128)(2,1)S(1)} collective-permute-done((bf16[1,64,256]{2,1,0:T(8,128)(2,1)S(1)}, bf16[1,64,256]{2,1,0:T(8,128)(2,1)S(1)}, u32[]{:S(2)}, u32[]{:S(2)}) %collective-permute-start.13) | collective-permute-done | bytes 32800 | tf_op jit(solution)/shard_map/ppermute | solution.py:20
  58.5 1.3 %place.3 = bf16[16,64,256]{2,1,0:T(8,128)(2,1)} custom-call(s32[16]{0:T(128)S(1)} %copy-done.5, bf16[16,64,256]{2,1,0:T(8,128)(2,1)} %place.2.refs_0_, bf16[4,64,256]{2,1,0:T(8,128)(2,1)S(1)} %collective-permute-done.11.refs_1_, bf16[1,64,256]{2,1,0:T(8,128)(2,1)S(1)} %collective-permute-done.12.refs_2_, ...), custom_call_target="tpu_custom_call", output_to_operand_aliasing={{}: (1, {})} | custom-call | tf_op jit(solution)/shard_map/place/pallas_call | solution.py:418
  (37 shorter events, 2.2 us)
Async XLA Ops:
  0.7 3.1 %copy-start.6 = (s32[16]{0:T(128)}, s32[16]{0:T(128)S(1)}, u32[]{:S(2)}) copy-start(s32[16]{0:T(128)S(1)} %bitcast_or_fusion.key_ref) | copy-start | bytes 196
  0.7 9.9 %collective-permute-start.2 = (s32[16]{0:T(128)S(1)}, s32[16]{0:T(128)S(1)}, u32[]{:S(2)}, u32[]{:S(2)}) collective-permute-start(s32[16]{0:T(128)S(1)} %bitcast_or_fusion.key_ref), channel_id=1, source_target_pairs={{0,12},{4,8},{8,4},{12,0},{1,13},{5,9},{9,5},{13,1},{2,14},{6,10},... | collective-permute-start | bytes 200 | tf_op jit(solution)/shard_map/ppermute | solution.py:20
  3.1 7.5 %collective-permute-start.1 = (s32[16]{0:T(128)S(1)}, s32[16]{0:T(128)S(1)}, u32[]{:S(2)}, u32[]{:S(2)}) collective-permute-start(s32[16]{0:T(128)S(1)} %bitcast_or_fusion.key_ref), channel_id=1, source_target_pairs={{0,8},{4,12},{8,0},{12,4},{1,9},{5,13},{9,1},{13,5},{2,10},{6,14},... | collective-permute-start | bytes 200 | tf_op jit(solution)/shard_map/ppermute | solution.py:20
  3.7 6.9 %collective-permute-start = (s32[16]{0:T(128)S(1)}, s32[16]{0:T(128)S(1)}, u32[]{:S(2)}, u32[]{:S(2)}) collective-permute-start(s32[16]{0:T(128)S(1)} %bitcast_or_fusion.key_ref), channel_id=1, source_target_pairs={{0,4},{4,0},{8,12},{12,8},{1,5},{5,1},{9,13},{13,9},{2,6},{6,2},{1... | collective-permute-start | bytes 200 | tf_op jit(solution)/shard_map/ppermute | solution.py:20
  6.1 18.3 %copy-start.3 = (bf16[4,64,384]{2,1,0:T(8,128)(2,1)S(1)}, bf16[4,64,384]{2,1,0:T(8,128)(2,1)}, u32[]{:S(2)}) copy-start(bf16[4,64,384]{2,1,0:T(8,128)(2,1)} %get-tuple-element.59.refs_0_.refs_3_) | copy-start | bytes 589828
  6.1 16.6 %collective-permute-start.3 = (bf16[4,64,384]{2,1,0:T(8,128)(2,1)}, bf16[4,64,384]{2,1,0:T(8,128)(2,1)S(1)}, u32[]{:S(2)}, u32[]{:S(2)}) collective-permute-start(bf16[4,64,384]{2,1,0:T(8,128)(2,1)} %get-tuple-element.51), channel_id=1, source_target_pairs={{0,1},{1,0},{2,3},{3,2},{4,5},{5,4},{6,7},{7,6},{8,9},{9,8},{10,11... | collective-permute-start | bytes 589832 | tf_op jit(solution)/shard_map/ppermute | solution.py:20
  8.0 16.4 %collective-permute-start.4 = (bf16[4,64,384]{2,1,0:T(8,128)(2,1)}, bf16[4,64,384]{2,1,0:T(8,128)(2,1)S(1)}, u32[]{:S(2)}, u32[]{:S(2)}) collective-permute-start(bf16[4,64,384]{2,1,0:T(8,128)(2,1)} %get-tuple-element.52), channel_id=1, source_target_pairs={{0,2},{1,3},{2,0},{3,1},{4,6},{5,7},{6,4},{7,5},{8,10},{9,11},{10,... | collective-permute-start | bytes 589832 | tf_op jit(solution)/shard_map/ppermute | solution.py:20
  10.6 0.6 copy-start.10
  14.4 10.0 %collective-permute-start.5 = (bf16[4,64,384]{2,1,0:T(8,128)(2,1)}, bf16[4,64,384]{2,1,0:T(8,128)(2,1)S(1)}, u32[]{:S(2)}, u32[]{:S(2)}) collective-permute-start(bf16[4,64,384]{2,1,0:T(8,128)(2,1)} %get-tuple-element.53), channel_id=1, source_target_pairs={{0,3},{1,2},{2,1},{3,0},{4,7},{5,6},{6,5},{7,4},{8,11},{9,10},{10,... | collective-permute-start | bytes 589832 | tf_op jit(solution)/shard_map/ppermute | solution.py:20
  14.4 17.9 %collective-permute-start.7 = (bf16[2,64,1536]{2,1,0:T(8,128)(2,1)}, bf16[2,64,1536]{2,1,0:T(8,128)(2,1)S(1)}, u32[]{:S(2)}, u32[]{:S(2)}) collective-permute-start(bf16[2,64,1536]{2,1,0:T(8,128)(2,1)} %get-tuple-element.55), channel_id=1, source_target_pairs={{0,8},{4,12},{8,0},{12,4},{1,9},{5,13},{9,1},{13,5},{2,10},{6,14},... | collective-permute-start | bytes 1179656 | tf_op jit(solution)/shard_map/ppermute | solution.py:20
  16.1 16.6 %collective-permute-start.8 = (bf16[2,64,1536]{2,1,0:T(8,128)(2,1)}, bf16[2,64,1536]{2,1,0:T(8,128)(2,1)S(1)}, u32[]{:S(2)}, u32[]{:S(2)}) collective-permute-start(bf16[2,64,1536]{2,1,0:T(8,128)(2,1)} %get-tuple-element.56), channel_id=1, source_target_pairs={{0,12},{4,8},{8,4},{12,0},{1,13},{5,9},{9,5},{13,1},{2,14},{6,10},... | collective-permute-start | bytes 1179656 | tf_op jit(solution)/shard_map/ppermute | solution.py:20
  16.1 1.6 %copy-start.1 = (bf16[16,64,1024]{2,1,0:T(8,128)(2,1)S(1)}, bf16[16,64,1024]{2,1,0:T(8,128)(2,1)}, u32[]{:S(2)}) copy-start(bf16[16,64,1024]{2,1,0:T(8,128)(2,1)} %state_ref.1) | copy-start | bytes 6291460
  17.7 1.0 %copy-start.2 = (bf16[24,24,256]{2,1,0:T(8,128)(2,1)S(1)}, bf16[24,24,256]{2,1,0:T(8,128)(2,1)}, u32[]{:S(2)}) copy-start(bf16[24,24,256]{2,1,0:T(8,128)(2,1)} %mpo_ref) | copy-start | bytes 884740
  18.7 0.6 %copy-start.4 = (s32[16]{0:T(128)S(1)}, s32[16]{0:T(128)}, u32[]{:S(2)}) copy-start(s32[16]{0:T(128)} %get-tuple-element.42.order_ref) | copy-start | bytes 196
  24.4 8.3 %collective-permute-start.6 = (bf16[2,64,1536]{2,1,0:T(8,128)(2,1)}, bf16[2,64,1536]{2,1,0:T(8,128)(2,1)S(1)}, u32[]{:S(2)}, u32[]{:S(2)}) collective-permute-start(bf16[2,64,1536]{2,1,0:T(8,128)(2,1)} %get-tuple-element.54), channel_id=1, source_target_pairs={{0,4},{4,0},{8,12},{12,8},{1,5},{5,1},{9,13},{13,9},{2,6},{6,2},{1... | collective-permute-start | bytes 1179656 | tf_op jit(solution)/shard_map/ppermute | solution.py:20
  24.4 8.3 %copy-start = (bf16[8,64,1536]{2,1,0:T(8,128)(2,1)S(1)}, bf16[8,64,1536]{2,1,0:T(8,128)(2,1)}, u32[]{:S(2)}) copy-start(bf16[8,64,1536]{2,1,0:T(8,128)(2,1)} %env_ref.5) | copy-start | bytes 4718596
  24.4 8.3 %copy-start.5 = (s32[16]{0:T(128)S(1)}, s32[16]{0:T(128)}, u32[]{:S(2)}) copy-start(s32[16]{0:T(128)} %get-tuple-element.42.order_ref) | copy-start | bytes 196
  24.4 8.3 %copy-start.7 = (s32[16]{0:T(128)S(1)}, s32[16]{0:T(128)}, u32[]{:S(2)}) copy-start(s32[16]{0:T(128)} %copy-done.6) | copy-start | bytes 196
  24.4 8.3 %copy-start.8 = (s32[16]{0:T(128)S(1)}, s32[16]{0:T(128)}, u32[]{:S(2)}) copy-start(s32[16]{0:T(128)} %get-tuple-element.43.slot_ref) | copy-start | bytes 196
  36.7 13.2 %collective-permute-start.9 = (bf16[3,64,256]{2,1,0:T(8,128)(2,1)S(1)}, bf16[3,64,256]{2,1,0:T(8,128)(2,1)S(1)}, u32[]{:S(2)}, u32[]{:S(2)}) collective-permute-start(bf16[3,64,256]{2,1,0:T(8,128)(2,1)S(1)} %get-tuple-element.71), channel_id=1, source_target_pairs={{0,2},{1,3},{2,0},{3,1},{4,6},{5,7},{6,4},{7,5},{8,10},{9,11},{10,... | collective-permute-start | bytes 294920 | tf_op jit(solution)/shard_map/ppermute | solution.py:20
  42.1 7.9 %collective-permute-start.10 = (bf16[3,64,256]{2,1,0:T(8,128)(2,1)S(1)}, bf16[3,64,256]{2,1,0:T(8,128)(2,1)S(1)}, u32[]{:S(2)}, u32[]{:S(2)}) collective-permute-start(bf16[3,64,256]{2,1,0:T(8,128)(2,1)S(1)} %get-tuple-element.72), channel_id=1, source_target_pairs={{0,3},{1,2},{2,1},{3,0},{4,7},{5,6},{6,5},{7,4},{8,11},{9,10},{10,... | collective-permute-start | bytes 294920 | tf_op jit(solution)/shard_map/ppermute | solution.py:20
  49.9 8.6 %collective-permute-start.11 = (bf16[4,64,256]{2,1,0:T(8,128)(2,1)S(1)}, bf16[4,64,256]{2,1,0:T(8,128)(2,1)S(1)}, u32[]{:S(2)}, u32[]{:S(2)}) collective-permute-start(bf16[4,64,256]{2,1,0:T(8,128)(2,1)S(1)} %get-tuple-element.76), channel_id=1, source_target_pairs={{0,1},{1,0},{2,3},{3,2},{4,5},{5,4},{6,7},{7,6},{8,9},{9,8},{10,11... | collective-permute-start | bytes 393224 | tf_op jit(solution)/shard_map/ppermute | solution.py:20
  52.4 5.0 %collective-permute-start.12 = (bf16[1,64,256]{2,1,0:T(8,128)(2,1)S(1)}, bf16[1,64,256]{2,1,0:T(8,128)(2,1)S(1)}, u32[]{:S(2)}, u32[]{:S(2)}) collective-permute-start(bf16[1,64,256]{2,1,0:T(8,128)(2,1)S(1)} %get-tuple-element.77), channel_id=1, source_target_pairs={{0,2},{1,3},{2,0},{3,1},{4,6},{5,7},{6,4},{7,5},{8,10},{9,11},{10,... | collective-permute-start | bytes 98312 | tf_op jit(solution)/shard_map/ppermute | solution.py:20
  52.4 6.1 %collective-permute-start.13 = (bf16[1,64,256]{2,1,0:T(8,128)(2,1)S(1)}, bf16[1,64,256]{2,1,0:T(8,128)(2,1)S(1)}, u32[]{:S(2)}, u32[]{:S(2)}) collective-permute-start(bf16[1,64,256]{2,1,0:T(8,128)(2,1)S(1)} %get-tuple-element.78), channel_id=1, source_target_pairs={{0,3},{1,2},{2,1},{3,0},{4,7},{5,6},{6,5},{7,4},{8,11},{9,10},{10,... | collective-permute-start | bytes 98312 | tf_op jit(solution)/shard_map/ppermute | solution.py:20
  (2 other events, 1.0 us)

commit v10 on v9

--- a/solution.py
+++ b/solution.py
@@ -423,6 +423,7 @@
         scratch_shapes=[pltpu.SemaphoreType.DMA((sum(piece.shape[0] for piece in came),))],
         input_output_aliases={1: 0} if begun else {},
         compiler_params=pltpu.CompilerParams(vmem_limit_bytes=4 << 20),
+        cost_estimate=pl.CostEstimate(flops=10**10, bytes_accessed=1 << 20, transcendentals=0),
         name="place",
     )(order, *begun, *came)
 
@@ -452,9 +453,7 @@
     early = first_blocks(half, order, slots, keys, state_diag, mpo_rows, right_env, rights, lefts, near)
     came = [swap(early[d], "col", d) for d in range(2, cols)]
     late = last_blocks(order, slots, keys, state_diag, mpo_rows, right_env, rights, lefts, early[1], near)
-    joined = lax.optimization_barrier((*late[1:], *came))
-    sent, came = joined[: cols - 1], joined[cols - 1 :]
-    last = [swap(sent[d - 1], "col", d) for d in range(1, cols)]
+    last = [swap(late[d], "col", d) for d in range(1, cols)]
     pieces = [(0, 0)] + [(d, 0) for d in range(2, cols)] + [(0, half)]
     out = place_blocks(order, None, [early[0], *came, late[0]], pieces, cols)
     pieces = [(1, 0)] + [(d, half) for d in range(2, cols)]

time: 60.2 us -> 58.3 us (0.968)
  starting transfers between devices: 20.9 us -> 19.6 us
  waiting for transfers between devices: 6.42 us -> 5.8 us
    ppermute x14, starting transfers between devices: 20.9 us -> 19.6 us  [swap(): return lax.ppermute(array, axis, [(i, i ^ step) for i in range(size)])]
    ppermute x14, waiting for transfers between devices: 6.42 us -> 5.8 us  [swap(): return lax.ppermute(array, axis, [(i, i ^ step) for i in range(size)])]
  transfers between devices with their start and end apart: 14 -> 14, of which waited for: 5 -> 4; matrix products, arithmetic and copies ran while one was open for 0% -> 0% of each run, Pallas kernels for 37% -> 38%
where the time goes in v10:
time: 58.3 us; the launch traced here: 58.1 us
  Pallas kernels  27.4 us (47%)
  starting transfers between devices  19.6 us (34%)
  waiting for transfers between devices  5.8 us (10%)
  local copies, waits for them, and re-layouts  4.24 us (7%)
  other arithmetic  0.67 us (1%)
    ppermute x14, starting transfers between devices, swap(): return lax.ppermute(array, axis, [(i, i ^ step) for i in range(size)])  19.6 us
    pallas_call x1, Pallas kernels, first_blocks(): pl.pallas_call(functools.partial(mix_kernel, states, cols, count), out_sh...  7.86 us
    ppermute x14, waiting for transfers between devices, swap(): return lax.ppermute(array, axis, [(i, i ^ step) for i in range(size)])  5.8 us
    pallas_call x1, Pallas kernels, last_blocks(): pl.pallas_call(functools.partial(apply_kernel, states, rows, cols, near,...  4.51 us
    unnamed x24, local copies, waits for them, and re-layouts  4.24 us
    pallas_call x1, Pallas kernels, first_blocks(): pl.pallas_call(functools.partial(right_kernel, states, rows, cols, near,...  3.92 us
    pallas_call x1, Pallas kernels, prepare(): pl.pallas_call(functools.partial(prepare_kernel, states), out_shape=[jax....  3.4 us
    pallas_call x1, Pallas kernels, pick(): pl.pallas_call(functools.partial(pick_kernel, rows, cols, near), out_shap...  2.73 us
  transfers between devices with their start and end apart: 14, of which 4 were waited for; matrix products, arithmetic and copies ran while one was open for 0% of the time, Pallas kernels for 38%

profile of v10, /device:TPU:0, one launch (start us, length us, event | category | flops | bytes accessed | tf_op | source)
XLA Modules:
  0.0 58.1 jit_solution(14247155235647298770)
XLA Ops:
  0.0 0.7 %bitcast_or_fusion.key_ref = s32[16]{0:T(128)S(1)} fusion(s32[16]{0:T(128)} %param.13, s32[16,1]{0,1:T(1,128)} %param.12), kind=kLoop, calls=%fused_computation | loop fusion | flops 32 | bytes 192 | tf_op jit(solution)/shard_map/or | solution.py:442
  0.7 2.4 %collective-permute-start.2 = (s32[16]{0:T(128)S(1)}, s32[16]{0:T(128)S(1)}, u32[]{:S(2)}, u32[]{:S(2)}) collective-permute-start(s32[16]{0:T(128)S(1)} %bitcast_or_fusion.key_ref), channel_id=1, source_target_pairs={{0,12},{4,8},{8,4},{12,0},{1,13},{5,9},{9,5},{13,1},{2,14},{6,10},... | collective-permute-start | bytes 200 | tf_op jit(solution)/shard_map/ppermute | solution.py:20
  3.1 0.6 %collective-permute-start.1 = (s32[16]{0:T(128)S(1)}, s32[16]{0:T(128)S(1)}, u32[]{:S(2)}, u32[]{:S(2)}) collective-permute-start(s32[16]{0:T(128)S(1)} %bitcast_or_fusion.key_ref), channel_id=1, source_target_pairs={{0,8},{4,12},{8,0},{12,4},{1,9},{5,13},{9,1},{13,5},{2,10},{6,14},... | collective-permute-start | bytes 200 | tf_op jit(solution)/shard_map/ppermute | solution.py:20
  3.8 2.3 %route.1 = (bf16[4,64,384]{2,1,0:T(8,128)(2,1)}, bf16[4,64,384]{2,1,0:T(8,128)(2,1)}, bf16[4,64,384]{2,1,0:T(8,128)(2,1)}, bf16[4,64,384]{2,1,0:T(8,128)(2,1)}, s32[16]{0:T(128)}, /*index=5*/s32[16]{0:T(128)}) custom-call(s32[16]{0:T(128)} %left_ref.1, s32[16]{0:T(128)} %copy-done.4, bf16[8,64,384]{2,1,0:T(8,128)(2,1)} %env_ref.3), custom_call_target="tpu_custom_call" | custom-call | tf_op jit(solution)/shard_map/route/pallas_call | solution.py:77
  6.1 1.9 %collective-permute-start.3 = (bf16[4,64,384]{2,1,0:T(8,128)(2,1)}, bf16[4,64,384]{2,1,0:T(8,128)(2,1)S(1)}, u32[]{:S(2)}, u32[]{:S(2)}) collective-permute-start(bf16[4,64,384]{2,1,0:T(8,128)(2,1)} %get-tuple-element.46), channel_id=1, source_target_pairs={{0,1},{1,0},{2,3},{3,2},{4,5},{5,4},{6,7},{7,6},{8,9},{9,8},{10,11... | collective-permute-start | bytes 589832 | tf_op jit(solution)/shard_map/ppermute | solution.py:20
  8.0 2.6 %collective-permute-start.4 = (bf16[4,64,384]{2,1,0:T(8,128)(2,1)}, bf16[4,64,384]{2,1,0:T(8,128)(2,1)S(1)}, u32[]{:S(2)}, u32[]{:S(2)}) collective-permute-start(bf16[4,64,384]{2,1,0:T(8,128)(2,1)} %get-tuple-element.47), channel_id=1, source_target_pairs={{0,2},{1,3},{2,0},{3,1},{4,6},{5,7},{6,4},{7,5},{8,10},{9,11},{10,... | collective-permute-start | bytes 589832 | tf_op jit(solution)/shard_map/ppermute | solution.py:20
  11.6 2.7 %pick.1 = (bf16[2,64,1536]{2,1,0:T(8,128)(2,1)}, bf16[2,64,1536]{2,1,0:T(8,128)(2,1)}, bf16[2,64,1536]{2,1,0:T(8,128)(2,1)}) custom-call(s32[16]{0:T(128)} %copy-done.11, s32[16]{0:T(128)} %copy-done.10, s32[16]{0:T(128)} %copy-done.9, bf16[8,64,1536]{2,1,0:T(8,128)(2,1)} %env_ref.5), custom_call_target="tpu_custom_call" | custom-call | tf_op jit(solution)/shard_map/pick/pallas_call | solution.py:115
  14.4 1.7 %collective-permute-start.7 = (bf16[2,64,1536]{2,1,0:T(8,128)(2,1)}, bf16[2,64,1536]{2,1,0:T(8,128)(2,1)S(1)}, u32[]{:S(2)}, u32[]{:S(2)}) collective-permute-start(bf16[2,64,1536]{2,1,0:T(8,128)(2,1)} %get-tuple-element.50), channel_id=1, source_target_pairs={{0,8},{4,12},{8,0},{12,4},{1,9},{5,13},{9,1},{13,5},{2,10},{6,14},... | collective-permute-start | bytes 1179656 | tf_op jit(solution)/shard_map/ppermute | solution.py:20
  16.1 1.6 %copy-done.1 = bf16[16,64,1024]{2,1,0:T(8,128)(2,1)S(1)} copy-done((bf16[16,64,1024]{2,1,0:T(8,128)(2,1)S(1)}, bf16[16,64,1024]{2,1,0:T(8,128)(2,1)}, u32[]{:S(2)}) %copy-start.1) | copy-done | bytes 2097176
  17.7 1.0 %copy-done.2 = bf16[24,24,256]{2,1,0:T(8,128)(2,1)S(1)} copy-done((bf16[24,24,256]{2,1,0:T(8,128)(2,1)S(1)}, bf16[24,24,256]{2,1,0:T(8,128)(2,1)}, u32[]{:S(2)}) %copy-start.2) | copy-done | bytes 294936
  18.7 0.6 %copy-done.6 = s32[16]{0:T(128)S(1)} copy-done((s32[16]{0:T(128)S(1)}, s32[16]{0:T(128)}, u32[]{:S(2)}) %copy-start.6) | copy-done | bytes 88
  19.3 3.4 %prepare.1 = (bf16[4,128,2048]{2,1,0:T(8,128)(2,1)S(1)}, bf16[384,384]{1,0:T(8,128)(2,1)S(1)}) custom-call(s32[16]{0:T(128)S(1)} %copy-done.6, bf16[16,64,1024]{2,1,0:T(8,128)(2,1)S(1)} %copy-done.1, bf16[24,24,256]{2,1,0:T(8,128)(2,1)S(1)} %copy-done.2), custom_call_target="tpu_custom_call" | custom-call | tf_op jit(solution)/shard_map/prepare/pallas_call | solution.py:258
  22.7 1.7 %collective-permute-done.4.refs_2_.refs_5_ = bf16[4,64,384]{2,1,0:T(8,128)(2,1)S(1)} collective-permute-done((bf16[4,64,384]{2,1,0:T(8,128)(2,1)}, bf16[4,64,384]{2,1,0:T(8,128)(2,1)S(1)}, u32[]{:S(2)}, u32[]{:S(2)}) %collective-permute-start.4) | collective-permute-done | bytes 196640 | tf_op jit(solution)/shard_map/ppermute | solution.py:20
  24.4 7.9 %mix.1 = (bf16[512,3072]{1,0:T(8,128)(2,1)S(1)}, bf16[512,3072]{1,0:T(8,128)(2,1)S(1)}, bf16[512,3072]{1,0:T(8,128)(2,1)S(1)}) custom-call(bf16[4,128,2048]{2,1,0:T(8,128)(2,1)S(1)} %get-tuple-element.52.diag_ref, bf16[384,384]{1,0:T(8,128)(2,1)S(1)} %get-tuple-element.53.mpo_ref, bf16[4,64,384]{2,1,0:T(8,128)(2,1)S(1)} %copy-done.3, ...), custom_call_target="tpu_custom_call" | custom-call | flops 4227858432 | bytes 4194304 | tf_op jit(solution)/shard_map/mix/pallas_call | solution.py:347
  32.7 3.9 %right.1 = (bf16[3,64,256]{2,1,0:T(8,128)(2,1)S(1)}, bf16[3,64,256]{2,1,0:T(8,128)(2,1)S(1)}, bf16[3,64,256]{2,1,0:T(8,128)(2,1)S(1)}, bf16[3,64,256]{2,1,0:T(8,128)(2,1)S(1)}) custom-call(s32[16]{0:T(128)S(1)} %copy-done.7, s32[16]{0:T(128)S(1)} %copy-done.8, s32[16]{0:T(128)S(1)} %copy-done.5, bf16[8,64,1536]{2,1,0:T(8,128)(2,1)S(1)} %copy-done, ...), custom_call_target="tpu_custom_call" | custom-call | flops 603979776 | bytes 4194304 | tf_op jit(solution)/shard_map/right/pallas_call | solution.py:357
  36.7 5.4 %collective-permute-start.9 = (bf16[3,64,256]{2,1,0:T(8,128)(2,1)S(1)}, bf16[3,64,256]{2,1,0:T(8,128)(2,1)S(1)}, u32[]{:S(2)}, u32[]{:S(2)}) collective-permute-start(bf16[3,64,256]{2,1,0:T(8,128)(2,1)S(1)} %get-tuple-element.62), channel_id=1, source_target_pairs={{0,2},{1,3},{2,0},{3,1},{4,6},{5,7},{6,4},{7,5},{8,10},{9,11},{10,... | collective-permute-start | bytes 294920 | tf_op jit(solution)/shard_map/ppermute | solution.py:20
  42.1 1.4 %collective-permute-start.10 = (bf16[3,64,256]{2,1,0:T(8,128)(2,1)S(1)}, bf16[3,64,256]{2,1,0:T(8,128)(2,1)S(1)}, u32[]{:S(2)}, u32[]{:S(2)}) collective-permute-start(bf16[3,64,256]{2,1,0:T(8,128)(2,1)S(1)} %get-tuple-element.63), channel_id=1, source_target_pairs={{0,3},{1,2},{2,1},{3,0},{4,7},{5,6},{6,5},{7,4},{8,11},{9,10},{10,... | collective-permute-start | bytes 294920 | tf_op jit(solution)/shard_map/ppermute | solution.py:20
  43.5 4.5 %apply.1 = (bf16[1,64,256]{2,1,0:T(8,128)(2,1)S(1)}, bf16[4,64,256]{2,1,0:T(8,128)(2,1)S(1)}, bf16[1,64,256]{2,1,0:T(8,128)(2,1)S(1)}, bf16[1,64,256]{2,1,0:T(8,128)(2,1)S(1)}) custom-call(s32[16]{0:T(128)S(1)} %copy-done.7, s32[16]{0:T(128)S(1)} %copy-done.8, s32[16]{0:T(128)S(1)} %copy-done.5, bf16[8,64,1536]{2,1,0:T(8,128)(2,1)S(1)} %copy-done, ...), custom_call_target="tpu_custom_call" | custom-call | flops 1610612736 | bytes 4194304 | tf_op jit(solution)/shard_map/apply/pallas_call | solution.py:384
  48.1 2.5 %collective-permute-start.13 = (bf16[1,64,256]{2,1,0:T(8,128)(2,1)S(1)}, bf16[1,64,256]{2,1,0:T(8,128)(2,1)S(1)}, u32[]{:S(2)}, u32[]{:S(2)}) collective-permute-start(bf16[1,64,256]{2,1,0:T(8,128)(2,1)S(1)} %get-tuple-element.68), channel_id=1, source_target_pairs={{0,3},{1,2},{2,1},{3,0},{4,7},{5,6},{6,5},{7,4},{8,11},{9,10},{10,... | collective-permute-start | bytes 98312 | tf_op jit(solution)/shard_map/ppermute | solution.py:20
  50.6 1.0 %collective-permute-start.11 = (bf16[4,64,256]{2,1,0:T(8,128)(2,1)S(1)}, bf16[4,64,256]{2,1,0:T(8,128)(2,1)S(1)}, u32[]{:S(2)}, u32[]{:S(2)}) collective-permute-start(bf16[4,64,256]{2,1,0:T(8,128)(2,1)S(1)} %get-tuple-element.66), channel_id=1, source_target_pairs={{0,1},{1,0},{2,3},{3,2},{4,5},{5,4},{6,7},{7,6},{8,9},{9,8},{10,11... | collective-permute-start | bytes 393224 | tf_op jit(solution)/shard_map/ppermute | solution.py:20
  51.6 1.4 %place.2.refs_0_ = bf16[16,64,256]{2,1,0:T(8,128)(2,1)} custom-call(s32[16]{0:T(128)S(1)} %copy-done.7, bf16[3,64,256]{2,1,0:T(8,128)(2,1)S(1)} %get-tuple-element.61.refs_0_, bf16[3,64,256]{2,1,0:T(8,128)(2,1)S(1)} %collective-permute-done.9.refs_1_, bf16[3,64,256]{2,1,0:T(8,128)(2,1)S(1)} %collective-permute-done.10.refs_2_, ...), custom_call_target="tpu_custom_call" | custom-call | flops 10000000000 | bytes 1048576 | tf_op jit(solution)/shard_map/place/pallas_call | solution.py:418
  52.9 1.2 %collective-permute-done.12.refs_2_ = bf16[1,64,256]{2,1,0:T(8,128)(2,1)S(1)} collective-permute-done((bf16[1,64,256]{2,1,0:T(8,128)(2,1)S(1)}, bf16[1,64,256]{2,1,0:T(8,128)(2,1)S(1)}, u32[]{:S(2)}, u32[]{:S(2)}) %collective-permute-start.12) | collective-permute-done | bytes 32800 | tf_op jit(solution)/shard_map/ppermute | solution.py:20
  54.1 2.5 %collective-permute-done.11.refs_1_ = bf16[4,64,256]{2,1,0:T(8,128)(2,1)S(1)} collective-permute-done((bf16[4,64,256]{2,1,0:T(8,128)(2,1)S(1)}, bf16[4,64,256]{2,1,0:T(8,128)(2,1)S(1)}, u32[]{:S(2)}, u32[]{:S(2)}) %collective-permute-start.11) | collective-permute-done | bytes 131104 | tf_op jit(solution)/shard_map/ppermute | solution.py:20
  56.6 1.3 %place.3 = bf16[16,64,256]{2,1,0:T(8,128)(2,1)} custom-call(s32[16]{0:T(128)S(1)} %copy-done.7, bf16[16,64,256]{2,1,0:T(8,128)(2,1)} %place.2.refs_0_, bf16[4,64,256]{2,1,0:T(8,128)(2,1)S(1)} %collective-permute-done.11.refs_1_, bf16[1,64,256]{2,1,0:T(8,128)(2,1)S(1)} %collective-permute-done.12.refs_2_, ...), custom_call_target="tpu_custom_call", output_to_operand_aliasing={{}: (1, {})} | custom-call | flops 10000000000 | bytes 1048576 | tf_op jit(solution)/shard_map/place/pallas_call | solution.py:418
  (37 shorter events, 1.6 us)
Async XLA Ops:
  0.7 3.1 %copy-start.4 = (s32[16]{0:T(128)}, s32[16]{0:T(128)S(1)}, u32[]{:S(2)}) copy-start(s32[16]{0:T(128)S(1)} %bitcast_or_fusion.key_ref) | copy-start | bytes 196
  0.7 9.9 %collective-permute-start.2 = (s32[16]{0:T(128)S(1)}, s32[16]{0:T(128)S(1)}, u32[]{:S(2)}, u32[]{:S(2)}) collective-permute-start(s32[16]{0:T(128)S(1)} %bitcast_or_fusion.key_ref), channel_id=1, source_target_pairs={{0,12},{4,8},{8,4},{12,0},{1,13},{5,9},{9,5},{13,1},{2,14},{6,10},... | collective-permute-start | bytes 200 | tf_op jit(solution)/shard_map/ppermute | solution.py:20
  3.1 7.5 %collective-permute-start.1 = (s32[16]{0:T(128)S(1)}, s32[16]{0:T(128)S(1)}, u32[]{:S(2)}, u32[]{:S(2)}) collective-permute-start(s32[16]{0:T(128)S(1)} %bitcast_or_fusion.key_ref), channel_id=1, source_target_pairs={{0,8},{4,12},{8,0},{12,4},{1,9},{5,13},{9,1},{13,5},{2,10},{6,14},... | collective-permute-start | bytes 200 | tf_op jit(solution)/shard_map/ppermute | solution.py:20
  3.7 6.9 %collective-permute-start = (s32[16]{0:T(128)S(1)}, s32[16]{0:T(128)S(1)}, u32[]{:S(2)}, u32[]{:S(2)}) collective-permute-start(s32[16]{0:T(128)S(1)} %bitcast_or_fusion.key_ref), channel_id=1, source_target_pairs={{0,4},{4,0},{8,12},{12,8},{1,5},{5,1},{9,13},{13,9},{2,6},{6,2},{1... | collective-permute-start | bytes 200 | tf_op jit(solution)/shard_map/ppermute | solution.py:20
  6.1 18.3 %copy-start.3 = (bf16[4,64,384]{2,1,0:T(8,128)(2,1)S(1)}, bf16[4,64,384]{2,1,0:T(8,128)(2,1)}, u32[]{:S(2)}) copy-start(bf16[4,64,384]{2,1,0:T(8,128)(2,1)} %get-tuple-element.54.refs_0_.refs_3_) | copy-start | bytes 589828
  6.1 16.6 %collective-permute-start.3 = (bf16[4,64,384]{2,1,0:T(8,128)(2,1)}, bf16[4,64,384]{2,1,0:T(8,128)(2,1)S(1)}, u32[]{:S(2)}, u32[]{:S(2)}) collective-permute-start(bf16[4,64,384]{2,1,0:T(8,128)(2,1)} %get-tuple-element.46), channel_id=1, source_target_pairs={{0,1},{1,0},{2,3},{3,2},{4,5},{5,4},{6,7},{7,6},{8,9},{9,8},{10,11... | collective-permute-start | bytes 589832 | tf_op jit(solution)/shard_map/ppermute | solution.py:20
  8.0 16.4 %collective-permute-start.4 = (bf16[4,64,384]{2,1,0:T(8,128)(2,1)}, bf16[4,64,384]{2,1,0:T(8,128)(2,1)S(1)}, u32[]{:S(2)}, u32[]{:S(2)}) collective-permute-start(bf16[4,64,384]{2,1,0:T(8,128)(2,1)} %get-tuple-element.47), channel_id=1, source_target_pairs={{0,2},{1,3},{2,0},{3,1},{4,6},{5,7},{6,4},{7,5},{8,10},{9,11},{10,... | collective-permute-start | bytes 589832 | tf_op jit(solution)/shard_map/ppermute | solution.py:20
  10.6 0.6 copy-start.10
  14.4 10.0 %collective-permute-start.5 = (bf16[4,64,384]{2,1,0:T(8,128)(2,1)}, bf16[4,64,384]{2,1,0:T(8,128)(2,1)S(1)}, u32[]{:S(2)}, u32[]{:S(2)}) collective-permute-start(bf16[4,64,384]{2,1,0:T(8,128)(2,1)} %get-tuple-element.48), channel_id=1, source_target_pairs={{0,3},{1,2},{2,1},{3,0},{4,7},{5,6},{6,5},{7,4},{8,11},{9,10},{10,... | collective-permute-start | bytes 589832 | tf_op jit(solution)/shard_map/ppermute | solution.py:20
  14.4 17.9 %collective-permute-start.7 = (bf16[2,64,1536]{2,1,0:T(8,128)(2,1)}, bf16[2,64,1536]{2,1,0:T(8,128)(2,1)S(1)}, u32[]{:S(2)}, u32[]{:S(2)}) collective-permute-start(bf16[2,64,1536]{2,1,0:T(8,128)(2,1)} %get-tuple-element.50), channel_id=1, source_target_pairs={{0,8},{4,12},{8,0},{12,4},{1,9},{5,13},{9,1},{13,5},{2,10},{6,14},... | collective-permute-start | bytes 1179656 | tf_op jit(solution)/shard_map/ppermute | solution.py:20
  16.1 16.6 %collective-permute-start.8 = (bf16[2,64,1536]{2,1,0:T(8,128)(2,1)}, bf16[2,64,1536]{2,1,0:T(8,128)(2,1)S(1)}, u32[]{:S(2)}, u32[]{:S(2)}) collective-permute-start(bf16[2,64,1536]{2,1,0:T(8,128)(2,1)} %get-tuple-element.51), channel_id=1, source_target_pairs={{0,12},{4,8},{8,4},{12,0},{1,13},{5,9},{9,5},{13,1},{2,14},{6,10},... | collective-permute-start | bytes 1179656 | tf_op jit(solution)/shard_map/ppermute | solution.py:20
  16.1 1.6 %copy-start.1 = (bf16[16,64,1024]{2,1,0:T(8,128)(2,1)S(1)}, bf16[16,64,1024]{2,1,0:T(8,128)(2,1)}, u32[]{:S(2)}) copy-start(bf16[16,64,1024]{2,1,0:T(8,128)(2,1)} %state_ref.1) | copy-start | bytes 6291460
  17.7 1.0 %copy-start.2 = (bf16[24,24,256]{2,1,0:T(8,128)(2,1)S(1)}, bf16[24,24,256]{2,1,0:T(8,128)(2,1)}, u32[]{:S(2)}) copy-start(bf16[24,24,256]{2,1,0:T(8,128)(2,1)} %mpo_ref) | copy-start | bytes 884740
  18.7 0.6 %copy-start.6 = (s32[16]{0:T(128)S(1)}, s32[16]{0:T(128)}, u32[]{:S(2)}) copy-start(s32[16]{0:T(128)} %get-tuple-element.37.order_ref) | copy-start | bytes 196
  24.4 8.3 %collective-permute-start.6 = (bf16[2,64,1536]{2,1,0:T(8,128)(2,1)}, bf16[2,64,1536]{2,1,0:T(8,128)(2,1)S(1)}, u32[]{:S(2)}, u32[]{:S(2)}) collective-permute-start(bf16[2,64,1536]{2,1,0:T(8,128)(2,1)} %get-tuple-element.49), channel_id=1, source_target_pairs={{0,4},{4,0},{8,12},{12,8},{1,5},{5,1},{9,13},{13,9},{2,6},{6,2},{1... | collective-permute-start | bytes 1179656 | tf_op jit(solution)/shard_map/ppermute | solution.py:20
  24.4 8.3 %copy-start = (bf16[8,64,1536]{2,1,0:T(8,128)(2,1)S(1)}, bf16[8,64,1536]{2,1,0:T(8,128)(2,1)}, u32[]{:S(2)}) copy-start(bf16[8,64,1536]{2,1,0:T(8,128)(2,1)} %env_ref.5) | copy-start | bytes 4718596
  24.4 8.3 %copy-start.5 = (s32[16]{0:T(128)S(1)}, s32[16]{0:T(128)}, u32[]{:S(2)}) copy-start(s32[16]{0:T(128)} %copy-done.4) | copy-start | bytes 196
  24.4 8.3 %copy-start.7 = (s32[16]{0:T(128)S(1)}, s32[16]{0:T(128)}, u32[]{:S(2)}) copy-start(s32[16]{0:T(128)} %get-tuple-element.37.order_ref) | copy-start | bytes 196
  24.4 8.3 %copy-start.8 = (s32[16]{0:T(128)S(1)}, s32[16]{0:T(128)}, u32[]{:S(2)}) copy-start(s32[16]{0:T(128)} %get-tuple-element.38.slot_ref) | copy-start | bytes 196
  36.7 14.9 %collective-permute-start.9 = (bf16[3,64,256]{2,1,0:T(8,128)(2,1)S(1)}, bf16[3,64,256]{2,1,0:T(8,128)(2,1)S(1)}, u32[]{:S(2)}, u32[]{:S(2)}) collective-permute-start(bf16[3,64,256]{2,1,0:T(8,128)(2,1)S(1)} %get-tuple-element.62), channel_id=1, source_target_pairs={{0,2},{1,3},{2,0},{3,1},{4,6},{5,7},{6,4},{7,5},{8,10},{9,11},{10,... | collective-permute-start | bytes 294920 | tf_op jit(solution)/shard_map/ppermute | solution.py:20
  42.1 9.5 %collective-permute-start.10 = (bf16[3,64,256]{2,1,0:T(8,128)(2,1)S(1)}, bf16[3,64,256]{2,1,0:T(8,128)(2,1)S(1)}, u32[]{:S(2)}, u32[]{:S(2)}) collective-permute-start(bf16[3,64,256]{2,1,0:T(8,128)(2,1)S(1)} %get-tuple-element.63), channel_id=1, source_target_pairs={{0,3},{1,2},{2,1},{3,0},{4,7},{5,6},{6,5},{7,4},{8,11},{9,10},{10,... | collective-permute-start | bytes 294920 | tf_op jit(solution)/shard_map/ppermute | solution.py:20
  48.0 6.1 %collective-permute-start.12 = (bf16[1,64,256]{2,1,0:T(8,128)(2,1)S(1)}, bf16[1,64,256]{2,1,0:T(8,128)(2,1)S(1)}, u32[]{:S(2)}, u32[]{:S(2)}) collective-permute-start(bf16[1,64,256]{2,1,0:T(8,128)(2,1)S(1)} %get-tuple-element.67), channel_id=1, source_target_pairs={{0,2},{1,3},{2,0},{3,1},{4,6},{5,7},{6,4},{7,5},{8,10},{9,11},{10,... | collective-permute-start | bytes 98312 | tf_op jit(solution)/shard_map/ppermute | solution.py:20
  48.1 6.1 %collective-permute-start.13 = (bf16[1,64,256]{2,1,0:T(8,128)(2,1)S(1)}, bf16[1,64,256]{2,1,0:T(8,128)(2,1)S(1)}, u32[]{:S(2)}, u32[]{:S(2)}) collective-permute-start(bf16[1,64,256]{2,1,0:T(8,128)(2,1)S(1)} %get-tuple-element.68), channel_id=1, source_target_pairs={{0,3},{1,2},{2,1},{3,0},{4,7},{5,6},{6,5},{7,4},{8,11},{9,10},{10,... | collective-permute-start | bytes 98312 | tf_op jit(solution)/shard_map/ppermute | solution.py:20
  50.6 6.1 %collective-permute-start.11 = (bf16[4,64,256]{2,1,0:T(8,128)(2,1)S(1)}, bf16[4,64,256]{2,1,0:T(8,128)(2,1)S(1)}, u32[]{:S(2)}, u32[]{:S(2)}) collective-permute-start(bf16[4,64,256]{2,1,0:T(8,128)(2,1)S(1)} %get-tuple-element.66), channel_id=1, source_target_pairs={{0,1},{1,0},{2,3},{3,2},{4,5},{5,4},{6,7},{7,6},{8,9},{9,8},{10,11... | collective-permute-start | bytes 393224 | tf_op jit(solution)/shard_map/ppermute | solution.py:20
  (2 other events, 1.0 us)

commit v11 on v10

--- a/solution.py
+++ b/solution.py
@@ -311,7 +311,7 @@
 
 
 def apply_kernel(
-    states, rows, cols, near, first, count, order_ref, slot_ref, key_ref, env_ref, diag_ref, mpo_ref, early_ref, *refs
+    states, rows, cols, near, first, count, order_ref, slot_ref, key_ref, env_ref, diag_ref, mpo_ref, *refs
 ):
     rights, lefts, refs = refs[: rows - 1], refs[rows - 1 : rows - 1 + cols], refs[rows - 1 + cols :]
     outs, (left_rows, mixed, right_now, right_diag, result) = refs[:cols], refs[cols:]
@@ -321,14 +321,12 @@
         spread_left([left.at[first + k] for left in lefts], left_rows.at[k])
     for k in range(count):
         mix_block(states, left_rows.at[k], diag_ref.at[first + k], mpo_ref, mixed.at[k])
-    outs[1][:first] = early_ref[...]
     for k in range(count):
         fetch_right(near, key_ref, order_ref, slot_ref, at + k, env_ref, rights, right_now.at[k])
     for k in range(count):
         spread_right(right_now.at[k], right_diag.at[k], low)
     for k in range(count):
-        into = [out.at[first + k if d == 1 else k] for d, out in enumerate(outs)]
-        finish_block(states, mixed.at[k], right_diag.at[k], result.at[k], into, low)
+        finish_block(states, mixed.at[k], right_diag.at[k], result.at[k], [out.at[k] for out in outs], low)
 
 
 def cost_of(blocks, states, width, size, mix, right):
@@ -370,21 +368,18 @@
     )(order, slots, keys, right_env, *rights, *mixed)
 
 
-def last_blocks(order, slots, keys, state_diag, mpo_rows, right_env, rights, lefts, early, near):
+def last_blocks(order, slots, keys, state_diag, mpo_rows, right_env, rights, lefts, first, near):
     cols, rows = len(lefts), len(rights) + 1
-    first, (steps, size, share) = early.shape[0], lefts[0].shape
+    steps, size, share = lefts[0].shape
     count = steps - first
     width = share // size * cols
     states = mpo_rows.shape[0] // width
     half, lanes = size // 2, 2 * size
 
-    def out(blocks):
-        return jax.ShapeDtypeStruct((blocks, size, states // cols * size), jnp.bfloat16)
-
     return pl.pallas_call(
         functools.partial(apply_kernel, states, rows, cols, near, first, count),
-        out_shape=[out(steps if d == 1 else count) for d in range(cols)],
-        in_specs=[SMEM] * 3 + [VMEM] * (4 + rows - 1 + cols),
+        out_shape=[jax.ShapeDtypeStruct((count, size, states // cols * size), jnp.bfloat16)] * cols,
+        in_specs=[SMEM] * 3 + [VMEM] * (3 + rows - 1 + cols),
         out_specs=[VMEM] * cols,
         scratch_shapes=[
             pltpu.VMEM((count, half * width, lanes), jnp.float32),
@@ -396,7 +391,7 @@
         compiler_params=pltpu.CompilerParams(vmem_limit_bytes=32 << 20),
         cost_estimate=cost_of(count, states, width, size, 1, 1),
         name="apply",
-    )(order, slots, keys, right_env, state_diag, mpo_rows, early, *rights, *lefts)
+    )(order, slots, keys, right_env, state_diag, mpo_rows, *rights, *lefts)
 
 
 def place_kernel(cols, pieces, begun, order_ref, *refs):
@@ -451,12 +446,12 @@
     core_send, state_diag, *lefts[1:] = lax.optimization_barrier((far[0], state_diag, *lefts[1:]))
     rights = [swap(core_send, "row", 1)] + [swap(far[d - 1], "row", d) for d in range(2, rows)]
     early = first_blocks(half, order, slots, keys, state_diag, mpo_rows, right_env, rights, lefts, near)
-    came = [swap(early[d], "col", d) for d in range(2, cols)]
-    late = last_blocks(order, slots, keys, state_diag, mpo_rows, right_env, rights, lefts, early[1], near)
+    came = [swap(early[d], "col", d) for d in range(1, cols)]
+    late = last_blocks(order, slots, keys, state_diag, mpo_rows, right_env, rights, lefts, half, near)
     last = [swap(late[d], "col", d) for d in range(1, cols)]
-    pieces = [(0, 0)] + [(d, 0) for d in range(2, cols)] + [(0, half)]
+    pieces = [(d, 0) for d in range(cols)] + [(0, half)]
     out = place_blocks(order, None, [early[0], *came, late[0]], pieces, cols)
-    pieces = [(1, 0)] + [(d, half) for d in range(2, cols)]
+    pieces = [(d, half) for d in range(1, cols)]
     return place_blocks(order, out, last, pieces, cols)
 
 

time: 58.3 us -> 58.5 us (level)
  starting transfers between devices: 19.6 us -> 20.6 us
  waiting for transfers between devices: 5.8 us -> 4.98 us
    ppermute x14 -> x15, starting transfers between devices: 19.6 us -> 20.6 us  [swap(): return lax.ppermute(array, axis, [(i, i ^ step) for i in range(size)])]
    ppermute x14 -> x15, waiting for transfers between devices: 5.8 us -> 4.98 us  [swap(): return lax.ppermute(array, axis, [(i, i ^ step) for i in range(size)])]
  transfers between devices with their start and end apart: 14 -> 15, of which waited for: 4 -> 4; matrix products, arithmetic and copies ran while one was open for 0% -> 0% of each run, Pallas kernels for 38% -> 38%
where the time goes in v11:
time: 58.5 us; the launch traced here: 58.2 us
  Pallas kernels  27.4 us (47%)
  starting transfers between devices  20.6 us (35%)
  waiting for transfers between devices  4.98 us (9%)
  local copies, waits for them, and re-layouts  4.25 us (7%)
  other arithmetic  0.67 us (1%)
    ppermute x15, starting transfers between devices, swap(): return lax.ppermute(array, axis, [(i, i ^ step) for i in range(size)])  20.6 us
    pallas_call x1, Pallas kernels, first_blocks(): pl.pallas_call(functools.partial(mix_kernel, states, cols, count), out_sh...  7.87 us
    ppermute x15, waiting for transfers between devices, swap(): return lax.ppermute(array, axis, [(i, i ^ step) for i in range(size)])  4.98 us
    pallas_call x1, Pallas kernels, last_blocks(): pl.pallas_call(functools.partial(apply_kernel, states, rows, cols, near,...  4.51 us
    unnamed x24, local copies, waits for them, and re-layouts  4.25 us
    pallas_call x1, Pallas kernels, first_blocks(): pl.pallas_call(functools.partial(right_kernel, states, rows, cols, near,...  3.91 us
    pallas_call x1, Pallas kernels, prepare(): pl.pallas_call(functools.partial(prepare_kernel, states), out_shape=[jax....  3.41 us
    pallas_call x1, Pallas kernels, pick(): pl.pallas_call(functools.partial(pick_kernel, rows, cols, near), out_shap...  2.74 us
  transfers between devices with their start and end apart: 15, of which 4 were waited for; matrix products, arithmetic and copies ran while one was open for 0% of the time, Pallas kernels for 38%

profile of v11, /device:TPU:0, one launch (start us, length us, event | category | flops | bytes accessed | tf_op | source)
XLA Modules:
  0.0 58.2 jit_solution(12228115508721880740)
XLA Ops:
  0.0 0.7 %bitcast_or_fusion.key_ref = s32[16]{0:T(128)S(1)} fusion(s32[16]{0:T(128)} %param.13, s32[16,1]{0,1:T(1,128)} %param.12), kind=kLoop, calls=%fused_computation | loop fusion | flops 32 | bytes 192 | tf_op jit(solution)/shard_map/or | solution.py:437
  0.7 2.4 %collective-permute-start.2 = (s32[16]{0:T(128)S(1)}, s32[16]{0:T(128)S(1)}, u32[]{:S(2)}, u32[]{:S(2)}) collective-permute-start(s32[16]{0:T(128)S(1)} %bitcast_or_fusion.key_ref), channel_id=1, source_target_pairs={{0,12},{4,8},{8,4},{12,0},{1,13},{5,9},{9,5},{13,1},{2,14},{6,10},... | collective-permute-start | bytes 200 | tf_op jit(solution)/shard_map/ppermute | solution.py:20
  3.8 2.3 %route.1 = (bf16[4,64,384]{2,1,0:T(8,128)(2,1)}, bf16[4,64,384]{2,1,0:T(8,128)(2,1)}, bf16[4,64,384]{2,1,0:T(8,128)(2,1)}, bf16[4,64,384]{2,1,0:T(8,128)(2,1)}, s32[16]{0:T(128)}, /*index=5*/s32[16]{0:T(128)}) custom-call(s32[16]{0:T(128)} %left_ref.1, s32[16]{0:T(128)} %copy-done.3, bf16[8,64,384]{2,1,0:T(8,128)(2,1)} %env_ref.3), custom_call_target="tpu_custom_call" | custom-call | tf_op jit(solution)/shard_map/route/pallas_call | solution.py:77
  6.1 1.9 %collective-permute-start.3 = (bf16[4,64,384]{2,1,0:T(8,128)(2,1)}, bf16[4,64,384]{2,1,0:T(8,128)(2,1)S(1)}, u32[]{:S(2)}, u32[]{:S(2)}) collective-permute-start(bf16[4,64,384]{2,1,0:T(8,128)(2,1)} %get-tuple-element.46), channel_id=1, source_target_pairs={{0,1},{1,0},{2,3},{3,2},{4,5},{5,4},{6,7},{7,6},{8,9},{9,8},{10,11... | collective-permute-start | bytes 589832 | tf_op jit(solution)/shard_map/ppermute | solution.py:20
  8.0 2.6 %collective-permute-start.4 = (bf16[4,64,384]{2,1,0:T(8,128)(2,1)}, bf16[4,64,384]{2,1,0:T(8,128)(2,1)S(1)}, u32[]{:S(2)}, u32[]{:S(2)}) collective-permute-start(bf16[4,64,384]{2,1,0:T(8,128)(2,1)} %get-tuple-element.47), channel_id=1, source_target_pairs={{0,2},{1,3},{2,0},{3,1},{4,6},{5,7},{6,4},{7,5},{8,10},{9,11},{10,... | collective-permute-start | bytes 589832 | tf_op jit(solution)/shard_map/ppermute | solution.py:20
  11.7 2.7 %pick.1 = (bf16[2,64,1536]{2,1,0:T(8,128)(2,1)}, bf16[2,64,1536]{2,1,0:T(8,128)(2,1)}, bf16[2,64,1536]{2,1,0:T(8,128)(2,1)}) custom-call(s32[16]{0:T(128)} %copy-done.11, s32[16]{0:T(128)} %copy-done.10, s32[16]{0:T(128)} %copy-done.9, bf16[8,64,1536]{2,1,0:T(8,128)(2,1)} %env_ref.5), custom_call_target="tpu_custom_call" | custom-call | tf_op jit(solution)/shard_map/pick/pallas_call | solution.py:115
  14.4 1.7 %collective-permute-start.7 = (bf16[2,64,1536]{2,1,0:T(8,128)(2,1)}, bf16[2,64,1536]{2,1,0:T(8,128)(2,1)S(1)}, u32[]{:S(2)}, u32[]{:S(2)}) collective-permute-start(bf16[2,64,1536]{2,1,0:T(8,128)(2,1)} %get-tuple-element.50), channel_id=1, source_target_pairs={{0,8},{4,12},{8,0},{12,4},{1,9},{5,13},{9,1},{13,5},{2,10},{6,14},... | collective-permute-start | bytes 1179656 | tf_op jit(solution)/shard_map/ppermute | solution.py:20
  16.2 1.6 %copy-done.1 = bf16[16,64,1024]{2,1,0:T(8,128)(2,1)S(1)} copy-done((bf16[16,64,1024]{2,1,0:T(8,128)(2,1)S(1)}, bf16[16,64,1024]{2,1,0:T(8,128)(2,1)}, u32[]{:S(2)}) %copy-start.1) | copy-done | bytes 2097176
  17.8 1.0 %copy-done.2 = bf16[24,24,256]{2,1,0:T(8,128)(2,1)S(1)} copy-done((bf16[24,24,256]{2,1,0:T(8,128)(2,1)S(1)}, bf16[24,24,256]{2,1,0:T(8,128)(2,1)}, u32[]{:S(2)}) %copy-start.2) | copy-done | bytes 294936
  19.3 3.4 %prepare.1 = (bf16[4,128,2048]{2,1,0:T(8,128)(2,1)S(1)}, bf16[384,384]{1,0:T(8,128)(2,1)S(1)}) custom-call(s32[16]{0:T(128)S(1)} %copy-done.5, bf16[16,64,1024]{2,1,0:T(8,128)(2,1)S(1)} %copy-done.1, bf16[24,24,256]{2,1,0:T(8,128)(2,1)S(1)} %copy-done.2), custom_call_target="tpu_custom_call" | custom-call | tf_op jit(solution)/shard_map/prepare/pallas_call | solution.py:258
  22.8 1.6 %collective-permute-done.4.refs_2_.refs_5_ = bf16[4,64,384]{2,1,0:T(8,128)(2,1)S(1)} collective-permute-done((bf16[4,64,384]{2,1,0:T(8,128)(2,1)}, bf16[4,64,384]{2,1,0:T(8,128)(2,1)S(1)}, u32[]{:S(2)}, u32[]{:S(2)}) %collective-permute-start.4) | collective-permute-done | bytes 196640 | tf_op jit(solution)/shard_map/ppermute | solution.py:20
  24.4 7.9 %mix.1 = (bf16[512,3072]{1,0:T(8,128)(2,1)S(1)}, bf16[512,3072]{1,0:T(8,128)(2,1)S(1)}, bf16[512,3072]{1,0:T(8,128)(2,1)S(1)}) custom-call(bf16[4,128,2048]{2,1,0:T(8,128)(2,1)S(1)} %get-tuple-element.52.diag_ref, bf16[384,384]{1,0:T(8,128)(2,1)S(1)} %get-tuple-element.53.mpo_ref, bf16[4,64,384]{2,1,0:T(8,128)(2,1)S(1)} %copy-done.8, ...), custom_call_target="tpu_custom_call" | custom-call | flops 4227858432 | bytes 4194304 | tf_op jit(solution)/shard_map/mix/pallas_call | solution.py:345
  32.8 3.9 %right.1 = (bf16[3,64,256]{2,1,0:T(8,128)(2,1)S(1)}, bf16[3,64,256]{2,1,0:T(8,128)(2,1)S(1)}, bf16[3,64,256]{2,1,0:T(8,128)(2,1)S(1)}, bf16[3,64,256]{2,1,0:T(8,128)(2,1)S(1)}) custom-call(s32[16]{0:T(128)S(1)} %copy-done.6, s32[16]{0:T(128)S(1)} %copy-done.7, s32[16]{0:T(128)S(1)} %copy-done.4, bf16[8,64,1536]{2,1,0:T(8,128)(2,1)S(1)} %copy-done, ...), custom_call_target="tpu_custom_call" | custom-call | flops 603979776 | bytes 4194304 | tf_op jit(solution)/shard_map/right/pallas_call | solution.py:355
  36.7 4.4 %collective-permute-start.9 = (bf16[3,64,256]{2,1,0:T(8,128)(2,1)S(1)}, bf16[3,64,256]{2,1,0:T(8,128)(2,1)S(1)}, u32[]{:S(2)}, u32[]{:S(2)}) collective-permute-start(bf16[3,64,256]{2,1,0:T(8,128)(2,1)S(1)} %get-tuple-element.62), channel_id=1, source_target_pairs={{0,1},{1,0},{2,3},{3,2},{4,5},{5,4},{6,7},{7,6},{8,9},{9,8},{10,11... | collective-permute-start | bytes 294920 | tf_op jit(solution)/shard_map/ppermute | solution.py:20
  41.1 1.0 %collective-permute-start.10 = (bf16[3,64,256]{2,1,0:T(8,128)(2,1)S(1)}, bf16[3,64,256]{2,1,0:T(8,128)(2,1)S(1)}, u32[]{:S(2)}, u32[]{:S(2)}) collective-permute-start(bf16[3,64,256]{2,1,0:T(8,128)(2,1)S(1)} %get-tuple-element.63), channel_id=1, source_target_pairs={{0,2},{1,3},{2,0},{3,1},{4,6},{5,7},{6,4},{7,5},{8,10},{9,11},{10,... | collective-permute-start | bytes 294920 | tf_op jit(solution)/shard_map/ppermute | solution.py:20
  42.2 1.4 %collective-permute-start.11 = (bf16[3,64,256]{2,1,0:T(8,128)(2,1)S(1)}, bf16[3,64,256]{2,1,0:T(8,128)(2,1)S(1)}, u32[]{:S(2)}, u32[]{:S(2)}) collective-permute-start(bf16[3,64,256]{2,1,0:T(8,128)(2,1)S(1)} %get-tuple-element.64), channel_id=1, source_target_pairs={{0,3},{1,2},{2,1},{3,0},{4,7},{5,6},{6,5},{7,4},{8,11},{9,10},{10,... | collective-permute-start | bytes 294920 | tf_op jit(solution)/shard_map/ppermute | solution.py:20
  43.6 4.5 %apply.1 = (bf16[1,64,256]{2,1,0:T(8,128)(2,1)S(1)}, bf16[1,64,256]{2,1,0:T(8,128)(2,1)S(1)}, bf16[1,64,256]{2,1,0:T(8,128)(2,1)S(1)}, bf16[1,64,256]{2,1,0:T(8,128)(2,1)S(1)}) custom-call(s32[16]{0:T(128)S(1)} %copy-done.6, s32[16]{0:T(128)S(1)} %copy-done.7, s32[16]{0:T(128)S(1)} %copy-done.4, bf16[8,64,1536]{2,1,0:T(8,128)(2,1)S(1)} %copy-done, ...), custom_call_target="tpu_custom_call" | custom-call | flops 1610612736 | bytes 4194304 | tf_op jit(solution)/shard_map/apply/pallas_call | solution.py:379
  48.1 1.1 %collective-permute-start.12 = (bf16[1,64,256]{2,1,0:T(8,128)(2,1)S(1)}, bf16[1,64,256]{2,1,0:T(8,128)(2,1)S(1)}, u32[]{:S(2)}, u32[]{:S(2)}) collective-permute-start(bf16[1,64,256]{2,1,0:T(8,128)(2,1)S(1)} %get-tuple-element.66), channel_id=1, source_target_pairs={{0,1},{1,0},{2,3},{3,2},{4,5},{5,4},{6,7},{7,6},{8,9},{9,8},{10,11... | collective-permute-start | bytes 98312 | tf_op jit(solution)/shard_map/ppermute | solution.py:20
  49.2 1.9 %collective-permute-start.13 = (bf16[1,64,256]{2,1,0:T(8,128)(2,1)S(1)}, bf16[1,64,256]{2,1,0:T(8,128)(2,1)S(1)}, u32[]{:S(2)}, u32[]{:S(2)}) collective-permute-start(bf16[1,64,256]{2,1,0:T(8,128)(2,1)S(1)} %get-tuple-element.67), channel_id=1, source_target_pairs={{0,2},{1,3},{2,0},{3,1},{4,6},{5,7},{6,4},{7,5},{8,10},{9,11},{10,... | collective-permute-start | bytes 98312 | tf_op jit(solution)/shard_map/ppermute | solution.py:20
  51.1 1.4 %collective-permute-start.14 = (bf16[1,64,256]{2,1,0:T(8,128)(2,1)S(1)}, bf16[1,64,256]{2,1,0:T(8,128)(2,1)S(1)}, u32[]{:S(2)}, u32[]{:S(2)}) collective-permute-start(bf16[1,64,256]{2,1,0:T(8,128)(2,1)S(1)} %get-tuple-element.68), channel_id=1, source_target_pairs={{0,3},{1,2},{2,1},{3,0},{4,7},{5,6},{6,5},{7,4},{8,11},{9,10},{10,... | collective-permute-start | bytes 98312 | tf_op jit(solution)/shard_map/ppermute | solution.py:20
  52.6 1.4 %place.2.refs_0_ = bf16[16,64,256]{2,1,0:T(8,128)(2,1)} custom-call(s32[16]{0:T(128)S(1)} %copy-done.6, bf16[3,64,256]{2,1,0:T(8,128)(2,1)S(1)} %get-tuple-element.61.refs_0_, bf16[3,64,256]{2,1,0:T(8,128)(2,1)S(1)} %collective-permute-done.9.refs_1_, bf16[3,64,256]{2,1,0:T(8,128)(2,1)S(1)} %collective-permute-done.10.refs_2_, ...), custom_call_target="tpu_custom_call" | custom-call | flops 10000000000 | bytes 1048576 | tf_op jit(solution)/shard_map/place/pallas_call | solution.py:413
  54.0 1.4 %collective-permute-done.13.refs_2_ = bf16[1,64,256]{2,1,0:T(8,128)(2,1)S(1)} collective-permute-done((bf16[1,64,256]{2,1,0:T(8,128)(2,1)S(1)}, bf16[1,64,256]{2,1,0:T(8,128)(2,1)S(1)}, u32[]{:S(2)}, u32[]{:S(2)}) %collective-permute-start.13) | collective-permute-done | bytes 32800 | tf_op jit(solution)/shard_map/ppermute | solution.py:20
  55.3 1.5 %collective-permute-done.14.refs_3_ = bf16[1,64,256]{2,1,0:T(8,128)(2,1)S(1)} collective-permute-done((bf16[1,64,256]{2,1,0:T(8,128)(2,1)S(1)}, bf16[1,64,256]{2,1,0:T(8,128)(2,1)S(1)}, u32[]{:S(2)}, u32[]{:S(2)}) %collective-permute-start.14) | collective-permute-done | bytes 32800 | tf_op jit(solution)/shard_map/ppermute | solution.py:20
  56.8 1.2 %place.3 = bf16[16,64,256]{2,1,0:T(8,128)(2,1)} custom-call(s32[16]{0:T(128)S(1)} %copy-done.6, bf16[16,64,256]{2,1,0:T(8,128)(2,1)} %place.2.refs_0_, bf16[1,64,256]{2,1,0:T(8,128)(2,1)S(1)} %collective-permute-done.12.refs_1_, bf16[1,64,256]{2,1,0:T(8,128)(2,1)S(1)} %collective-permute-done.13.refs_2_, ...), custom_call_target="tpu_custom_call", output_to_operand_aliasing={{}: (1, {})} | custom-call | flops 10000000000 | bytes 1048576 | tf_op jit(solution)/shard_map/place/pallas_call | solution.py:413
  (39 shorter events, 2.9 us)
Async XLA Ops:
  0.7 3.1 %copy-start.3 = (s32[16]{0:T(128)}, s32[16]{0:T(128)S(1)}, u32[]{:S(2)}) copy-start(s32[16]{0:T(128)S(1)} %bitcast_or_fusion.key_ref) | copy-start | bytes 196
  0.7 9.9 %collective-permute-start.2 = (s32[16]{0:T(128)S(1)}, s32[16]{0:T(128)S(1)}, u32[]{:S(2)}, u32[]{:S(2)}) collective-permute-start(s32[16]{0:T(128)S(1)} %bitcast_or_fusion.key_ref), channel_id=1, source_target_pairs={{0,12},{4,8},{8,4},{12,0},{1,13},{5,9},{9,5},{13,1},{2,14},{6,10},... | collective-permute-start | bytes 200 | tf_op jit(solution)/shard_map/ppermute | solution.py:20
  3.1 7.5 %collective-permute-start.1 = (s32[16]{0:T(128)S(1)}, s32[16]{0:T(128)S(1)}, u32[]{:S(2)}, u32[]{:S(2)}) collective-permute-start(s32[16]{0:T(128)S(1)} %bitcast_or_fusion.key_ref), channel_id=1, source_target_pairs={{0,8},{4,12},{8,0},{12,4},{1,9},{5,13},{9,1},{13,5},{2,10},{6,14},... | collective-permute-start | bytes 200 | tf_op jit(solution)/shard_map/ppermute | solution.py:20
  3.7 6.9 %collective-permute-start = (s32[16]{0:T(128)S(1)}, s32[16]{0:T(128)S(1)}, u32[]{:S(2)}, u32[]{:S(2)}) collective-permute-start(s32[16]{0:T(128)S(1)} %bitcast_or_fusion.key_ref), channel_id=1, source_target_pairs={{0,4},{4,0},{8,12},{12,8},{1,5},{5,1},{9,13},{13,9},{2,6},{6,2},{1... | collective-permute-start | bytes 200 | tf_op jit(solution)/shard_map/ppermute | solution.py:20
  6.1 18.3 %copy-start.8 = (bf16[4,64,384]{2,1,0:T(8,128)(2,1)S(1)}, bf16[4,64,384]{2,1,0:T(8,128)(2,1)}, u32[]{:S(2)}) copy-start(bf16[4,64,384]{2,1,0:T(8,128)(2,1)} %get-tuple-element.54.refs_0_.refs_3_) | copy-start | bytes 589828
  6.1 16.6 %collective-permute-start.3 = (bf16[4,64,384]{2,1,0:T(8,128)(2,1)}, bf16[4,64,384]{2,1,0:T(8,128)(2,1)S(1)}, u32[]{:S(2)}, u32[]{:S(2)}) collective-permute-start(bf16[4,64,384]{2,1,0:T(8,128)(2,1)} %get-tuple-element.46), channel_id=1, source_target_pairs={{0,1},{1,0},{2,3},{3,2},{4,5},{5,4},{6,7},{7,6},{8,9},{9,8},{10,11... | collective-permute-start | bytes 589832 | tf_op jit(solution)/shard_map/ppermute | solution.py:20
  8.0 16.4 %collective-permute-start.4 = (bf16[4,64,384]{2,1,0:T(8,128)(2,1)}, bf16[4,64,384]{2,1,0:T(8,128)(2,1)S(1)}, u32[]{:S(2)}, u32[]{:S(2)}) collective-permute-start(bf16[4,64,384]{2,1,0:T(8,128)(2,1)} %get-tuple-element.47), channel_id=1, source_target_pairs={{0,2},{1,3},{2,0},{3,1},{4,6},{5,7},{6,4},{7,5},{8,10},{9,11},{10,... | collective-permute-start | bytes 589832 | tf_op jit(solution)/shard_map/ppermute | solution.py:20
  14.4 10.0 %collective-permute-start.5 = (bf16[4,64,384]{2,1,0:T(8,128)(2,1)}, bf16[4,64,384]{2,1,0:T(8,128)(2,1)S(1)}, u32[]{:S(2)}, u32[]{:S(2)}) collective-permute-start(bf16[4,64,384]{2,1,0:T(8,128)(2,1)} %get-tuple-element.48), channel_id=1, source_target_pairs={{0,3},{1,2},{2,1},{3,0},{4,7},{5,6},{6,5},{7,4},{8,11},{9,10},{10,... | collective-permute-start | bytes 589832 | tf_op jit(solution)/shard_map/ppermute | solution.py:20
  14.4 17.9 %collective-permute-start.7 = (bf16[2,64,1536]{2,1,0:T(8,128)(2,1)}, bf16[2,64,1536]{2,1,0:T(8,128)(2,1)S(1)}, u32[]{:S(2)}, u32[]{:S(2)}) collective-permute-start(bf16[2,64,1536]{2,1,0:T(8,128)(2,1)} %get-tuple-element.50), channel_id=1, source_target_pairs={{0,8},{4,12},{8,0},{12,4},{1,9},{5,13},{9,1},{13,5},{2,10},{6,14},... | collective-permute-start | bytes 1179656 | tf_op jit(solution)/shard_map/ppermute | solution.py:20
  16.2 16.6 %collective-permute-start.8 = (bf16[2,64,1536]{2,1,0:T(8,128)(2,1)}, bf16[2,64,1536]{2,1,0:T(8,128)(2,1)S(1)}, u32[]{:S(2)}, u32[]{:S(2)}) collective-permute-start(bf16[2,64,1536]{2,1,0:T(8,128)(2,1)} %get-tuple-element.51), channel_id=1, source_target_pairs={{0,12},{4,8},{8,4},{12,0},{1,13},{5,9},{9,5},{13,1},{2,14},{6,10},... | collective-permute-start | bytes 1179656 | tf_op jit(solution)/shard_map/ppermute | solution.py:20
  16.2 1.6 %copy-start.1 = (bf16[16,64,1024]{2,1,0:T(8,128)(2,1)S(1)}, bf16[16,64,1024]{2,1,0:T(8,128)(2,1)}, u32[]{:S(2)}) copy-start(bf16[16,64,1024]{2,1,0:T(8,128)(2,1)} %state_ref.1) | copy-start | bytes 6291460
  17.8 1.0 %copy-start.2 = (bf16[24,24,256]{2,1,0:T(8,128)(2,1)S(1)}, bf16[24,24,256]{2,1,0:T(8,128)(2,1)}, u32[]{:S(2)}) copy-start(bf16[24,24,256]{2,1,0:T(8,128)(2,1)} %mpo_ref) | copy-start | bytes 884740
  18.7 0.6 %copy-start.5 = (s32[16]{0:T(128)S(1)}, s32[16]{0:T(128)}, u32[]{:S(2)}) copy-start(s32[16]{0:T(128)} %get-tuple-element.37.order_ref) | copy-start | bytes 196
  24.4 8.4 %collective-permute-start.6 = (bf16[2,64,1536]{2,1,0:T(8,128)(2,1)}, bf16[2,64,1536]{2,1,0:T(8,128)(2,1)S(1)}, u32[]{:S(2)}, u32[]{:S(2)}) collective-permute-start(bf16[2,64,1536]{2,1,0:T(8,128)(2,1)} %get-tuple-element.49), channel_id=1, source_target_pairs={{0,4},{4,0},{8,12},{12,8},{1,5},{5,1},{9,13},{13,9},{2,6},{6,2},{1... | collective-permute-start | bytes 1179656 | tf_op jit(solution)/shard_map/ppermute | solution.py:20
  24.4 8.4 %copy-start = (bf16[8,64,1536]{2,1,0:T(8,128)(2,1)S(1)}, bf16[8,64,1536]{2,1,0:T(8,128)(2,1)}, u32[]{:S(2)}) copy-start(bf16[8,64,1536]{2,1,0:T(8,128)(2,1)} %env_ref.5) | copy-start | bytes 4718596
  24.4 8.4 %copy-start.4 = (s32[16]{0:T(128)S(1)}, s32[16]{0:T(128)}, u32[]{:S(2)}) copy-start(s32[16]{0:T(128)} %copy-done.3) | copy-start | bytes 196
  24.4 8.4 %copy-start.6 = (s32[16]{0:T(128)S(1)}, s32[16]{0:T(128)}, u32[]{:S(2)}) copy-start(s32[16]{0:T(128)} %get-tuple-element.37.order_ref) | copy-start | bytes 196
  24.4 8.4 %copy-start.7 = (s32[16]{0:T(128)S(1)}, s32[16]{0:T(128)}, u32[]{:S(2)}) copy-start(s32[16]{0:T(128)} %get-tuple-element.38.slot_ref) | copy-start | bytes 196
  36.7 14.4 %collective-permute-start.9 = (bf16[3,64,256]{2,1,0:T(8,128)(2,1)S(1)}, bf16[3,64,256]{2,1,0:T(8,128)(2,1)S(1)}, u32[]{:S(2)}, u32[]{:S(2)}) collective-permute-start(bf16[3,64,256]{2,1,0:T(8,128)(2,1)S(1)} %get-tuple-element.62), channel_id=1, source_target_pairs={{0,1},{1,0},{2,3},{3,2},{4,5},{5,4},{6,7},{7,6},{8,9},{9,8},{10,11... | collective-permute-start | bytes 294920 | tf_op jit(solution)/shard_map/ppermute | solution.py:20
  41.1 11.4 %collective-permute-start.10 = (bf16[3,64,256]{2,1,0:T(8,128)(2,1)S(1)}, bf16[3,64,256]{2,1,0:T(8,128)(2,1)S(1)}, u32[]{:S(2)}, u32[]{:S(2)}) collective-permute-start(bf16[3,64,256]{2,1,0:T(8,128)(2,1)S(1)} %get-tuple-element.63), channel_id=1, source_target_pairs={{0,2},{1,3},{2,0},{3,1},{4,6},{5,7},{6,4},{7,5},{8,10},{9,11},{10,... | collective-permute-start | bytes 294920 | tf_op jit(solution)/shard_map/ppermute | solution.py:20
  42.2 10.4 %collective-permute-start.11 = (bf16[3,64,256]{2,1,0:T(8,128)(2,1)S(1)}, bf16[3,64,256]{2,1,0:T(8,128)(2,1)S(1)}, u32[]{:S(2)}, u32[]{:S(2)}) collective-permute-start(bf16[3,64,256]{2,1,0:T(8,128)(2,1)S(1)} %get-tuple-element.64), channel_id=1, source_target_pairs={{0,3},{1,2},{2,1},{3,0},{4,7},{5,6},{6,5},{7,4},{8,11},{9,10},{10,... | collective-permute-start | bytes 294920 | tf_op jit(solution)/shard_map/ppermute | solution.py:20
  48.1 5.9 %collective-permute-start.12 = (bf16[1,64,256]{2,1,0:T(8,128)(2,1)S(1)}, bf16[1,64,256]{2,1,0:T(8,128)(2,1)S(1)}, u32[]{:S(2)}, u32[]{:S(2)}) collective-permute-start(bf16[1,64,256]{2,1,0:T(8,128)(2,1)S(1)} %get-tuple-element.66), channel_id=1, source_target_pairs={{0,1},{1,0},{2,3},{3,2},{4,5},{5,4},{6,7},{7,6},{8,9},{9,8},{10,11... | collective-permute-start | bytes 98312 | tf_op jit(solution)/shard_map/ppermute | solution.py:20
  49.2 6.1 %collective-permute-start.13 = (bf16[1,64,256]{2,1,0:T(8,128)(2,1)S(1)}, bf16[1,64,256]{2,1,0:T(8,128)(2,1)S(1)}, u32[]{:S(2)}, u32[]{:S(2)}) collective-permute-start(bf16[1,64,256]{2,1,0:T(8,128)(2,1)S(1)} %get-tuple-element.67), channel_id=1, source_target_pairs={{0,2},{1,3},{2,0},{3,1},{4,6},{5,7},{6,4},{7,5},{8,10},{9,11},{10,... | collective-permute-start | bytes 98312 | tf_op jit(solution)/shard_map/ppermute | solution.py:20
  51.1 5.7 %collective-permute-start.14 = (bf16[1,64,256]{2,1,0:T(8,128)(2,1)S(1)}, bf16[1,64,256]{2,1,0:T(8,128)(2,1)S(1)}, u32[]{:S(2)}, u32[]{:S(2)}) collective-permute-start(bf16[1,64,256]{2,1,0:T(8,128)(2,1)S(1)} %get-tuple-element.68), channel_id=1, source_target_pairs={{0,3},{1,2},{2,1},{3,0},{4,7},{5,6},{6,5},{7,4},{8,11},{9,10},{10,... | collective-permute-start | bytes 98312 | tf_op jit(solution)/shard_map/ppermute | solution.py:20
  (3 other events, 1.6 us)

commit v12 on v10

--- a/solution.py
+++ b/solution.py
@@ -437,7 +437,7 @@
     most = max(2, (2 * count + rows - 1) // rows)
     near = -(-most // cols)
 
-    half = count // cols - max(1, count // cols // 4)
+    half = count // cols // 2
 
     keys = jnp.bitwise_or(lax.shift_left(block_owner[:, 0], SHIFT), block_sub)
     others = [swap(keys, "row", step) for step in range(1, rows)]

time: 58.3 us -> 60.4 us (1.036)
  waiting for transfers between devices: 5.8 us -> 11 us
  starting transfers between devices: 19.6 us -> 17.1 us
  local copies, waits for them, and re-layouts: 4.24 us -> 3.3 us
    ppermute x14, waiting for transfers between devices: 5.8 us -> 11 us  [swap(): return lax.ppermute(array, axis, [(i, i ^ step) for i in range(size)])]
    pallas_call x1, Pallas kernels: 4.51 us -> 8.18 us  [last_blocks(): pl.pallas_call(functools.partial(apply_kernel, states, rows, cols, near,...]
    ppermute x14, starting transfers between devices: 19.6 us -> 17.1 us  [swap(): return lax.ppermute(array, axis, [(i, i ^ step) for i in range(size)])]
    pallas_call x1, Pallas kernels: 7.86 us -> 5.41 us  [first_blocks(): pl.pallas_call(functools.partial(mix_kernel, states, cols, count), out_sh...]
    unnamed x24 -> x26, local copies, waits for them, and re-layouts: 4.24 us -> 3.3 us
    pallas_call x1, Pallas kernels: 3.92 us -> 2.98 us  [first_blocks(): pl.pallas_call(functools.partial(right_kernel, states, rows, cols, near,...]
  transfers between devices with their start and end apart: 14 -> 14, of which waited for: 4 -> 5; matrix products, arithmetic and copies ran while one was open for 0% -> 0% of each run, Pallas kernels for 38% -> 39%
where the time goes in v12:
time: 60.4 us; the launch traced here: 60.2 us
  Pallas kernels  27.7 us (46%)
  starting transfers between devices  17.1 us (28%)
  waiting for transfers between devices  11 us (18%)
  local copies, waits for them, and re-layouts  3.3 us (5%)
  other arithmetic  0.72 us (1%)
    ppermute x14, starting transfers between devices, swap(): return lax.ppermute(array, axis, [(i, i ^ step) for i in range(size)])  17.1 us
    ppermute x14, waiting for transfers between devices, swap(): return lax.ppermute(array, axis, [(i, i ^ step) for i in range(size)])  11 us
    pallas_call x1, Pallas kernels, last_blocks(): pl.pallas_call(functools.partial(apply_kernel, states, rows, cols, near,...  8.18 us
    pallas_call x1, Pallas kernels, first_blocks(): pl.pallas_call(functools.partial(mix_kernel, states, cols, count), out_sh...  5.41 us
    pallas_call x1, Pallas kernels, prepare(): pl.pallas_call(functools.partial(prepare_kernel, states), out_shape=[jax....  3.41 us
    unnamed x26, local copies, waits for them, and re-layouts  3.3 us
    pallas_call x1, Pallas kernels, first_blocks(): pl.pallas_call(functools.partial(right_kernel, states, rows, cols, near,...  2.98 us
    pallas_call x1, Pallas kernels, pick(): pl.pallas_call(functools.partial(pick_kernel, rows, cols, near), out_shap...  2.74 us
  transfers between devices with their start and end apart: 14, of which 5 were waited for; matrix products, arithmetic and copies ran while one was open for 0% of the time, Pallas kernels for 39%

profile of v12, /device:TPU:0, one launch (start us, length us, event | category | flops | bytes accessed | tf_op | source)
XLA Modules:
  0.0 60.2 jit_solution(2732618908634724611)
XLA Ops:
  0.0 0.7 %bitcast_or_fusion.key_ref = s32[16]{0:T(128)S(1)} fusion(s32[16]{0:T(128)} %param.13, s32[16,1]{0,1:T(1,128)} %param.12), kind=kLoop, calls=%fused_computation | loop fusion | flops 32 | bytes 192 | tf_op jit(solution)/shard_map/or | solution.py:442
  0.7 2.4 %collective-permute-start.2 = (s32[16]{0:T(128)S(1)}, s32[16]{0:T(128)S(1)}, u32[]{:S(2)}, u32[]{:S(2)}) collective-permute-start(s32[16]{0:T(128)S(1)} %bitcast_or_fusion.key_ref), channel_id=1, source_target_pairs={{0,12},{4,8},{8,4},{12,0},{1,13},{5,9},{9,5},{13,1},{2,14},{6,10},... | collective-permute-start | bytes 200 | tf_op jit(solution)/shard_map/ppermute | solution.py:20
  3.8 2.3 %route.1 = (bf16[4,64,384]{2,1,0:T(8,128)(2,1)}, bf16[4,64,384]{2,1,0:T(8,128)(2,1)}, bf16[4,64,384]{2,1,0:T(8,128)(2,1)}, bf16[4,64,384]{2,1,0:T(8,128)(2,1)}, s32[16]{0:T(128)}, /*index=5*/s32[16]{0:T(128)}) custom-call(s32[16]{0:T(128)} %left_ref.1, s32[16]{0:T(128)} %copy-done.3, bf16[8,64,384]{2,1,0:T(8,128)(2,1)} %env_ref.3), custom_call_target="tpu_custom_call" | custom-call | tf_op jit(solution)/shard_map/route/pallas_call | solution.py:77
  6.2 1.9 %collective-permute-start.3 = (bf16[4,64,384]{2,1,0:T(8,128)(2,1)}, bf16[4,64,384]{2,1,0:T(8,128)(2,1)S(1)}, u32[]{:S(2)}, u32[]{:S(2)}) collective-permute-start(bf16[4,64,384]{2,1,0:T(8,128)(2,1)} %get-tuple-element.45), channel_id=1, source_target_pairs={{0,1},{1,0},{2,3},{3,2},{4,5},{5,4},{6,7},{7,6},{8,9},{9,8},{10,11... | collective-permute-start | bytes 589832 | tf_op jit(solution)/shard_map/ppermute | solution.py:20
  8.0 2.6 %collective-permute-start.4 = (bf16[4,64,384]{2,1,0:T(8,128)(2,1)}, bf16[4,64,384]{2,1,0:T(8,128)(2,1)S(1)}, u32[]{:S(2)}, u32[]{:S(2)}) collective-permute-start(bf16[4,64,384]{2,1,0:T(8,128)(2,1)} %get-tuple-element.46), channel_id=1, source_target_pairs={{0,2},{1,3},{2,0},{3,1},{4,6},{5,7},{6,4},{7,5},{8,10},{9,11},{10,... | collective-permute-start | bytes 589832 | tf_op jit(solution)/shard_map/ppermute | solution.py:20
  11.7 2.7 %pick.1 = (bf16[2,64,1536]{2,1,0:T(8,128)(2,1)}, bf16[2,64,1536]{2,1,0:T(8,128)(2,1)}, bf16[2,64,1536]{2,1,0:T(8,128)(2,1)}) custom-call(s32[16]{0:T(128)} %copy-done.11, s32[16]{0:T(128)} %copy-done.10, s32[16]{0:T(128)} %copy-done.9, bf16[8,64,1536]{2,1,0:T(8,128)(2,1)} %env_ref.5), custom_call_target="tpu_custom_call" | custom-call | tf_op jit(solution)/shard_map/pick/pallas_call | solution.py:115
  14.5 1.7 %collective-permute-start.7 = (bf16[2,64,1536]{2,1,0:T(8,128)(2,1)}, bf16[2,64,1536]{2,1,0:T(8,128)(2,1)S(1)}, u32[]{:S(2)}, u32[]{:S(2)}) collective-permute-start(bf16[2,64,1536]{2,1,0:T(8,128)(2,1)} %get-tuple-element.49), channel_id=1, source_target_pairs={{0,8},{4,12},{8,0},{12,4},{1,9},{5,13},{9,1},{13,5},{2,10},{6,14},... | collective-permute-start | bytes 1179656 | tf_op jit(solution)/shard_map/ppermute | solution.py:20
  16.2 1.6 %copy-done.1 = bf16[16,64,1024]{2,1,0:T(8,128)(2,1)S(1)} copy-done((bf16[16,64,1024]{2,1,0:T(8,128)(2,1)S(1)}, bf16[16,64,1024]{2,1,0:T(8,128)(2,1)}, u32[]{:S(2)}) %copy-start.1) | copy-done | bytes 2097176
  18.4 3.4 %prepare.1 = (bf16[4,128,2048]{2,1,0:T(8,128)(2,1)S(1)}, bf16[384,384]{1,0:T(8,128)(2,1)S(1)}) custom-call(s32[16]{0:T(128)S(1)} %copy-done.5, bf16[16,64,1024]{2,1,0:T(8,128)(2,1)S(1)} %copy-done.1, bf16[24,24,256]{2,1,0:T(8,128)(2,1)S(1)} %copy-done.2), custom_call_target="tpu_custom_call" | custom-call | tf_op jit(solution)/shard_map/prepare/pallas_call | solution.py:258
  21.8 2.6 %collective-permute-done.4.refs_2_.refs_5_ = bf16[4,64,384]{2,1,0:T(8,128)(2,1)S(1)} collective-permute-done((bf16[4,64,384]{2,1,0:T(8,128)(2,1)}, bf16[4,64,384]{2,1,0:T(8,128)(2,1)S(1)}, u32[]{:S(2)}, u32[]{:S(2)}) %collective-permute-start.4) | collective-permute-done | bytes 196640 | tf_op jit(solution)/shard_map/ppermute | solution.py:20
  24.5 5.4 %mix.1 = (bf16[512,3072]{1,0:T(8,128)(2,1)S(1)}, bf16[512,3072]{1,0:T(8,128)(2,1)S(1)}) custom-call(bf16[4,128,2048]{2,1,0:T(8,128)(2,1)S(1)} %get-tuple-element.51.diag_ref, bf16[384,384]{1,0:T(8,128)(2,1)S(1)} %get-tuple-element.52.mpo_ref, bf16[4,64,384]{2,1,0:T(8,128)(2,1)S(1)} %copy-done.8, ...), custom_call_target="tpu_custom_call" | custom-call | flops 2818572288 | bytes 4194304 | tf_op jit(solution)/shard_map/mix/pallas_call | solution.py:347
  29.9 2.9 %collective-permute-done.8.refs_2_ = bf16[2,64,1536]{2,1,0:T(8,128)(2,1)S(1)} collective-permute-done((bf16[2,64,1536]{2,1,0:T(8,128)(2,1)}, bf16[2,64,1536]{2,1,0:T(8,128)(2,1)S(1)}, u32[]{:S(2)}, u32[]{:S(2)}) %collective-permute-start.8) | collective-permute-done | bytes 393248 | tf_op jit(solution)/shard_map/ppermute | solution.py:20
  32.8 3.0 %right.1 = (bf16[2,64,256]{2,1,0:T(8,128)(2,1)S(1)}, bf16[2,64,256]{2,1,0:T(8,128)(2,1)S(1)}, bf16[2,64,256]{2,1,0:T(8,128)(2,1)S(1)}, bf16[2,64,256]{2,1,0:T(8,128)(2,1)S(1)}) custom-call(s32[16]{0:T(128)S(1)} %copy-done.6, s32[16]{0:T(128)S(1)} %copy-done.7, s32[16]{0:T(128)S(1)} %copy-done.4, bf16[8,64,1536]{2,1,0:T(8,128)(2,1)S(1)} %copy-done, ...), custom_call_target="tpu_custom_call" | custom-call | flops 402653184 | bytes 4194304 | tf_op jit(solution)/shard_map/right/pallas_call | solution.py:357
  35.8 2.9 %collective-permute-start.9 = (bf16[2,64,256]{2,1,0:T(8,128)(2,1)S(1)}, bf16[2,64,256]{2,1,0:T(8,128)(2,1)S(1)}, u32[]{:S(2)}, u32[]{:S(2)}) collective-permute-start(bf16[2,64,256]{2,1,0:T(8,128)(2,1)S(1)} %get-tuple-element.60), channel_id=1, source_target_pairs={{0,2},{1,3},{2,0},{3,1},{4,6},{5,7},{6,4},{7,5},{8,10},{9,11},{10,... | collective-permute-start | bytes 196616 | tf_op jit(solution)/shard_map/ppermute | solution.py:20
  38.8 1.4 %collective-permute-start.10 = (bf16[2,64,256]{2,1,0:T(8,128)(2,1)S(1)}, bf16[2,64,256]{2,1,0:T(8,128)(2,1)S(1)}, u32[]{:S(2)}, u32[]{:S(2)}) collective-permute-start(bf16[2,64,256]{2,1,0:T(8,128)(2,1)S(1)} %get-tuple-element.61), channel_id=1, source_target_pairs={{0,3},{1,2},{2,1},{3,0},{4,7},{5,6},{6,5},{7,4},{8,11},{9,10},{10,... | collective-permute-start | bytes 196616 | tf_op jit(solution)/shard_map/ppermute | solution.py:20
  40.1 8.2 %apply.1 = (bf16[2,64,256]{2,1,0:T(8,128)(2,1)S(1)}, bf16[4,64,256]{2,1,0:T(8,128)(2,1)S(1)}, bf16[2,64,256]{2,1,0:T(8,128)(2,1)S(1)}, bf16[2,64,256]{2,1,0:T(8,128)(2,1)S(1)}) custom-call(s32[16]{0:T(128)S(1)} %copy-done.6, s32[16]{0:T(128)S(1)} %copy-done.7, s32[16]{0:T(128)S(1)} %copy-done.4, bf16[8,64,1536]{2,1,0:T(8,128)(2,1)S(1)} %copy-done, ...), custom_call_target="tpu_custom_call" | custom-call | flops 3221225472 | bytes 4194304 | tf_op jit(solution)/shard_map/apply/pallas_call | solution.py:384
  48.3 1.4 %collective-permute-start.12 = (bf16[2,64,256]{2,1,0:T(8,128)(2,1)S(1)}, bf16[2,64,256]{2,1,0:T(8,128)(2,1)S(1)}, u32[]{:S(2)}, u32[]{:S(2)}) collective-permute-start(bf16[2,64,256]{2,1,0:T(8,128)(2,1)S(1)} %get-tuple-element.65), channel_id=1, source_target_pairs={{0,2},{1,3},{2,0},{3,1},{4,6},{5,7},{6,4},{7,5},{8,10},{9,11},{10,... | collective-permute-start | bytes 196616 | tf_op jit(solution)/shard_map/ppermute | solution.py:20
  49.7 1.2 %collective-permute-start.13 = (bf16[2,64,256]{2,1,0:T(8,128)(2,1)S(1)}, bf16[2,64,256]{2,1,0:T(8,128)(2,1)S(1)}, u32[]{:S(2)}, u32[]{:S(2)}) collective-permute-start(bf16[2,64,256]{2,1,0:T(8,128)(2,1)S(1)} %get-tuple-element.66), channel_id=1, source_target_pairs={{0,3},{1,2},{2,1},{3,0},{4,7},{5,6},{6,5},{7,4},{8,11},{9,10},{10,... | collective-permute-start | bytes 196616 | tf_op jit(solution)/shard_map/ppermute | solution.py:20
  50.9 1.0 %collective-permute-start.11 = (bf16[4,64,256]{2,1,0:T(8,128)(2,1)S(1)}, bf16[4,64,256]{2,1,0:T(8,128)(2,1)S(1)}, u32[]{:S(2)}, u32[]{:S(2)}) collective-permute-start(bf16[4,64,256]{2,1,0:T(8,128)(2,1)S(1)} %get-tuple-element.64), channel_id=1, source_target_pairs={{0,1},{1,0},{2,3},{3,2},{4,5},{5,4},{6,7},{7,6},{8,9},{9,8},{10,11... | collective-permute-start | bytes 393224 | tf_op jit(solution)/shard_map/ppermute | solution.py:20
  51.9 1.3 %place.2.refs_0_ = bf16[16,64,256]{2,1,0:T(8,128)(2,1)} custom-call(s32[16]{0:T(128)S(1)} %copy-done.6, bf16[2,64,256]{2,1,0:T(8,128)(2,1)S(1)} %get-tuple-element.59.refs_0_, bf16[2,64,256]{2,1,0:T(8,128)(2,1)S(1)} %collective-permute-done.9.refs_1_, bf16[2,64,256]{2,1,0:T(8,128)(2,1)S(1)} %collective-permute-done.10.refs_2_, ...), custom_call_target="tpu_custom_call" | custom-call | flops 10000000000 | bytes 1048576 | tf_op jit(solution)/shard_map/place/pallas_call | solution.py:418
  53.2 2.4 %collective-permute-done.12.refs_2_ = bf16[2,64,256]{2,1,0:T(8,128)(2,1)S(1)} collective-permute-done((bf16[2,64,256]{2,1,0:T(8,128)(2,1)S(1)}, bf16[2,64,256]{2,1,0:T(8,128)(2,1)S(1)}, u32[]{:S(2)}, u32[]{:S(2)}) %collective-permute-start.12) | collective-permute-done | bytes 65568 | tf_op jit(solution)/shard_map/ppermute | solution.py:20
  55.6 0.8 %collective-permute-done.13.refs_3_ = bf16[2,64,256]{2,1,0:T(8,128)(2,1)S(1)} collective-permute-done((bf16[2,64,256]{2,1,0:T(8,128)(2,1)S(1)}, bf16[2,64,256]{2,1,0:T(8,128)(2,1)S(1)}, u32[]{:S(2)}, u32[]{:S(2)}) %collective-permute-start.13) | collective-permute-done | bytes 65568 | tf_op jit(solution)/shard_map/ppermute | solution.py:20
  56.5 2.2 %collective-permute-done.11.refs_1_ = bf16[4,64,256]{2,1,0:T(8,128)(2,1)S(1)} collective-permute-done((bf16[4,64,256]{2,1,0:T(8,128)(2,1)S(1)}, bf16[4,64,256]{2,1,0:T(8,128)(2,1)S(1)}, u32[]{:S(2)}, u32[]{:S(2)}) %collective-permute-start.11) | collective-permute-done | bytes 131104 | tf_op jit(solution)/shard_map/ppermute | solution.py:20
  58.7 1.3 %place.3 = bf16[16,64,256]{2,1,0:T(8,128)(2,1)} custom-call(s32[16]{0:T(128)S(1)} %copy-done.6, bf16[16,64,256]{2,1,0:T(8,128)(2,1)} %place.2.refs_0_, bf16[4,64,256]{2,1,0:T(8,128)(2,1)S(1)} %collective-permute-done.11.refs_1_, bf16[2,64,256]{2,1,0:T(8,128)(2,1)S(1)} %collective-permute-done.12.refs_2_, ...), custom_call_target="tpu_custom_call", output_to_operand_aliasing={{}: (1, {})} | custom-call | flops 10000000000 | bytes 1048576 | tf_op jit(solution)/shard_map/place/pallas_call | solution.py:418
  (39 shorter events, 2.4 us)
Async XLA Ops:
  0.0 16.2 %copy-start.2 = (bf16[24,24,256]{2,1,0:T(8,128)(2,1)S(1)}, bf16[24,24,256]{2,1,0:T(8,128)(2,1)}, u32[]{:S(2)}) copy-start(bf16[24,24,256]{2,1,0:T(8,128)(2,1)} %mpo_ref) | copy-start | bytes 884740
  0.7 3.1 %copy-start.3 = (s32[16]{0:T(128)}, s32[16]{0:T(128)S(1)}, u32[]{:S(2)}) copy-start(s32[16]{0:T(128)S(1)} %bitcast_or_fusion.key_ref) | copy-start | bytes 196
  0.7 9.9 %collective-permute-start.2 = (s32[16]{0:T(128)S(1)}, s32[16]{0:T(128)S(1)}, u32[]{:S(2)}, u32[]{:S(2)}) collective-permute-start(s32[16]{0:T(128)S(1)} %bitcast_or_fusion.key_ref), channel_id=1, source_target_pairs={{0,12},{4,8},{8,4},{12,0},{1,13},{5,9},{9,5},{13,1},{2,14},{6,10},... | collective-permute-start | bytes 200 | tf_op jit(solution)/shard_map/ppermute | solution.py:20
  3.1 7.5 %collective-permute-start.1 = (s32[16]{0:T(128)S(1)}, s32[16]{0:T(128)S(1)}, u32[]{:S(2)}, u32[]{:S(2)}) collective-permute-start(s32[16]{0:T(128)S(1)} %bitcast_or_fusion.key_ref), channel_id=1, source_target_pairs={{0,8},{4,12},{8,0},{12,4},{1,9},{5,13},{9,1},{13,5},{2,10},{6,14},... | collective-permute-start | bytes 200 | tf_op jit(solution)/shard_map/ppermute | solution.py:20
  3.8 6.9 %collective-permute-start = (s32[16]{0:T(128)S(1)}, s32[16]{0:T(128)S(1)}, u32[]{:S(2)}, u32[]{:S(2)}) collective-permute-start(s32[16]{0:T(128)S(1)} %bitcast_or_fusion.key_ref), channel_id=1, source_target_pairs={{0,4},{4,0},{8,12},{12,8},{1,5},{5,1},{9,13},{13,9},{2,6},{6,2},{1... | collective-permute-start | bytes 200 | tf_op jit(solution)/shard_map/ppermute | solution.py:20
  6.2 18.3 %copy-start.8 = (bf16[4,64,384]{2,1,0:T(8,128)(2,1)S(1)}, bf16[4,64,384]{2,1,0:T(8,128)(2,1)}, u32[]{:S(2)}) copy-start(bf16[4,64,384]{2,1,0:T(8,128)(2,1)} %get-tuple-element.53.refs_0_.refs_3_) | copy-start | bytes 589828
  6.2 15.7 %collective-permute-start.3 = (bf16[4,64,384]{2,1,0:T(8,128)(2,1)}, bf16[4,64,384]{2,1,0:T(8,128)(2,1)S(1)}, u32[]{:S(2)}, u32[]{:S(2)}) collective-permute-start(bf16[4,64,384]{2,1,0:T(8,128)(2,1)} %get-tuple-element.45), channel_id=1, source_target_pairs={{0,1},{1,0},{2,3},{3,2},{4,5},{5,4},{6,7},{7,6},{8,9},{9,8},{10,11... | collective-permute-start | bytes 589832 | tf_op jit(solution)/shard_map/ppermute | solution.py:20
  8.0 16.4 %collective-permute-start.4 = (bf16[4,64,384]{2,1,0:T(8,128)(2,1)}, bf16[4,64,384]{2,1,0:T(8,128)(2,1)S(1)}, u32[]{:S(2)}, u32[]{:S(2)}) collective-permute-start(bf16[4,64,384]{2,1,0:T(8,128)(2,1)} %get-tuple-element.46), channel_id=1, source_target_pairs={{0,2},{1,3},{2,0},{3,1},{4,6},{5,7},{6,4},{7,5},{8,10},{9,11},{10,... | collective-permute-start | bytes 589832 | tf_op jit(solution)/shard_map/ppermute | solution.py:20
  14.5 10.0 %collective-permute-start.5 = (bf16[4,64,384]{2,1,0:T(8,128)(2,1)}, bf16[4,64,384]{2,1,0:T(8,128)(2,1)S(1)}, u32[]{:S(2)}, u32[]{:S(2)}) collective-permute-start(bf16[4,64,384]{2,1,0:T(8,128)(2,1)} %get-tuple-element.47), channel_id=1, source_target_pairs={{0,3},{1,2},{2,1},{3,0},{4,7},{5,6},{6,5},{7,4},{8,11},{9,10},{10,... | collective-permute-start | bytes 589832 | tf_op jit(solution)/shard_map/ppermute | solution.py:20
  14.5 15.4 %collective-permute-start.7 = (bf16[2,64,1536]{2,1,0:T(8,128)(2,1)}, bf16[2,64,1536]{2,1,0:T(8,128)(2,1)S(1)}, u32[]{:S(2)}, u32[]{:S(2)}) collective-permute-start(bf16[2,64,1536]{2,1,0:T(8,128)(2,1)} %get-tuple-element.49), channel_id=1, source_target_pairs={{0,8},{4,12},{8,0},{12,4},{1,9},{5,13},{9,1},{13,5},{2,10},{6,14},... | collective-permute-start | bytes 1179656 | tf_op jit(solution)/shard_map/ppermute | solution.py:20
  16.2 16.6 %collective-permute-start.8 = (bf16[2,64,1536]{2,1,0:T(8,128)(2,1)}, bf16[2,64,1536]{2,1,0:T(8,128)(2,1)S(1)}, u32[]{:S(2)}, u32[]{:S(2)}) collective-permute-start(bf16[2,64,1536]{2,1,0:T(8,128)(2,1)} %get-tuple-element.50), channel_id=1, source_target_pairs={{0,12},{4,8},{8,4},{12,0},{1,13},{5,9},{9,5},{13,1},{2,14},{6,10},... | collective-permute-start | bytes 1179656 | tf_op jit(solution)/shard_map/ppermute | solution.py:20
  16.2 1.6 %copy-start.1 = (bf16[16,64,1024]{2,1,0:T(8,128)(2,1)S(1)}, bf16[16,64,1024]{2,1,0:T(8,128)(2,1)}, u32[]{:S(2)}) copy-start(bf16[16,64,1024]{2,1,0:T(8,128)(2,1)} %state_ref.1) | copy-start | bytes 6291460
  17.8 0.6 %copy-start.5 = (s32[16]{0:T(128)S(1)}, s32[16]{0:T(128)}, u32[]{:S(2)}) copy-start(s32[16]{0:T(128)} %get-tuple-element.36.order_ref) | copy-start | bytes 196
  18.4 6.0 %copy-start.12 = (bf16[2,64,1536]{2,1,0:T(8,128)(2,1)S(1)}, bf16[2,64,1536]{2,1,0:T(8,128)(2,1)}, u32[]{:S(2)}) copy-start(bf16[2,64,1536]{2,1,0:T(8,128)(2,1)} %get-tuple-element.48) | copy-start | bytes 1179652
  24.4 8.4 %collective-permute-start.6 = (bf16[2,64,1536]{2,1,0:T(8,128)(2,1)S(1)}, bf16[2,64,1536]{2,1,0:T(8,128)(2,1)S(1)}, u32[]{:S(2)}, u32[]{:S(2)}) collective-permute-start(bf16[2,64,1536]{2,1,0:T(8,128)(2,1)S(1)} %copy-done.12), channel_id=1, source_target_pairs={{0,4},{4,0},{8,12},{12,8},{1,5},{5,1},{9,13},{13,9},{2,6},{6,2},{1... | collective-permute-start | bytes 1179656 | tf_op jit(solution)/shard_map/ppermute | solution.py:20
  24.5 8.4 %copy-start = (bf16[8,64,1536]{2,1,0:T(8,128)(2,1)S(1)}, bf16[8,64,1536]{2,1,0:T(8,128)(2,1)}, u32[]{:S(2)}) copy-start(bf16[8,64,1536]{2,1,0:T(8,128)(2,1)} %env_ref.5) | copy-start | bytes 4718596
  24.5 8.4 %copy-start.4 = (s32[16]{0:T(128)S(1)}, s32[16]{0:T(128)}, u32[]{:S(2)}) copy-start(s32[16]{0:T(128)} %copy-done.3) | copy-start | bytes 196
  24.5 8.4 %copy-start.6 = (s32[16]{0:T(128)S(1)}, s32[16]{0:T(128)}, u32[]{:S(2)}) copy-start(s32[16]{0:T(128)} %get-tuple-element.36.order_ref) | copy-start | bytes 196
  24.5 8.4 %copy-start.7 = (s32[16]{0:T(128)S(1)}, s32[16]{0:T(128)}, u32[]{:S(2)}) copy-start(s32[16]{0:T(128)} %get-tuple-element.37.slot_ref) | copy-start | bytes 196
  35.8 16.1 %collective-permute-start.9 = (bf16[2,64,256]{2,1,0:T(8,128)(2,1)S(1)}, bf16[2,64,256]{2,1,0:T(8,128)(2,1)S(1)}, u32[]{:S(2)}, u32[]{:S(2)}) collective-permute-start(bf16[2,64,256]{2,1,0:T(8,128)(2,1)S(1)} %get-tuple-element.60), channel_id=1, source_target_pairs={{0,2},{1,3},{2,0},{3,1},{4,6},{5,7},{6,4},{7,5},{8,10},{9,11},{10,... | collective-permute-start | bytes 196616 | tf_op jit(solution)/shard_map/ppermute | solution.py:20
  38.8 13.1 %collective-permute-start.10 = (bf16[2,64,256]{2,1,0:T(8,128)(2,1)S(1)}, bf16[2,64,256]{2,1,0:T(8,128)(2,1)S(1)}, u32[]{:S(2)}, u32[]{:S(2)}) collective-permute-start(bf16[2,64,256]{2,1,0:T(8,128)(2,1)S(1)} %get-tuple-element.61), channel_id=1, source_target_pairs={{0,3},{1,2},{2,1},{3,0},{4,7},{5,6},{6,5},{7,4},{8,11},{9,10},{10,... | collective-permute-start | bytes 196616 | tf_op jit(solution)/shard_map/ppermute | solution.py:20
  48.3 7.3 %collective-permute-start.12 = (bf16[2,64,256]{2,1,0:T(8,128)(2,1)S(1)}, bf16[2,64,256]{2,1,0:T(8,128)(2,1)S(1)}, u32[]{:S(2)}, u32[]{:S(2)}) collective-permute-start(bf16[2,64,256]{2,1,0:T(8,128)(2,1)S(1)} %get-tuple-element.65), channel_id=1, source_target_pairs={{0,2},{1,3},{2,0},{3,1},{4,6},{5,7},{6,4},{7,5},{8,10},{9,11},{10,... | collective-permute-start | bytes 196616 | tf_op jit(solution)/shard_map/ppermute | solution.py:20
  49.7 6.8 %collective-permute-start.13 = (bf16[2,64,256]{2,1,0:T(8,128)(2,1)S(1)}, bf16[2,64,256]{2,1,0:T(8,128)(2,1)S(1)}, u32[]{:S(2)}, u32[]{:S(2)}) collective-permute-start(bf16[2,64,256]{2,1,0:T(8,128)(2,1)S(1)} %get-tuple-element.66), channel_id=1, source_target_pairs={{0,3},{1,2},{2,1},{3,0},{4,7},{5,6},{6,5},{7,4},{8,11},{9,10},{10,... | collective-permute-start | bytes 196616 | tf_op jit(solution)/shard_map/ppermute | solution.py:20
  50.9 7.8 %collective-permute-start.11 = (bf16[4,64,256]{2,1,0:T(8,128)(2,1)S(1)}, bf16[4,64,256]{2,1,0:T(8,128)(2,1)S(1)}, u32[]{:S(2)}, u32[]{:S(2)}) collective-permute-start(bf16[4,64,256]{2,1,0:T(8,128)(2,1)S(1)} %get-tuple-element.64), channel_id=1, source_target_pairs={{0,1},{1,0},{2,3},{3,2},{4,5},{5,4},{6,7},{7,6},{8,9},{9,8},{10,11... | collective-permute-start | bytes 393224 | tf_op jit(solution)/shard_map/ppermute | solution.py:20
  (3 other events, 1.6 us)
